TPU v7x, 32 devices: a whole 2x2x4 slice. The times are simulated.
32 devices in a mesh: dp: 8 (over y, x, core), tensor: 4 (over z).
Axes of the slice: x: 2, y: 2, z: 4, core: 2. Of those that a mesh axis runs over, the one named last changes fastest.
Arguments:
- tokens: bfloat16 [8192, 768], P('dp'), may hold values from -6 to 6
- segments: int32 [8, 1024], P('dp'), may hold values from 0 to 3, as said below
- routes: int32 [8192, 2], P('dp'), may hold values from 0 to 3, all different within a row; in each aligned block of 1024 rows (0 to 1023, 1024 to 2047, ...) at most 704 rows name the same one
- grad_out: bfloat16 [8192, 768], P('dp'), may hold values from -6 to 6
- gain_attn: bfloat16 [768], replicated, may hold values from 0.5 to 1.5
- w_qkv: bfloat16 [3, 768, 768], P(None, None, 'tensor'), may hold values from -0.21875 to 0.21875
- w_out: bfloat16 [768, 768], P('tensor'), may hold values from -0.875 to 0.875
- rel_bias: bfloat16 [32, 12], P(None, 'tensor'), may hold values from -4 to 4
- gain_moe: bfloat16 [768], replicated, may hold values from 0.5 to 1.5
- w_router: bfloat16 [768, 4], replicated, may hold values from -0.15625 to 0.15625
- w_in: bfloat16 [4, 768, 3072], P(None, None, 'tensor'), may hold values from -0.21875 to 0.21875
- w_down: bfloat16 [4, 3072, 768], P(None, 'tensor'), may hold values from -0.15625 to 0.15625
Outputs:
- result: bfloat16 [8192, 768], P('dp')
- grad_tokens: float32 [8192, 768], P('dp')
- grad_gain_attn: float32 [768], replicated
- grad_w_qkv: float32 [3, 768, 768], P(None, None, 'tensor')
- grad_w_out: float32 [768, 768], P('tensor')
- grad_rel_bias: float32 [32, 12], P(None, 'tensor')
- grad_gain_moe: float32 [768], replicated
- grad_w_router: float32 [768, 4], replicated
- grad_w_in: float32 [4, 768, 3072], P(None, None, 'tensor')
- grad_w_down: float32 [4, 3072, 768], P(None, 'tensor')
Inputs may be any that keep to these rules, and one draw needn't show every extreme that they name: `routes`: the two experts of a token differ. Among the 1024 rows of one index of dp no expert is named more than 704 times, a bound that some block reaches. `segments`: document numbers start at 0 and rise by one at each document's end; a sequence holds 2 to 4 documents, each of 204 positions or more.
All inputs are finite; a program needn't handle non-finite values.
Results may differ from a plain program's by a relative error of at most 0.017.
Values may be sent and summed in bfloat16 or wider, within the bound.
No kernel may reach another device: no remote copies, remote signals or barrier semaphores. Data moves between devices by JAX's collectives and lax.ppermute only.
A program may use at most 192 MiB of HBM per device.

v0:
```python
import functools
import math

import jax
import jax.numpy as jnp
import numpy as np
from jax import lax
from jax.experimental import pallas as pl
from jax.experimental.pallas import tpu as pltpu
from jax.sharding import PartitionSpec as P

NB = 32
DIST = 128
EPSILON = 1e-06
NEGATIVE = -1e30
HIGHEST = lax.Precision.HIGHEST
F32 = jnp.float32
BF16 = jnp.bfloat16
BLK = 256
LANES = 128
VMEM_LIMIT = 56 * 1024 * 1024

NN = (((1,), (0,)), ((), ()))
NT = (((1,), (1,)), ((), ()))
TN = (((0,), (0,)), ((), ()))


def dot(a, b, dims=NN, precision=None):
    return lax.dot_general(a, b, dims, precision=precision, preferred_element_type=F32)


def bucket_of(distance):
    halfway = NB // 2
    thresholds = [
        int(math.ceil(halfway * (DIST / halfway) ** (step / halfway))) for step in range(halfway)
    ]
    beyond = sum((distance >= threshold).astype(np.int64) for threshold in thresholds)
    return np.where(distance < halfway, distance, halfway - 1 + beyond)


def near_tables():
    lanes = np.arange(2 * BLK)
    offset = np.where(lanes < BLK, lanes, lanes - 2 * BLK)
    build = np.stack([np.maximum(offset, 0), np.maximum(BLK + offset, 0)])
    gather = np.stack([lanes - (BLK - 1), lanes + 1])
    eye = np.eye(NB, dtype=np.float32)
    build_hot = eye[bucket_of(build)]
    gather_hot = eye[bucket_of(np.maximum(gather, 0))] * (gather >= 0)[..., None]
    return build_hot, gather_hot


def row_scale(values):
    return lax.rsqrt(jnp.mean(values * values, axis=-1, keepdims=True) + EPSILON)


def lane_pick(values, index):
    lanes = lax.broadcasted_iota(jnp.int32, values.shape, 1)
    return jnp.sum(jnp.where(lanes == index, values, 0.0), axis=1, keepdims=True)


def masked_scores(k_tile, qh_tile, bias, seg_k, seg_q, diagonal):
    scores = dot(k_tile, qh_tile, NT) + bias
    allowed = seg_k == seg_q
    if diagonal:
        key_at = lax.broadcasted_iota(jnp.int32, scores.shape, 0)
        query_at = lax.broadcasted_iota(jnp.int32, scores.shape, 1)
        allowed = allowed & (key_at <= query_at)
    return jnp.where(allowed, scores, NEGATIVE)


def tile_bias(bias_ref, far_ref, head, delta):
    if delta < 2:
        return bias_ref[2 * head + delta]
    return far_ref[pl.ds(head, 1), 0:1]


def column_of(row):
    spread = jnp.broadcast_to(row.astype(F32), (8, row.shape[1]))
    return spread.T[:, 0:1]


def attn_fwd_kernel(piece, pieces, heads, head_size, *refs):
    tok, gain, w, seg = refs[:4]
    refs = refs[4:]
    if piece == 0:
        rel, build = refs[:2]
        refs = refs[2:]
    else:
        bias, far = refs[:2]
        refs = refs[2:]
    old_k, refs = refs[:piece], refs[piece:]
    old_vt, refs = refs[:piece], refs[piece:]
    normed, qh, k, v, vt, att, ot, lse = refs[:8]
    if piece == 0:
        bias, far = refs[8:]
    keys_of, vt_of = [*old_k, k], [*old_vt, vt]
    rows_total = tok.shape[0] // pieces
    base = piece * rows_total
    features = w.shape[1]
    blocks = rows_total // BLK
    gain_row = gain[...].astype(F32)
    lanes = lax.broadcasted_iota(jnp.int32, (BLK, features), 1)
    for block in range(blocks):
        rows = pl.ds(block * BLK, BLK)
        x = tok[pl.ds(base + block * BLK, BLK), :].astype(F32)
        n = (x * row_scale(x) * gain_row).astype(BF16)
        normed[rows, :] = n
        q_rows = dot(n, w[0], NT).astype(BF16).astype(F32) * (head_size**-0.5)
        for head in range(heads):
            inside = (lanes >= head * head_size) & (lanes < (head + 1) * head_size)
            qh[head, rows, :] = jnp.where(inside, q_rows, 0.0).astype(BF16)
        k[rows, :] = dot(n, w[1], NT).astype(BF16)
        v_rows = dot(n, w[2], NT).astype(BF16)
        v[rows, :] = v_rows
        vt[:, rows] = v_rows.astype(F32).T.astype(BF16)
    if piece == 0:
        far[...] = jnp.zeros_like(far)
        far[0:heads, :] = jnp.broadcast_to(rel[:, NB - 1 : NB].astype(F32), (heads, LANES))
        for delta in range(2):
            near = dot(rel[...], build[delta])
            for head in range(heads):
                spread = jnp.broadcast_to(near[head : head + 1, :], (BLK, 2 * BLK))
                turned = pltpu.roll(spread, 0, 1, stride=1, stride_axis=0)
                bias[2 * head + delta] = turned[:, :BLK]
    lse[...] = jnp.zeros_like(lse)
    seg_row = seg[...].astype(F32)
    seg_col = column_of(seg[...])

    def one_head(head, carry):
        part = pl.ds(pl.multiple_of(head * head_size, head_size), head_size)
        for block in range(blocks):
            qb = piece * blocks + block
            cols = pl.ds(block * BLK, BLK)
            q_tile = qh[head, cols, :]
            tiles = []
            for kb in range(qb + 1):
                keys = pl.ds(kb % blocks * BLK, BLK)
                tiles.append(
                    masked_scores(
                        keys_of[kb // blocks][keys, :], q_tile,
                        tile_bias(bias, far, head, qb - kb),
                        seg_col[kb * BLK : (kb + 1) * BLK, :],
                        seg_row[:, qb * BLK : (qb + 1) * BLK], kb == qb,
                    )
                )
            peak = functools.reduce(
                jnp.maximum, [jnp.max(t, axis=0, keepdims=True) for t in tiles]
            )
            total = jnp.zeros((1, BLK), F32)
            out = jnp.zeros((head_size, BLK), F32)
            for kb in range(qb + 1):
                raised = jnp.exp(tiles[kb] - peak)
                total = total + jnp.sum(raised, axis=0, keepdims=True)
                values = vt_of[kb // blocks][part, pl.ds(kb % blocks * BLK, BLK)]
                out = out + dot(values, raised.astype(BF16))
            ot[part, cols] = out / total
            lse[pl.ds(head, 1), cols] = peak + jnp.log(total)
        return carry

    lax.fori_loop(0, heads, one_head, 0)
    for block in range(blocks):
        cols = pl.ds(block * BLK, BLK)
        att[cols, :] = ot[:, cols].T.astype(BF16)


def attn_bwd_kernel(piece, pieces, heads, head_size, shares, idx, *refs):
    held = piece + 1
    last = held == pieces
    go_parts, refs = refs[:shares], refs[shares:]
    qh, ot, lse = refs[:3]
    refs = refs[3:]
    ks, refs = refs[:held], refs[held:]
    vs, refs = refs[:held], refs[held:]
    bias, far, seg = refs[:3]
    refs = refs[3:]
    if piece:
        gk_in, refs = refs[:piece], refs[piece:]
        gv_in, refs = refs[:piece], refs[piece:]
        gq_in, refs = refs[:piece], refs[piece:]
        acc_in, refs = refs[0], refs[1:]
    if last:
        w, hot = refs[:2]
        refs = refs[2:]
        gn_parts, refs = refs[:shares], refs[shares:]
        gproj, rel_out = refs[:2]
        refs = refs[2:]
        gk, refs = refs[:held], refs[held:]
        gv, refs = refs[:held], refs[held:]
        gq_t, acc = refs[:2]
        refs = refs[2:]
    else:
        gk, refs = refs[:held], refs[held:]
        gv, refs = refs[:held], refs[held:]
        gq_t, acc = refs[:2]
        refs = refs[2:]
    go, kt, d_row, near_sum, far_sum = refs
    rows_total, features = ks[0].shape
    blocks = rows_total // BLK
    share = rows_total // shares
    me = idx[0]
    for step in range(shares):
        start = pl.multiple_of((me ^ step) * share, share)
        go[pl.ds(start, share), :] = go_parts[step][...]
    for index in range(held):
        for block in range(blocks):
            cols = pl.ds(block * BLK, BLK)
            kt[:, pl.ds((index * blocks + block) * BLK, BLK)] = (
                ks[index][cols, :].astype(F32).T.astype(BF16)
            )
        if index < piece:
            gk[index][...] = gk_in[index][...]
            gv[index][...] = gv_in[index][...]
        else:
            gk[index][...] = jnp.zeros_like(gk[index])
            gv[index][...] = jnp.zeros_like(gv[index])
    if piece:
        acc[...] = acc_in[...]
    else:
        acc[...] = jnp.zeros_like(acc)
    for block in range(blocks):
        cols = pl.ds(block * BLK, BLK)
        product = go[cols, :].astype(F32).T * ot[:, cols]
        for head in range(heads):
            part = product[head * head_size : (head + 1) * head_size, :]
            d_row[head : head + 1, cols] = jnp.sum(part, axis=0, keepdims=True)
    near_sum[...] = jnp.zeros_like(near_sum)
    far_sum[...] = jnp.zeros_like(far_sum)
    key_at = lax.broadcasted_iota(jnp.int32, (BLK, BLK), 0)
    other_at = lax.broadcasted_iota(jnp.int32, (BLK, BLK), 1)
    flip = (key_at + other_at == BLK - 1).astype(F32)
    seg_row = seg[...].astype(F32)
    seg_col = column_of(seg[...])

    def one_head(head, carry):
        part = pl.ds(pl.multiple_of(head * head_size, head_size), head_size)
        lanes = lax.broadcasted_iota(jnp.int32, (BLK, features), 1)
        inside = (lanes >= head * head_size) & (lanes < (head + 1) * head_size)
        for block in range(blocks):
            qb = piece * blocks + block
            cols = pl.ds(block * BLK, BLK)
            q_tile = qh[head, cols, :]
            go_tile = jnp.where(inside, go[cols, :].astype(F32), 0.0).astype(BF16)
            log_total = lse[pl.ds(head, 1), cols]
            d_tile = d_row[pl.ds(head, 1), cols]
            gq = jnp.zeros((head_size, BLK), F32)
            for kb in range(qb + 1):
                index = kb // blocks
                keys = pl.ds(kb % blocks * BLK, BLK)
                delta = qb - kb
                scores = masked_scores(
                    ks[index][keys, :], q_tile, tile_bias(bias, far, head, delta),
                    seg_col[kb * BLK : (kb + 1) * BLK, :],
                    seg_row[:, qb * BLK : (qb + 1) * BLK], delta == 0,
                )
                probs = jnp.exp(scores - log_total)
                gs = probs * (dot(vs[index][keys, :], go_tile, NT) - d_tile)
                if delta < 2:
                    acc[2 * head + delta] += gs
                else:
                    far_sum[pl.ds(head, 1), :] += jnp.sum(gs, axis=0, keepdims=True)
                gs_low = gs.astype(BF16)
                gv[index][keys, :] += dot(probs.astype(BF16), go_tile)
                gk[index][keys, :] += dot(gs_low, q_tile)
                gq = gq + dot(kt[part, kb * BLK : (kb + 1) * BLK], gs_low)
            gq_t[part, cols] = gq * (head_size**-0.5)
        return carry

    lax.fori_loop(0, heads, one_head, 0)
    if not last:
        return
    gqs = [*(gq_in if piece else ()), gq_t]
    for index in range(held):
        for block in range(blocks):
            rows = pl.ds(block * BLK, BLK)
            out = pl.ds((index * blocks + block) * BLK, BLK)
            gproj[0, out, :] = gqs[index][:, rows].T.astype(BF16)
            gproj[1, out, :] = gk[index][rows, :].astype(BF16)
            gproj[2, out, :] = gv[index][rows, :].astype(BF16)
    for step in range(shares):
        for index in range(pieces):
            start = index * rows_total + (me ^ step) * share
            rows = pl.ds(pl.multiple_of(start, share), share)
            total = dot(gproj[0, rows, :], w[0])
            total = total + dot(gproj[1, rows, :], w[1])
            total = total + dot(gproj[2, rows, :], w[2])
            gn_parts[step][pl.ds(index * share, share), :] = total.astype(BF16)
    for head in range(heads):
        for delta in range(2):
            turned = dot(flip, acc[2 * head + delta], NN, HIGHEST)
            wide = jnp.concatenate([turned, jnp.zeros_like(turned)], axis=1)
            sheared = pltpu.roll(wide, 0, 1, stride=1, stride_axis=0)
            near_sum[delta, head : head + 1, :] = jnp.sum(sheared, axis=0, keepdims=True)
    summed = dot(near_sum[0], hot[0], NN, HIGHEST) + dot(near_sum[1], hot[1], NN, HIGHEST)
    buckets = lax.broadcasted_iota(jnp.int32, summed.shape, 1)
    beyond = jnp.sum(far_sum[...], axis=1, keepdims=True)
    rel_out[...] = summed + jnp.where(buckets == NB - 1, beyond, 0.0)


def qkv_weights_kernel(pieces, *refs):
    normed = refs[:pieces]
    gproj, out = refs[pieces:]
    rows_total = normed[0].shape[0]
    for c in range(3):
        total = dot(gproj[c, pl.ds(0, rows_total), :], normed[0][...], TN)
        for index in range(1, pieces):
            rows = pl.ds(index * rows_total, rows_total)
            total = total + dot(gproj[c, rows, :], normed[index][...], TN)
        out[c] = total.astype(BF16)


def gelu_pair(values):
    squared = values * values
    bent = jnp.tanh(values * (0.7978845608028654 + 0.7978845608028654 * 0.044715 * squared))
    half = 0.5 * (1.0 + bent)
    lifted = values * half
    slope = 0.7978845608028654 + 3.0 * 0.7978845608028654 * 0.044715 * squared
    return lifted, half + lifted * (1.0 - bent) * slope


def padded_rows(values, rows):
    missing = jnp.zeros((rows - values.shape[0], values.shape[1]), values.dtype)
    return jnp.concatenate([values, missing], axis=0)


def moe_fwd_kernel(piece, pieces, shares, experts, idx, *refs):
    att, refs = refs[:shares], refs[shares:]
    if piece == 0:
        wo_own, wo_swapped, refs = refs[0], refs[1], refs[2:]
        wo_fetched, refs = refs[: shares - 1], refs[shares - 1 :]
    else:
        wo, refs = refs[0], refs[1:]
    tok, gain, router, routes, cot, w_in, w_down = refs[:7]
    refs = refs[7:]
    parts, refs = refs[:shares], refs[shares:]
    if piece == 0:
        wo, refs = refs[0], refs[1:]
    normed, own, gates, ggate, act, slope, acc = refs
    rows_total = tok.shape[0] // pieces
    base = piece * rows_total
    share = rows_total // shares
    me = idx[0]
    expert = pl.program_id(0)

    @pl.when(expert == 0)
    def _():
        gain_row = gain[...].astype(F32)
        router_wide = padded_rows(router[...].astype(F32), LANES).astype(BF16)
        if piece == 0:
            half = wo_own.shape[0] // 2
            mine = pl.ds(pl.multiple_of(idx[1] * half, half), half)
            other = pl.ds(pl.multiple_of((1 - idx[1]) * half, half), half)
            wo[0] = wo_own[...]
            for step in range(1, shares):
                wo[step, mine, :] = wo_fetched[step - 1][...]
                wo[step, other, :] = wo_swapped[step - 1]
        for block in range(rows_total // BLK):
            rows = pl.ds(block * BLK, BLK)
            outer = pl.ds(base + block * BLK, BLK)
            attn = dot(att[0][rows, :], wo[0])
            for step in range(1, shares):
                attn = attn + dot(att[step][rows, :], wo[step])
            hidden = tok[outer, :].astype(F32) + attn
            acc[rows, :] = hidden
            n = (hidden * row_scale(hidden) * gain_row).astype(BF16)
            normed[rows, :] = n
            logits = dot(n, router_wide, NT)
            lanes = lax.broadcasted_iota(jnp.int32, logits.shape, 1)
            first = lanes == routes[outer, 0:1]
            second = lanes == routes[outer, 1:2]
            one = jnp.sum(jnp.where(first, logits, 0.0), axis=1, keepdims=True)
            two = jnp.sum(jnp.where(second, logits, 0.0), axis=1, keepdims=True)
            peak = jnp.maximum(one, two)
            one = jnp.exp(one - peak)
            two = jnp.exp(two - peak)
            both = one + two
            gates[rows, :] = jnp.where(first, one / both, jnp.where(second, two / both, 0.0))
        own[...] = acc[pl.ds(pl.multiple_of(me * share, share), share), :]
        acc[...] = jnp.zeros_like(acc)
        ggate[...] = jnp.zeros_like(ggate)

    for block in range(rows_total // ROWS):
        rows = pl.ds(block * ROWS, ROWS)
        outer = pl.ds(base + block * ROWS, ROWS)
        lifted, bend = gelu_pair(dot(normed[rows, :], w_in[0]))
        lifted = lifted.astype(BF16)
        act[0, rows, :] = lifted
        slope[0, rows, :] = bend.astype(BF16)
        out = dot(lifted, w_down[0])
        gate = lane_pick(gates[rows, :], expert)
        acc[rows, :] += gate * out
        pulled = jnp.sum(cot[outer, :].astype(F32) * out, axis=1, keepdims=True)
        held = ggate[rows, :]
        lanes = lax.broadcasted_iota(jnp.int32, held.shape, 1)
        ggate[rows, :] = jnp.where(lanes == expert, pulled, held)

    @pl.when(expert == experts - 1)
    def _():
        for step in range(shares):
            start = pl.multiple_of((me ^ step) * share, share)
            parts[step][...] = acc[pl.ds(start, share), :].astype(BF16)


def moe_bwd_kernel(piece, shares, experts, idx, *refs):
    gates, ggate, cot, slope, router, w_in, w_down = refs[:7]
    refs = refs[7:]
    parts, refs = refs[:shares], refs[shares:]
    glog, gpre, acc = refs
    rows_total = gates.shape[0]
    base = piece * rows_total
    share = rows_total // shares
    me = idx[0]
    expert = pl.program_id(0)

    @pl.when(expert == 0)
    def _():
        router_wide = padded_rows(router[...].astype(F32), LANES)
        for block in range(rows_total // ROWS):
            rows = pl.ds(block * ROWS, ROWS)
            g, gg = gates[rows, :], ggate[rows, :]
            back = g * (gg - jnp.sum(g * gg, axis=1, keepdims=True))
            glog[rows, :] = back
            acc[rows, :] = dot(back, router_wide, NN, HIGHEST)

    for block in range(rows_total // ROWS):
        rows = pl.ds(block * ROWS, ROWS)
        gate = lane_pick(gates[rows, :], expert)
        weighted = cot[pl.ds(base + block * ROWS, ROWS), :].astype(F32)
        weighted = (gate * weighted).astype(BF16)
        gp = (dot(weighted, w_down[0], NT) * slope[0, rows, :].astype(F32)).astype(BF16)
        gpre[0, rows, :] = gp
        acc[rows, :] += dot(gp, w_in[0], NT)

    @pl.when(expert == experts - 1)
    def _():
        for step in range(shares):
            start = pl.multiple_of((me ^ step) * share, share)
            parts[step][...] = acc[pl.ds(start, share), :].astype(BF16)


def moe_weights_kernel(pieces, cot, *refs):
    gates, refs = refs[:pieces], refs[pieces:]
    glog, refs = refs[:pieces], refs[pieces:]
    normed, refs = refs[:pieces], refs[pieces:]
    act, refs = refs[:pieces], refs[pieces:]
    gpre, refs = refs[:pieces], refs[pieces:]
    out, router = refs
    rows_total = normed[0].shape[0]
    expert = pl.program_id(0)

    @pl.when(expert == 0)
    def _():
        total = jnp.zeros((LANES, cot.shape[1]), F32)
        for index in range(pieces):
            back = glog[index][...]
            high = back.astype(BF16)
            low = (back - high.astype(F32)).astype(BF16)
            total = total + dot(high, normed[index][...], TN)
            total = total + dot(low, normed[index][...], TN)
        router[...] = total[0:8, :]

    grad_in = jnp.zeros((normed[0].shape[1], gpre[0].shape[2]), F32)
    grad_down = jnp.zeros((act[0].shape[2], cot.shape[1]), F32)
    for index in range(pieces):
        gate = lane_pick(gates[index][...], expert)
        weighted = cot[pl.ds(index * rows_total, rows_total), :].astype(F32)
        weighted = (gate * weighted).astype(BF16)
        grad_in = grad_in + dot(normed[index][...], gpre[index][0], TN)
        grad_down = grad_down + dot(act[index][0], weighted, TN)
    out[0, 0] = grad_in.astype(BF16)
    out[0, 1] = grad_down.astype(BF16)


def hidden_back_kernel(piece, pieces, shares, got, idx, *refs):
    gx, refs = refs[:got], refs[got:]
    wo, own, cot, gain = refs[:4]
    refs = refs[4:]
    ga, refs = refs[:shares], refs[shares:]
    gh, gh_low, ggain = refs
    share = own.shape[0]
    grad = gx[0][...].astype(F32)
    for step in range(1, got):
        grad = grad + gx[step][...].astype(F32)
    hidden = own[...]
    scale = row_scale(hidden)
    unit = hidden * scale
    ggain[...] = jnp.sum(grad * unit, axis=0, keepdims=True)
    gained = grad * gain[...].astype(F32)
    start = piece * (cot.shape[0] // pieces) + idx[0] * share
    mine = cot[pl.ds(pl.multiple_of(start, share), share), :].astype(F32)
    back = mine + scale * (gained - unit * jnp.mean(gained * unit, axis=-1, keepdims=True))
    gh[...] = back
    low = back.astype(BF16)
    gh_low[...] = low
    for step in range(shares):
        ga[step][...] = dot(low, wo[step], NT).astype(BF16)


def w_out_back_kernel(pieces, shares, idx, *refs):
    att, refs = refs[: pieces * shares], refs[pieces * shares :]
    gh_low, out = refs[:pieces], refs[pieces]
    share = gh_low[0].shape[0]
    rows = pl.ds(pl.multiple_of(idx[0] * share, share), share)
    for step in range(shares):
        total = dot(att[step][rows, :], gh_low[0][...], TN)
        for index in range(1, pieces):
            total = total + dot(att[index * shares + step][rows, :], gh_low[index][...], TN)
        out[step] = total.astype(BF16)


def join_kernel(pieces, count, *refs):
    own, refs = refs[:pieces], refs[pieces:]
    got, out = refs[: pieces * count], refs[pieces * count]
    share = own[0].shape[0]
    for index in range(pieces):
        total = own[index][...]
        for step in range(count):
            total = total + got[index * count + step][...].astype(F32)
        out[pl.ds(index * share, share), :] = total.astype(BF16)


def input_back_kernel(pieces, got, idx, *refs):
    gn, refs = refs[:got], refs[got:]
    ghs, refs = refs[:pieces], refs[pieces:]
    tok, gain, gt, ggain = refs
    share = ghs[0].shape[0]
    gain_row = gain[...].astype(F32)
    total = jnp.zeros_like(ggain)
    for index in range(pieces):
        rows = pl.ds(index * share, share)
        grad = gn[0][rows, :].astype(F32)
        for step in range(1, got):
            grad = grad + gn[step][rows, :].astype(F32)
        start = index * (tok.shape[0] // pieces) + idx[0] * share
        x = tok[pl.ds(pl.multiple_of(start, share), share), :].astype(F32)
        scale = row_scale(x)
        unit = x * scale
        total = total + jnp.sum(grad * unit, axis=0, keepdims=True)
        gained = grad * gain_row
        back = scale * (gained - unit * jnp.mean(gained * unit, axis=-1, keepdims=True))
        gt[rows, :] = (ghs[index][...] + back).astype(BF16)
    ggain[...] = total


def place_kernel(pieces, shares, idx, *refs):
    blocks, out = refs[:shares], refs[shares]
    rows_total = out.shape[0] // pieces
    share = rows_total // shares
    for step in range(shares):
        owner = idx[0] ^ step
        for index in range(pieces):
            start = pl.multiple_of(index * rows_total + owner * share, share)
            got = blocks[step][pl.ds(index * share, share), :]
            out[pl.ds(start, share), :] = got.astype(out.dtype)


ROWS = 512
PIECES = 2

SMEM = pl.BlockSpec(memory_space=pltpu.SMEM)
VMEM = pl.BlockSpec(memory_space=pltpu.VMEM)


def shaped(shape, dtype):
    return jax.ShapeDtypeStruct(shape, dtype)


def whole_call(kernel, outs, args, scratch=(), flops=0, moved=0, with_index=True):
    specs = ([SMEM] if with_index else []) + [VMEM] * (len(args) - (1 if with_index else 0))
    return pl.pallas_call(
        kernel,
        out_shape=outs,
        in_specs=specs,
        out_specs=[VMEM] * len(outs),
        scratch_shapes=list(scratch),
        compiler_params=pltpu.CompilerParams(vmem_limit_bytes=VMEM_LIMIT),
        cost_estimate=pl.CostEstimate(flops=flops, bytes_accessed=moved, transcendentals=0),
    )(*args)


def swap(value, axis, bit):
    count = lax.axis_size(axis)
    return lax.ppermute(value, axis, [(i, i ^ bit) for i in range(count)])


def sum_over(value, axis):
    bit = 1
    while bit < lax.axis_size(axis):
        value = value + swap(value, axis, bit)
        bit *= 2
    return value


def gather_parts(value, axis):
    count = lax.axis_size(axis)
    if count != 4:
        return [value] + [swap(value, axis, bit) for bit in range(1, count)]
    two = swap(value, axis, 2)
    one = swap(value, axis, 1)
    return [value, one, two, swap(two, axis, 1)]


def reduce_parts(parts, axis):
    count = lax.axis_size(axis)
    if count != 4:
        return [parts[0]] + [swap(parts[bit], axis, bit) for bit in range(1, count)]
    near = swap(parts[3], axis, 1)
    pair = (parts[2].astype(F32) + near.astype(F32)).astype(parts[2].dtype)
    return [parts[0], swap(parts[1], axis, 1), swap(pair, axis, 2)]


def halves_of(value, axis, chosen):
    half = value.shape[axis] // 2
    keep = lax.dynamic_slice_in_dim(value, chosen * half, half, axis)
    send = lax.dynamic_slice_in_dim(value, (1 - chosen) * half, half, axis)
    return keep, send


def bits_of(axis):
    count = lax.axis_size(axis)
    return [1 << level for level in range(count.bit_length() - 1)]


def scatter_sum(value, mesh_axis, axis):
    me = lax.axis_index(mesh_axis)
    for bit in bits_of(mesh_axis):
        keep, send = halves_of(value, axis, (me // bit) % 2)
        got = swap(send, mesh_axis, bit)
        value = (keep.astype(F32) + got.astype(F32)).astype(value.dtype)
    return value


def after(value, *others):
    return lax.optimization_barrier((value, *others))[0]


def body(
    tokens, segments, routes, grad_out, gain_attn, w_qkv, w_out, rel_bias,
    gain_moe, w_router, w_in, w_down,
):
    tok_rows, width = tokens.shape
    heads = rel_bias.shape[1]
    features = w_qkv.shape[2]
    head_size = features // heads
    experts, _, hidden_units = w_in.shape
    shares = lax.axis_size("tensor")
    rows = tok_rows // PIECES
    share = rows // shares
    me = lax.axis_index("tensor").astype(jnp.int32)
    side = (lax.axis_index("dp") % 2).astype(jnp.int32)
    idx = jnp.stack([me, side])
    mib = 1 << 20
    others = range(1, shares)

    build_hot, gather_hot = near_tables()
    build_hot = jnp.asarray(np.swapaxes(build_hot, 1, 2), BF16)
    gather_hot = jnp.asarray(gather_hot, F32)
    w_qkv_t = jnp.swapaxes(w_qkv, 1, 2)
    router_t = w_router.T
    gain_one = gain_attn.reshape(1, width)
    gain_two = gain_moe.reshape(1, width)

    def attend(piece, bias_args, old_k, old_vt):
        outs = [
            shaped((rows, width), BF16),
            shaped((heads, rows, features), BF16),
            shaped((rows, features), BF16),
            shaped((rows, features), BF16),
            shaped((features, rows), BF16),
            shaped((rows, features), BF16),
            shaped((features, rows), F32),
            shaped((8, rows), F32),
        ]
        if piece == 0:
            outs += [shaped((2 * heads, BLK, BLK), F32), shaped((8, LANES), F32)]
        return whole_call(
            functools.partial(attn_fwd_kernel, piece, PIECES, heads, head_size),
            outs,
            [tokens, gain_one, w_qkv_t, segments, *bias_args, *old_k, *old_vt],
            flops=3 * 10**9, moved=8 * mib, with_index=False,
        )

    stages = []
    bias_args = [rel_bias.T, build_hot]
    for piece in range(PIECES):
        got = attend(piece, bias_args, [s[2] for s in stages], [s[4] for s in stages])
        if piece == 0:
            bias_args = got[8:]
        stages.append(got[:8])
    bias, far = bias_args
    normed_one = [s[0] for s in stages]

    half_rows = features // 2
    my_half = lax.dynamic_slice_in_dim(w_out, side * half_rows, half_rows, 0)
    my_half = after(my_half, stages[0][5])
    halves = [swap(my_half, "tensor", by) for by in others]
    swapped = swap(after(jnp.stack(halves), stages[-1][5]), "dp", 1)

    atts = []
    for stage in stages:
        mine = after(stage[5], *atts[-1][1:]) if atts else stage[5]
        atts.append(gather_parts(mine, "tensor"))

    full = lambda shape: pl.BlockSpec(shape, lambda e: (0,) * len(shape))
    per_expert = lambda shape: pl.BlockSpec((1,) + shape, lambda e: (e, 0, 0))
    params = pltpu.CompilerParams(
        vmem_limit_bytes=VMEM_LIMIT, dimension_semantics=("arbitrary",)
    )
    moe_flops = 4 * experts * rows * width * hidden_units

    def moe_forward(piece, wo_args):
        wo_specs = [full(one.shape) for one in wo_args]
        wo_shape = (shares, features, width)
        return pl.pallas_call(
            functools.partial(moe_fwd_kernel, piece, PIECES, shares, experts),
            grid=(experts,),
            in_specs=[SMEM]
            + [full((rows, features))] * shares
            + wo_specs
            + [
                full((tok_rows, width)), full((1, width)), full((experts, width)),
                full((tok_rows, 2)), full((tok_rows, width)),
                per_expert((width, hidden_units)), per_expert((hidden_units, width)),
            ],
            out_specs=[full((share, width))] * shares
            + [full(wo_shape)] * (piece == 0)
            + [
                full((rows, width)), full((share, width)), full((rows, LANES)),
                full((rows, LANES)), per_expert((rows, hidden_units)),
                per_expert((rows, hidden_units)),
            ],
            out_shape=[shaped((share, width), BF16)] * shares
            + [shaped(wo_shape, BF16)] * (piece == 0)
            + [
                shaped((rows, width), BF16),
                shaped((share, width), F32),
                shaped((rows, LANES), F32),
                shaped((rows, LANES), F32),
                shaped((experts, rows, hidden_units), BF16),
                shaped((experts, rows, hidden_units), BF16),
            ],
            scratch_shapes=[pltpu.VMEM((rows, width), F32)],
            compiler_params=params,
            cost_estimate=pl.CostEstimate(
                flops=moe_flops, bytes_accessed=20 * mib, transcendentals=0
            ),
        )(
            idx, *atts[piece], *wo_args, tokens, gain_two, router_t, routes, grad_out,
            w_in, w_down,
        )

    def moe_backward(piece, gates, ggate, slope):
        return pl.pallas_call(
            functools.partial(moe_bwd_kernel, piece, shares, experts),
            grid=(experts,),
            in_specs=[
                SMEM, full((rows, LANES)), full((rows, LANES)), full((tok_rows, width)),
                per_expert((rows, hidden_units)), full((experts, width)),
                per_expert((width, hidden_units)), per_expert((hidden_units, width)),
            ],
            out_specs=[full((share, width))] * shares
            + [full((rows, LANES)), per_expert((rows, hidden_units))],
            out_shape=[shaped((share, width), BF16)] * shares
            + [
                shaped((rows, LANES), F32),
                shaped((experts, rows, hidden_units), BF16),
            ],
            scratch_shapes=[pltpu.VMEM((rows, width), F32)],
            compiler_params=params,
            cost_estimate=pl.CostEstimate(
                flops=moe_flops, bytes_accessed=16 * mib, transcendentals=0
            ),
        )(idx, gates, ggate, grad_out, slope, router_t, w_in, w_down)

    moe_got, gx_got, forwards, backwards = [], [], [], []
    wo_args = [w_out, swapped, *halves]
    for piece in range(PIECES):
        fwd = moe_forward(piece, wo_args)
        parts, kept = fwd[:shares], fwd[shares:]
        if piece == 0:
            wo, kept = kept[0], kept[1:]
            wo_args = [wo]
        moe_got.append(reduce_parts(parts, "tensor"))
        gates, ggate, slope = kept[2], kept[3], kept[5]
        bwd = moe_backward(piece, gates, ggate, slope)
        parts = bwd[:shares]
        gx_got.append(reduce_parts(parts, "tensor"))
        forwards.append(kept)
        backwards.append(bwd[shares:])
    normed_two = [f[0] for f in forwards]
    own_hidden = [f[1] for f in forwards]
    all_gates = [f[2] for f in forwards]
    acts = [f[4] for f in forwards]
    glogs = [b[0] for b in backwards]
    gpres = [b[1] for b in backwards]

    def hidden_back(piece, own):
        got = whole_call(
            functools.partial(hidden_back_kernel, piece, PIECES, shares, len(gx_got[piece])),
            [shaped((share, features), BF16)] * shares
            + [
                shaped((share, width), F32), shaped((share, width), BF16),
                shaped((1, width), F32),
            ],
            [idx, *gx_got[piece], wo, own, grad_out, gain_two],
            flops=2 * 10**8, moved=5 * mib,
        )
        parts = got[:shares]
        go = [parts[0]] + [swap(parts[by], "tensor", by) for by in others]
        return go, got[shares:]

    def attend_back(piece, go, carried):
        held = piece + 1
        last = held == PIECES
        outs, scratch = [], []
        if last:
            outs += [shaped((PIECES * share, width), BF16)] * shares
            outs += [shaped((3, tok_rows, features), BF16), shaped((8, NB), F32)]
        sums = [((rows, features), F32)] * (2 * held)
        sums += [((features, rows), F32), ((2 * heads, BLK, BLK), F32)]
        if last:
            scratch += [pltpu.VMEM(*one) for one in sums]
        else:
            outs += [shaped(*one) for one in sums]
        scratch += [
            pltpu.VMEM((rows, features), BF16),
            pltpu.VMEM((features, tok_rows), BF16),
            pltpu.VMEM((8, rows), F32),
            pltpu.VMEM((2, 8, 2 * BLK), F32),
            pltpu.VMEM((8, BLK), F32),
        ]
        return whole_call(
            functools.partial(attn_bwd_kernel, piece, PIECES, heads, head_size, shares),
            outs,
            [
                idx, *go, stages[piece][1], stages[piece][6], stages[piece][7],
                *[s[2] for s in stages[:held]], *[s[3] for s in stages[:held]],
                bias, far, segments, *carried, *([w_qkv_t, gather_hot] if last else []),
            ],
            scratch,
            flops=7 * 10**9, moved=8 * mib,
        )

    go, back_first = hidden_back(0, own_hidden[0])
    expert_grads, router_rows = pl.pallas_call(
        functools.partial(moe_weights_kernel, PIECES),
        grid=(experts,),
        in_specs=[full((tok_rows, width))]
        + [full((rows, LANES))] * (2 * PIECES)
        + [full((rows, width))] * PIECES
        + [per_expert((rows, hidden_units))] * (2 * PIECES),
        out_specs=[
            pl.BlockSpec((1, 2, width, width), lambda e: (e, 0, 0, 0)), full((8, width))
        ],
        out_shape=[shaped((experts, 2, width, width), BF16), shaped((8, width), F32)],
        compiler_params=params,
        cost_estimate=pl.CostEstimate(
            flops=2 * moe_flops, bytes_accessed=26 * mib, transcendentals=0
        ),
    )(after(grad_out, back_first[1]), *all_gates, *glogs, *normed_two, *acts, *gpres)
    expert_rows = lax.psum_scatter(
        expert_grads.reshape(experts * 2 * width, width), "dp", scatter_dimension=0, tiled=True
    )

    go_second, back_second = hidden_back(1, after(own_hidden[1], router_rows))
    result_share = whole_call(
        functools.partial(join_kernel, PIECES, len(moe_got[0])),
        [shaped((PIECES * share, width), BF16)],
        [*own_hidden, *moe_got[0], *moe_got[1]],
        moved=4 * mib, with_index=False,
    )[0]
    go = [after(go[0], back_second[1]), *go[1:]]
    first = attend_back(0, go, [])
    go_second = [after(go_second[0], first[0], result_share), *go_second[1:]]
    second = attend_back(1, go_second, first)
    grad_hidden = [back_first[0], back_second[0]]
    ggain_two = back_first[2] + back_second[2]
    gn_parts = second[:shares]
    gproj, grad_rel = second[shares:]
    gn_got = reduce_parts(gn_parts, "tensor")

    result_got = gather_parts(result_share, "tensor")
    result = whole_call(
        functools.partial(place_kernel, PIECES, shares),
        [shaped((tok_rows, width), BF16)], [idx, *result_got], moved=3 * mib,
    )[0]
    w_out_rows = whole_call(
        functools.partial(w_out_back_kernel, PIECES, shares),
        [shaped((shares, features, width), BF16)],
        [idx, *atts[0], *atts[1], back_first[1], after(back_second[1], gproj)],
        flops=3 * 10**8, moved=4 * mib,
    )[0]
    qkv_rows = whole_call(
        functools.partial(qkv_weights_kernel, PIECES),
        [shaped((3, features, width), BF16)],
        [*normed_one, gproj],
        flops=10**9, moved=4 * mib, with_index=False,
    )[0]

    gt_share, ggain_one = whole_call(
        functools.partial(input_back_kernel, PIECES, len(gn_got)),
        [shaped((PIECES * share, width), BF16), shaped((1, width), F32)],
        [idx, *gn_got, *grad_hidden, tokens, gain_one],
        moved=5 * mib,
    )
    gt_got = gather_parts(gt_share, "tensor")
    grad_tokens = whole_call(
        functools.partial(place_kernel, PIECES, shares),
        [shaped((tok_rows, width), F32)], [idx, *gt_got], moved=5 * mib,
    )[0]

    late = after(jnp.concatenate([qkv_rows, w_out_rows], axis=0), gt_share)
    late = scatter_sum(late, "dp", 1)
    out_sum = late[3].astype(F32)
    for by in others:
        out_sum = out_sum + swap(late[3 + by], "tensor", by).astype(F32)
    late_rows = late.shape[1]
    late = jnp.concatenate([late[:3], out_sum.astype(BF16)[None]], axis=0)
    shard = expert_rows.shape[0]
    both = jnp.concatenate([after(expert_rows, late), late.reshape(4 * late_rows, width)], axis=0)
    both = lax.all_gather(both, "dp", axis=0)
    expert_rows = both[:, :shard].reshape(experts, 2, width, width)
    grad_w_in = expert_rows[:, 0].astype(F32)
    grad_w_down = expert_rows[:, 1].astype(F32)
    levels = len(bits_of("dp"))
    late = both[:, shard:].reshape([2] * levels + [4, late_rows, width])
    late = jnp.transpose(late, [levels, *reversed(range(levels)), levels + 1, levels + 2])
    late = late.reshape(4, features, width)
    grad_w_qkv = jnp.swapaxes(late[:3], 1, 2).astype(F32)
    grad_w_out = late[3].astype(F32)

    rel_rows = jnp.pad(grad_rel, ((0, 0), (0, width - NB)))
    small = jnp.concatenate([rel_rows, router_rows, ggain_one, ggain_two], axis=0)
    small = sum_over(small, "dp")
    grad_rel_bias = small[:heads, :NB].T
    shared = sum_over(small[8:], "tensor")
    return (
        result,
        grad_tokens,
        shared[8],
        grad_w_qkv,
        grad_w_out,
        grad_rel_bias,
        shared[9],
        shared[:experts].T,
        grad_w_in,
        grad_w_down,
    )


def solution(mesh):
    placed = (
        P("dp", None),
        P("dp", None),
        P("dp", None),
        P("dp", None),
        P(),
        P(None, None, "tensor"),
        P("tensor", None),
        P(None, "tensor"),
        P(),
        P(),
        P(None, None, "tensor"),
        P(None, "tensor", None),
    )
    return jax.shard_map(
        body,
        mesh=mesh,
        in_specs=placed,
        out_specs=(
            P("dp", None),
            P("dp", None),
            P(),
            P(None, None, "tensor"),
            P("tensor", None),
            P(None, "tensor"),
            P(),
            P(),
            P(None, None, "tensor"),
            P(None, "tensor", None),
        ),
        check_vma=False,
    )
```

profile of v0, /device:TPU:0, one launch (start us, length us, event | category | flops | bytes accessed | tf_op | source)
XLA Modules:
  0.0 407.3 jit_solution(3377711068088398839)
XLA Ops:
  9.4 7.5 %shard_map.213 = (bf16[512,768]{1,0:T(8,128)(2,1)}, bf16[3,512,192]{2,1,0:T(8,128)(2,1)}, bf16[512,192]{1,0:T(8,128)(2,1)}, bf16[512,192]{1,0:T(8,128)(2,1)}, bf...) custom-call(bf16[1024,768]{1,0:T(8,128)(2,1)} %refs_5_.12, ...), custom_call_target="tpu_custom_call" | custom-call | flops 3000000000 | bytes 8388608 | tf_op jit(solution)/shard_map/pallas_call | solution.py:569
  16.9 5.1 %collective-permute-start.5 = (bf16[96,768]{1,0:T(8,128)(2,1)S(1)}, bf16[96,768]{1,0:T(8,128)(2,1)S(1)}, u32[]{:S(2)}, u32[]{:S(2)}) collective-permute-start(bf16[96,768]{1,0:T(8,128)(2,1)S(1)} %constant_dynamic-slice_fusion.3), channel_id=1, source_target_pairs={{0,3},{1,2},{2,1},{3,0},{4,7},{5,6},{6,5},{7,4},{8,11},{9,10},{10,... | collective-permute-start | bytes 442376 | tf_op jit(solution)/shard_map/ppermute | solution.py:582
  22.6 8.1 %shard_map.214 = (bf16[512,768]{1,0:T(8,128)(2,1)}, bf16[3,512,192]{2,1,0:T(8,128)(2,1)}, bf16[512,192]{1,0:T(8,128)(2,1)}, bf16[512,192]{1,0:T(8,128)(2,1)}, bf...) custom-call(bf16[1024,768]{1,0:T(8,128)(2,1)} %refs_5_.12, ...), custom_call_target="tpu_custom_call" | custom-call | flops 3000000000 | bytes 8388608 | tf_op jit(solution)/shard_map/pallas_call | solution.py:569
  30.7 3.7 collective-permute-done.4.refs_7_
  37.8 12.1 %collective-permute-done.1.refs_2_ = bf16[512,192]{1,0:T(8,128)(2,1)S(1)} collective-permute-done((bf16[512,192]{1,0:T(8,128)(2,1)S(1)}, bf16[512,192]{1,0:T(8,128)(2,1)S(1)}, u32[]{:S(2)}, u32[]{:S(2)}) %collective-permute-start.1) | collective-permute-done | bytes 196640 | tf_op jit(solution)/shard_map/ppermute | solution.py:582
  52.1 6.0 %collective-permute-done.2.refs_3_ = bf16[512,192]{1,0:T(8,128)(2,1)S(1)} collective-permute-done((bf16[512,192]{1,0:T(8,128)(2,1)S(1)}, bf16[512,192]{1,0:T(8,128)(2,1)S(1)}, u32[]{:S(2)}, u32[]{:S(2)}) %collective-permute-start.2) | collective-permute-done | bytes 196640 | tf_op jit(solution)/shard_map/ppermute | solution.py:582
  58.9 16.3 %shard_map.215 = (bf16[128,768]{1,0:T(8,128)(2,1)}, bf16[128,768]{1,0:T(8,128)(2,1)}, bf16[128,768]{1,0:T(8,128)(2,1)}, bf16[128,768]{1,0:T(8,128)(2,1)}, bf16[4...) custom-call(s32[2]{0:T(128)} %pad_add_fusion.idx, ...), custom_call_target="tpu_custom_call" | custom-call | flops 4831838208 | bytes 20971520 | tf_op jit(solution)/shard_map/pallas_call | solution.py:713
  75.2 12.8 %shard_map.220 = (bf16[128,768]{1,0:T(8,128)(2,1)}, bf16[128,768]{1,0:T(8,128)(2,1)}, bf16[128,768]{1,0:T(8,128)(2,1)}, bf16[128,768]{1,0:T(8,128)(2,1)}, f32[51...) custom-call(s32[2]{0:T(128)} %pad_add_fusion.idx, f32[512,128]{1,0:T(8,128)} %get-tuple-element.125.refs_0_, ...), custom_call_target="tpu_custom_call" | custom-call | flops 4831838208 | bytes 16777216 | tf_op jit(solution)/shard_map/pallas_call | solution.py:752
  92.1 4.0 collective-permute-done.23
  99.9 6.0 %collective-permute-done.7.refs_1_.refs_5_ = bf16[512,192]{1,0:T(8,128)(2,1)S(1)} collective-permute-done((bf16[512,192]{1,0:T(8,128)(2,1)S(1)}, bf16[512,192]{1,0:T(8,128)(2,1)S(1)}, u32[]{:S(2)}, u32[]{:S(2)}) %collective-permute-start.7) | collective-permute-done | bytes 196640 | tf_op jit(solution)/shard_map/ppermute | solution.py:582
  105.9 8.0 %collective-permute-done.9.refs_3_.refs_7_ = bf16[512,192]{1,0:T(8,128)(2,1)S(1)} collective-permute-done((bf16[512,192]{1,0:T(8,128)(2,1)S(1)}, bf16[512,192]{1,0:T(8,128)(2,1)S(1)}, u32[]{:S(2)}, u32[]{:S(2)}) %collective-permute-start.9) | collective-permute-done | bytes 196640 | tf_op jit(solution)/shard_map/ppermute | solution.py:582
  114.6 16.1 %shard_map.216 = (bf16[128,768]{1,0:T(8,128)(2,1)}, bf16[128,768]{1,0:T(8,128)(2,1)}, bf16[128,768]{1,0:T(8,128)(2,1)}, bf16[128,768]{1,0:T(8,128)(2,1)}, bf16[5...) custom-call(s32[2]{0:T(128)} %pad_add_fusion.idx, ...), custom_call_target="tpu_custom_call" | custom-call | flops 4831838208 | bytes 20971520 | tf_op jit(solution)/shard_map/pallas_call | solution.py:713
  130.7 12.8 %shard_map.219 = (bf16[128,768]{1,0:T(8,128)(2,1)}, bf16[128,768]{1,0:T(8,128)(2,1)}, bf16[128,768]{1,0:T(8,128)(2,1)}, bf16[128,768]{1,0:T(8,128)(2,1)}, f32[51...) custom-call(s32[2]{0:T(128)} %pad_add_fusion.idx, f32[512,128]{1,0:T(8,128)} %get-tuple-element.118.refs_0_.refs_1_, ...), custom_call_target="tpu_custom_call" | custom-call | flops 4831838208 | bytes 16777216 | tf_op jit(solution)/shard_map/pallas_call | solution.py:752
  144.2 3.6 shard_map.221
  147.7 16.1 %shard_map.222 = (bf16[4,2,768,768]{3,2,1,0:T(8,128)(2,1)}, f32[8,768]{1,0:T(8,128)}) custom-call(bf16[1024,768]{1,0:T(8,128)(2,1)} %refs_5_.11, f32[512,128]{1,0:T(8,128)} %get-tuple-element.125.refs_0_, f32[512,128]{1,0:T(8,128)} %get-tuple-element.118.refs_0_.refs_1_, f32[512,128]{1,0:T(8,128)} %get-tuple-element.134.refs_2_, ...), custom_call_target="tpu_custom_call" | custom-call | flops 9663676416 | bytes 27262976 | tf_op jit(solution)/shard_map/pallas_call | solution.py:844
  168.9 5.8 %collective-permute-done.20 = bf16[128,768]{1,0:T(8,128)(2,1)S(1)} collective-permute-done((bf16[128,768]{1,0:T(8,128)(2,1)S(1)}, bf16[128,768]{1,0:T(8,128)(2,1)S(1)}, u32[]{:S(2)}, u32[]{:S(2)}) %collective-permute-start.20) | collective-permute-done | bytes 196640 | tf_op jit(solution)/shard_map/ppermute | solution.py:582
  175.5 11.9 %collective-permute-done.11 = bf16[128,768]{1,0:T(8,128)(2,1)S(1)} collective-permute-done((bf16[128,768]{1,0:T(8,128)(2,1)S(1)}, bf16[128,768]{1,0:T(8,128)(2,1)S(1)}, u32[]{:S(2)}, u32[]{:S(2)}) %collective-permute-start.11) | collective-permute-done | bytes 196640 | tf_op jit(solution)/shard_map/ppermute | solution.py:582
  188.1 3.5 collective-permute-done.14
  197.1 3.6 shard_map.223
  208.0 17.2 %shard_map.224 = (f32[512,192]{1,0:T(8,128)}, f32[512,192]{1,0:T(8,128)}, f32[192,512]{1,0:T(8,128)}, f32[6,256,256]{2,1,0:T(8,128)}) custom-call(s32[2]{0:T(128)} %pad_add_fusion.idx, bf16[128,192]{1,0:T(8,128)(2,1)} %get-tuple-element.147.refs_0_, bf16[128,192]{1,0:T(8,128)(2,1)} %copy-done.50, bf16[128,192]{1,0:T(8,128)(2,1)} %copy-done.52, ...), custom_call_target="tpu_custom_call" | custom-call | flops 7000000000 | bytes 8388608 | tf_op jit(solution)/shard_map/pallas_call | solution.py:569
  229.1 14.2 %shard_map.225 = (bf16[256,768]{1,0:T(8,128)(2,1)}, bf16[256,768]{1,0:T(8,128)(2,1)}, bf16[256,768]{1,0:T(8,128)(2,1)}, bf16[256,768]{1,0:T(8,128)(2,1)}, bf16[3...) custom-call(s32[2]{0:T(128)} %pad_add_fusion.idx, bf16[128,192]{1,0:T(8,128)(2,1)} %get-tuple-element.156.refs_0_, ...), custom_call_target="tpu_custom_call" | custom-call | flops 7000000000 | bytes 8388608 | tf_op jit(solution)/shard_map/pallas_call | solution.py:569
  245.6 11.8 %collective-permute-done.32 = bf16[256,768]{1,0:T(8,128)(2,1)S(1)} collective-permute-done((bf16[256,768]{1,0:T(8,128)(2,1)}, bf16[256,768]{1,0:T(8,128)(2,1)S(1)}, u32[]{:S(2)}, u32[]{:S(2)}) %collective-permute-start.32) | collective-permute-done | bytes 393248 | tf_op jit(solution)/shard_map/ppermute | solution.py:582
  263.3 4.0 shard_map.228
  281.2 12.3 %collective-permute-done.43 = bf16[7,48,768]{2,1,0:T(8,128)(2,1)S(1)} collective-permute-done((bf16[7,48,768]{2,1,0:T(8,128)(2,1)S(1)}, bf16[7,48,768]{2,1,0:T(8,128)(2,1)S(1)}, u32[]{:S(2)}, u32[]{:S(2)}) %collective-permute-start.43) | collective-permute-done | bytes 516128 | tf_op jit(solution)/shard_map/ppermute | solution.py:582
  295.2 5.9 %collective-permute-done.44 = bf16[7,24,768]{2,1,0:T(8,128)(2,1)S(1)} collective-permute-done((bf16[7,24,768]{2,1,0:T(8,128)(2,1)S(1)}, bf16[7,24,768]{2,1,0:T(8,128)(2,1)S(1)}, u32[]{:S(2)}, u32[]{:S(2)}) %collective-permute-start.44) | collective-permute-done | bytes 258080 | tf_op jit(solution)/shard_map/ppermute | solution.py:582
  313.6 14.8 %collective-permute-done.17.refs_2_ = bf16[256,768]{1,0:T(8,128)(2,1)S(1)} collective-permute-done((bf16[256,768]{1,0:T(8,128)(2,1)S(1)}, bf16[256,768]{1,0:T(8,128)(2,1)S(1)}, u32[]{:S(2)}, u32[]{:S(2)}) %collective-permute-start.17) | collective-permute-done | bytes 393248 | tf_op jit(solution)/shard_map/ppermute | solution.py:582
  332.3 4.5 %collective-permute-done.38 = f32[18,768]{1,0:T(8,128)S(1)} collective-permute-done((f32[18,768]{1,0:T(8,128)S(1)}, f32[18,768]{1,0:T(8,128)S(1)}, u32[]{:S(2)}, u32[]{:S(2)}) %collective-permute-start.38) | collective-permute-done | bytes 55328 | tf_op jit(solution)/shard_map/ppermute | solution.py:582
  341.5 7.5 %collective-permute-done.18.refs_3_ = bf16[256,768]{1,0:T(8,128)(2,1)S(1)} collective-permute-done((bf16[256,768]{1,0:T(8,128)(2,1)S(1)}, bf16[256,768]{1,0:T(8,128)(2,1)S(1)}, u32[]{:S(2)}, u32[]{:S(2)}) %collective-permute-start.18) | collective-permute-done | bytes 393248 | tf_op jit(solution)/shard_map/ppermute | solution.py:582
  356.4 6.6 %collective-permute-done.41 = f32[10,768]{1,0:T(8,128)S(1)} collective-permute-done((f32[10,768]{1,0:T(8,128)S(1)}, f32[10,768]{1,0:T(8,128)S(1)}, u32[]{:S(2)}, u32[]{:S(2)}) %collective-permute-start.41) | collective-permute-done | bytes 30752 | tf_op jit(solution)/shard_map/ppermute | solution.py:582
  365.4 6.8 %collective-permute-done.36.refs_3_ = bf16[256,768]{1,0:T(8,128)(2,1)S(1)} collective-permute-done((bf16[256,768]{1,0:T(8,128)(2,1)S(1)}, bf16[256,768]{1,0:T(8,128)(2,1)S(1)}, u32[]{:S(2)}, u32[]{:S(2)}) %collective-permute-start.36) | collective-permute-done | bytes 393248 | tf_op jit(solution)/shard_map/ppermute | solution.py:582
  377.8 7.9 %slice.79 = bf16[8,768,768]{2,1,0:T(8,128)(2,1)} slice(bf16[8,864,768]{2,1,0:T(8,128)(2,1)} %bitcast.48), slice={[0:8], [0:768], [0:768]} | slice | bytes 18874368 | tf_op jit(solution)/shard_map/slice | solution.py:921
  387.9 12.3 %fusion = (f32[4,768,768]{2,1,0:T(8,128)}, f32[4,768,768]{2,1,0:T(8,128)}) fusion(bf16[4,2,768,768]{3,2,1,0:T(8,128)(2,1)} %bitcast.46), kind=kLoop, calls=%fused_computation.1 | loop fusion | flops 4718592 | bytes 28311552 | tf_op jit(solution)/shard_map/convert_element_type | solution.py:923
  (240 shorter events, 103.7 us)
Async XLA Ops:
  7.2 301.0 %reduce-scatter.2.cloned.1.call-start = ((), (), s32[]{:S(2)}) async-start(), calls=%async_computation.1 | async-start | bytes 10616832 | tf_op jit(solution)/shard_map/reduce_scatter | solution.py:860
  16.9 13.8 %collective-permute-start.5 = (bf16[96,768]{1,0:T(8,128)(2,1)S(1)}, bf16[96,768]{1,0:T(8,128)(2,1)S(1)}, u32[]{:S(2)}, u32[]{:S(2)}) collective-permute-start(bf16[96,768]{1,0:T(8,128)(2,1)S(1)} %constant_dynamic-slice_fusion.3), channel_id=1, source_target_pairs={{0,3},{1,2},{2,1},{3,0},{4,7},{5,6},{6,5},{7,4},{8,11},{9,10},{10,... | collective-permute-start | bytes 442376 | tf_op jit(solution)/shard_map/ppermute | solution.py:582
  34.5 23.6 %collective-permute-start.6 = (bf16[3,96,768]{2,1,0:T(8,128)(2,1)S(1)}, bf16[3,96,768]{2,1,0:T(8,128)(2,1)S(1)}, u32[]{:S(2)}, u32[]{:S(2)}) collective-permute-start(bf16[3,96,768]{2,1,0:T(8,128)(2,1)S(1)} %pad_maximum_fusion.2), channel_id=1, source_target_pairs={{0,4},{4,0},{8,12},{12,8},{16,20},{20,16},{24,28},{28,24},{1,5},{5... | collective-permute-start | bytes 1327112 | tf_op jit(solution)/shard_map/ppermute | solution.py:582
  34.6 15.2 %collective-permute-start.1 = (bf16[512,192]{1,0:T(8,128)(2,1)S(1)}, bf16[512,192]{1,0:T(8,128)(2,1)S(1)}, u32[]{:S(2)}, u32[]{:S(2)}) collective-permute-start(bf16[512,192]{1,0:T(8,128)(2,1)S(1)} %copy-done.11), channel_id=1, source_target_pairs={{0,2},{1,3},{2,0},{3,1},{4,6},{5,7},{6,4},{7,5},{8,10},{9,11},{10,... | collective-permute-start | bytes 589832 | tf_op jit(solution)/shard_map/ppermute | solution.py:582
  34.7 17.4 %collective-permute-start = (bf16[512,192]{1,0:T(8,128)(2,1)S(1)}, bf16[512,192]{1,0:T(8,128)(2,1)S(1)}, u32[]{:S(2)}, u32[]{:S(2)}) collective-permute-start(bf16[512,192]{1,0:T(8,128)(2,1)S(1)} %copy-done.11), channel_id=1, source_target_pairs={{0,1},{1,0},{2,3},{3,2},{4,5},{5,4},{6,7},{7,6},{8,9},{9,8},{10,11... | collective-permute-start | bytes 589832 | tf_op jit(solution)/shard_map/ppermute | solution.py:582
  58.0 33.8 %collective-permute-start.8 = (bf16[512,192]{1,0:T(8,128)(2,1)}, bf16[512,192]{1,0:T(8,128)(2,1)S(1)}, u32[]{:S(2)}, u32[]{:S(2)}) collective-permute-start(bf16[512,192]{1,0:T(8,128)(2,1)} %get-tuple-element.107.refs_0_.refs_4_), channel_id=1, source_target_pairs={{0,2},{1,3},{2,0},{3,1},{4,6},{5,7},{6,4},{7,5},{8,10},{9,11},{10,... | collective-permute-start | bytes 589832 | tf_op jit(solution)/shard_map/ppermute | solution.py:582
  89.8 16.2 %collective-permute-start.7 = (bf16[512,192]{1,0:T(8,128)(2,1)S(1)}, bf16[512,192]{1,0:T(8,128)(2,1)S(1)}, u32[]{:S(2)}, u32[]{:S(2)}) collective-permute-start(bf16[512,192]{1,0:T(8,128)(2,1)S(1)} %copy-done.12), channel_id=1, source_target_pairs={{0,1},{1,0},{2,3},{3,2},{4,5},{5,4},{6,7},{7,6},{8,9},{9,8},{10,11... | collective-permute-start | bytes 589832 | tf_op jit(solution)/shard_map/ppermute | solution.py:582
  90.1 53.4 %collective-permute-start.22 = (bf16[128,768]{1,0:T(8,128)(2,1)}, bf16[128,768]{1,0:T(8,128)(2,1)S(1)}, u32[]{:S(2)}, u32[]{:S(2)}) collective-permute-start(bf16[128,768]{1,0:T(8,128)(2,1)} %get-tuple-element.129), channel_id=1, source_target_pairs={{0,1},{1,0},{2,3},{3,2},{4,5},{5,4},{6,7},{7,6},{8,9},{9,8},{10,11... | collective-permute-start | bytes 589832 | tf_op jit(solution)/shard_map/ppermute | solution.py:582
  91.8 22.1 %collective-permute-start.9 = (bf16[512,192]{1,0:T(8,128)(2,1)S(1)}, bf16[512,192]{1,0:T(8,128)(2,1)S(1)}, u32[]{:S(2)}, u32[]{:S(2)}) collective-permute-start(bf16[512,192]{1,0:T(8,128)(2,1)S(1)} %collective-permute-done.8.refs_2_.refs_6_), channel_id=1, source_target_pairs={{0,1},{1,0},{2,3},{3,2},{4,5},{5,4},{6,7},{7,6},{8,9},{9,8},{10,11... | collective-permute-start | bytes 589832 | tf_op jit(solution)/shard_map/ppermute | solution.py:582
  97.1 46.4 %collective-permute-start.24 = (bf16[128,768]{1,0:T(8,128)(2,1)S(1)}, bf16[128,768]{1,0:T(8,128)(2,1)S(1)}, u32[]{:S(2)}, u32[]{:S(2)}) collective-permute-start(bf16[128,768]{1,0:T(8,128)(2,1)S(1)} %add_convert_fusion.4), channel_id=1, source_target_pairs={{0,2},{1,3},{2,0},{3,1},{4,6},{5,7},{6,4},{7,5},{8,10},{9,11},{10,... | collective-permute-start | bytes 589832 | tf_op jit(solution)/shard_map/ppermute | solution.py:582
  164.0 212.2 %all-gather.3.cloned.1.call-start = ((), (), s32[]{:S(2)}) async-start(), calls=%async_computation.2 | async-start | bytes 11943936 | tf_op jit(solution)/shard_map/all_gather | solution.py:920
  164.9 35.9 %collective-permute-start.10 = (bf16[128,768]{1,0:T(8,128)(2,1)S(1)}, bf16[128,768]{1,0:T(8,128)(2,1)S(1)}, u32[]{:S(2)}, u32[]{:S(2)}) collective-permute-start(bf16[128,768]{1,0:T(8,128)(2,1)S(1)} %copy-done.41), channel_id=1, source_target_pairs={{0,1},{1,0},{2,3},{3,2},{4,5},{5,4},{6,7},{7,6},{8,9},{9,8},{10,11... | collective-permute-start | bytes 589832 | tf_op jit(solution)/shard_map/ppermute | solution.py:582
  166.8 20.6 %collective-permute-start.11 = (bf16[128,768]{1,0:T(8,128)(2,1)S(1)}, bf16[128,768]{1,0:T(8,128)(2,1)S(1)}, u32[]{:S(2)}, u32[]{:S(2)}) collective-permute-start(bf16[128,768]{1,0:T(8,128)(2,1)S(1)} %copy-done.43), channel_id=1, source_target_pairs={{0,1},{1,0},{2,3},{3,2},{4,5},{5,4},{6,7},{7,6},{8,9},{9,8},{10,11... | collective-permute-start | bytes 589832 | tf_op jit(solution)/shard_map/ppermute | solution.py:582
  166.9 24.7 %collective-permute-start.14 = (bf16[128,768]{1,0:T(8,128)(2,1)S(1)}, bf16[128,768]{1,0:T(8,128)(2,1)S(1)}, u32[]{:S(2)}, u32[]{:S(2)}) collective-permute-start(bf16[128,768]{1,0:T(8,128)(2,1)S(1)} %copy-done.44), channel_id=1, source_target_pairs={{0,1},{1,0},{2,3},{3,2},{4,5},{5,4},{6,7},{7,6},{8,9},{9,8},{10,11... | collective-permute-start | bytes 589832 | tf_op jit(solution)/shard_map/ppermute | solution.py:582
  168.8 25.2 %collective-permute-start.19 = (bf16[128,768]{1,0:T(8,128)(2,1)S(1)}, bf16[128,768]{1,0:T(8,128)(2,1)S(1)}, u32[]{:S(2)}, u32[]{:S(2)}) collective-permute-start(bf16[128,768]{1,0:T(8,128)(2,1)S(1)} %copy-done.45), channel_id=1, source_target_pairs={{0,1},{1,0},{2,3},{3,2},{4,5},{5,4},{6,7},{7,6},{8,9},{9,8},{10,11... | collective-permute-start | bytes 589832 | tf_op jit(solution)/shard_map/ppermute | solution.py:582
  174.8 20.3 %collective-permute-start.21 = (bf16[128,768]{1,0:T(8,128)(2,1)S(1)}, bf16[128,768]{1,0:T(8,128)(2,1)S(1)}, u32[]{:S(2)}, u32[]{:S(2)}) collective-permute-start(bf16[128,768]{1,0:T(8,128)(2,1)S(1)} %add_convert_fusion.5), channel_id=1, source_target_pairs={{0,2},{1,3},{2,0},{3,1},{4,6},{5,7},{6,4},{7,5},{8,10},{9,11},{10,... | collective-permute-start | bytes 589832 | tf_op jit(solution)/shard_map/ppermute | solution.py:582
  187.4 15.3 %collective-permute-start.12 = (bf16[128,768]{1,0:T(8,128)(2,1)S(1)}, bf16[128,768]{1,0:T(8,128)(2,1)S(1)}, u32[]{:S(2)}, u32[]{:S(2)}) collective-permute-start(bf16[128,768]{1,0:T(8,128)(2,1)S(1)} %add_convert_fusion.7), channel_id=1, source_target_pairs={{0,2},{1,3},{2,0},{3,1},{4,6},{5,7},{6,4},{7,5},{8,10},{9,11},{10,... | collective-permute-start | bytes 589832 | tf_op jit(solution)/shard_map/ppermute | solution.py:582
  200.8 24.4 %collective-permute-start.13 = (bf16[128,768]{1,0:T(8,128)(2,1)S(1)}, bf16[128,768]{1,0:T(8,128)(2,1)S(1)}, u32[]{:S(2)}, u32[]{:S(2)}) collective-permute-start(bf16[128,768]{1,0:T(8,128)(2,1)S(1)} %copy-done.42), channel_id=1, source_target_pairs={{0,1},{1,0},{2,3},{3,2},{4,5},{5,4},{6,7},{7,6},{8,9},{9,8},{10,11... | collective-permute-start | bytes 589832 | tf_op jit(solution)/shard_map/ppermute | solution.py:582
  202.8 22.5 %collective-permute-start.15 = (bf16[128,768]{1,0:T(8,128)(2,1)S(1)}, bf16[128,768]{1,0:T(8,128)(2,1)S(1)}, u32[]{:S(2)}, u32[]{:S(2)}) collective-permute-start(bf16[128,768]{1,0:T(8,128)(2,1)S(1)} %add_convert_fusion.6), channel_id=1, source_target_pairs={{0,2},{1,3},{2,0},{3,1},{4,6},{5,7},{6,4},{7,5},{8,10},{9,11},{10,... | collective-permute-start | bytes 589832 | tf_op jit(solution)/shard_map/ppermute | solution.py:582
  203.5 24.9 %collective-permute-start.28 = (bf16[128,192]{1,0:T(8,128)(2,1)}, bf16[128,192]{1,0:T(8,128)(2,1)S(1)}, u32[]{:S(2)}, u32[]{:S(2)}) collective-permute-start(bf16[128,192]{1,0:T(8,128)(2,1)} %get-tuple-element.157), channel_id=1, source_target_pairs={{0,1},{1,0},{2,3},{3,2},{4,5},{5,4},{6,7},{7,6},{8,9},{9,8},{10,11... | collective-permute-start | bytes 147464 | tf_op jit(solution)/shard_map/ppermute | solution.py:582
  206.7 21.7 %collective-permute-start.29 = (bf16[128,192]{1,0:T(8,128)(2,1)}, bf16[128,192]{1,0:T(8,128)(2,1)S(1)}, u32[]{:S(2)}, u32[]{:S(2)}) collective-permute-start(bf16[128,192]{1,0:T(8,128)(2,1)} %get-tuple-element.158), channel_id=1, source_target_pairs={{0,2},{1,3},{2,0},{3,1},{4,6},{5,7},{6,4},{7,5},{8,10},{9,11},{10,... | collective-permute-start | bytes 147464 | tf_op jit(solution)/shard_map/ppermute | solution.py:582
  206.7 21.7 %collective-permute-start.30 = (bf16[128,192]{1,0:T(8,128)(2,1)}, bf16[128,192]{1,0:T(8,128)(2,1)S(1)}, u32[]{:S(2)}, u32[]{:S(2)}) collective-permute-start(bf16[128,192]{1,0:T(8,128)(2,1)} %get-tuple-element.159), channel_id=1, source_target_pairs={{0,3},{1,2},{2,1},{3,0},{4,7},{5,6},{6,5},{7,4},{8,11},{9,10},{10,... | collective-permute-start | bytes 147464 | tf_op jit(solution)/shard_map/ppermute | solution.py:582
  243.3 14.2 %collective-permute-start.32 = (bf16[256,768]{1,0:T(8,128)(2,1)}, bf16[256,768]{1,0:T(8,128)(2,1)S(1)}, u32[]{:S(2)}, u32[]{:S(2)}) collective-permute-start(bf16[256,768]{1,0:T(8,128)(2,1)} %get-tuple-element.171), channel_id=1, source_target_pairs={{0,1},{1,0},{2,3},{3,2},{4,5},{5,4},{6,7},{7,6},{8,9},{9,8},{10,11... | collective-permute-start | bytes 1179656 | tf_op jit(solution)/shard_map/ppermute | solution.py:582
  245.5 23.1 %collective-permute-start.31 = (bf16[256,768]{1,0:T(8,128)(2,1)}, bf16[256,768]{1,0:T(8,128)(2,1)S(1)}, u32[]{:S(2)}, u32[]{:S(2)}) collective-permute-start(bf16[256,768]{1,0:T(8,128)(2,1)} %get-tuple-element.169), channel_id=1, source_target_pairs={{0,1},{1,0},{2,3},{3,2},{4,5},{5,4},{6,7},{7,6},{8,9},{9,8},{10,11... | collective-permute-start | bytes 1179656 | tf_op jit(solution)/shard_map/ppermute | solution.py:582
  279.6 13.9 %collective-permute-start.43 = (bf16[7,48,768]{2,1,0:T(8,128)(2,1)S(1)}, bf16[7,48,768]{2,1,0:T(8,128)(2,1)S(1)}, u32[]{:S(2)}, u32[]{:S(2)}) collective-permute-start(bf16[7,48,768]{2,1,0:T(8,128)(2,1)S(1)} %constant_dynamic-slice_fusion.1), channel_id=1, source_target_pairs={{0,8},{4,12},{8,0},{12,4},{16,24},{20,28},{24,16},{28,20},{1,9},{5... | collective-permute-start | bytes 1548296 | tf_op jit(solution)/shard_map/ppermute | solution.py:582
  310.8 17.6 %collective-permute-start.17 = (bf16[256,768]{1,0:T(8,128)(2,1)S(1)}, bf16[256,768]{1,0:T(8,128)(2,1)S(1)}, u32[]{:S(2)}, u32[]{:S(2)}) collective-permute-start(bf16[256,768]{1,0:T(8,128)(2,1)S(1)} %copy-done.1), channel_id=1, source_target_pairs={{0,2},{1,3},{2,0},{3,1},{4,6},{5,7},{6,4},{7,5},{8,10},{9,11},{10,... | collective-permute-start | bytes 1179656 | tf_op jit(solution)/shard_map/ppermute | solution.py:582
  312.6 18.1 %collective-permute-start.37 = (f32[18,768]{1,0:T(8,128)S(1)}, f32[18,768]{1,0:T(8,128)S(1)}, u32[]{:S(2)}, u32[]{:S(2)}) collective-permute-start(f32[18,768]{1,0:T(8,128)S(1)} %fusion.3), channel_id=1, source_target_pairs={{0,4},{4,0},{8,12},{12,8},{16,20},{20,16},{24,28},{28,24},{1,5},{5... | collective-permute-start | bytes 165896 | tf_op jit(solution)/shard_map/ppermute | solution.py:582
  312.7 28.9 %collective-permute-start.16 = (bf16[256,768]{1,0:T(8,128)(2,1)S(1)}, bf16[256,768]{1,0:T(8,128)(2,1)S(1)}, u32[]{:S(2)}, u32[]{:S(2)}) collective-permute-start(bf16[256,768]{1,0:T(8,128)(2,1)S(1)} %copy-done.1), channel_id=1, source_target_pairs={{0,1},{1,0},{2,3},{3,2},{4,5},{5,4},{6,7},{7,6},{8,9},{9,8},{10,11... | collective-permute-start | bytes 1179656 | tf_op jit(solution)/shard_map/ppermute | solution.py:582
  328.4 20.7 %collective-permute-start.18 = (bf16[256,768]{1,0:T(8,128)(2,1)S(1)}, bf16[256,768]{1,0:T(8,128)(2,1)S(1)}, u32[]{:S(2)}, u32[]{:S(2)}) collective-permute-start(bf16[256,768]{1,0:T(8,128)(2,1)S(1)} %collective-permute-done.17.refs_2_), channel_id=1, source_target_pairs={{0,1},{1,0},{2,3},{3,2},{4,5},{5,4},{6,7},{7,6},{8,9},{9,8},{10,11... | collective-permute-start | bytes 1179656 | tf_op jit(solution)/shard_map/ppermute | solution.py:582
  328.4 27.4 %collective-permute-start.35 = (bf16[256,768]{1,0:T(8,128)(2,1)S(1)}, bf16[256,768]{1,0:T(8,128)(2,1)S(1)}, u32[]{:S(2)}, u32[]{:S(2)}) collective-permute-start(bf16[256,768]{1,0:T(8,128)(2,1)S(1)} %copy-done.2), channel_id=1, source_target_pairs={{0,2},{1,3},{2,0},{3,1},{4,6},{5,7},{6,4},{7,5},{8,10},{9,11},{10,... | collective-permute-start | bytes 1179656 | tf_op jit(solution)/shard_map/ppermute | solution.py:582
  352.4 13.0 %collective-permute-start.34 = (bf16[256,768]{1,0:T(8,128)(2,1)S(1)}, bf16[256,768]{1,0:T(8,128)(2,1)S(1)}, u32[]{:S(2)}, u32[]{:S(2)}) collective-permute-start(bf16[256,768]{1,0:T(8,128)(2,1)S(1)} %copy-done.2), channel_id=1, source_target_pairs={{0,1},{1,0},{2,3},{3,2},{4,5},{5,4},{6,7},{7,6},{8,9},{9,8},{10,11... | collective-permute-start | bytes 1179656 | tf_op jit(solution)/shard_map/ppermute | solution.py:582
  355.8 16.4 %collective-permute-start.36 = (bf16[256,768]{1,0:T(8,128)(2,1)S(1)}, bf16[256,768]{1,0:T(8,128)(2,1)S(1)}, u32[]{:S(2)}, u32[]{:S(2)}) collective-permute-start(bf16[256,768]{1,0:T(8,128)(2,1)S(1)} %collective-permute-done.35.refs_2_), channel_id=1, source_target_pairs={{0,1},{1,0},{2,3},{3,2},{4,5},{5,4},{6,7},{7,6},{8,9},{9,8},{10,11... | collective-permute-start | bytes 1179656 | tf_op jit(solution)/shard_map/ppermute | solution.py:582
  (74 other events, 703.8 us)
Sparse Core Ops, SparseCore 0:
  164.1 76.6 reduce-scatter.1
  310.9 64.6 all-gather.2
where the time goes:
time: 413 us; the launch traced here: 407 us
  waiting for transfers between devices  148 us (36%)
  Pallas kernels  147 us (36%)
  starting transfers between devices  52.1 us (13%)
  local copies, waits for them, and re-layouts  24.1 us (6%)
  other arithmetic  21 us (5%)
  between operations  15 us (4%)
    ppermute x48, waiting for transfers between devices, swap(): return lax.ppermute(value, axis, [(i, i ^ bit) for i in range(count)])  148 us
    pallas_call x12, Pallas kernels, whole_call(): pl.pallas_call(kernel, out_shape=outs, in_specs=specs, out_specs=[VMEM] *...  73.1 us
    ppermute x48, starting transfers between devices, swap(): return lax.ppermute(value, axis, [(i, i ^ bit) for i in range(count)])  52.1 us
    pallas_call x2, Pallas kernels, moe_forward(): pl.pallas_call(functools.partial(moe_fwd_kernel, piece, PIECES, shares, e...  32.3 us
    pallas_call x2, Pallas kernels, moe_backward(): pl.pallas_call(functools.partial(moe_bwd_kernel, piece, shares, experts),...  25.6 us
    pallas_call x1, Pallas kernels, body(): pl.pallas_call(functools.partial(moe_weights_kernel, PIECES), grid=(exper...  16.1 us
    convert_element_type x1, other arithmetic, body(): grad_w_down = expert_rows[:, 1].astype(F32)  12.3 us
  transfers between devices with their start and end apart: 50, of which 27 were waited for; matrix products, arithmetic and copies ran while one was open for 2% of the time, Pallas kernels for 29%

commit v1 on v0

--- a/solution.py
+++ b/solution.py
@@ -322,21 +322,15 @@
     return jnp.concatenate([values, missing], axis=0)
 
 
-def moe_fwd_kernel(piece, pieces, shares, experts, idx, *refs):
+def block_start(index, size):
+    return pl.multiple_of(index * size, size)
+
+
+def moe_fwd_kernel(shares, experts, idx, *refs):
     att, refs = refs[:shares], refs[shares:]
-    if piece == 0:
-        wo_own, wo_swapped, refs = refs[0], refs[1], refs[2:]
-        wo_fetched, refs = refs[: shares - 1], refs[shares - 1 :]
-    else:
-        wo, refs = refs[0], refs[1:]
-    tok, gain, router, routes, cot, w_in, w_down = refs[:7]
-    refs = refs[7:]
-    parts, refs = refs[:shares], refs[shares:]
-    if piece == 0:
-        wo, refs = refs[0], refs[1:]
-    normed, own, gates, ggate, act, slope, acc = refs
-    rows_total = tok.shape[0] // pieces
-    base = piece * rows_total
+    wo, tok, gain, router, routes, cot, w_in, w_down, parts = refs[:9]
+    normed, own, gates, ggate, act, slope, acc = refs[9:]
+    rows_total, features = att[0].shape
     share = rows_total // shares
     me = idx[0]
     expert = pl.program_id(0)
@@ -345,28 +339,20 @@
     def _():
         gain_row = gain[...].astype(F32)
         router_wide = padded_rows(router[...].astype(F32), LANES).astype(BF16)
-        if piece == 0:
-            half = wo_own.shape[0] // 2
-            mine = pl.ds(pl.multiple_of(idx[1] * half, half), half)
-            other = pl.ds(pl.multiple_of((1 - idx[1]) * half, half), half)
-            wo[0] = wo_own[...]
-            for step in range(1, shares):
-                wo[step, mine, :] = wo_fetched[step - 1][...]
-                wo[step, other, :] = wo_swapped[step - 1]
         for block in range(rows_total // BLK):
             rows = pl.ds(block * BLK, BLK)
-            outer = pl.ds(base + block * BLK, BLK)
-            attn = dot(att[0][rows, :], wo[0])
+            attn = dot(att[0][rows, :], wo[pl.ds(block_start(me, features), features), :])
             for step in range(1, shares):
-                attn = attn + dot(att[step][rows, :], wo[step])
-            hidden = tok[outer, :].astype(F32) + attn
+                held = wo[pl.ds(block_start(me ^ step, features), features), :]
+                attn = attn + dot(att[step][rows, :], held)
+            hidden = tok[rows, :].astype(F32) + attn
             acc[rows, :] = hidden
             n = (hidden * row_scale(hidden) * gain_row).astype(BF16)
             normed[rows, :] = n
             logits = dot(n, router_wide, NT)
             lanes = lax.broadcasted_iota(jnp.int32, logits.shape, 1)
-            first = lanes == routes[outer, 0:1]
-            second = lanes == routes[outer, 1:2]
+            first = lanes == routes[rows, 0:1]
+            second = lanes == routes[rows, 1:2]
             one = jnp.sum(jnp.where(first, logits, 0.0), axis=1, keepdims=True)
             two = jnp.sum(jnp.where(second, logits, 0.0), axis=1, keepdims=True)
             peak = jnp.maximum(one, two)
@@ -380,7 +366,6 @@
 
     for block in range(rows_total // ROWS):
         rows = pl.ds(block * ROWS, ROWS)
-        outer = pl.ds(base + block * ROWS, ROWS)
         lifted, bend = gelu_pair(dot(normed[rows, :], w_in[0]))
         lifted = lifted.astype(BF16)
         act[0, rows, :] = lifted
@@ -388,25 +373,22 @@
         out = dot(lifted, w_down[0])
         gate = lane_pick(gates[rows, :], expert)
         acc[rows, :] += gate * out
-        pulled = jnp.sum(cot[outer, :].astype(F32) * out, axis=1, keepdims=True)
+        pulled = jnp.sum(cot[rows, :].astype(F32) * out, axis=1, keepdims=True)
         held = ggate[rows, :]
         lanes = lax.broadcasted_iota(jnp.int32, held.shape, 1)
         ggate[rows, :] = jnp.where(lanes == expert, pulled, held)
 
     @pl.when(expert == experts - 1)
     def _():
-        for step in range(shares):
-            start = pl.multiple_of((me ^ step) * share, share)
-            parts[step][...] = acc[pl.ds(start, share), :].astype(BF16)
-
-
-def moe_bwd_kernel(piece, shares, experts, idx, *refs):
+        parts[...] = acc[...].astype(BF16)
+
+
+def moe_bwd_kernel(shares, experts, idx, *refs):
     gates, ggate, cot, slope, router, w_in, w_down = refs[:7]
     refs = refs[7:]
     parts, refs = refs[:shares], refs[shares:]
     glog, gpre, acc = refs
     rows_total = gates.shape[0]
-    base = piece * rows_total
     share = rows_total // shares
     me = idx[0]
     expert = pl.program_id(0)
@@ -424,8 +406,7 @@
     for block in range(rows_total // ROWS):
         rows = pl.ds(block * ROWS, ROWS)
         gate = lane_pick(gates[rows, :], expert)
-        weighted = cot[pl.ds(base + block * ROWS, ROWS), :].astype(F32)
-        weighted = (gate * weighted).astype(BF16)
+        weighted = (gate * cot[rows, :].astype(F32)).astype(BF16)
         gp = (dot(weighted, w_down[0], NT) * slope[0, rows, :].astype(F32)).astype(BF16)
         gpre[0, rows, :] = gp
         acc[rows, :] += dot(gp, w_in[0], NT)
@@ -492,7 +473,9 @@
     low = back.astype(BF16)
     gh_low[...] = low
     for step in range(shares):
-        ga[step][...] = dot(low, wo[step], NT).astype(BF16)
+        features = ga[step].shape[1]
+        held = wo[pl.ds(block_start(idx[0] ^ step, features), features), :]
+        ga[step][...] = dot(low, held, NT).astype(BF16)
 
 
 def w_out_back_kernel(pieces, shares, idx, *refs):
@@ -590,6 +573,10 @@
     return value
 
 
+def exchange(parts, axis):
+    return [parts[0]] + [swap(parts[bit], axis, bit) for bit in range(1, len(parts))]
+
+
 def gather_parts(value, axis):
     count = lax.axis_size(axis)
     if count != 4:
@@ -626,6 +613,17 @@
         keep, send = halves_of(value, axis, (me // bit) % 2)
         got = swap(send, mesh_axis, bit)
         value = (keep.astype(F32) + got.astype(F32)).astype(value.dtype)
+    return value
+
+
+def gather_back(value, mesh_axis, axis):
+    me = lax.axis_index(mesh_axis)
+    for bit in reversed(bits_of(mesh_axis)):
+        got = swap(value, mesh_axis, bit)
+        low = (me // bit) % 2 == 0
+        value = jnp.concatenate(
+            [jnp.where(low, value, got), jnp.where(low, got, value)], axis=axis
+        )
     return value
 
 
@@ -646,11 +644,11 @@
     rows = tok_rows // PIECES
     share = rows // shares
     me = lax.axis_index("tensor").astype(jnp.int32)
-    side = (lax.axis_index("dp") % 2).astype(jnp.int32)
-    idx = jnp.stack([me, side])
+    idx = me.reshape(1)
     mib = 1 << 20
     others = range(1, shares)
 
+    wo = lax.all_gather(w_out, "tensor", axis=0, tiled=True)
     build_hot, gather_hot = near_tables()
     build_hot = jnp.asarray(np.swapaxes(build_hot, 1, 2), BF16)
     gather_hot = jnp.asarray(gather_hot, F32)
@@ -689,16 +687,10 @@
     bias, far = bias_args
     normed_one = [s[0] for s in stages]
 
-    half_rows = features // 2
-    my_half = lax.dynamic_slice_in_dim(w_out, side * half_rows, half_rows, 0)
-    my_half = after(my_half, stages[0][5])
-    halves = [swap(my_half, "tensor", by) for by in others]
-    swapped = swap(after(jnp.stack(halves), stages[-1][5]), "dp", 1)
-
     atts = []
     for stage in stages:
         mine = after(stage[5], *atts[-1][1:]) if atts else stage[5]
-        atts.append(gather_parts(mine, "tensor"))
+        atts.append(exchange([mine] * shares, "tensor"))
 
     full = lambda shape: pl.BlockSpec(shape, lambda e: (0,) * len(shape))
     per_expert = lambda shape: pl.BlockSpec((1,) + shape, lambda e: (e, 0, 0))
@@ -707,30 +699,27 @@
     )
     moe_flops = 4 * experts * rows * width * hidden_units
 
-    def moe_forward(piece, wo_args):
-        wo_specs = [full(one.shape) for one in wo_args]
-        wo_shape = (shares, features, width)
+    per_piece = lambda piece, lanes: pl.BlockSpec((rows, lanes), lambda e: (piece, 0))
+
+    def moe_forward(piece):
         return pl.pallas_call(
-            functools.partial(moe_fwd_kernel, piece, PIECES, shares, experts),
+            functools.partial(moe_fwd_kernel, shares, experts),
             grid=(experts,),
             in_specs=[SMEM]
             + [full((rows, features))] * shares
-            + wo_specs
             + [
-                full((tok_rows, width)), full((1, width)), full((experts, width)),
-                full((tok_rows, 2)), full((tok_rows, width)),
+                full((width, width)), per_piece(piece, width), full((1, width)),
+                full((experts, width)), per_piece(piece, 2), per_piece(piece, width),
                 per_expert((width, hidden_units)), per_expert((hidden_units, width)),
             ],
-            out_specs=[full((share, width))] * shares
-            + [full(wo_shape)] * (piece == 0)
-            + [
+            out_specs=[
+                full((rows, width)),
                 full((rows, width)), full((share, width)), full((rows, LANES)),
                 full((rows, LANES)), per_expert((rows, hidden_units)),
                 per_expert((rows, hidden_units)),
             ],
-            out_shape=[shaped((share, width), BF16)] * shares
-            + [shaped(wo_shape, BF16)] * (piece == 0)
-            + [
+            out_shape=[
+                shaped((rows, width), BF16),
                 shaped((rows, width), BF16),
                 shaped((share, width), F32),
                 shaped((rows, LANES), F32),
@@ -744,16 +733,15 @@
                 flops=moe_flops, bytes_accessed=20 * mib, transcendentals=0
             ),
         )(
-            idx, *atts[piece], *wo_args, tokens, gain_two, router_t, routes, grad_out,
-            w_in, w_down,
+            idx, *atts[piece], wo, tokens, gain_two, router_t, routes, grad_out, w_in, w_down
         )
 
     def moe_backward(piece, gates, ggate, slope):
         return pl.pallas_call(
-            functools.partial(moe_bwd_kernel, piece, shares, experts),
+            functools.partial(moe_bwd_kernel, shares, experts),
             grid=(experts,),
             in_specs=[
-                SMEM, full((rows, LANES)), full((rows, LANES)), full((tok_rows, width)),
+                SMEM, full((rows, LANES)), full((rows, LANES)), per_piece(piece, width),
                 per_expert((rows, hidden_units)), full((experts, width)),
                 per_expert((width, hidden_units)), per_expert((hidden_units, width)),
             ],
@@ -772,18 +760,16 @@
         )(idx, gates, ggate, grad_out, slope, router_t, w_in, w_down)
 
     moe_got, gx_got, forwards, backwards = [], [], [], []
-    wo_args = [w_out, swapped, *halves]
     for piece in range(PIECES):
-        fwd = moe_forward(piece, wo_args)
-        parts, kept = fwd[:shares], fwd[shares:]
-        if piece == 0:
-            wo, kept = kept[0], kept[1:]
-            wo_args = [wo]
-        moe_got.append(reduce_parts(parts, "tensor"))
+        fwd = moe_forward(piece)
+        moe_sum, kept = fwd[0], fwd[1:]
+        moe_got.append(
+            [lax.psum_scatter(moe_sum, "tensor", scatter_dimension=0, tiled=True)]
+        )
         gates, ggate, slope = kept[2], kept[3], kept[5]
         bwd = moe_backward(piece, gates, ggate, slope)
         parts = bwd[:shares]
-        gx_got.append(reduce_parts(parts, "tensor"))
+        gx_got.append(exchange(parts, "tensor"))
         forwards.append(kept)
         backwards.append(bwd[shares:])
     normed_two = [f[0] for f in forwards]
@@ -805,7 +791,7 @@
             flops=2 * 10**8, moved=5 * mib,
         )
         parts = got[:shares]
-        go = [parts[0]] + [swap(parts[by], "tensor", by) for by in others]
+        go = exchange(parts, "tensor")
         return go, got[shares:]
 
     def attend_back(piece, go, carried):
@@ -908,23 +894,17 @@
         [shaped((tok_rows, width), F32)], [idx, *gt_got], moved=5 * mib,
     )[0]
 
-    late = after(jnp.concatenate([qkv_rows, w_out_rows], axis=0), gt_share)
+    late = after(jnp.concatenate([qkv_rows, w_out_rows], axis=0), gt_got[2])
     late = scatter_sum(late, "dp", 1)
     out_sum = late[3].astype(F32)
     for by in others:
         out_sum = out_sum + swap(late[3 + by], "tensor", by).astype(F32)
-    late_rows = late.shape[1]
     late = jnp.concatenate([late[:3], out_sum.astype(BF16)[None]], axis=0)
-    shard = expert_rows.shape[0]
-    both = jnp.concatenate([after(expert_rows, late), late.reshape(4 * late_rows, width)], axis=0)
-    both = lax.all_gather(both, "dp", axis=0)
-    expert_rows = both[:, :shard].reshape(experts, 2, width, width)
+    late = gather_back(late, "dp", 1)
+    expert_rows = lax.all_gather(after(expert_rows, gt_got[2]), "dp", axis=0, tiled=True)
+    expert_rows = expert_rows.reshape(experts, 2, width, width)
     grad_w_in = expert_rows[:, 0].astype(F32)
     grad_w_down = expert_rows[:, 1].astype(F32)
-    levels = len(bits_of("dp"))
-    late = both[:, shard:].reshape([2] * levels + [4, late_rows, width])
-    late = jnp.transpose(late, [levels, *reversed(range(levels)), levels + 1, levels + 2])
-    late = late.reshape(4, features, width)
     grad_w_qkv = jnp.swapaxes(late[:3], 1, 2).astype(F32)
     grad_w_out = late[3].astype(F32)
 

time: 413 us -> 446 us (1.080)
  waiting for transfers between devices: 148 us -> 201 us
  local copies, waits for them, and re-layouts: 24.1 us -> 11.1 us
  Pallas kernels: 147 us -> 135 us
  starting transfers between devices: 52.1 us -> 60 us
    ppermute x48 -> x41, waiting for transfers between devices: 148 us -> 193 us  [swap(): return lax.ppermute(value, axis, [(i, i ^ bit) for i in range(count)])]
    pallas_call x12, Pallas kernels: 73.1 us -> 63 us  [whole_call(): pl.pallas_call(kernel, out_shape=outs, in_specs=specs, out_specs=[VMEM] *...]
    slice x2 -> x0, local copies, waits for them, and re-layouts: 9.2 us -> none  [the longest x1 7.85 us: body(): expert_rows = both[:, :shard].reshape(experts, 2, width, width)]
    all_gather x1 -> x2, waiting for transfers between devices: 0.01 us -> 7.47 us  [the longest x1 7.47 us: body(): wo = lax.all_gather(w_out, 'tensor', axis=0, tiled=True)]
    ppermute x48 -> x41, starting transfers between devices: 52.1 us -> 59.2 us  [swap(): return lax.ppermute(value, axis, [(i, i ^ bit) for i in range(count)])]
  transfers between devices with their start and end apart: 50 -> 46, of which waited for: 27 -> 25; matrix products, arithmetic and copies ran while one was open for 2% -> 3% of each run, Pallas kernels for 29% -> 27%
where the time goes in v1:
time: 446 us; the launch traced here: 441 us
  waiting for transfers between devices  201 us (45%)
  Pallas kernels  135 us (30%)
  starting transfers between devices  60 us (13%)
  other arithmetic  19.3 us (4%)
  between operations  14.8 us (3%)
  local copies, waits for them, and re-layouts  11.1 us (2%)
    ppermute x41, waiting for transfers between devices, swap(): return lax.ppermute(value, axis, [(i, i ^ bit) for i in range(count)])  193 us
    pallas_call x12, Pallas kernels, whole_call(): pl.pallas_call(kernel, out_shape=outs, in_specs=specs, out_specs=[VMEM] *...  63 us
    ppermute x41, starting transfers between devices, swap(): return lax.ppermute(value, axis, [(i, i ^ bit) for i in range(count)])  59.2 us
    pallas_call x2, Pallas kernels, moe_forward(): pl.pallas_call(functools.partial(moe_fwd_kernel, shares, experts), grid=(...  30.4 us
    pallas_call x2, Pallas kernels, moe_backward(): pl.pallas_call(functools.partial(moe_bwd_kernel, shares, experts), grid=(...  25 us
    pallas_call x1, Pallas kernels, body(): pl.pallas_call(functools.partial(moe_weights_kernel, PIECES), grid=(exper...  16.1 us
    convert_element_type x1, other arithmetic, body(): grad_w_down = expert_rows[:, 1].astype(F32)  12.3 us
  transfers between devices with their start and end apart: 46, of which 25 were waited for; matrix products, arithmetic and copies ran while one was open for 3% of the time, Pallas kernels for 27%

profile of v1, /device:TPU:0, one launch (start us, length us, event | category | flops | bytes accessed | tf_op | source)
XLA Modules:
  0.0 441.0 jit_solution(7762277569490444698)
XLA Ops:
  9.2 7.5 %shard_map.213 = (bf16[512,768]{1,0:T(8,128)(2,1)}, bf16[3,512,192]{2,1,0:T(8,128)(2,1)}, bf16[512,192]{1,0:T(8,128)(2,1)}, bf16[512,192]{1,0:T(8,128)(2,1)}, bf...) custom-call(bf16[1024,768]{1,0:T(8,128)(2,1)} %refs_5_.10, ...), custom_call_target="tpu_custom_call" | custom-call | flops 3000000000 | bytes 8388608 | tf_op jit(solution)/shard_map/pallas_call | solution.py:552
  24.0 16.2 %collective-permute-done.refs_1_ = bf16[512,192]{1,0:T(8,128)(2,1)S(1)} collective-permute-done((bf16[512,192]{1,0:T(8,128)(2,1)}, bf16[512,192]{1,0:T(8,128)(2,1)S(1)}, u32[]{:S(2)}, u32[]{:S(2)}) %collective-permute-start) | collective-permute-done | bytes 196640 | tf_op jit(solution)/shard_map/ppermute | solution.py:565
  40.2 11.7 %collective-permute-done.1.refs_2_ = bf16[512,192]{1,0:T(8,128)(2,1)S(1)} collective-permute-done((bf16[512,192]{1,0:T(8,128)(2,1)}, bf16[512,192]{1,0:T(8,128)(2,1)S(1)}, u32[]{:S(2)}, u32[]{:S(2)}) %collective-permute-start.1) | collective-permute-done | bytes 196640 | tf_op jit(solution)/shard_map/ppermute | solution.py:565
  51.9 4.3 collective-permute-done.2.refs_3_
  56.2 7.5 %all-gather.3.cloned.1.call-done.refs_4_ = bf16[768,768]{1,0:T(8,128)(2,1)} async-done(((bf16[192,768]{1,0:T(8,128)(2,1)}), bf16[768,768]{1,0:T(8,128)(2,1)}) %all-gather.3.cloned.1.call-update) | async-done | bytes 1179664 | tf_op jit(solution)/shard_map/all_gather | solution.py:651
  63.6 15.2 %shard_map.214 = (bf16[512,768]{1,0:T(8,128)(2,1)}, bf16[512,768]{1,0:T(8,128)(2,1)}, f32[128,768]{1,0:T(8,128)}, f32[512,128]{1,0:T(8,128)}, f32[512,128]{1,0:T...) custom-call(s32[1]{0:T(128)} %bitcast.idx, bf16[512,192]{1,0:T(8,128)(2,1)} %get-tuple-element.89.refs_0_, ...), custom_call_target="tpu_custom_call" | custom-call | flops 4831838208 | bytes 20971520 | tf_op jit(solution)/shard_map/pallas_call | solution.py:705
  79.1 8.0 %shard_map.215 = (bf16[512,768]{1,0:T(8,128)(2,1)}, bf16[3,512,192]{2,1,0:T(8,128)(2,1)}, bf16[512,192]{1,0:T(8,128)(2,1)}, bf16[512,192]{1,0:T(8,128)(2,1)}, bf...) custom-call(bf16[1024,768]{1,0:T(8,128)(2,1)} %refs_5_.10, ...), custom_call_target="tpu_custom_call" | custom-call | flops 3000000000 | bytes 8388608 | tf_op jit(solution)/shard_map/pallas_call | solution.py:552
  91.6 19.3 %collective-permute-done.3.refs_1_.refs_5_ = bf16[512,192]{1,0:T(8,128)(2,1)S(1)} collective-permute-done((bf16[512,192]{1,0:T(8,128)(2,1)}, bf16[512,192]{1,0:T(8,128)(2,1)S(1)}, u32[]{:S(2)}, u32[]{:S(2)}) %collective-permute-start.3) | collective-permute-done | bytes 196640 | tf_op jit(solution)/shard_map/ppermute | solution.py:565
  111.3 7.2 %collective-permute-done.5.refs_3_.refs_7_ = bf16[512,192]{1,0:T(8,128)(2,1)S(1)} collective-permute-done((bf16[512,192]{1,0:T(8,128)(2,1)}, bf16[512,192]{1,0:T(8,128)(2,1)S(1)}, u32[]{:S(2)}, u32[]{:S(2)}) %collective-permute-start.5) | collective-permute-done | bytes 196640 | tf_op jit(solution)/shard_map/ppermute | solution.py:565
  119.2 15.2 %shard_map.216 = (bf16[512,768]{1,0:T(8,128)(2,1)}, bf16[512,768]{1,0:T(8,128)(2,1)}, f32[128,768]{1,0:T(8,128)}, f32[512,128]{1,0:T(8,128)}, f32[512,128]{1,0:T...) custom-call(s32[1]{0:T(128)} %bitcast.idx, bf16[512,192]{1,0:T(8,128)(2,1)} %get-tuple-element.96.refs_0_.refs_4_, ...), custom_call_target="tpu_custom_call" | custom-call | flops 4831838208 | bytes 20971520 | tf_op jit(solution)/shard_map/pallas_call | solution.py:705
  134.7 12.6 %shard_map.220 = (bf16[128,768]{1,0:T(8,128)(2,1)}, bf16[128,768]{1,0:T(8,128)(2,1)}, bf16[128,768]{1,0:T(8,128)(2,1)}, bf16[128,768]{1,0:T(8,128)(2,1)}, f32[51...) custom-call(s32[1]{0:T(128)} %bitcast.idx, f32[512,128]{1,0:T(8,128)} %get-tuple-element.107.refs_0_, ...), custom_call_target="tpu_custom_call" | custom-call | flops 4831838208 | bytes 16777216 | tf_op jit(solution)/shard_map/pallas_call | solution.py:740
  147.3 5.2 %collective-permute-start.12 = (bf16[128,768]{1,0:T(8,128)(2,1)}, bf16[128,768]{1,0:T(8,128)(2,1)S(1)}, u32[]{:S(2)}, u32[]{:S(2)}) collective-permute-start(bf16[128,768]{1,0:T(8,128)(2,1)} %get-tuple-element.111), channel_id=1, source_target_pairs={{0,1},{1,0},{2,3},{3,2},{4,5},{5,4},{6,7},{7,6},{8,9},{9,8},{10,11... | collective-permute-start | bytes 589832 | tf_op jit(solution)/shard_map/ppermute | solution.py:565
  155.0 12.4 %shard_map.219 = (bf16[128,768]{1,0:T(8,128)(2,1)}, bf16[128,768]{1,0:T(8,128)(2,1)}, bf16[128,768]{1,0:T(8,128)(2,1)}, bf16[128,768]{1,0:T(8,128)(2,1)}, f32[51...) custom-call(s32[1]{0:T(128)} %bitcast.idx, f32[512,128]{1,0:T(8,128)} %get-tuple-element.100.refs_0_.refs_1_, ...), custom_call_target="tpu_custom_call" | custom-call | flops 4831838208 | bytes 16777216 | tf_op jit(solution)/shard_map/pallas_call | solution.py:740
  167.5 5.3 %collective-permute-done.14.refs_3_ = bf16[128,768]{1,0:T(8,128)(2,1)S(1)} collective-permute-done((bf16[128,768]{1,0:T(8,128)(2,1)}, bf16[128,768]{1,0:T(8,128)(2,1)S(1)}, u32[]{:S(2)}, u32[]{:S(2)}) %collective-permute-start.14) | collective-permute-done | bytes 196640 | tf_op jit(solution)/shard_map/ppermute | solution.py:565
  177.2 16.1 %shard_map.222 = (bf16[4,2,768,768]{3,2,1,0:T(8,128)(2,1)}, f32[8,768]{1,0:T(8,128)}) custom-call(bf16[1024,768]{1,0:T(8,128)(2,1)} %refs_6_.7, f32[512,128]{1,0:T(8,128)} %get-tuple-element.107.refs_0_, f32[512,128]{1,0:T(8,128)} %get-tuple-element.100.refs_0_.refs_1_, f32[512,128]{1,0:T(8,128)} %get-tuple-element.116.refs_2_, ...), custom_call_target="tpu_custom_call" | custom-call | flops 9663676416 | bytes 27262976 | tf_op jit(solution)/shard_map/pallas_call | solution.py:830
  194.2 4.1 collective-permute-start.9
  208.6 9.7 %collective-permute-done.10.refs_2_ = bf16[128,768]{1,0:T(8,128)(2,1)S(1)} collective-permute-done((bf16[128,768]{1,0:T(8,128)(2,1)S(1)}, bf16[128,768]{1,0:T(8,128)(2,1)S(1)}, u32[]{:S(2)}, u32[]{:S(2)}) %collective-permute-start.10) | collective-permute-done | bytes 196640 | tf_op jit(solution)/shard_map/ppermute | solution.py:565
  223.0 4.3 collective-permute-start.18
  230.4 7.0 %shard_map.224 = (f32[512,192]{1,0:T(8,128)}, f32[512,192]{1,0:T(8,128)}, f32[192,512]{1,0:T(8,128)}, f32[6,256,256]{2,1,0:T(8,128)}) custom-call(s32[1]{0:T(128)} %bitcast.idx, bf16[128,192]{1,0:T(8,128)(2,1)} %get-tuple-element.129.refs_0_, bf16[128,192]{1,0:T(8,128)(2,1)} %copy-done.37, bf16[128,192]{1,0:T(8,128)(2,1)} %copy-done.38, ...), custom_call_target="tpu_custom_call" | custom-call | flops 7000000000 | bytes 8388608 | tf_op jit(solution)/shard_map/pallas_call | solution.py:552
  240.2 14.2 %shard_map.225 = (bf16[256,768]{1,0:T(8,128)(2,1)}, bf16[256,768]{1,0:T(8,128)(2,1)}, bf16[256,768]{1,0:T(8,128)(2,1)}, bf16[256,768]{1,0:T(8,128)(2,1)}, bf16[3...) custom-call(s32[1]{0:T(128)} %bitcast.idx, bf16[128,192]{1,0:T(8,128)(2,1)} %get-tuple-element.138.refs_0_, ...), custom_call_target="tpu_custom_call" | custom-call | flops 7000000000 | bytes 8388608 | tf_op jit(solution)/shard_map/pallas_call | solution.py:552
  256.4 14.2 %collective-permute-done.22 = bf16[256,768]{1,0:T(8,128)(2,1)S(1)} collective-permute-done((bf16[256,768]{1,0:T(8,128)(2,1)}, bf16[256,768]{1,0:T(8,128)(2,1)S(1)}, u32[]{:S(2)}, u32[]{:S(2)}) %collective-permute-start.22) | collective-permute-done | bytes 393248 | tf_op jit(solution)/shard_map/ppermute | solution.py:565
  274.9 16.6 %collective-permute-done.23.refs_2_ = bf16[256,768]{1,0:T(8,128)(2,1)S(1)} collective-permute-done((bf16[256,768]{1,0:T(8,128)(2,1)S(1)}, bf16[256,768]{1,0:T(8,128)(2,1)S(1)}, u32[]{:S(2)}, u32[]{:S(2)}) %collective-permute-start.23) | collective-permute-done | bytes 393248 | tf_op jit(solution)/shard_map/ppermute | solution.py:565
  295.4 11.5 %collective-permute-done.25.refs_2_ = bf16[256,768]{1,0:T(8,128)(2,1)S(1)} collective-permute-done((bf16[256,768]{1,0:T(8,128)(2,1)}, bf16[256,768]{1,0:T(8,128)(2,1)S(1)}, u32[]{:S(2)}, u32[]{:S(2)}) %collective-permute-start.25) | collective-permute-done | bytes 393248 | tf_op jit(solution)/shard_map/ppermute | solution.py:565
  310.5 4.0 shard_map.228
  322.6 19.0 %collective-permute-done.33 = bf16[7,48,768]{2,1,0:T(8,128)(2,1)S(1)} collective-permute-done((bf16[7,48,768]{2,1,0:T(8,128)(2,1)S(1)}, bf16[7,48,768]{2,1,0:T(8,128)(2,1)S(1)}, u32[]{:S(2)}, u32[]{:S(2)}) %collective-permute-start.33) | collective-permute-done | bytes 516128 | tf_op jit(solution)/shard_map/ppermute | solution.py:565
  343.4 11.0 %collective-permute-done.34 = bf16[7,24,768]{2,1,0:T(8,128)(2,1)S(1)} collective-permute-done((bf16[7,24,768]{2,1,0:T(8,128)(2,1)S(1)}, bf16[7,24,768]{2,1,0:T(8,128)(2,1)S(1)}, u32[]{:S(2)}, u32[]{:S(2)}) %collective-permute-start.34) | collective-permute-done | bytes 258080 | tf_op jit(solution)/shard_map/ppermute | solution.py:565
  360.7 5.6 %collective-permute-done.36 = bf16[24,768]{1,0:T(8,128)(2,1)S(1)} collective-permute-done((bf16[24,768]{1,0:T(8,128)(2,1)S(1)}, bf16[24,768]{1,0:T(8,128)(2,1)S(1)}, u32[]{:S(2)}, u32[]{:S(2)}) %collective-permute-start.36) | collective-permute-done | bytes 36896 | tf_op jit(solution)/shard_map/ppermute | solution.py:565
  369.2 7.8 %collective-permute-done.7.refs_2_ = bf16[256,768]{1,0:T(8,128)(2,1)S(1)} collective-permute-done((bf16[256,768]{1,0:T(8,128)(2,1)S(1)}, bf16[256,768]{1,0:T(8,128)(2,1)S(1)}, u32[]{:S(2)}, u32[]{:S(2)}) %collective-permute-start.7) | collective-permute-done | bytes 393248 | tf_op jit(solution)/shard_map/ppermute | solution.py:565
  379.4 8.9 %collective-permute-done.28 = f32[18,768]{1,0:T(8,128)S(1)} collective-permute-done((f32[18,768]{1,0:T(8,128)S(1)}, f32[18,768]{1,0:T(8,128)S(1)}, u32[]{:S(2)}, u32[]{:S(2)}) %collective-permute-start.28) | collective-permute-done | bytes 55328 | tf_op jit(solution)/shard_map/ppermute | solution.py:565
  396.4 6.0 %collective-permute-done.30 = f32[10,768]{1,0:T(8,128)S(1)} collective-permute-done((f32[10,768]{1,0:T(8,128)S(1)}, f32[10,768]{1,0:T(8,128)S(1)}, u32[]{:S(2)}, u32[]{:S(2)}) %collective-permute-start.30) | collective-permute-done | bytes 30752 | tf_op jit(solution)/shard_map/ppermute | solution.py:565
  409.0 6.3 %collective-permute-done.26.refs_3_ = bf16[256,768]{1,0:T(8,128)(2,1)S(1)} collective-permute-done((bf16[256,768]{1,0:T(8,128)(2,1)S(1)}, bf16[256,768]{1,0:T(8,128)(2,1)S(1)}, u32[]{:S(2)}, u32[]{:S(2)}) %collective-permute-start.26) | collective-permute-done | bytes 393248 | tf_op jit(solution)/shard_map/ppermute | solution.py:565
  421.7 12.3 %fusion = (f32[4,768,768]{2,1,0:T(8,128)}, f32[4,768,768]{2,1,0:T(8,128)}) fusion(bf16[4,2,768,768]{3,2,1,0:T(8,128)(2,1)} %bitcast.40), kind=kLoop, calls=%fused_computation.1 | loop fusion | flops 4718592 | bytes 28311552 | tf_op jit(solution)/shard_map/convert_element_type | solution.py:907
  (198 shorter events, 100.0 us)
Async XLA Ops:
  7.2 56.4 %all-gather.3.cloned.1.call-start = ((), (), s32[]{:S(2)}) async-start(), calls=%async_computation.3 | async-start | bytes 1474560 | tf_op jit(solution)/shard_map/all_gather | solution.py:651
  7.9 229.4 %reduce-scatter.4.cloned.1.call-start = ((), (), s32[]{:S(2)}) async-start(), calls=%async_computation.4 | async-start | bytes 983040 | tf_op jit(solution)/shard_map/reduce_scatter | solution.py:767
  16.7 23.4 %collective-permute-start = (bf16[512,192]{1,0:T(8,128)(2,1)}, bf16[512,192]{1,0:T(8,128)(2,1)S(1)}, u32[]{:S(2)}, u32[]{:S(2)}) collective-permute-start(bf16[512,192]{1,0:T(8,128)(2,1)} %get-tuple-element.89.refs_0_), channel_id=1, source_target_pairs={{0,1},{1,0},{2,3},{3,2},{4,5},{5,4},{6,7},{7,6},{8,9},{9,8},{10,11... | collective-permute-start | bytes 589832 | tf_op jit(solution)/shard_map/ppermute | solution.py:565
  19.8 32.1 %collective-permute-start.1 = (bf16[512,192]{1,0:T(8,128)(2,1)}, bf16[512,192]{1,0:T(8,128)(2,1)S(1)}, u32[]{:S(2)}, u32[]{:S(2)}) collective-permute-start(bf16[512,192]{1,0:T(8,128)(2,1)} %get-tuple-element.89.refs_0_), channel_id=1, source_target_pairs={{0,2},{1,3},{2,0},{3,1},{4,6},{5,7},{6,4},{7,5},{8,10},{9,11},{10,... | collective-permute-start | bytes 589832 | tf_op jit(solution)/shard_map/ppermute | solution.py:565
  22.3 33.8 %collective-permute-start.2 = (bf16[512,192]{1,0:T(8,128)(2,1)}, bf16[512,192]{1,0:T(8,128)(2,1)S(1)}, u32[]{:S(2)}, u32[]{:S(2)}) collective-permute-start(bf16[512,192]{1,0:T(8,128)(2,1)} %get-tuple-element.89.refs_0_), channel_id=1, source_target_pairs={{0,3},{1,2},{2,1},{3,0},{4,7},{5,6},{6,5},{7,4},{8,11},{9,10},{10,... | collective-permute-start | bytes 589832 | tf_op jit(solution)/shard_map/ppermute | solution.py:565
  78.8 158.5 %reduce-scatter.6.cloned.1.call-start = ((), (), s32[]{:S(2)}) async-start(), calls=%async_computation.5 | async-start | bytes 983040 | tf_op jit(solution)/shard_map/reduce_scatter | solution.py:767
  87.1 23.9 %collective-permute-start.3 = (bf16[512,192]{1,0:T(8,128)(2,1)}, bf16[512,192]{1,0:T(8,128)(2,1)S(1)}, u32[]{:S(2)}, u32[]{:S(2)}) collective-permute-start(bf16[512,192]{1,0:T(8,128)(2,1)} %get-tuple-element.96.refs_0_.refs_4_), channel_id=1, source_target_pairs={{0,1},{1,0},{2,3},{3,2},{4,5},{5,4},{6,7},{7,6},{8,9},{9,8},{10,11... | collective-permute-start | bytes 589832 | tf_op jit(solution)/shard_map/ppermute | solution.py:565
  89.2 22.1 %collective-permute-start.4 = (bf16[512,192]{1,0:T(8,128)(2,1)}, bf16[512,192]{1,0:T(8,128)(2,1)S(1)}, u32[]{:S(2)}, u32[]{:S(2)}) collective-permute-start(bf16[512,192]{1,0:T(8,128)(2,1)} %get-tuple-element.96.refs_0_.refs_4_), channel_id=1, source_target_pairs={{0,2},{1,3},{2,0},{3,1},{4,6},{5,7},{6,4},{7,5},{8,10},{9,11},{10,... | collective-permute-start | bytes 589832 | tf_op jit(solution)/shard_map/ppermute | solution.py:565
  89.5 29.0 %collective-permute-start.5 = (bf16[512,192]{1,0:T(8,128)(2,1)}, bf16[512,192]{1,0:T(8,128)(2,1)S(1)}, u32[]{:S(2)}, u32[]{:S(2)}) collective-permute-start(bf16[512,192]{1,0:T(8,128)(2,1)} %get-tuple-element.96.refs_0_.refs_4_), channel_id=1, source_target_pairs={{0,3},{1,2},{2,1},{3,0},{4,7},{5,6},{6,5},{7,4},{8,11},{9,10},{10,... | collective-permute-start | bytes 589832 | tf_op jit(solution)/shard_map/ppermute | solution.py:565
  134.4 172.5 %reduce-scatter.8.cloned.1.call-start = ((), (), s32[]{:S(2)}) async-start(), calls=%async_computation.6 | async-start | bytes 10616832 | tf_op jit(solution)/shard_map/reduce_scatter | solution.py:846
  147.3 20.1 %collective-permute-start.12 = (bf16[128,768]{1,0:T(8,128)(2,1)}, bf16[128,768]{1,0:T(8,128)(2,1)S(1)}, u32[]{:S(2)}, u32[]{:S(2)}) collective-permute-start(bf16[128,768]{1,0:T(8,128)(2,1)} %get-tuple-element.111), channel_id=1, source_target_pairs={{0,1},{1,0},{2,3},{3,2},{4,5},{5,4},{6,7},{7,6},{8,9},{9,8},{10,11... | collective-permute-start | bytes 589832 | tf_op jit(solution)/shard_map/ppermute | solution.py:565
  152.5 14.9 %collective-permute-start.13 = (bf16[128,768]{1,0:T(8,128)(2,1)}, bf16[128,768]{1,0:T(8,128)(2,1)S(1)}, u32[]{:S(2)}, u32[]{:S(2)}) collective-permute-start(bf16[128,768]{1,0:T(8,128)(2,1)} %get-tuple-element.112), channel_id=1, source_target_pairs={{0,2},{1,3},{2,0},{3,1},{4,6},{5,7},{6,4},{7,5},{8,10},{9,11},{10,... | collective-permute-start | bytes 589832 | tf_op jit(solution)/shard_map/ppermute | solution.py:565
  152.5 20.2 %collective-permute-start.14 = (bf16[128,768]{1,0:T(8,128)(2,1)}, bf16[128,768]{1,0:T(8,128)(2,1)S(1)}, u32[]{:S(2)}, u32[]{:S(2)}) collective-permute-start(bf16[128,768]{1,0:T(8,128)(2,1)} %get-tuple-element.113), channel_id=1, source_target_pairs={{0,3},{1,2},{2,1},{3,0},{4,7},{5,6},{6,5},{7,4},{8,11},{9,10},{10,... | collective-permute-start | bytes 589832 | tf_op jit(solution)/shard_map/ppermute | solution.py:565
  193.4 228.4 %all-gather.5.cloned.1.call-start = ((), (), s32[]{:S(2)}) async-start(), calls=%async_computation.7 | async-start | bytes 10616832 | tf_op jit(solution)/shard_map/all_gather | solution.py:904
  194.2 12.4 %collective-permute-start.9 = (bf16[128,768]{1,0:T(8,128)(2,1)S(1)}, bf16[128,768]{1,0:T(8,128)(2,1)S(1)}, u32[]{:S(2)}, u32[]{:S(2)}) collective-permute-start(bf16[128,768]{1,0:T(8,128)(2,1)S(1)} %copy-done.31), channel_id=1, source_target_pairs={{0,1},{1,0},{2,3},{3,2},{4,5},{5,4},{6,7},{7,6},{8,9},{9,8},{10,11... | collective-permute-start | bytes 589832 | tf_op jit(solution)/shard_map/ppermute | solution.py:565
  198.3 20.0 %collective-permute-start.10 = (bf16[128,768]{1,0:T(8,128)(2,1)S(1)}, bf16[128,768]{1,0:T(8,128)(2,1)S(1)}, u32[]{:S(2)}, u32[]{:S(2)}) collective-permute-start(bf16[128,768]{1,0:T(8,128)(2,1)S(1)} %copy-done.30), channel_id=1, source_target_pairs={{0,2},{1,3},{2,0},{3,1},{4,6},{5,7},{6,4},{7,5},{8,10},{9,11},{10,... | collective-permute-start | bytes 589832 | tf_op jit(solution)/shard_map/ppermute | solution.py:565
  198.4 19.9 %collective-permute-start.11 = (bf16[128,768]{1,0:T(8,128)(2,1)S(1)}, bf16[128,768]{1,0:T(8,128)(2,1)S(1)}, u32[]{:S(2)}, u32[]{:S(2)}) collective-permute-start(bf16[128,768]{1,0:T(8,128)(2,1)S(1)} %copy-done.29), channel_id=1, source_target_pairs={{0,3},{1,2},{2,1},{3,0},{4,7},{5,6},{6,5},{7,4},{8,11},{9,10},{10,... | collective-permute-start | bytes 589832 | tf_op jit(solution)/shard_map/ppermute | solution.py:565
  200.8 27.0 %collective-permute-start.15 = (bf16[128,192]{1,0:T(8,128)(2,1)S(1)}, bf16[128,192]{1,0:T(8,128)(2,1)S(1)}, u32[]{:S(2)}, u32[]{:S(2)}) collective-permute-start(bf16[128,192]{1,0:T(8,128)(2,1)S(1)} %copy-done.34), channel_id=1, source_target_pairs={{0,1},{1,0},{2,3},{3,2},{4,5},{5,4},{6,7},{7,6},{8,9},{9,8},{10,11... | collective-permute-start | bytes 147464 | tf_op jit(solution)/shard_map/ppermute | solution.py:565
  201.8 27.9 %collective-permute-start.16 = (bf16[128,192]{1,0:T(8,128)(2,1)S(1)}, bf16[128,192]{1,0:T(8,128)(2,1)S(1)}, u32[]{:S(2)}, u32[]{:S(2)}) collective-permute-start(bf16[128,192]{1,0:T(8,128)(2,1)S(1)} %copy-done.33), channel_id=1, source_target_pairs={{0,2},{1,3},{2,0},{3,1},{4,6},{5,7},{6,4},{7,5},{8,10},{9,11},{10,... | collective-permute-start | bytes 147464 | tf_op jit(solution)/shard_map/ppermute | solution.py:565
  206.6 23.1 %collective-permute-start.17 = (bf16[128,192]{1,0:T(8,128)(2,1)S(1)}, bf16[128,192]{1,0:T(8,128)(2,1)S(1)}, u32[]{:S(2)}, u32[]{:S(2)}) collective-permute-start(bf16[128,192]{1,0:T(8,128)(2,1)S(1)} %copy-done.32), channel_id=1, source_target_pairs={{0,3},{1,2},{2,1},{3,0},{4,7},{5,6},{6,5},{7,4},{8,11},{9,10},{10,... | collective-permute-start | bytes 147464 | tf_op jit(solution)/shard_map/ppermute | solution.py:565
  223.0 16.5 %collective-permute-start.18 = (bf16[128,192]{1,0:T(8,128)(2,1)}, bf16[128,192]{1,0:T(8,128)(2,1)S(1)}, u32[]{:S(2)}, u32[]{:S(2)}) collective-permute-start(bf16[128,192]{1,0:T(8,128)(2,1)} %get-tuple-element.139), channel_id=1, source_target_pairs={{0,1},{1,0},{2,3},{3,2},{4,5},{5,4},{6,7},{7,6},{8,9},{9,8},{10,11... | collective-permute-start | bytes 147464 | tf_op jit(solution)/shard_map/ppermute | solution.py:565
  254.3 16.3 %collective-permute-start.22 = (bf16[256,768]{1,0:T(8,128)(2,1)}, bf16[256,768]{1,0:T(8,128)(2,1)S(1)}, u32[]{:S(2)}, u32[]{:S(2)}) collective-permute-start(bf16[256,768]{1,0:T(8,128)(2,1)} %get-tuple-element.153), channel_id=1, source_target_pairs={{0,1},{1,0},{2,3},{3,2},{4,5},{5,4},{6,7},{7,6},{8,9},{9,8},{10,11... | collective-permute-start | bytes 1179656 | tf_op jit(solution)/shard_map/ppermute | solution.py:565
  255.6 19.3 %collective-permute-start.21 = (bf16[256,768]{1,0:T(8,128)(2,1)}, bf16[256,768]{1,0:T(8,128)(2,1)S(1)}, u32[]{:S(2)}, u32[]{:S(2)}) collective-permute-start(bf16[256,768]{1,0:T(8,128)(2,1)} %get-tuple-element.151), channel_id=1, source_target_pairs={{0,1},{1,0},{2,3},{3,2},{4,5},{5,4},{6,7},{7,6},{8,9},{9,8},{10,11... | collective-permute-start | bytes 1179656 | tf_op jit(solution)/shard_map/ppermute | solution.py:565
  271.7 19.7 %collective-permute-start.23 = (bf16[256,768]{1,0:T(8,128)(2,1)S(1)}, bf16[256,768]{1,0:T(8,128)(2,1)S(1)}, u32[]{:S(2)}, u32[]{:S(2)}) collective-permute-start(bf16[256,768]{1,0:T(8,128)(2,1)S(1)} %add_convert_fusion.2), channel_id=1, source_target_pairs={{0,2},{1,3},{2,0},{3,1},{4,6},{5,7},{6,4},{7,5},{8,10},{9,11},{10,... | collective-permute-start | bytes 1179656 | tf_op jit(solution)/shard_map/ppermute | solution.py:565
  320.5 21.1 %collective-permute-start.33 = (bf16[7,48,768]{2,1,0:T(8,128)(2,1)S(1)}, bf16[7,48,768]{2,1,0:T(8,128)(2,1)S(1)}, u32[]{:S(2)}, u32[]{:S(2)}) collective-permute-start(bf16[7,48,768]{2,1,0:T(8,128)(2,1)S(1)} %constant_dynamic-slice_fusion.1), channel_id=1, source_target_pairs={{0,8},{4,12},{8,0},{12,4},{16,24},{20,28},{24,16},{28,20},{1,9},{5... | collective-permute-start | bytes 1548296 | tf_op jit(solution)/shard_map/ppermute | solution.py:565
  341.8 12.5 %collective-permute-start.34 = (bf16[7,24,768]{2,1,0:T(8,128)(2,1)S(1)}, bf16[7,24,768]{2,1,0:T(8,128)(2,1)S(1)}, u32[]{:S(2)}, u32[]{:S(2)}) collective-permute-start(bf16[7,24,768]{2,1,0:T(8,128)(2,1)S(1)} %constant_dynamic-slice_fusion), channel_id=1, source_target_pairs={{0,16},{4,20},{8,24},{12,28},{16,0},{20,4},{24,8},{28,12},{1,17},{... | collective-permute-start | bytes 774152 | tf_op jit(solution)/shard_map/ppermute | solution.py:565
  358.9 18.2 %collective-permute-start.7 = (bf16[256,768]{1,0:T(8,128)(2,1)S(1)}, bf16[256,768]{1,0:T(8,128)(2,1)S(1)}, u32[]{:S(2)}, u32[]{:S(2)}) collective-permute-start(bf16[256,768]{1,0:T(8,128)(2,1)S(1)} %copy-done.1), channel_id=1, source_target_pairs={{0,2},{1,3},{2,0},{3,1},{4,6},{5,7},{6,4},{7,5},{8,10},{9,11},{10,... | collective-permute-start | bytes 1179656 | tf_op jit(solution)/shard_map/ppermute | solution.py:565
  369.2 23.6 %collective-permute-start.6 = (bf16[256,768]{1,0:T(8,128)(2,1)S(1)}, bf16[256,768]{1,0:T(8,128)(2,1)S(1)}, u32[]{:S(2)}, u32[]{:S(2)}) collective-permute-start(bf16[256,768]{1,0:T(8,128)(2,1)S(1)} %copy-done.1), channel_id=1, source_target_pairs={{0,1},{1,0},{2,3},{3,2},{4,5},{5,4},{6,7},{7,6},{8,9},{9,8},{10,11... | collective-permute-start | bytes 1179656 | tf_op jit(solution)/shard_map/ppermute | solution.py:565
  377.0 15.7 %collective-permute-start.8 = (bf16[256,768]{1,0:T(8,128)(2,1)S(1)}, bf16[256,768]{1,0:T(8,128)(2,1)}, u32[]{:S(2)}, u32[]{:S(2)}) collective-permute-start(bf16[256,768]{1,0:T(8,128)(2,1)S(1)} %collective-permute-done.7.refs_2_), channel_id=1, source_target_pairs={{0,1},{1,0},{2,3},{3,2},{4,5},{5,4},{6,7},{7,6},{8,9},{9,8},{10,11... | collective-permute-start | bytes 1179656 | tf_op jit(solution)/shard_map/ppermute | solution.py:565
  377.2 18.9 %collective-permute-start.39 = (bf16[4,48,768]{2,1,0:T(8,128)(2,1)S(1)}, bf16[4,48,768]{2,1,0:T(8,128)(2,1)S(1)}, u32[]{:S(2)}, u32[]{:S(2)}) collective-permute-start(bf16[4,48,768]{2,1,0:T(8,128)(2,1)S(1)} %pad_maximum_fusion.3), channel_id=1, source_target_pairs={{0,8},{4,12},{8,0},{12,4},{16,24},{20,28},{24,16},{28,20},{1,9},{5... | collective-permute-start | bytes 884744 | tf_op jit(solution)/shard_map/ppermute | solution.py:565
  390.7 18.3 %collective-permute-start.24 = (bf16[256,768]{1,0:T(8,128)(2,1)S(1)}, bf16[256,768]{1,0:T(8,128)(2,1)S(1)}, u32[]{:S(2)}, u32[]{:S(2)}) collective-permute-start(bf16[256,768]{1,0:T(8,128)(2,1)S(1)} %copy-done.2), channel_id=1, source_target_pairs={{0,1},{1,0},{2,3},{3,2},{4,5},{5,4},{6,7},{7,6},{8,9},{9,8},{10,11... | collective-permute-start | bytes 1179656 | tf_op jit(solution)/shard_map/ppermute | solution.py:565
  396.3 23.0 %collective-permute-start.40 = (bf16[4,96,768]{2,1,0:T(8,128)(2,1)S(1)}, bf16[4,96,768]{2,1,0:T(8,128)(2,1)S(1)}, u32[]{:S(2)}, u32[]{:S(2)}) collective-permute-start(bf16[4,96,768]{2,1,0:T(8,128)(2,1)S(1)} %pad_maximum_fusion.1), channel_id=1, source_target_pairs={{0,4},{4,0},{8,12},{12,8},{16,20},{20,16},{24,28},{28,24},{1,5},{5... | collective-permute-start | bytes 1769480 | tf_op jit(solution)/shard_map/ppermute | solution.py:565
  (55 other events, 766.1 us)
Sparse Core Ops, SparseCore 0:
  9.6 53.9 all-gather.2
  79.0 32.7 reduce-scatter.3
  134.6 31.2 reduce-scatter.5
  193.5 78.1 reduce-scatter.7
  307.1 73.3 all-gather.4

commit v2 on v0

--- a/solution.py
+++ b/solution.py
@@ -98,7 +98,7 @@
     base = piece * rows_total
     features = w.shape[1]
     blocks = rows_total // BLK
-    gain_row = gain[...].astype(F32)
+    gain_row = gain[...].astype(F32).reshape(1, -1)
     lanes = lax.broadcasted_iota(jnp.int32, (BLK, features), 1)
     for block in range(blocks):
         rows = pl.ds(block * BLK, BLK)
@@ -166,9 +166,8 @@
 def attn_bwd_kernel(piece, pieces, heads, head_size, shares, idx, *refs):
     held = piece + 1
     last = held == pieces
-    go_parts, refs = refs[:shares], refs[shares:]
-    qh, ot, lse = refs[:3]
-    refs = refs[3:]
+    go, qh, ot, lse = refs[:4]
+    refs = refs[4:]
     ks, refs = refs[:held], refs[held:]
     vs, refs = refs[:held], refs[held:]
     bias, far, seg = refs[:3]
@@ -193,14 +192,11 @@
         gv, refs = refs[:held], refs[held:]
         gq_t, acc = refs[:2]
         refs = refs[2:]
-    go, kt, d_row, near_sum, far_sum = refs
+    kt, d_row, near_sum, far_sum = refs
     rows_total, features = ks[0].shape
     blocks = rows_total // BLK
     share = rows_total // shares
     me = idx[0]
-    for step in range(shares):
-        start = pl.multiple_of((me ^ step) * share, share)
-        go[pl.ds(start, share), :] = go_parts[step][...]
     for index in range(held):
         for block in range(blocks):
             cols = pl.ds(block * BLK, BLK)
@@ -325,13 +321,12 @@
 def moe_fwd_kernel(piece, pieces, shares, experts, idx, *refs):
     att, refs = refs[:shares], refs[shares:]
     if piece == 0:
-        wo_own, wo_swapped, refs = refs[0], refs[1], refs[2:]
-        wo_fetched, refs = refs[: shares - 1], refs[shares - 1 :]
+        wo_fetched, wo_swapped, refs = refs[0], refs[1], refs[2:]
     else:
         wo, refs = refs[0], refs[1:]
     tok, gain, router, routes, cot, w_in, w_down = refs[:7]
     refs = refs[7:]
-    parts, refs = refs[:shares], refs[shares:]
+    parts, refs = refs[0], refs[1:]
     if piece == 0:
         wo, refs = refs[0], refs[1:]
     normed, own, gates, ggate, act, slope, acc = refs
@@ -343,16 +338,15 @@
 
     @pl.when(expert == 0)
     def _():
-        gain_row = gain[...].astype(F32)
+        gain_row = gain[...].astype(F32).reshape(1, -1)
         router_wide = padded_rows(router[...].astype(F32), LANES).astype(BF16)
         if piece == 0:
-            half = wo_own.shape[0] // 2
+            half = wo_fetched.shape[1]
             mine = pl.ds(pl.multiple_of(idx[1] * half, half), half)
             other = pl.ds(pl.multiple_of((1 - idx[1]) * half, half), half)
-            wo[0] = wo_own[...]
-            for step in range(1, shares):
-                wo[step, mine, :] = wo_fetched[step - 1][...]
-                wo[step, other, :] = wo_swapped[step - 1]
+            for step in range(shares):
+                wo[step, mine, :] = wo_fetched[me ^ step]
+                wo[step, other, :] = wo_swapped[me ^ step]
         for block in range(rows_total // BLK):
             rows = pl.ds(block * BLK, BLK)
             outer = pl.ds(base + block * BLK, BLK)
@@ -395,9 +389,7 @@
 
     @pl.when(expert == experts - 1)
     def _():
-        for step in range(shares):
-            start = pl.multiple_of((me ^ step) * share, share)
-            parts[step][...] = acc[pl.ds(start, share), :].astype(BF16)
+        parts[...] = acc[...].astype(BF16)
 
 
 def moe_bwd_kernel(piece, shares, experts, idx, *refs):
@@ -474,8 +466,7 @@
     gx, refs = refs[:got], refs[got:]
     wo, own, cot, gain = refs[:4]
     refs = refs[4:]
-    ga, refs = refs[:shares], refs[shares:]
-    gh, gh_low, ggain = refs
+    ga, gh, gh_low, ggain = refs
     share = own.shape[0]
     grad = gx[0][...].astype(F32)
     for step in range(1, got):
@@ -484,7 +475,7 @@
     scale = row_scale(hidden)
     unit = hidden * scale
     ggain[...] = jnp.sum(grad * unit, axis=0, keepdims=True)
-    gained = grad * gain[...].astype(F32)
+    gained = grad * gain[...].astype(F32).reshape(1, -1)
     start = piece * (cot.shape[0] // pieces) + idx[0] * share
     mine = cot[pl.ds(pl.multiple_of(start, share), share), :].astype(F32)
     back = mine + scale * (gained - unit * jnp.mean(gained * unit, axis=-1, keepdims=True))
@@ -492,7 +483,7 @@
     low = back.astype(BF16)
     gh_low[...] = low
     for step in range(shares):
-        ga[step][...] = dot(low, wo[step], NT).astype(BF16)
+        ga[idx[0] ^ step] = dot(low, wo[step], NT).astype(BF16)
 
 
 def w_out_back_kernel(pieces, shares, idx, *refs):
@@ -523,7 +514,7 @@
     ghs, refs = refs[:pieces], refs[pieces:]
     tok, gain, gt, ggain = refs
     share = ghs[0].shape[0]
-    gain_row = gain[...].astype(F32)
+    gain_row = gain[...].astype(F32).reshape(1, -1)
     total = jnp.zeros_like(ggain)
     for index in range(pieces):
         rows = pl.ds(index * share, share)
@@ -554,7 +545,7 @@
 
 
 ROWS = 512
-PIECES = 2
+PIECES = 1
 
 SMEM = pl.BlockSpec(memory_space=pltpu.SMEM)
 VMEM = pl.BlockSpec(memory_space=pltpu.VMEM)
@@ -599,13 +590,17 @@
     return [value, one, two, swap(two, axis, 1)]
 
 
-def reduce_parts(parts, axis):
-    count = lax.axis_size(axis)
-    if count != 4:
-        return [parts[0]] + [swap(parts[bit], axis, bit) for bit in range(1, count)]
-    near = swap(parts[3], axis, 1)
-    pair = (parts[2].astype(F32) + near.astype(F32)).astype(parts[2].dtype)
-    return [parts[0], swap(parts[1], axis, 1), swap(pair, axis, 2)]
+def reduce_near(parts, axis):
+    return swap(parts[3], axis, 1), swap(parts[1], axis, 1)
+
+
+def reduce_far(parts, near, axis):
+    pair = (parts[2].astype(F32) + near[0].astype(F32)).astype(parts[2].dtype)
+    return [parts[0], near[1], swap(pair, axis, 2)], pair
+
+
+def exchange(parts, axis):
+    return [parts[0]] + [swap(parts[bit], axis, bit) for bit in range(1, len(parts))]
 
 
 def halves_of(value, axis, chosen):
@@ -620,12 +615,14 @@
     return [1 << level for level in range(count.bit_length() - 1)]
 
 
-def scatter_sum(value, mesh_axis, axis):
+def gather_back(value, mesh_axis, axis):
     me = lax.axis_index(mesh_axis)
-    for bit in bits_of(mesh_axis):
-        keep, send = halves_of(value, axis, (me // bit) % 2)
-        got = swap(send, mesh_axis, bit)
-        value = (keep.astype(F32) + got.astype(F32)).astype(value.dtype)
+    for bit in reversed(bits_of(mesh_axis)):
+        got = swap(value, mesh_axis, bit)
+        low = (me // bit) % 2 == 0
+        value = jnp.concatenate(
+            [jnp.where(low, value, got), jnp.where(low, got, value)], axis=axis
+        )
     return value
 
 
@@ -650,17 +647,21 @@
     idx = jnp.stack([me, side])
     mib = 1 << 20
     others = range(1, shares)
+    four = shares == 4
+
+    half_rows = features // 2
+    my_half = lax.dynamic_slice_in_dim(w_out, side * half_rows, half_rows, 0)
+    halves = lax.all_gather(my_half, "tensor", axis=0)
 
     build_hot, gather_hot = near_tables()
     build_hot = jnp.asarray(np.swapaxes(build_hot, 1, 2), BF16)
     gather_hot = jnp.asarray(gather_hot, F32)
     w_qkv_t = jnp.swapaxes(w_qkv, 1, 2)
     router_t = w_router.T
-    gain_one = gain_attn.reshape(1, width)
-    gain_two = gain_moe.reshape(1, width)
-
-    def attend(piece, bias_args, old_k, old_vt):
-        outs = [
+
+    normed_one, qh, k, v, _, att, ot, lse, bias, far = whole_call(
+        functools.partial(attn_fwd_kernel, 0, PIECES, heads, head_size),
+        [
             shaped((rows, width), BF16),
             shaped((heads, rows, features), BF16),
             shaped((rows, features), BF16),
@@ -669,36 +670,14 @@
             shaped((rows, features), BF16),
             shaped((features, rows), F32),
             shaped((8, rows), F32),
-        ]
-        if piece == 0:
-            outs += [shaped((2 * heads, BLK, BLK), F32), shaped((8, LANES), F32)]
-        return whole_call(
-            functools.partial(attn_fwd_kernel, piece, PIECES, heads, head_size),
-            outs,
-            [tokens, gain_one, w_qkv_t, segments, *bias_args, *old_k, *old_vt],
-            flops=3 * 10**9, moved=8 * mib, with_index=False,
-        )
-
-    stages = []
-    bias_args = [rel_bias.T, build_hot]
-    for piece in range(PIECES):
-        got = attend(piece, bias_args, [s[2] for s in stages], [s[4] for s in stages])
-        if piece == 0:
-            bias_args = got[8:]
-        stages.append(got[:8])
-    bias, far = bias_args
-    normed_one = [s[0] for s in stages]
-
-    half_rows = features // 2
-    my_half = lax.dynamic_slice_in_dim(w_out, side * half_rows, half_rows, 0)
-    my_half = after(my_half, stages[0][5])
-    halves = [swap(my_half, "tensor", by) for by in others]
-    swapped = swap(after(jnp.stack(halves), stages[-1][5]), "dp", 1)
-
-    atts = []
-    for stage in stages:
-        mine = after(stage[5], *atts[-1][1:]) if atts else stage[5]
-        atts.append(gather_parts(mine, "tensor"))
+            shaped((2 * heads, BLK, BLK), F32),
+            shaped((8, LANES), F32),
+        ],
+        [tokens, gain_attn, w_qkv_t, segments, rel_bias.T, build_hot],
+        flops=6 * 10**9, moved=8 * mib, with_index=False,
+    )
+    atts = gather_parts(att, "tensor")
+    swapped = swap(after(halves, att), "dp", 1)
 
     full = lambda shape: pl.BlockSpec(shape, lambda e: (0,) * len(shape))
     per_expert = lambda shape: pl.BlockSpec((1,) + shape, lambda e: (e, 0, 0))
@@ -707,224 +686,194 @@
     )
     moe_flops = 4 * experts * rows * width * hidden_units
 
-    def moe_forward(piece, wo_args):
-        wo_specs = [full(one.shape) for one in wo_args]
-        wo_shape = (shares, features, width)
-        return pl.pallas_call(
-            functools.partial(moe_fwd_kernel, piece, PIECES, shares, experts),
-            grid=(experts,),
-            in_specs=[SMEM]
-            + [full((rows, features))] * shares
-            + wo_specs
-            + [
-                full((tok_rows, width)), full((1, width)), full((experts, width)),
-                full((tok_rows, 2)), full((tok_rows, width)),
-                per_expert((width, hidden_units)), per_expert((hidden_units, width)),
-            ],
-            out_specs=[full((share, width))] * shares
-            + [full(wo_shape)] * (piece == 0)
-            + [
-                full((rows, width)), full((share, width)), full((rows, LANES)),
-                full((rows, LANES)), per_expert((rows, hidden_units)),
-                per_expert((rows, hidden_units)),
-            ],
-            out_shape=[shaped((share, width), BF16)] * shares
-            + [shaped(wo_shape, BF16)] * (piece == 0)
-            + [
-                shaped((rows, width), BF16),
-                shaped((share, width), F32),
-                shaped((rows, LANES), F32),
-                shaped((rows, LANES), F32),
-                shaped((experts, rows, hidden_units), BF16),
-                shaped((experts, rows, hidden_units), BF16),
-            ],
-            scratch_shapes=[pltpu.VMEM((rows, width), F32)],
-            compiler_params=params,
-            cost_estimate=pl.CostEstimate(
-                flops=moe_flops, bytes_accessed=20 * mib, transcendentals=0
-            ),
-        )(
-            idx, *atts[piece], *wo_args, tokens, gain_two, router_t, routes, grad_out,
-            w_in, w_down,
-        )
-
-    def moe_backward(piece, gates, ggate, slope):
-        return pl.pallas_call(
-            functools.partial(moe_bwd_kernel, piece, shares, experts),
-            grid=(experts,),
-            in_specs=[
-                SMEM, full((rows, LANES)), full((rows, LANES)), full((tok_rows, width)),
-                per_expert((rows, hidden_units)), full((experts, width)),
-                per_expert((width, hidden_units)), per_expert((hidden_units, width)),
-            ],
-            out_specs=[full((share, width))] * shares
-            + [full((rows, LANES)), per_expert((rows, hidden_units))],
-            out_shape=[shaped((share, width), BF16)] * shares
-            + [
-                shaped((rows, LANES), F32),
-                shaped((experts, rows, hidden_units), BF16),
-            ],
-            scratch_shapes=[pltpu.VMEM((rows, width), F32)],
-            compiler_params=params,
-            cost_estimate=pl.CostEstimate(
-                flops=moe_flops, bytes_accessed=16 * mib, transcendentals=0
-            ),
-        )(idx, gates, ggate, grad_out, slope, router_t, w_in, w_down)
-
-    moe_got, gx_got, forwards, backwards = [], [], [], []
-    wo_args = [w_out, swapped, *halves]
-    for piece in range(PIECES):
-        fwd = moe_forward(piece, wo_args)
-        parts, kept = fwd[:shares], fwd[shares:]
-        if piece == 0:
-            wo, kept = kept[0], kept[1:]
-            wo_args = [wo]
-        moe_got.append(reduce_parts(parts, "tensor"))
-        gates, ggate, slope = kept[2], kept[3], kept[5]
-        bwd = moe_backward(piece, gates, ggate, slope)
-        parts = bwd[:shares]
-        gx_got.append(reduce_parts(parts, "tensor"))
-        forwards.append(kept)
-        backwards.append(bwd[shares:])
-    normed_two = [f[0] for f in forwards]
-    own_hidden = [f[1] for f in forwards]
-    all_gates = [f[2] for f in forwards]
-    acts = [f[4] for f in forwards]
-    glogs = [b[0] for b in backwards]
-    gpres = [b[1] for b in backwards]
-
-    def hidden_back(piece, own):
-        got = whole_call(
-            functools.partial(hidden_back_kernel, piece, PIECES, shares, len(gx_got[piece])),
-            [shaped((share, features), BF16)] * shares
-            + [
-                shaped((share, width), F32), shaped((share, width), BF16),
-                shaped((1, width), F32),
-            ],
-            [idx, *gx_got[piece], wo, own, grad_out, gain_two],
-            flops=2 * 10**8, moved=5 * mib,
-        )
-        parts = got[:shares]
-        go = [parts[0]] + [swap(parts[by], "tensor", by) for by in others]
-        return go, got[shares:]
-
-    def attend_back(piece, go, carried):
-        held = piece + 1
-        last = held == PIECES
-        outs, scratch = [], []
-        if last:
-            outs += [shaped((PIECES * share, width), BF16)] * shares
-            outs += [shaped((3, tok_rows, features), BF16), shaped((8, NB), F32)]
-        sums = [((rows, features), F32)] * (2 * held)
-        sums += [((features, rows), F32), ((2 * heads, BLK, BLK), F32)]
-        if last:
-            scratch += [pltpu.VMEM(*one) for one in sums]
-        else:
-            outs += [shaped(*one) for one in sums]
-        scratch += [
-            pltpu.VMEM((rows, features), BF16),
-            pltpu.VMEM((features, tok_rows), BF16),
+    fwd = pl.pallas_call(
+        functools.partial(moe_fwd_kernel, 0, PIECES, shares, experts),
+        grid=(experts,),
+        in_specs=[SMEM]
+        + [full((rows, features))] * shares
+        + [full((shares, half_rows, width))] * 2
+        + [
+            full((rows, width)), full((width,)), full((experts, width)),
+            full((rows, 2)), full((rows, width)),
+            per_expert((width, hidden_units)), per_expert((hidden_units, width)),
+        ],
+        out_specs=[
+            full((rows, width)), full((shares, features, width)), full((rows, width)),
+            full((share, width)), full((rows, LANES)), full((rows, LANES)),
+            per_expert((rows, hidden_units)), per_expert((rows, hidden_units)),
+        ],
+        out_shape=[
+            shaped((rows, width), BF16),
+            shaped((shares, features, width), BF16),
+            shaped((rows, width), BF16),
+            shaped((share, width), F32),
+            shaped((rows, LANES), F32),
+            shaped((rows, LANES), F32),
+            shaped((experts, rows, hidden_units), BF16),
+            shaped((experts, rows, hidden_units), BF16),
+        ],
+        scratch_shapes=[pltpu.VMEM((rows, width), F32)],
+        compiler_params=params,
+        cost_estimate=pl.CostEstimate(
+            flops=moe_flops, bytes_accessed=32 * mib, transcendentals=0
+        ),
+    )(
+        idx, *atts, halves, swapped, tokens, gain_moe, router_t, routes, grad_out,
+        w_in, w_down,
+    )
+    moe_sum, wo, normed_two, own_hidden, gates, ggate, act, slope = fwd
+    moe_rows = lax.psum_scatter(moe_sum, "tensor", scatter_dimension=0, tiled=True)
+
+    bwd = pl.pallas_call(
+        functools.partial(moe_bwd_kernel, 0, shares, experts),
+        grid=(experts,),
+        in_specs=[
+            SMEM, full((rows, LANES)), full((rows, LANES)), full((rows, width)),
+            per_expert((rows, hidden_units)), full((experts, width)),
+            per_expert((width, hidden_units)), per_expert((hidden_units, width)),
+        ],
+        out_specs=[full((share, width))] * shares
+        + [full((rows, LANES)), per_expert((rows, hidden_units))],
+        out_shape=[shaped((share, width), BF16)] * shares
+        + [
+            shaped((rows, LANES), F32),
+            shaped((experts, rows, hidden_units), BF16),
+        ],
+        scratch_shapes=[pltpu.VMEM((rows, width), F32)],
+        compiler_params=params,
+        cost_estimate=pl.CostEstimate(
+            flops=moe_flops, bytes_accessed=26 * mib, transcendentals=0
+        ),
+    )(idx, gates, ggate, grad_out, slope, router_t, w_in, w_down)
+    gx_parts = bwd[:shares]
+    glog, gpre = bwd[shares:]
+    gx_near = reduce_near(gx_parts, "tensor") if four else exchange(gx_parts, "tensor")[1:]
+
+    expert_grads, router_rows = pl.pallas_call(
+        functools.partial(moe_weights_kernel, PIECES),
+        grid=(experts,),
+        in_specs=[
+            full((rows, width)), full((rows, LANES)), full((rows, LANES)), full((rows, width)),
+            per_expert((rows, hidden_units)), per_expert((rows, hidden_units)),
+        ],
+        out_specs=[
+            pl.BlockSpec((1, 2, width, width), lambda e: (e, 0, 0, 0)), full((8, width))
+        ],
+        out_shape=[shaped((experts, 2, width, width), BF16), shaped((8, width), F32)],
+        compiler_params=params,
+        cost_estimate=pl.CostEstimate(
+            flops=moe_flops, bytes_accessed=26 * mib, transcendentals=0
+        ),
+    )(grad_out, gates, glog, normed_two, act, gpre)
+    expert_rows = after(expert_grads.reshape(experts * 2 * width, width), *gx_near)
+    expert_rows = lax.psum_scatter(expert_rows, "dp", scatter_dimension=0, tiled=True)
+
+    if four:
+        gx_near = after(gx_near[0], router_rows), gx_near[1]
+        gx_got, _ = reduce_far(gx_parts, gx_near, "tensor")
+    else:
+        gx_got = [gx_parts[0], *gx_near]
+    ga, grad_hidden, gh_low, ggain_two = whole_call(
+        functools.partial(hidden_back_kernel, 0, PIECES, shares, len(gx_got)),
+        [
+            shaped((shares, share, features), BF16), shaped((share, width), F32),
+            shaped((share, width), BF16), shaped((1, width), F32),
+        ],
+        [idx, *gx_got, wo, own_hidden, grad_out, gain_moe],
+        flops=3 * 10**8, moved=5 * mib,
+    )
+    go = lax.all_to_all(ga, "tensor", split_axis=0, concat_axis=0, tiled=True)
+    go = go.reshape(rows, features)
+
+    result_share = whole_call(
+        functools.partial(join_kernel, PIECES, 1),
+        [shaped((share, width), BF16)],
+        [own_hidden, moe_rows],
+        moved=2 * mib, with_index=False,
+    )[0]
+    result_got = gather_parts(result_share, "tensor")
+    result = whole_call(
+        functools.partial(place_kernel, PIECES, shares),
+        [shaped((rows, width), BF16)], [idx, *result_got], moved=3 * mib,
+    )[0]
+
+    attn_back = whole_call(
+        functools.partial(attn_bwd_kernel, 0, PIECES, heads, head_size, shares),
+        [shaped((share, width), BF16)] * shares
+        + [shaped((3, rows, features), BF16), shaped((8, NB), F32)],
+        [
+            idx, after(go, result_share), qh, ot, lse, k, v, bias, far, segments,
+            w_qkv_t, gather_hot,
+        ],
+        [pltpu.VMEM((rows, features), F32)] * 2
+        + [
+            pltpu.VMEM((features, rows), F32),
+            pltpu.VMEM((2 * heads, BLK, BLK), F32),
+            pltpu.VMEM((features, rows), BF16),
             pltpu.VMEM((8, rows), F32),
             pltpu.VMEM((2, 8, 2 * BLK), F32),
             pltpu.VMEM((8, BLK), F32),
-        ]
-        return whole_call(
-            functools.partial(attn_bwd_kernel, piece, PIECES, heads, head_size, shares),
-            outs,
-            [
-                idx, *go, stages[piece][1], stages[piece][6], stages[piece][7],
-                *[s[2] for s in stages[:held]], *[s[3] for s in stages[:held]],
-                bias, far, segments, *carried, *([w_qkv_t, gather_hot] if last else []),
-            ],
-            scratch,
-            flops=7 * 10**9, moved=8 * mib,
-        )
-
-    go, back_first = hidden_back(0, own_hidden[0])
-    expert_grads, router_rows = pl.pallas_call(
-        functools.partial(moe_weights_kernel, PIECES),
-        grid=(experts,),
-        in_specs=[full((tok_rows, width))]
-        + [full((rows, LANES))] * (2 * PIECES)
-        + [full((rows, width))] * PIECES
-        + [per_expert((rows, hidden_units))] * (2 * PIECES),
-        out_specs=[
-            pl.BlockSpec((1, 2, width, width), lambda e: (e, 0, 0, 0)), full((8, width))
-        ],
-        out_shape=[shaped((experts, 2, width, width), BF16), shaped((8, width), F32)],
-        compiler_params=params,
-        cost_estimate=pl.CostEstimate(
-            flops=2 * moe_flops, bytes_accessed=26 * mib, transcendentals=0
-        ),
-    )(after(grad_out, back_first[1]), *all_gates, *glogs, *normed_two, *acts, *gpres)
-    expert_rows = lax.psum_scatter(
-        expert_grads.reshape(experts * 2 * width, width), "dp", scatter_dimension=0, tiled=True
+        ],
+        flops=14 * 10**9, moved=8 * mib,
     )
-
-    go_second, back_second = hidden_back(1, after(own_hidden[1], router_rows))
-    result_share = whole_call(
-        functools.partial(join_kernel, PIECES, len(moe_got[0])),
-        [shaped((PIECES * share, width), BF16)],
-        [*own_hidden, *moe_got[0], *moe_got[1]],
-        moved=4 * mib, with_index=False,
-    )[0]
-    go = [after(go[0], back_second[1]), *go[1:]]
-    first = attend_back(0, go, [])
-    go_second = [after(go_second[0], first[0], result_share), *go_second[1:]]
-    second = attend_back(1, go_second, first)
-    grad_hidden = [back_first[0], back_second[0]]
-    ggain_two = back_first[2] + back_second[2]
-    gn_parts = second[:shares]
-    gproj, grad_rel = second[shares:]
-    gn_got = reduce_parts(gn_parts, "tensor")
-
-    result_got = gather_parts(result_share, "tensor")
-    result = whole_call(
-        functools.partial(place_kernel, PIECES, shares),
-        [shaped((tok_rows, width), BF16)], [idx, *result_got], moved=3 * mib,
+    gn_parts = attn_back[:shares]
+    gproj, grad_rel = attn_back[shares:]
+
+    qkv_rows = whole_call(
+        functools.partial(qkv_weights_kernel, PIECES),
+        [shaped((3, features, width), BF16)],
+        [normed_one, gproj],
+        flops=10**9, moved=4 * mib, with_index=False,
     )[0]
     w_out_rows = whole_call(
         functools.partial(w_out_back_kernel, PIECES, shares),
         [shaped((shares, features, width), BF16)],
-        [idx, *atts[0], *atts[1], back_first[1], after(back_second[1], gproj)],
+        [idx, *atts, after(gh_low, gproj)],
         flops=3 * 10**8, moved=4 * mib,
     )[0]
-    qkv_rows = whole_call(
-        functools.partial(qkv_weights_kernel, PIECES),
-        [shaped((3, features, width), BF16)],
-        [*normed_one, gproj],
-        flops=10**9, moved=4 * mib, with_index=False,
-    )[0]
+    late = jnp.concatenate([qkv_rows, w_out_rows], axis=0)
+    if four:
+        near = reduce_near(gn_parts, "tensor")
+        gn_got, mark = reduce_far(gn_parts, (after(near[0], late), near[1]), "tensor")
+    else:
+        gn_got = exchange(gn_parts, "tensor")
+        mark = gn_got[-1]
+
+    place = lax.axis_index("dp")
+
+    def halve(value, bit, *ready):
+        keep, send = halves_of(value, 1, (place // bit) % 2)
+        got = swap(after(send, *ready), "dp", bit)
+        return (keep.astype(F32) + got.astype(F32)).astype(BF16)
+
+    late = after(late, mark)
+    for bit in bits_of("dp")[:2]:
+        late = halve(late, bit)
+    grad_hidden = after(grad_hidden, late)
 
     gt_share, ggain_one = whole_call(
         functools.partial(input_back_kernel, PIECES, len(gn_got)),
-        [shaped((PIECES * share, width), BF16), shaped((1, width), F32)],
-        [idx, *gn_got, *grad_hidden, tokens, gain_one],
+        [shaped((share, width), BF16), shaped((1, width), F32)],
+        [idx, *gn_got, grad_hidden, tokens, gain_attn],
         moved=5 * mib,
     )
     gt_got = gather_parts(gt_share, "tensor")
     grad_tokens = whole_call(
         functools.partial(place_kernel, PIECES, shares),
-        [shaped((tok_rows, width), F32)], [idx, *gt_got], moved=5 * mib,
+        [shaped((rows, width), F32)], [idx, *gt_got], moved=5 * mib,
     )[0]
 
-    late = after(jnp.concatenate([qkv_rows, w_out_rows], axis=0), gt_share)
-    late = scatter_sum(late, "dp", 1)
+    for bit in bits_of("dp")[2:]:
+        late = halve(late, bit, gt_got[2])
     out_sum = late[3].astype(F32)
     for by in others:
         out_sum = out_sum + swap(late[3 + by], "tensor", by).astype(F32)
-    late_rows = late.shape[1]
     late = jnp.concatenate([late[:3], out_sum.astype(BF16)[None]], axis=0)
-    shard = expert_rows.shape[0]
-    both = jnp.concatenate([after(expert_rows, late), late.reshape(4 * late_rows, width)], axis=0)
-    both = lax.all_gather(both, "dp", axis=0)
-    expert_rows = both[:, :shard].reshape(experts, 2, width, width)
+    late = gather_back(late, "dp", 1)
+    expert_rows = lax.all_gather(after(expert_rows, gt_share), "dp", axis=0, tiled=True)
+    expert_rows = expert_rows.reshape(experts, 2, width, width)
     grad_w_in = expert_rows[:, 0].astype(F32)
     grad_w_down = expert_rows[:, 1].astype(F32)
-    levels = len(bits_of("dp"))
-    late = both[:, shard:].reshape([2] * levels + [4, late_rows, width])
-    late = jnp.transpose(late, [levels, *reversed(range(levels)), levels + 1, levels + 2])
-    late = late.reshape(4, features, width)
     grad_w_qkv = jnp.swapaxes(late[:3], 1, 2).astype(F32)
     grad_w_out = late[3].astype(F32)
 

time: 413 us -> 389 us (0.942); the launches traced: 407 us -> 388 us
  blocking collectives: 0 us -> 51.6 us
  Pallas kernels: 147 us -> 112 us
  local copies, waits for them, and re-layouts: 24.1 us -> 10.9 us
  waiting for transfers between devices: 148 us -> 137 us
  starting transfers between devices: 52.1 us -> 41.5 us
    all_gather x0 -> x1, blocking collectives: none -> 36.7 us  [body(): halves = lax.all_gather(my_half, 'tensor', axis=0)]
    pallas_call x12 -> x9, Pallas kernels: 73.1 us -> 51.3 us  [whole_call(): pl.pallas_call(kernel, out_shape=outs, in_specs=specs, out_specs=[VMEM] *...]
    all_to_all x0 -> x1, blocking collectives: none -> 14.9 us  [body(): go = lax.all_to_all(ga, 'tensor', split_axis=0, concat_axis=0, tiled=True)]
    pallas_call x4 -> x2, Pallas kernels: 57.9 us -> 45.1 us  [the longest x1 25.7 us: body(): pl.pallas_call(functools.partial(moe_fwd_kernel, 0, PIECES, shares, exper...]
    ppermute x48 -> x30, starting transfers between devices: 52.1 us -> 41.2 us  [swap(): return lax.ppermute(value, axis, [(i, i ^ bit) for i in range(count)])]
    ppermute x48 -> x30, waiting for transfers between devices: 148 us -> 137 us  [swap(): return lax.ppermute(value, axis, [(i, i ^ bit) for i in range(count)])]
    slice x2 -> x0, local copies, waits for them, and re-layouts: 9.2 us -> none  [the longest x1 7.85 us: body(): expert_rows = both[:, :shard].reshape(experts, 2, width, width)]
  transfers between devices with their start and end apart: 50 -> 33, of which waited for: 27 -> 19; matrix products, arithmetic and copies ran while one was open for 2% -> 4% of each run, Pallas kernels for 29% -> 19%
where the time goes in v2:
time: 389 us; the launch traced here: 388 us
  waiting for transfers between devices  137 us (35%)
  Pallas kernels  112 us (29%)
  blocking collectives  51.6 us (13%)
  starting transfers between devices  41.5 us (11%)
  other arithmetic  20.7 us (5%)
  between operations  14.2 us (4%)
  local copies, waits for them, and re-layouts  10.9 us (3%)
    ppermute x30, waiting for transfers between devices, swap(): return lax.ppermute(value, axis, [(i, i ^ bit) for i in range(count)])  137 us
    pallas_call x9, Pallas kernels, whole_call(): pl.pallas_call(kernel, out_shape=outs, in_specs=specs, out_specs=[VMEM] *...  51.3 us
    ppermute x30, starting transfers between devices, swap(): return lax.ppermute(value, axis, [(i, i ^ bit) for i in range(count)])  41.2 us
    all_gather x1, blocking collectives, body(): halves = lax.all_gather(my_half, 'tensor', axis=0)  36.7 us
    pallas_call x1, Pallas kernels, body(): pl.pallas_call(functools.partial(moe_fwd_kernel, 0, PIECES, shares, exper...  25.7 us
    pallas_call x1, Pallas kernels, body(): pl.pallas_call(functools.partial(moe_bwd_kernel, 0, shares, experts), gri...  19.4 us
    pallas_call x1, Pallas kernels, body(): pl.pallas_call(functools.partial(moe_weights_kernel, PIECES), grid=(exper...  15.9 us
    all_to_all x1, blocking collectives, body(): go = lax.all_to_all(ga, 'tensor', split_axis=0, concat_axis=0, tiled=True)  14.9 us
  transfers between devices with their start and end apart: 33, of which 19 were waited for; matrix products, arithmetic and copies ran while one was open for 4% of the time, Pallas kernels for 19%

profile of v2, /device:TPU:0, one launch (start us, length us, event | category | flops | bytes accessed | tf_op | source)
XLA Modules:
  0.0 388.3 jit_solution(2221046328947078504)
XLA Ops:
  7.2 12.3 %shard_map.213 = (bf16[1024,768]{1,0:T(8,128)(2,1)}, bf16[3,1024,192]{2,1,0:T(8,128)(2,1)}, bf16[1024,192]{1,0:T(8,128)(2,1)}, bf16[1024,192]{1,0:T(8,128)(2,1)}...) custom-call(bf16[1024,768]{1,0:T(8,128)(2,1)} %refs_4_.1, ...), custom_call_target="tpu_custom_call" | custom-call | flops 6000000000 | bytes 8388608 | tf_op jit(solution)/shard_map/pallas_call | solution.py:560
  19.5 4.0 %collective-permute-start.1 = (bf16[1024,192]{1,0:T(8,128)(2,1)}, bf16[1024,192]{1,0:T(8,128)(2,1)S(1)}, u32[]{:S(2)}, u32[]{:S(2)}) collective-permute-start(bf16[1024,192]{1,0:T(8,128)(2,1)} %get-tuple-element.57.refs_0_), channel_id=1, source_target_pairs={{0,2},{1,3},{2,0},{3,1},{4,6},{5,7},{6,4},{7,5},{8,10},{9,11},{10,... | collective-permute-start | bytes 1179656 | tf_op jit(solution)/shard_map/ppermute | solution.py:573
  23.6 36.7 %all-gather = bf16[384,768]{1,0:T(8,128)(2,1)S(1)} all-gather(bf16[96,768]{1,0:T(8,128)(2,1)S(1)} %constant_dynamic-slice_fusion.3), channel_id=2, replica_groups=mesh['dp'=8,'tensor'=4] {'tensor'}, dimensions={0}, use_global_device_ids=true | all-gather | bytes 737280 | tf_op jit(solution)/shard_map/all_gather | solution.py:654
  64.0 11.3 %collective-permute-done.refs_1_ = bf16[1024,192]{1,0:T(8,128)(2,1)S(1)} collective-permute-done((bf16[1024,192]{1,0:T(8,128)(2,1)}, bf16[1024,192]{1,0:T(8,128)(2,1)S(1)}, u32[]{:S(2)}, u32[]{:S(2)}) %collective-permute-start) | collective-permute-done | bytes 393248 | tf_op jit(solution)/shard_map/ppermute | solution.py:573
  75.2 10.9 %collective-permute-done.2.refs_3_ = bf16[1024,192]{1,0:T(8,128)(2,1)S(1)} collective-permute-done((bf16[1024,192]{1,0:T(8,128)(2,1)S(1)}, bf16[1024,192]{1,0:T(8,128)(2,1)S(1)}, u32[]{:S(2)}, u32[]{:S(2)}) %collective-permute-start.2) | collective-permute-done | bytes 393248 | tf_op jit(solution)/shard_map/ppermute | solution.py:573
  86.9 25.7 %shard_map.214 = (bf16[1024,768]{1,0:T(8,128)(2,1)}, bf16[4,192,768]{2,1,0:T(8,128)(2,1)}, bf16[1024,768]{1,0:T(8,128)(2,1)}, f32[256,768]{1,0:T(8,128)}, f32[10...) custom-call(s32[2]{0:T(128)} %pad_add_fusion.idx, ...), custom_call_target="tpu_custom_call" | custom-call | flops 9663676416 | bytes 33554432 | tf_op jit(solution)/shard_map/pallas_call | solution.py:689
  112.9 19.4 %shard_map.217 = (bf16[256,768]{1,0:T(8,128)(2,1)}, bf16[256,768]{1,0:T(8,128)(2,1)}, bf16[256,768]{1,0:T(8,128)(2,1)}, bf16[256,768]{1,0:T(8,128)(2,1)}, f32[10...) custom-call(s32[2]{0:T(128)} %pad_add_fusion.idx, f32[1024,128]{1,0:T(8,128)} %get-tuple-element.61.refs_0_, ...), custom_call_target="tpu_custom_call" | custom-call | flops 9663676416 | bytes 27262976 | tf_op jit(solution)/shard_map/pallas_call | solution.py:727
  134.3 15.9 %shard_map.218 = (bf16[4,2,768,768]{3,2,1,0:T(8,128)(2,1)}, f32[8,768]{1,0:T(8,128)}) custom-call(bf16[1024,768]{1,0:T(8,128)(2,1)} %refs_5_.5, f32[1024,128]{1,0:T(8,128)} %get-tuple-element.61.refs_0_, f32[1024,128]{1,0:T(8,128)} %get-tuple-element.68.refs_1_, bf16[1024,768]{1,0:T(8,128)(2,1)} %get-tuple-element.69.refs_2_, ...), custom_call_target="tpu_custom_call" | custom-call | flops 9663676416 | bytes 27262976 | tf_op jit(solution)/shard_map/pallas_call | solution.py:752
  152.1 9.2 %collective-permute-done.8 = bf16[256,768]{1,0:T(8,128)(2,1)S(1)} collective-permute-done((bf16[256,768]{1,0:T(8,128)(2,1)}, bf16[256,768]{1,0:T(8,128)(2,1)S(1)}, u32[]{:S(2)}, u32[]{:S(2)}) %collective-permute-start.8) | collective-permute-done | bytes 393248 | tf_op jit(solution)/shard_map/ppermute | solution.py:573
  164.9 17.7 %collective-permute-done.9.refs_2_ = bf16[256,768]{1,0:T(8,128)(2,1)S(1)} collective-permute-done((bf16[256,768]{1,0:T(8,128)(2,1)S(1)}, bf16[256,768]{1,0:T(8,128)(2,1)S(1)}, u32[]{:S(2)}, u32[]{:S(2)}) %collective-permute-start.9) | collective-permute-done | bytes 393248 | tf_op jit(solution)/shard_map/ppermute | solution.py:573
  183.4 4.1 %shard_map.219 = (bf16[4,256,192]{2,1,0:T(8,128)(2,1)}, f32[256,768]{1,0:T(8,128)}, bf16[256,768]{1,0:T(8,128)(2,1)}, f32[1,768]{1,0:T(1,128)}) custom-call(s32[2]{0:T(128)} %pad_add_fusion.idx, bf16[256,768]{1,0:T(8,128)(2,1)} %get-tuple-element.64.refs_0_, bf16[256,768]{1,0:T(8,128)(2,1)} %copy-done.11, bf16[256,768]{1,0:T(8,128)(2,1)} %copy-done.15, ...), custom_call_target="tpu_custom_call" | custom-call | flops 300000000 | bytes 5242880 | tf_op jit(solution)/shard_map/pallas_call | solution.py:560
  188.9 14.9 %all_to_all.5 = bf16[4,256,192]{1,2,0:T(8,128)(2,1)S(1)} all-to-all(bf16[4,256,192]{1,2,0:T(8,128)(2,1)S(1)} %copy.27), channel_id=1, replica_groups=mesh['dp'=8,'tensor'=4] {'tensor'}, dimensions={0} | all-to-all | bytes 786432 | tf_op jit(solution)/shard_map/all_to_all | solution.py:785
  206.8 16.5 %shard_map.220 = (bf16[256,768]{1,0:T(8,128)(2,1)}, bf16[256,768]{1,0:T(8,128)(2,1)}, bf16[256,768]{1,0:T(8,128)(2,1)}, bf16[256,768]{1,0:T(8,128)(2,1)}, bf16[3...) custom-call(s32[2]{0:T(128)} %pad_add_fusion.idx, bf16[1024,192]{1,0:T(8,128)(2,1)} %bitcast.47, ...), custom_call_target="tpu_custom_call" | custom-call | flops 14000000000 | bytes 8388608 | tf_op jit(solution)/shard_map/pallas_call | solution.py:560
  223.7 3.2 shard_map.222
  226.9 4.1 %shard_map.221 = bf16[3,192,768]{2,1,0:T(8,128)(2,1)} custom-call(bf16[1024,768]{1,0:T(8,128)(2,1)} %get-tuple-element.88.refs_0_, bf16[3,1024,192]{2,1,0:T(8,128)(2,1)} %get-tuple-element.89.refs_1_), custom_call_target="tpu_custom_call" | custom-call | flops 1000000000 | bytes 4194304 | tf_op jit(solution)/shard_map/pallas_call | solution.py:560
  234.1 2.7 collective-permute-done.13
  243.0 9.2 %collective-permute-done.14 = bf16[7,48,768]{2,1,0:T(8,128)(2,1)S(1)} collective-permute-done((bf16[7,48,768]{2,1,0:T(8,128)(2,1)S(1)}, bf16[7,48,768]{2,1,0:T(8,128)(2,1)S(1)}, u32[]{:S(2)}, u32[]{:S(2)}) %collective-permute-start.14) | collective-permute-done | bytes 516128 | tf_op jit(solution)/shard_map/ppermute | solution.py:573
  252.3 6.2 %collective-permute-done.10.refs_1_ = bf16[256,768]{1,0:T(8,128)(2,1)S(1)} collective-permute-done((bf16[256,768]{1,0:T(8,128)(2,1)}, bf16[256,768]{1,0:T(8,128)(2,1)S(1)}, u32[]{:S(2)}, u32[]{:S(2)}) %collective-permute-start.10) | collective-permute-done | bytes 393248 | tf_op jit(solution)/shard_map/ppermute | solution.py:573
  258.6 2.6 collective-permute-done.12.refs_2_
  261.9 3.3 shard_map.223
  265.7 16.9 %collective-permute-done.16.refs_2_ = bf16[256,768]{1,0:T(8,128)(2,1)S(1)} collective-permute-done((bf16[256,768]{1,0:T(8,128)(2,1)}, bf16[256,768]{1,0:T(8,128)(2,1)S(1)}, u32[]{:S(2)}, u32[]{:S(2)}) %collective-permute-start.16) | collective-permute-done | bytes 393248 | tf_op jit(solution)/shard_map/ppermute | solution.py:573
  283.9 9.3 %collective-permute-done.23 = bf16[7,24,768]{2,1,0:T(8,128)(2,1)S(1)} collective-permute-done((bf16[7,24,768]{2,1,0:T(8,128)(2,1)S(1)}, bf16[7,24,768]{2,1,0:T(8,128)(2,1)S(1)}, u32[]{:S(2)}, u32[]{:S(2)}) %collective-permute-start.23) | collective-permute-done | bytes 258080 | tf_op jit(solution)/shard_map/ppermute | solution.py:573
  300.4 3.1 collective-permute-done.26
  304.2 6.7 %collective-permute-start.4 = (bf16[256,768]{1,0:T(8,128)(2,1)S(1)}, bf16[256,768]{1,0:T(8,128)(2,1)S(1)}, u32[]{:S(2)}, u32[]{:S(2)}) collective-permute-start(bf16[256,768]{1,0:T(8,128)(2,1)S(1)} %copy-done.3), channel_id=1, source_target_pairs={{0,1},{1,0},{2,3},{3,2},{4,5},{5,4},{6,7},{7,6},{8,9},{9,8},{10,11... | collective-permute-start | bytes 1179656 | tf_op jit(solution)/shard_map/ppermute | solution.py:573
  310.9 7.4 %collective-permute-done.5.refs_2_ = bf16[256,768]{1,0:T(8,128)(2,1)S(1)} collective-permute-done((bf16[256,768]{1,0:T(8,128)(2,1)S(1)}, bf16[256,768]{1,0:T(8,128)(2,1)S(1)}, u32[]{:S(2)}, u32[]{:S(2)}) %collective-permute-start.5) | collective-permute-done | bytes 393248 | tf_op jit(solution)/shard_map/ppermute | solution.py:573
  321.2 12.0 %collective-permute-done.19 = f32[18,768]{1,0:T(8,128)S(1)} collective-permute-done((f32[18,768]{1,0:T(8,128)S(1)}, f32[18,768]{1,0:T(8,128)S(1)}, u32[]{:S(2)}, u32[]{:S(2)}) %collective-permute-start.19) | collective-permute-done | bytes 55328 | tf_op jit(solution)/shard_map/ppermute | solution.py:573
  336.2 2.6 shard_map.216
  342.1 8.4 %collective-permute-done.21 = f32[10,768]{1,0:T(8,128)S(1)} collective-permute-done((f32[10,768]{1,0:T(8,128)S(1)}, f32[10,768]{1,0:T(8,128)S(1)}, u32[]{:S(2)}, u32[]{:S(2)}) %collective-permute-start.21) | collective-permute-done | bytes 30752 | tf_op jit(solution)/shard_map/ppermute | solution.py:573
  350.5 2.5 collective-permute-start.22
  356.9 6.1 %collective-permute-done.17.refs_3_ = bf16[256,768]{1,0:T(8,128)(2,1)S(1)} collective-permute-done((bf16[256,768]{1,0:T(8,128)(2,1)S(1)}, bf16[256,768]{1,0:T(8,128)(2,1)S(1)}, u32[]{:S(2)}, u32[]{:S(2)}) %collective-permute-start.17) | collective-permute-done | bytes 393248 | tf_op jit(solution)/shard_map/ppermute | solution.py:573
  363.8 3.2 shard_map.224
  369.4 12.4 %fusion = (f32[4,768,768]{2,1,0:T(8,128)}, f32[4,768,768]{2,1,0:T(8,128)}) fusion(bf16[4,2,768,768]{3,2,1,0:T(8,128)(2,1)} %bitcast.43), kind=kLoop, calls=%fused_computation.1 | loop fusion | flops 4718592 | bytes 28311552 | tf_op jit(solution)/shard_map/convert_element_type | solution.py:876
  (141 shorter events, 53.9 us)
Async XLA Ops:
  7.2 197.6 %reduce-scatter.3.cloned.1.call-start = ((), (), s32[]{:S(2)}) async-start(), calls=%async_computation.3 | async-start | bytes 1966080 | tf_op jit(solution)/shard_map/reduce_scatter | solution.py:725
  19.5 40.8 %collective-permute-start.1 = (bf16[1024,192]{1,0:T(8,128)(2,1)}, bf16[1024,192]{1,0:T(8,128)(2,1)S(1)}, u32[]{:S(2)}, u32[]{:S(2)}) collective-permute-start(bf16[1024,192]{1,0:T(8,128)(2,1)} %get-tuple-element.57.refs_0_), channel_id=1, source_target_pairs={{0,2},{1,3},{2,0},{3,1},{4,6},{5,7},{6,4},{7,5},{8,10},{9,11},{10,... | collective-permute-start | bytes 1179656 | tf_op jit(solution)/shard_map/ppermute | solution.py:573
  60.3 14.9 %collective-permute-start.3 = (bf16[4,96,768]{2,1,0:T(8,128)(2,1)S(1)}, bf16[4,96,768]{2,1,0:T(8,128)(2,1)S(1)}, u32[]{:S(2)}, u32[]{:S(2)}) collective-permute-start(bf16[4,96,768]{2,1,0:T(8,128)(2,1)S(1)} %bitcast.45), channel_id=1, source_target_pairs={{0,4},{4,0},{8,12},{12,8},{16,20},{20,16},{24,28},{28,24},{1,5},{5... | collective-permute-start | bytes 1769480 | tf_op jit(solution)/shard_map/ppermute | solution.py:573
  60.3 14.9 %collective-permute-start = (bf16[1024,192]{1,0:T(8,128)(2,1)}, bf16[1024,192]{1,0:T(8,128)(2,1)S(1)}, u32[]{:S(2)}, u32[]{:S(2)}) collective-permute-start(bf16[1024,192]{1,0:T(8,128)(2,1)} %get-tuple-element.57.refs_0_), channel_id=1, source_target_pairs={{0,1},{1,0},{2,3},{3,2},{4,5},{5,4},{6,7},{7,6},{8,9},{9,8},{10,11... | collective-permute-start | bytes 1179656 | tf_op jit(solution)/shard_map/ppermute | solution.py:573
  60.3 25.8 %collective-permute-start.2 = (bf16[1024,192]{1,0:T(8,128)(2,1)S(1)}, bf16[1024,192]{1,0:T(8,128)(2,1)S(1)}, u32[]{:S(2)}, u32[]{:S(2)}) collective-permute-start(bf16[1024,192]{1,0:T(8,128)(2,1)S(1)} %collective-permute-done.1.refs_2_), channel_id=1, source_target_pairs={{0,1},{1,0},{2,3},{3,2},{4,5},{5,4},{6,7},{7,6},{8,9},{9,8},{10,11... | collective-permute-start | bytes 1179656 | tf_op jit(solution)/shard_map/ppermute | solution.py:573
  112.6 152.6 %reduce-scatter.5.cloned.1.call-start = ((), (), s32[]{:S(2)}) async-start(), calls=%async_computation.4 | async-start | bytes 10616832 | tf_op jit(solution)/shard_map/reduce_scatter | solution.py:769
  132.3 19.9 %collective-permute-start.7 = (bf16[256,768]{1,0:T(8,128)(2,1)}, bf16[256,768]{1,0:T(8,128)(2,1)S(1)}, u32[]{:S(2)}, u32[]{:S(2)}) collective-permute-start(bf16[256,768]{1,0:T(8,128)(2,1)} %get-tuple-element.65), channel_id=1, source_target_pairs={{0,1},{1,0},{2,3},{3,2},{4,5},{5,4},{6,7},{7,6},{8,9},{9,8},{10,11... | collective-permute-start | bytes 1179656 | tf_op jit(solution)/shard_map/ppermute | solution.py:573
  132.5 28.8 %collective-permute-start.8 = (bf16[256,768]{1,0:T(8,128)(2,1)}, bf16[256,768]{1,0:T(8,128)(2,1)S(1)}, u32[]{:S(2)}, u32[]{:S(2)}) collective-permute-start(bf16[256,768]{1,0:T(8,128)(2,1)} %get-tuple-element.67), channel_id=1, source_target_pairs={{0,1},{1,0},{2,3},{3,2},{4,5},{5,4},{6,7},{7,6},{8,9},{9,8},{10,11... | collective-permute-start | bytes 1179656 | tf_op jit(solution)/shard_map/ppermute | solution.py:573
  161.4 208.1 %all-gather.3.cloned.1.call-start = ((), (), s32[]{:S(2)}) async-start(), calls=%async_computation.5 | async-start | bytes 10616832 | tf_op jit(solution)/shard_map/all_gather | solution.py:873
  162.4 20.2 %collective-permute-start.9 = (bf16[256,768]{1,0:T(8,128)(2,1)S(1)}, bf16[256,768]{1,0:T(8,128)(2,1)S(1)}, u32[]{:S(2)}, u32[]{:S(2)}) collective-permute-start(bf16[256,768]{1,0:T(8,128)(2,1)S(1)} %add_convert_fusion.3), channel_id=1, source_target_pairs={{0,2},{1,3},{2,0},{3,1},{4,6},{5,7},{6,4},{7,5},{8,10},{9,11},{10,... | collective-permute-start | bytes 1179656 | tf_op jit(solution)/shard_map/ppermute | solution.py:573
  223.3 9.8 %collective-permute-start.11 = (bf16[256,768]{1,0:T(8,128)(2,1)}, bf16[256,768]{1,0:T(8,128)(2,1)S(1)}, u32[]{:S(2)}, u32[]{:S(2)}) collective-permute-start(bf16[256,768]{1,0:T(8,128)(2,1)} %get-tuple-element.87), channel_id=1, source_target_pairs={{0,1},{1,0},{2,3},{3,2},{4,5},{5,4},{6,7},{7,6},{8,9},{9,8},{10,11... | collective-permute-start | bytes 1179656 | tf_op jit(solution)/shard_map/ppermute | solution.py:573
  233.9 2.8 collective-permute-start.13
  238.3 13.9 %collective-permute-start.14 = (bf16[7,48,768]{2,1,0:T(8,128)(2,1)S(1)}, bf16[7,48,768]{2,1,0:T(8,128)(2,1)S(1)}, u32[]{:S(2)}, u32[]{:S(2)}) collective-permute-start(bf16[7,48,768]{2,1,0:T(8,128)(2,1)S(1)} %constant_dynamic-slice_fusion.1), channel_id=1, source_target_pairs={{0,8},{4,12},{8,0},{12,4},{16,24},{20,28},{24,16},{28,20},{1,9},{5... | collective-permute-start | bytes 1548296 | tf_op jit(solution)/shard_map/ppermute | solution.py:573
  239.9 18.7 %collective-permute-start.10 = (bf16[256,768]{1,0:T(8,128)(2,1)}, bf16[256,768]{1,0:T(8,128)(2,1)S(1)}, u32[]{:S(2)}, u32[]{:S(2)}) collective-permute-start(bf16[256,768]{1,0:T(8,128)(2,1)} %get-tuple-element.85), channel_id=1, source_target_pairs={{0,1},{1,0},{2,3},{3,2},{4,5},{5,4},{6,7},{7,6},{8,9},{9,8},{10,11... | collective-permute-start | bytes 1179656 | tf_op jit(solution)/shard_map/ppermute | solution.py:573
  240.9 20.2 %collective-permute-start.12 = (bf16[256,768]{1,0:T(8,128)(2,1)}, bf16[256,768]{1,0:T(8,128)(2,1)S(1)}, u32[]{:S(2)}, u32[]{:S(2)}) collective-permute-start(bf16[256,768]{1,0:T(8,128)(2,1)} %add_convert_fusion.2), channel_id=1, source_target_pairs={{0,2},{1,3},{2,0},{3,1},{4,6},{5,7},{6,4},{7,5},{8,10},{9,11},{10,... | collective-permute-start | bytes 1179656 | tf_op jit(solution)/shard_map/ppermute | solution.py:573
  265.2 17.3 %collective-permute-start.16 = (bf16[256,768]{1,0:T(8,128)(2,1)}, bf16[256,768]{1,0:T(8,128)(2,1)S(1)}, u32[]{:S(2)}, u32[]{:S(2)}) collective-permute-start(bf16[256,768]{1,0:T(8,128)(2,1)} %get-tuple-element.96.refs_0_), channel_id=1, source_target_pairs={{0,2},{1,3},{2,0},{3,1},{4,6},{5,7},{6,4},{7,5},{8,10},{9,11},{10,... | collective-permute-start | bytes 1179656 | tf_op jit(solution)/shard_map/ppermute | solution.py:573
  282.5 10.7 %collective-permute-start.23 = (bf16[7,24,768]{2,1,0:T(8,128)(2,1)S(1)}, bf16[7,24,768]{2,1,0:T(8,128)(2,1)S(1)}, u32[]{:S(2)}, u32[]{:S(2)}) collective-permute-start(bf16[7,24,768]{2,1,0:T(8,128)(2,1)S(1)} %constant_dynamic-slice_fusion), channel_id=1, source_target_pairs={{0,16},{4,20},{8,24},{12,28},{16,0},{20,4},{24,8},{28,12},{1,17},{... | collective-permute-start | bytes 774152 | tf_op jit(solution)/shard_map/ppermute | solution.py:573
  293.3 6.0 %collective-permute-start.24 = (bf16[24,768]{1,0:T(8,128)(2,1)S(1)}, bf16[24,768]{1,0:T(8,128)(2,1)S(1)}, u32[]{:S(2)}, u32[]{:S(2)}) collective-permute-start(bf16[24,768]{1,0:T(8,128)(2,1)S(1)} %get-tuple-element.114), channel_id=1, source_target_pairs={{0,1},{1,0},{2,3},{3,2},{4,5},{5,4},{6,7},{7,6},{8,9},{9,8},{10,11... | collective-permute-start | bytes 110600 | tf_op jit(solution)/shard_map/ppermute | solution.py:573
  294.8 5.5 %collective-permute-start.25 = (bf16[24,768]{1,0:T(8,128)(2,1)S(1)}, bf16[24,768]{1,0:T(8,128)(2,1)S(1)}, u32[]{:S(2)}, u32[]{:S(2)}) collective-permute-start(bf16[24,768]{1,0:T(8,128)(2,1)S(1)} %get-tuple-element.116), channel_id=1, source_target_pairs={{0,2},{1,3},{2,0},{3,1},{4,6},{5,7},{6,4},{7,5},{8,10},{9,11},{10,... | collective-permute-start | bytes 110600 | tf_op jit(solution)/shard_map/ppermute | solution.py:573
  297.2 6.3 %collective-permute-start.26 = (bf16[24,768]{1,0:T(8,128)(2,1)S(1)}, bf16[24,768]{1,0:T(8,128)(2,1)S(1)}, u32[]{:S(2)}, u32[]{:S(2)}) collective-permute-start(bf16[24,768]{1,0:T(8,128)(2,1)S(1)} %get-tuple-element.115), channel_id=1, source_target_pairs={{0,3},{1,2},{2,1},{3,0},{4,7},{5,6},{6,5},{7,4},{8,11},{9,10},{10,... | collective-permute-start | bytes 110600 | tf_op jit(solution)/shard_map/ppermute | solution.py:573
  297.7 20.5 %collective-permute-start.5 = (bf16[256,768]{1,0:T(8,128)(2,1)S(1)}, bf16[256,768]{1,0:T(8,128)(2,1)S(1)}, u32[]{:S(2)}, u32[]{:S(2)}) collective-permute-start(bf16[256,768]{1,0:T(8,128)(2,1)S(1)} %copy-done.3), channel_id=1, source_target_pairs={{0,2},{1,3},{2,0},{3,1},{4,6},{5,7},{6,4},{7,5},{8,10},{9,11},{10,... | collective-permute-start | bytes 1179656 | tf_op jit(solution)/shard_map/ppermute | solution.py:573
  303.6 14.8 %collective-permute-start.27 = (bf16[4,24,768]{2,1,0:T(8,128)(2,1)S(1)}, bf16[4,24,768]{2,1,0:T(8,128)(2,1)S(1)}, u32[]{:S(2)}, u32[]{:S(2)}) collective-permute-start(bf16[4,24,768]{2,1,0:T(8,128)(2,1)S(1)} %pad_maximum_fusion.4), channel_id=1, source_target_pairs={{0,16},{4,20},{8,24},{12,28},{16,0},{20,4},{24,8},{28,12},{1,17},{... | collective-permute-start | bytes 442376 | tf_op jit(solution)/shard_map/ppermute | solution.py:573
  304.2 30.5 %collective-permute-start.4 = (bf16[256,768]{1,0:T(8,128)(2,1)S(1)}, bf16[256,768]{1,0:T(8,128)(2,1)S(1)}, u32[]{:S(2)}, u32[]{:S(2)}) collective-permute-start(bf16[256,768]{1,0:T(8,128)(2,1)S(1)} %copy-done.3), channel_id=1, source_target_pairs={{0,1},{1,0},{2,3},{3,2},{4,5},{5,4},{6,7},{7,6},{8,9},{9,8},{10,11... | collective-permute-start | bytes 1179656 | tf_op jit(solution)/shard_map/ppermute | solution.py:573
  318.2 16.5 %collective-permute-start.6 = (bf16[256,768]{1,0:T(8,128)(2,1)S(1)}, bf16[256,768]{1,0:T(8,128)(2,1)S(1)}, u32[]{:S(2)}, u32[]{:S(2)}) collective-permute-start(bf16[256,768]{1,0:T(8,128)(2,1)S(1)} %collective-permute-done.5.refs_2_), channel_id=1, source_target_pairs={{0,1},{1,0},{2,3},{3,2},{4,5},{5,4},{6,7},{7,6},{8,9},{9,8},{10,11... | collective-permute-start | bytes 1179656 | tf_op jit(solution)/shard_map/ppermute | solution.py:573
  318.4 22.5 %collective-permute-start.28 = (bf16[4,48,768]{2,1,0:T(8,128)(2,1)S(1)}, bf16[4,48,768]{2,1,0:T(8,128)(2,1)}, u32[]{:S(2)}, u32[]{:S(2)}) collective-permute-start(bf16[4,48,768]{2,1,0:T(8,128)(2,1)S(1)} %pad_maximum_fusion.3), channel_id=1, source_target_pairs={{0,8},{4,12},{8,0},{12,4},{16,24},{20,28},{24,16},{28,20},{1,9},{5... | collective-permute-start | bytes 884744 | tf_op jit(solution)/shard_map/ppermute | solution.py:573
  320.0 13.1 %collective-permute-start.19 = (f32[18,768]{1,0:T(8,128)S(1)}, f32[18,768]{1,0:T(8,128)S(1)}, u32[]{:S(2)}, u32[]{:S(2)}) collective-permute-start(f32[18,768]{1,0:T(8,128)S(1)} %fusion.11), channel_id=1, source_target_pairs={{0,8},{4,12},{8,0},{12,4},{16,24},{20,28},{24,16},{28,20},{1,9},{5... | collective-permute-start | bytes 165896 | tf_op jit(solution)/shard_map/ppermute | solution.py:573
  333.1 7.1 %collective-permute-start.20 = (f32[18,768]{1,0:T(8,128)S(1)}, f32[18,768]{1,0:T(8,128)S(1)}, u32[]{:S(2)}, u32[]{:S(2)}) collective-permute-start(f32[18,768]{1,0:T(8,128)S(1)} %add.92), channel_id=1, source_target_pairs={{0,16},{4,20},{8,24},{12,28},{16,0},{20,4},{24,8},{28,12},{1,17},{... | collective-permute-start | bytes 165896 | tf_op jit(solution)/shard_map/ppermute | solution.py:573
  338.8 18.1 %collective-permute-start.15 = (bf16[256,768]{1,0:T(8,128)(2,1)S(1)}, bf16[256,768]{1,0:T(8,128)(2,1)S(1)}, u32[]{:S(2)}, u32[]{:S(2)}) collective-permute-start(bf16[256,768]{1,0:T(8,128)(2,1)S(1)} %copy-done.8), channel_id=1, source_target_pairs={{0,1},{1,0},{2,3},{3,2},{4,5},{5,4},{6,7},{7,6},{8,9},{9,8},{10,11... | collective-permute-start | bytes 1179656 | tf_op jit(solution)/shard_map/ppermute | solution.py:573
  340.3 10.2 %collective-permute-start.21 = (f32[10,768]{1,0:T(8,128)S(1)}, f32[10,768]{1,0:T(8,128)S(1)}, u32[]{:S(2)}, u32[]{:S(2)}) collective-permute-start(f32[10,768]{1,0:T(8,128)S(1)} %slice.56), channel_id=1, source_target_pairs={{0,1},{1,0},{2,3},{3,2},{4,5},{5,4},{6,7},{7,6},{8,9},{9,8},{10,11... | collective-permute-start | bytes 92168 | tf_op jit(solution)/shard_map/ppermute | solution.py:573
  342.0 25.0 %collective-permute-start.29 = (bf16[4,96,768]{2,1,0:T(8,128)(2,1)S(1)}, bf16[4,96,768]{2,1,0:T(8,128)(2,1)S(1)}, u32[]{:S(2)}, u32[]{:S(2)}) collective-permute-start(bf16[4,96,768]{2,1,0:T(8,128)(2,1)S(1)} %pad_maximum_fusion.1), channel_id=1, source_target_pairs={{0,4},{4,0},{8,12},{12,8},{16,20},{20,16},{24,28},{28,24},{1,5},{5... | collective-permute-start | bytes 1769480 | tf_op jit(solution)/shard_map/ppermute | solution.py:573
  350.5 5.2 %collective-permute-start.22 = (f32[10,768]{1,0:T(8,128)S(1)}, f32[10,768]{1,0:T(8,128)S(1)}, u32[]{:S(2)}, u32[]{:S(2)}) collective-permute-start(f32[10,768]{1,0:T(8,128)S(1)} %slice_add_fusion), channel_id=1, source_target_pairs={{0,2},{1,3},{2,0},{3,1},{4,6},{5,7},{6,4},{7,5},{8,10},{9,11},{10,... | collective-permute-start | bytes 92168 | tf_op jit(solution)/shard_map/ppermute | solution.py:573
  353.0 10.0 %collective-permute-start.17 = (bf16[256,768]{1,0:T(8,128)(2,1)S(1)}, bf16[256,768]{1,0:T(8,128)(2,1)S(1)}, u32[]{:S(2)}, u32[]{:S(2)}) collective-permute-start(bf16[256,768]{1,0:T(8,128)(2,1)S(1)} %collective-permute-done.16.refs_2_), channel_id=1, source_target_pairs={{0,1},{1,0},{2,3},{3,2},{4,5},{5,4},{6,7},{7,6},{8,9},{9,8},{10,11... | collective-permute-start | bytes 1179656 | tf_op jit(solution)/shard_map/ppermute | solution.py:573
  (28 other events, 540.7 us)
Sparse Core Ops, SparseCore 0:
  112.8 43.6 reduce-scatter.2
  161.5 76.4 reduce-scatter.4
  265.4 65.2 all-gather.2

commit v3 on v2

--- a/solution.py
+++ b/solution.py
@@ -166,8 +166,9 @@
 def attn_bwd_kernel(piece, pieces, heads, head_size, shares, idx, *refs):
     held = piece + 1
     last = held == pieces
-    go, qh, ot, lse = refs[:4]
-    refs = refs[4:]
+    go_parts, refs = refs[:shares], refs[shares:]
+    tok, router, gain_two, qh, ot, lse = refs[:6]
+    refs = refs[6:]
     ks, refs = refs[:held], refs[held:]
     vs, refs = refs[:held], refs[held:]
     bias, far, seg = refs[:3]
@@ -181,7 +182,7 @@
         w, hot = refs[:2]
         refs = refs[2:]
         gn_parts, refs = refs[:shares], refs[shares:]
-        gproj, rel_out = refs[:2]
+        gproj, misc = refs[:2]
         refs = refs[2:]
         gk, refs = refs[:held], refs[held:]
         gv, refs = refs[:held], refs[held:]
@@ -192,11 +193,14 @@
         gv, refs = refs[:held], refs[held:]
         gq_t, acc = refs[:2]
         refs = refs[2:]
-    kt, d_row, near_sum, far_sum = refs
+    go, misc_sum, kt, d_row, near_sum, far_sum = refs
     rows_total, features = ks[0].shape
     blocks = rows_total // BLK
     share = rows_total // shares
     me = idx[0]
+    for step in range(shares):
+        start = pl.multiple_of((me ^ step) * share, share)
+        go[pl.ds(start, share), :] = go_parts[step][...]
     for index in range(held):
         for block in range(blocks):
             cols = pl.ds(block * BLK, BLK)
@@ -272,6 +276,7 @@
             gproj[0, out, :] = gqs[index][:, rows].T.astype(BF16)
             gproj[1, out, :] = gk[index][rows, :].astype(BF16)
             gproj[2, out, :] = gv[index][rows, :].astype(BF16)
+    gain_one = jnp.zeros_like(gain_two)
     for step in range(shares):
         for index in range(pieces):
             start = index * rows_total + (me ^ step) * share
@@ -280,6 +285,8 @@
             total = total + dot(gproj[1, rows, :], w[1])
             total = total + dot(gproj[2, rows, :], w[2])
             gn_parts[step][pl.ds(index * share, share), :] = total.astype(BF16)
+            x = tok[rows, :].astype(F32)
+            gain_one = gain_one + jnp.sum(total * (x * row_scale(x)), axis=0, keepdims=True)
     for head in range(heads):
         for delta in range(2):
             turned = dot(flip, acc[2 * head + delta], NN, HIGHEST)
@@ -289,7 +296,13 @@
     summed = dot(near_sum[0], hot[0], NN, HIGHEST) + dot(near_sum[1], hot[1], NN, HIGHEST)
     buckets = lax.broadcasted_iota(jnp.int32, summed.shape, 1)
     beyond = jnp.sum(far_sum[...], axis=1, keepdims=True)
-    rel_out[...] = summed + jnp.where(buckets == NB - 1, beyond, 0.0)
+    summed = summed + jnp.where(buckets == NB - 1, beyond, 0.0)
+    misc_sum[...] = jnp.zeros_like(misc_sum)
+    misc_sum[pl.ds(pl.multiple_of(me * 8, 8), 8), 0:NB] = summed
+    misc_sum[8 * shares : 8 * shares + 8, :] = router[...]
+    misc_sum[8 * shares + 8 : 8 * shares + 9, :] = gain_one
+    misc_sum[8 * shares + 9 : 8 * shares + 10, :] = gain_two[...]
+    misc[...] = misc_sum[...].astype(BF16)
 
 
 def qkv_weights_kernel(pieces, *refs):
@@ -321,12 +334,13 @@
 def moe_fwd_kernel(piece, pieces, shares, experts, idx, *refs):
     att, refs = refs[:shares], refs[shares:]
     if piece == 0:
-        wo_fetched, wo_swapped, refs = refs[0], refs[1], refs[2:]
+        wo_own, wo_swapped, refs = refs[0], refs[1], refs[2:]
+        wo_fetched, refs = refs[: shares - 1], refs[shares - 1 :]
     else:
         wo, refs = refs[0], refs[1:]
     tok, gain, router, routes, cot, w_in, w_down = refs[:7]
     refs = refs[7:]
-    parts, refs = refs[0], refs[1:]
+    parts, refs = refs[:shares], refs[shares:]
     if piece == 0:
         wo, refs = refs[0], refs[1:]
     normed, own, gates, ggate, act, slope, acc = refs
@@ -341,12 +355,13 @@
         gain_row = gain[...].astype(F32).reshape(1, -1)
         router_wide = padded_rows(router[...].astype(F32), LANES).astype(BF16)
         if piece == 0:
-            half = wo_fetched.shape[1]
+            half = wo_own.shape[0] // 2
             mine = pl.ds(pl.multiple_of(idx[1] * half, half), half)
             other = pl.ds(pl.multiple_of((1 - idx[1]) * half, half), half)
-            for step in range(shares):
-                wo[step, mine, :] = wo_fetched[me ^ step]
-                wo[step, other, :] = wo_swapped[me ^ step]
+            wo[0] = wo_own[...]
+            for step in range(1, shares):
+                wo[step, mine, :] = wo_fetched[step - 1][...]
+                wo[step, other, :] = wo_swapped[step - 1]
         for block in range(rows_total // BLK):
             rows = pl.ds(block * BLK, BLK)
             outer = pl.ds(base + block * BLK, BLK)
@@ -389,7 +404,9 @@
 
     @pl.when(expert == experts - 1)
     def _():
-        parts[...] = acc[...].astype(BF16)
+        for step in range(shares):
+            start = pl.multiple_of((me ^ step) * share, share)
+            parts[step][...] = acc[pl.ds(start, share), :].astype(BF16)
 
 
 def moe_bwd_kernel(piece, shares, experts, idx, *refs):
@@ -466,7 +483,8 @@
     gx, refs = refs[:got], refs[got:]
     wo, own, cot, gain = refs[:4]
     refs = refs[4:]
-    ga, gh, gh_low, ggain = refs
+    ga, refs = refs[:shares], refs[shares:]
+    gh, gh_low, ggain = refs
     share = own.shape[0]
     grad = gx[0][...].astype(F32)
     for step in range(1, got):
@@ -483,7 +501,7 @@
     low = back.astype(BF16)
     gh_low[...] = low
     for step in range(shares):
-        ga[idx[0] ^ step] = dot(low, wo[step], NT).astype(BF16)
+        ga[step][...] = dot(low, wo[step], NT).astype(BF16)
 
 
 def w_out_back_kernel(pieces, shares, idx, *refs):
@@ -512,10 +530,9 @@
 def input_back_kernel(pieces, got, idx, *refs):
     gn, refs = refs[:got], refs[got:]
     ghs, refs = refs[:pieces], refs[pieces:]
-    tok, gain, gt, ggain = refs
+    tok, gain, gt = refs
     share = ghs[0].shape[0]
     gain_row = gain[...].astype(F32).reshape(1, -1)
-    total = jnp.zeros_like(ggain)
     for index in range(pieces):
         rows = pl.ds(index * share, share)
         grad = gn[0][rows, :].astype(F32)
@@ -525,11 +542,9 @@
         x = tok[pl.ds(pl.multiple_of(start, share), share), :].astype(F32)
         scale = row_scale(x)
         unit = x * scale
-        total = total + jnp.sum(grad * unit, axis=0, keepdims=True)
         gained = grad * gain_row
         back = scale * (gained - unit * jnp.mean(gained * unit, axis=-1, keepdims=True))
         gt[rows, :] = (ghs[index][...] + back).astype(BF16)
-    ggain[...] = total
 
 
 def place_kernel(pieces, shares, idx, *refs):
@@ -651,7 +666,7 @@
 
     half_rows = features // 2
     my_half = lax.dynamic_slice_in_dim(w_out, side * half_rows, half_rows, 0)
-    halves = lax.all_gather(my_half, "tensor", axis=0)
+    halves = [swap(my_half, "tensor", by) for by in others]
 
     build_hot, gather_hot = near_tables()
     build_hot = jnp.asarray(np.swapaxes(build_hot, 1, 2), BF16)
@@ -677,7 +692,7 @@
         flops=6 * 10**9, moved=8 * mib, with_index=False,
     )
     atts = gather_parts(att, "tensor")
-    swapped = swap(after(halves, att), "dp", 1)
+    swapped = swap(jnp.stack(halves), "dp", 1)
 
     full = lambda shape: pl.BlockSpec(shape, lambda e: (0,) * len(shape))
     per_expert = lambda shape: pl.BlockSpec((1,) + shape, lambda e: (e, 0, 0))
@@ -691,19 +706,21 @@
         grid=(experts,),
         in_specs=[SMEM]
         + [full((rows, features))] * shares
-        + [full((shares, half_rows, width))] * 2
+        + [full((features, width)), full((shares - 1, half_rows, width))]
+        + [full((half_rows, width))] * (shares - 1)
         + [
             full((rows, width)), full((width,)), full((experts, width)),
             full((rows, 2)), full((rows, width)),
             per_expert((width, hidden_units)), per_expert((hidden_units, width)),
         ],
-        out_specs=[
-            full((rows, width)), full((shares, features, width)), full((rows, width)),
+        out_specs=[full((share, width))] * shares
+        + [
+            full((shares, features, width)), full((rows, width)),
             full((share, width)), full((rows, LANES)), full((rows, LANES)),
             per_expert((rows, hidden_units)), per_expert((rows, hidden_units)),
         ],
-        out_shape=[
-            shaped((rows, width), BF16),
+        out_shape=[shaped((share, width), BF16)] * shares
+        + [
             shaped((shares, features, width), BF16),
             shaped((rows, width), BF16),
             shaped((share, width), F32),
@@ -718,11 +735,15 @@
             flops=moe_flops, bytes_accessed=32 * mib, transcendentals=0
         ),
     )(
-        idx, *atts, halves, swapped, tokens, gain_moe, router_t, routes, grad_out,
+        idx, *atts, w_out, swapped, *halves, tokens, gain_moe, router_t, routes, grad_out,
         w_in, w_down,
     )
-    moe_sum, wo, normed_two, own_hidden, gates, ggate, act, slope = fwd
-    moe_rows = lax.psum_scatter(moe_sum, "tensor", scatter_dimension=0, tiled=True)
+    moe_parts = fwd[:shares]
+    wo, normed_two, own_hidden, gates, ggate, act, slope = fwd[shares:]
+    if four:
+        moe_near = reduce_near(moe_parts, "tensor")
+    else:
+        moe_near = exchange(moe_parts, "tensor")[1:]
 
     bwd = pl.pallas_call(
         functools.partial(moe_bwd_kernel, 0, shares, experts),
@@ -745,7 +766,7 @@
             flops=moe_flops, bytes_accessed=26 * mib, transcendentals=0
         ),
     )(idx, gates, ggate, grad_out, slope, router_t, w_in, w_down)
-    gx_parts = bwd[:shares]
+    gx_parts = [after(part, *moe_near) for part in bwd[:shares]]
     glog, gpre = bwd[shares:]
     gx_near = reduce_near(gx_parts, "tensor") if four else exchange(gx_parts, "tensor")[1:]
 
@@ -773,42 +794,41 @@
         gx_got, _ = reduce_far(gx_parts, gx_near, "tensor")
     else:
         gx_got = [gx_parts[0], *gx_near]
-    ga, grad_hidden, gh_low, ggain_two = whole_call(
+    back = whole_call(
         functools.partial(hidden_back_kernel, 0, PIECES, shares, len(gx_got)),
-        [
-            shaped((shares, share, features), BF16), shaped((share, width), F32),
-            shaped((share, width), BF16), shaped((1, width), F32),
-        ],
+        [shaped((share, features), BF16)] * shares
+        + [shaped((share, width), F32), shaped((share, width), BF16), shaped((1, width), F32)],
         [idx, *gx_got, wo, own_hidden, grad_out, gain_moe],
         flops=3 * 10**8, moved=5 * mib,
     )
-    go = lax.all_to_all(ga, "tensor", split_axis=0, concat_axis=0, tiled=True)
-    go = go.reshape(rows, features)
-
+    go = exchange(back[:shares], "tensor")
+    grad_hidden, gh_low, ggain_two = back[shares:]
+
+    if four:
+        moe_near = after(moe_near[0], gh_low), moe_near[1]
+        moe_got, _ = reduce_far(moe_parts, moe_near, "tensor")
+    else:
+        moe_got = [moe_parts[0], *moe_near]
     result_share = whole_call(
-        functools.partial(join_kernel, PIECES, 1),
+        functools.partial(join_kernel, PIECES, len(moe_got)),
         [shaped((share, width), BF16)],
-        [own_hidden, moe_rows],
-        moved=2 * mib, with_index=False,
+        [own_hidden, *moe_got],
+        moved=3 * mib, with_index=False,
     )[0]
-    result_got = gather_parts(result_share, "tensor")
-    result = whole_call(
-        functools.partial(place_kernel, PIECES, shares),
-        [shaped((rows, width), BF16)], [idx, *result_got], moved=3 * mib,
-    )[0]
-
     attn_back = whole_call(
         functools.partial(attn_bwd_kernel, 0, PIECES, heads, head_size, shares),
         [shaped((share, width), BF16)] * shares
-        + [shaped((3, rows, features), BF16), shaped((8, NB), F32)],
+        + [shaped((3, rows, features), BF16), shaped((features, width), BF16)],
         [
-            idx, after(go, result_share), qh, ot, lse, k, v, bias, far, segments,
+            idx, *go, tokens, router_rows, ggain_two, qh, ot, lse, k, v, bias, far, segments,
             w_qkv_t, gather_hot,
         ],
         [pltpu.VMEM((rows, features), F32)] * 2
         + [
             pltpu.VMEM((features, rows), F32),
             pltpu.VMEM((2 * heads, BLK, BLK), F32),
+            pltpu.VMEM((rows, features), BF16),
+            pltpu.VMEM((features, width), F32),
             pltpu.VMEM((features, rows), BF16),
             pltpu.VMEM((8, rows), F32),
             pltpu.VMEM((2, 8, 2 * BLK), F32),
@@ -816,8 +836,8 @@
         ],
         flops=14 * 10**9, moved=8 * mib,
     )
-    gn_parts = attn_back[:shares]
-    gproj, grad_rel = attn_back[shares:]
+    gn_parts = [after(part, moe_got[-1]) for part in attn_back[:shares]]
+    gproj, misc = attn_back[shares:]
 
     qkv_rows = whole_call(
         functools.partial(qkv_weights_kernel, PIECES),
@@ -831,10 +851,11 @@
         [idx, *atts, after(gh_low, gproj)],
         flops=3 * 10**8, moved=4 * mib,
     )[0]
-    late = jnp.concatenate([qkv_rows, w_out_rows], axis=0)
+    late = jnp.concatenate([qkv_rows, misc[None], w_out_rows], axis=0)
     if four:
         near = reduce_near(gn_parts, "tensor")
-        gn_got, mark = reduce_far(gn_parts, (after(near[0], late), near[1]), "tensor")
+        near = after(near[0], late, near[1]), near[1]
+        gn_got, mark = reduce_far(gn_parts, near, "tensor")
     else:
         gn_got = exchange(gn_parts, "tensor")
         mark = gn_got[-1]
@@ -847,50 +868,61 @@
         return (keep.astype(F32) + got.astype(F32)).astype(BF16)
 
     late = after(late, mark)
-    for bit in bits_of("dp")[:2]:
-        late = halve(late, bit)
+    late = halve(late, 1)
     grad_hidden = after(grad_hidden, late)
 
-    gt_share, ggain_one = whole_call(
+    expert_rows = after(expert_rows, mark)
+    gt_share = whole_call(
         functools.partial(input_back_kernel, PIECES, len(gn_got)),
-        [shaped((share, width), BF16), shaped((1, width), F32)],
+        [shaped((share, width), BF16)],
         [idx, *gn_got, grad_hidden, tokens, gain_attn],
         moved=5 * mib,
-    )
+    )[0]
     gt_got = gather_parts(gt_share, "tensor")
     grad_tokens = whole_call(
         functools.partial(place_kernel, PIECES, shares),
         [shaped((rows, width), F32)], [idx, *gt_got], moved=5 * mib,
     )[0]
 
-    for bit in bits_of("dp")[2:]:
-        late = halve(late, bit, gt_got[2])
-    out_sum = late[3].astype(F32)
+    result_got = gather_parts(after(result_share, gt_got[2]), "tensor")
+    result = whole_call(
+        functools.partial(place_kernel, PIECES, shares),
+        [shaped((rows, width), BF16)], [idx, *result_got], moved=3 * mib,
+    )[0]
+
+    for level, bit in enumerate(bits_of("dp")[1:]):
+        late = halve(late, bit, gt_got[2] if level else gt_share)
+
+    out_sum, small = late[4].astype(F32), [late[3]]
     for by in others:
-        out_sum = out_sum + swap(late[3 + by], "tensor", by).astype(F32)
-    late = jnp.concatenate([late[:3], out_sum.astype(BF16)[None]], axis=0)
-    late = gather_back(late, "dp", 1)
-    expert_rows = lax.all_gather(after(expert_rows, gt_share), "dp", axis=0, tiled=True)
+        got = swap(jnp.stack([late[4 + by], late[3]]), "tensor", by)
+        out_sum = out_sum + got[0].astype(F32)
+        small.append(got[1])
+    small = [one.astype(F32) for one in small]
+    while len(small) > 1:
+        small = [small[at] + small[at + 1] for at in range(0, len(small), 2)]
+    late = jnp.concatenate(
+        [late[:3], jnp.stack([small[0].astype(BF16), out_sum.astype(BF16)])], axis=0
+    )
+    late = gather_back(after(late, *gt_got[1:], result_got[2]), "dp", 1)
+    expert_rows = lax.all_gather(expert_rows, "dp", axis=0, tiled=True)
     expert_rows = expert_rows.reshape(experts, 2, width, width)
     grad_w_in = expert_rows[:, 0].astype(F32)
     grad_w_down = expert_rows[:, 1].astype(F32)
     grad_w_qkv = jnp.swapaxes(late[:3], 1, 2).astype(F32)
-    grad_w_out = late[3].astype(F32)
-
-    rel_rows = jnp.pad(grad_rel, ((0, 0), (0, width - NB)))
-    small = jnp.concatenate([rel_rows, router_rows, ggain_one, ggain_two], axis=0)
-    small = sum_over(small, "dp")
-    grad_rel_bias = small[:heads, :NB].T
-    shared = sum_over(small[8:], "tensor")
+    grad_w_out = late[4].astype(F32)
+    small = late[3].astype(F32)
+    grad_rel = lax.dynamic_slice_in_dim(small, me * 8, 8, 0)
+    first = 8 * shares
     return (
         result,
         grad_tokens,
-        shared[8],
+        small[first + 8],
         grad_w_qkv,
         grad_w_out,
-        grad_rel_bias,
-        shared[9],
-        shared[:experts].T,
+        grad_rel[:heads, :NB].T,
+        small[first + 9],
+        small[first : first + experts].T,
         grad_w_in,
         grad_w_down,
     )

time: 389 us -> 393 us (1.010)
  waiting for transfers between devices: 137 us -> 192 us
  blocking collectives: 51.6 us -> 0 us
    ppermute x30 -> x34, waiting for transfers between devices: 137 us -> 192 us  [swap(): return lax.ppermute(value, axis, [(i, i ^ bit) for i in range(count)])]
    all_gather x1 -> x0, blocking collectives: 36.7 us -> none  [body(): halves = lax.all_gather(my_half, 'tensor', axis=0)]
    all_to_all x1 -> x0, blocking collectives: 14.9 us -> none  [body(): go = lax.all_to_all(ga, 'tensor', split_axis=0, concat_axis=0, tiled=True)]
    ppermute x30 -> x34, starting transfers between devices: 41.2 us -> 45 us  [swap(): return lax.ppermute(value, axis, [(i, i ^ bit) for i in range(count)])]
  transfers between devices with their start and end apart: 33 -> 36, of which waited for: 19 -> 22; matrix products, arithmetic and copies ran while one was open for 4% -> 3% of each run, Pallas kernels for 19% -> 19%
where the time goes in v3:
time: 393 us; the launch traced here: 392 us
  waiting for transfers between devices  192 us (49%)
  Pallas kernels  113 us (29%)
  starting transfers between devices  45 us (11%)
  other arithmetic  20.1 us (5%)
  between operations  14.4 us (4%)
  local copies, waits for them, and re-layouts  7.19 us (2%)
    ppermute x34, waiting for transfers between devices, swap(): return lax.ppermute(value, axis, [(i, i ^ bit) for i in range(count)])  192 us
    pallas_call x9, Pallas kernels, whole_call(): pl.pallas_call(kernel, out_shape=outs, in_specs=specs, out_specs=[VMEM] *...  52.4 us
    ppermute x34, starting transfers between devices, swap(): return lax.ppermute(value, axis, [(i, i ^ bit) for i in range(count)])  45 us
    pallas_call x1, Pallas kernels, body(): pl.pallas_call(functools.partial(moe_fwd_kernel, 0, PIECES, shares, exper...  25.7 us
    pallas_call x1, Pallas kernels, body(): pl.pallas_call(functools.partial(moe_bwd_kernel, 0, shares, experts), gri...  19.3 us
    pallas_call x1, Pallas kernels, body(): pl.pallas_call(functools.partial(moe_weights_kernel, PIECES), grid=(exper...  15.9 us
    convert_element_type x1, other arithmetic, body(): grad_w_down = expert_rows[:, 1].astype(F32)  12.3 us
  transfers between devices with their start and end apart: 36, of which 22 were waited for; matrix products, arithmetic and copies ran while one was open for 3% of the time, Pallas kernels for 19%

profile of v3, /device:TPU:0, one launch (start us, length us, event | category | flops | bytes accessed | tf_op | source)
XLA Modules:
  0.0 392.2 jit_solution(17291655637587083624)
XLA Ops:
  7.2 12.2 %shard_map.213 = (bf16[1024,768]{1,0:T(8,128)(2,1)}, bf16[3,1024,192]{2,1,0:T(8,128)(2,1)}, bf16[1024,192]{1,0:T(8,128)(2,1)}, bf16[1024,192]{1,0:T(8,128)(2,1)}...) custom-call(bf16[1024,768]{1,0:T(8,128)(2,1)} %refs_4_.5, ...), custom_call_target="tpu_custom_call" | custom-call | flops 6000000000 | bytes 8388608 | tf_op jit(solution)/shard_map/pallas_call | solution.py:575
  19.4 4.0 %collective-permute-start.1 = (bf16[1024,192]{1,0:T(8,128)(2,1)}, bf16[1024,192]{1,0:T(8,128)(2,1)S(1)}, u32[]{:S(2)}, u32[]{:S(2)}) collective-permute-start(bf16[1024,192]{1,0:T(8,128)(2,1)} %get-tuple-element.71.refs_0_), channel_id=1, source_target_pairs={{0,2},{1,3},{2,0},{3,1},{4,6},{5,7},{6,4},{7,5},{8,10},{9,11},{10,... | collective-permute-start | bytes 1179656 | tf_op jit(solution)/shard_map/ppermute | solution.py:588
  28.0 11.3 %collective-permute-done.3.refs_6_ = bf16[96,768]{1,0:T(8,128)(2,1)S(1)} collective-permute-done((bf16[96,768]{1,0:T(8,128)(2,1)S(1)}, bf16[96,768]{1,0:T(8,128)(2,1)S(1)}, u32[]{:S(2)}, u32[]{:S(2)}) %collective-permute-start.3) | collective-permute-done | bytes 147488 | tf_op jit(solution)/shard_map/ppermute | solution.py:588
  39.2 17.9 %collective-permute-done.4.refs_7_ = bf16[96,768]{1,0:T(8,128)(2,1)S(1)} collective-permute-done((bf16[96,768]{1,0:T(8,128)(2,1)S(1)}, bf16[96,768]{1,0:T(8,128)(2,1)S(1)}, u32[]{:S(2)}, u32[]{:S(2)}) %collective-permute-start.4) | collective-permute-done | bytes 147488 | tf_op jit(solution)/shard_map/ppermute | solution.py:588
  57.3 3.1 collective-permute-start
  62.1 11.3 %collective-permute-done.refs_1_ = bf16[1024,192]{1,0:T(8,128)(2,1)S(1)} collective-permute-done((bf16[1024,192]{1,0:T(8,128)(2,1)}, bf16[1024,192]{1,0:T(8,128)(2,1)S(1)}, u32[]{:S(2)}, u32[]{:S(2)}) %collective-permute-start) | collective-permute-done | bytes 393248 | tf_op jit(solution)/shard_map/ppermute | solution.py:588
  73.4 11.0 %collective-permute-done.2.refs_3_ = bf16[1024,192]{1,0:T(8,128)(2,1)S(1)} collective-permute-done((bf16[1024,192]{1,0:T(8,128)(2,1)S(1)}, bf16[1024,192]{1,0:T(8,128)(2,1)S(1)}, u32[]{:S(2)}, u32[]{:S(2)}) %collective-permute-start.2) | collective-permute-done | bytes 393248 | tf_op jit(solution)/shard_map/ppermute | solution.py:588
  85.2 25.7 %shard_map.214 = (bf16[256,768]{1,0:T(8,128)(2,1)}, bf16[256,768]{1,0:T(8,128)(2,1)}, bf16[256,768]{1,0:T(8,128)(2,1)}, bf16[256,768]{1,0:T(8,128)(2,1)}, bf16[4...) custom-call(s32[2]{0:T(128)} %pad_add_fusion.idx, ...), custom_call_target="tpu_custom_call" | custom-call | flops 9663676416 | bytes 33554432 | tf_op jit(solution)/shard_map/pallas_call | solution.py:704
  113.0 19.3 %shard_map.215 = (bf16[256,768]{1,0:T(8,128)(2,1)}, bf16[256,768]{1,0:T(8,128)(2,1)}, bf16[256,768]{1,0:T(8,128)(2,1)}, bf16[256,768]{1,0:T(8,128)(2,1)}, f32[10...) custom-call(s32[2]{0:T(128)} %pad_add_fusion.idx, f32[1024,128]{1,0:T(8,128)} %get-tuple-element.77.refs_0_, ...), custom_call_target="tpu_custom_call" | custom-call | flops 9663676416 | bytes 27262976 | tf_op jit(solution)/shard_map/pallas_call | solution.py:748
  134.5 15.9 %shard_map.216 = (bf16[4,2,768,768]{3,2,1,0:T(8,128)(2,1)}, f32[8,768]{1,0:T(8,128)}) custom-call(bf16[1024,768]{1,0:T(8,128)(2,1)} %refs_5_.5, f32[1024,128]{1,0:T(8,128)} %get-tuple-element.77.refs_0_, f32[1024,128]{1,0:T(8,128)} %get-tuple-element.88.refs_1_, bf16[1024,768]{1,0:T(8,128)(2,1)} %get-tuple-element.89.refs_2_, ...), custom_call_target="tpu_custom_call" | custom-call | flops 9663676416 | bytes 27262976 | tf_op jit(solution)/shard_map/pallas_call | solution.py:773
  152.7 3.5 collective-permute-start.11
  156.1 15.9 %collective-permute-done.11.refs_2_ = bf16[256,768]{1,0:T(8,128)(2,1)S(1)} collective-permute-done((bf16[256,768]{1,0:T(8,128)(2,1)S(1)}, bf16[256,768]{1,0:T(8,128)(2,1)S(1)}, u32[]{:S(2)}, u32[]{:S(2)}) %collective-permute-start.11) | collective-permute-done | bytes 393248 | tf_op jit(solution)/shard_map/ppermute | solution.py:588
  172.8 4.3 %shard_map.217 = (bf16[256,192]{1,0:T(8,128)(2,1)}, bf16[256,192]{1,0:T(8,128)(2,1)}, bf16[256,192]{1,0:T(8,128)(2,1)}, bf16[256,192]{1,0:T(8,128)(2,1)}, f32[25...) custom-call(s32[2]{0:T(128)} %pad_add_fusion.idx, bf16[256,768]{1,0:T(8,128)(2,1)} %get-tuple-element.81.refs_0_, ...), custom_call_target="tpu_custom_call" | custom-call | flops 300000000 | bytes 5242880 | tf_op jit(solution)/shard_map/pallas_call | solution.py:575
  177.2 3.4 collective-permute-start.14
  184.4 14.5 %collective-permute-done.14.refs_2_ = bf16[256,192]{1,0:T(8,128)(2,1)S(1)} collective-permute-done((bf16[256,192]{1,0:T(8,128)(2,1)}, bf16[256,192]{1,0:T(8,128)(2,1)S(1)}, u32[]{:S(2)}, u32[]{:S(2)}) %collective-permute-start.14) | collective-permute-done | bytes 98336 | tf_op jit(solution)/shard_map/ppermute | solution.py:588
  199.7 17.3 %shard_map.219 = (bf16[256,768]{1,0:T(8,128)(2,1)}, bf16[256,768]{1,0:T(8,128)(2,1)}, bf16[256,768]{1,0:T(8,128)(2,1)}, bf16[256,768]{1,0:T(8,128)(2,1)}, bf16[3...) custom-call(s32[2]{0:T(128)} %pad_add_fusion.idx, bf16[256,192]{1,0:T(8,128)(2,1)} %get-tuple-element.97.refs_0_, ...), custom_call_target="tpu_custom_call" | custom-call | flops 14000000000 | bytes 8388608 | tf_op jit(solution)/shard_map/pallas_call | solution.py:575
  216.9 3.4 collective-permute-start.17
  220.4 3.2 shard_map.221
  223.5 4.1 %shard_map.220 = bf16[3,192,768]{2,1,0:T(8,128)(2,1)} custom-call(bf16[1024,768]{1,0:T(8,128)(2,1)} %get-tuple-element.117.refs_0_, bf16[3,1024,192]{2,1,0:T(8,128)(2,1)} %get-tuple-element.118.refs_1_), custom_call_target="tpu_custom_call" | custom-call | flops 1000000000 | bytes 4194304 | tf_op jit(solution)/shard_map/pallas_call | solution.py:575
  230.5 5.3 %collective-permute-done.16.refs_1_ = bf16[256,768]{1,0:T(8,128)(2,1)} collective-permute-done((bf16[256,768]{1,0:T(8,128)(2,1)}, bf16[256,768]{1,0:T(8,128)(2,1)}, u32[]{:S(2)}, u32[]{:S(2)}) %collective-permute-start.16) | collective-permute-done | bytes 393248 | tf_op jit(solution)/shard_map/ppermute | solution.py:588
  241.4 16.7 %collective-permute-done.18.refs_2_ = bf16[256,768]{1,0:T(8,128)(2,1)} collective-permute-done((bf16[256,768]{1,0:T(8,128)(2,1)}, bf16[256,768]{1,0:T(8,128)(2,1)}, u32[]{:S(2)}, u32[]{:S(2)}) %collective-permute-start.18) | collective-permute-done | bytes 393248 | tf_op jit(solution)/shard_map/ppermute | solution.py:588
  258.0 3.2 shard_map.222.refs_0_
  262.8 22.5 %collective-permute-done.26 = bf16[8,48,768]{2,1,0:T(8,128)(2,1)S(1)} collective-permute-done((bf16[8,48,768]{2,1,0:T(8,128)(2,1)S(1)}, bf16[8,48,768]{2,1,0:T(8,128)(2,1)S(1)}, u32[]{:S(2)}, u32[]{:S(2)}) %collective-permute-start.26) | collective-permute-done | bytes 589856 | tf_op jit(solution)/shard_map/ppermute | solution.py:588
  287.0 13.1 %collective-permute-done.27 = bf16[8,24,768]{2,1,0:T(8,128)(2,1)S(1)} collective-permute-done((bf16[8,24,768]{2,1,0:T(8,128)(2,1)S(1)}, bf16[8,24,768]{2,1,0:T(8,128)(2,1)S(1)}, u32[]{:S(2)}, u32[]{:S(2)}) %collective-permute-start.27) | collective-permute-done | bytes 294944 | tf_op jit(solution)/shard_map/ppermute | solution.py:588
  309.5 15.5 %collective-permute-done.24.refs_1_ = bf16[256,768]{1,0:T(8,128)(2,1)S(1)} collective-permute-done((bf16[256,768]{1,0:T(8,128)(2,1)S(1)}, bf16[256,768]{1,0:T(8,128)(2,1)S(1)}, u32[]{:S(2)}, u32[]{:S(2)}) %collective-permute-start.24) | collective-permute-done | bytes 393248 | tf_op jit(solution)/shard_map/ppermute | solution.py:588
  325.2 6.5 %collective-permute-done.25.refs_3_ = bf16[256,768]{1,0:T(8,128)(2,1)S(1)} collective-permute-done((bf16[256,768]{1,0:T(8,128)(2,1)S(1)}, bf16[256,768]{1,0:T(8,128)(2,1)S(1)}, u32[]{:S(2)}, u32[]{:S(2)}) %collective-permute-start.25) | collective-permute-done | bytes 393248 | tf_op jit(solution)/shard_map/ppermute | solution.py:588
  332.8 4.4 %collective-permute-done.31 = bf16[5,24,768]{2,1,0:T(8,128)(2,1)S(1)} collective-permute-done((bf16[5,24,768]{2,1,0:T(8,128)(2,1)S(1)}, bf16[5,24,768]{2,1,0:T(8,128)(2,1)S(1)}, u32[]{:S(2)}, u32[]{:S(2)}) %collective-permute-start.31) | collective-permute-done | bytes 184352 | tf_op jit(solution)/shard_map/ppermute | solution.py:588
  338.8 6.2 %collective-permute-done.32 = bf16[5,48,768]{2,1,0:T(8,128)(2,1)S(1)} collective-permute-done((bf16[5,48,768]{2,1,0:T(8,128)(2,1)S(1)}, bf16[5,48,768]{2,1,0:T(8,128)(2,1)S(1)}, u32[]{:S(2)}, u32[]{:S(2)}) %collective-permute-start.32) | collective-permute-done | bytes 368672 | tf_op jit(solution)/shard_map/ppermute | solution.py:588
  347.5 3.2 shard_map.224
  350.7 6.7 %collective-permute-done.21.refs_1_ = bf16[256,768]{1,0:T(8,128)(2,1)S(1)} collective-permute-done((bf16[256,768]{1,0:T(8,128)(2,1)S(1)}, bf16[256,768]{1,0:T(8,128)(2,1)S(1)}, u32[]{:S(2)}, u32[]{:S(2)}) %collective-permute-start.21) | collective-permute-done | bytes 393248 | tf_op jit(solution)/shard_map/ppermute | solution.py:588
  357.4 8.0 %collective-permute-done.23.refs_3_ = bf16[256,768]{1,0:T(8,128)(2,1)S(1)} collective-permute-done((bf16[256,768]{1,0:T(8,128)(2,1)}, bf16[256,768]{1,0:T(8,128)(2,1)S(1)}, u32[]{:S(2)}, u32[]{:S(2)}) %collective-permute-start.23) | collective-permute-done | bytes 393248 | tf_op jit(solution)/shard_map/ppermute | solution.py:588
  373.0 12.3 %fusion = (f32[4,768,768]{2,1,0:T(8,128)}, f32[4,768,768]{2,1,0:T(8,128)}) fusion(bf16[4,2,768,768]{3,2,1,0:T(8,128)(2,1)} %bitcast.36), kind=kLoop, calls=%fused_computation.1 | loop fusion | flops 4718592 | bytes 28311552 | tf_op jit(solution)/shard_map/convert_element_type | solution.py:911
  (143 shorter events, 53.1 us)
Async XLA Ops:
  7.2 229.5 %reduce-scatter.2.cloned.1.call-start = ((), (), s32[]{:S(2)}) async-start(), calls=%async_computation.1 | async-start | bytes 10616832 | tf_op jit(solution)/shard_map/reduce_scatter | solution.py:790
  19.4 41.0 %collective-permute-start.1 = (bf16[1024,192]{1,0:T(8,128)(2,1)}, bf16[1024,192]{1,0:T(8,128)(2,1)S(1)}, u32[]{:S(2)}, u32[]{:S(2)}) collective-permute-start(bf16[1024,192]{1,0:T(8,128)(2,1)} %get-tuple-element.71.refs_0_), channel_id=1, source_target_pairs={{0,2},{1,3},{2,0},{3,1},{4,6},{5,7},{6,4},{7,5},{8,10},{9,11},{10,... | collective-permute-start | bytes 1179656 | tf_op jit(solution)/shard_map/ppermute | solution.py:588
  23.5 15.7 %collective-permute-start.3 = (bf16[96,768]{1,0:T(8,128)(2,1)S(1)}, bf16[96,768]{1,0:T(8,128)(2,1)S(1)}, u32[]{:S(2)}, u32[]{:S(2)}) collective-permute-start(bf16[96,768]{1,0:T(8,128)(2,1)S(1)} %constant_dynamic-slice_fusion.3), channel_id=1, source_target_pairs={{0,1},{1,0},{2,3},{3,2},{4,5},{5,4},{6,7},{7,6},{8,9},{9,8},{10,11... | collective-permute-start | bytes 442376 | tf_op jit(solution)/shard_map/ppermute | solution.py:588
  25.1 32.0 %collective-permute-start.4 = (bf16[96,768]{1,0:T(8,128)(2,1)S(1)}, bf16[96,768]{1,0:T(8,128)(2,1)S(1)}, u32[]{:S(2)}, u32[]{:S(2)}) collective-permute-start(bf16[96,768]{1,0:T(8,128)(2,1)S(1)} %constant_dynamic-slice_fusion.3), channel_id=1, source_target_pairs={{0,2},{1,3},{2,0},{3,1},{4,6},{5,7},{6,4},{7,5},{8,10},{9,11},{10,... | collective-permute-start | bytes 442376 | tf_op jit(solution)/shard_map/ppermute | solution.py:588
  25.5 31.7 %collective-permute-start.5 = (bf16[96,768]{1,0:T(8,128)(2,1)S(1)}, bf16[96,768]{1,0:T(8,128)(2,1)S(1)}, u32[]{:S(2)}, u32[]{:S(2)}) collective-permute-start(bf16[96,768]{1,0:T(8,128)(2,1)S(1)} %constant_dynamic-slice_fusion.3), channel_id=1, source_target_pairs={{0,3},{1,2},{2,1},{3,0},{4,7},{5,6},{6,5},{7,4},{8,11},{9,10},{10,... | collective-permute-start | bytes 442376 | tf_op jit(solution)/shard_map/ppermute | solution.py:588
  57.2 16.2 %collective-permute-start.6 = (bf16[3,96,768]{2,1,0:T(8,128)(2,1)S(1)}, bf16[3,96,768]{2,1,0:T(8,128)(2,1)S(1)}, u32[]{:S(2)}, u32[]{:S(2)}) collective-permute-start(bf16[3,96,768]{2,1,0:T(8,128)(2,1)S(1)} %pad_maximum_fusion.2), channel_id=1, source_target_pairs={{0,4},{4,0},{8,12},{12,8},{16,20},{20,16},{24,28},{28,24},{1,5},{5... | collective-permute-start | bytes 1327112 | tf_op jit(solution)/shard_map/ppermute | solution.py:588
  57.3 16.1 %collective-permute-start = (bf16[1024,192]{1,0:T(8,128)(2,1)}, bf16[1024,192]{1,0:T(8,128)(2,1)S(1)}, u32[]{:S(2)}, u32[]{:S(2)}) collective-permute-start(bf16[1024,192]{1,0:T(8,128)(2,1)} %get-tuple-element.71.refs_0_), channel_id=1, source_target_pairs={{0,1},{1,0},{2,3},{3,2},{4,5},{5,4},{6,7},{7,6},{8,9},{9,8},{10,11... | collective-permute-start | bytes 1179656 | tf_op jit(solution)/shard_map/ppermute | solution.py:588
  60.4 24.0 %collective-permute-start.2 = (bf16[1024,192]{1,0:T(8,128)(2,1)S(1)}, bf16[1024,192]{1,0:T(8,128)(2,1)S(1)}, u32[]{:S(2)}, u32[]{:S(2)}) collective-permute-start(bf16[1024,192]{1,0:T(8,128)(2,1)S(1)} %collective-permute-done.1.refs_2_), channel_id=1, source_target_pairs={{0,1},{1,0},{2,3},{3,2},{4,5},{5,4},{6,7},{7,6},{8,9},{9,8},{10,11... | collective-permute-start | bytes 1179656 | tf_op jit(solution)/shard_map/ppermute | solution.py:588
  110.9 21.4 %collective-permute-start.7 = (bf16[256,768]{1,0:T(8,128)(2,1)}, bf16[256,768]{1,0:T(8,128)(2,1)S(1)}, u32[]{:S(2)}, u32[]{:S(2)}) collective-permute-start(bf16[256,768]{1,0:T(8,128)(2,1)} %get-tuple-element.74), channel_id=1, source_target_pairs={{0,1},{1,0},{2,3},{3,2},{4,5},{5,4},{6,7},{7,6},{8,9},{9,8},{10,11... | collective-permute-start | bytes 1179656 | tf_op jit(solution)/shard_map/ppermute | solution.py:588
  112.7 19.6 %collective-permute-start.8 = (bf16[256,768]{1,0:T(8,128)(2,1)}, bf16[256,768]{1,0:T(8,128)(2,1)S(1)}, u32[]{:S(2)}, u32[]{:S(2)}) collective-permute-start(bf16[256,768]{1,0:T(8,128)(2,1)} %get-tuple-element.76), channel_id=1, source_target_pairs={{0,1},{1,0},{2,3},{3,2},{4,5},{5,4},{6,7},{7,6},{8,9},{9,8},{10,11... | collective-permute-start | bytes 1179656 | tf_op jit(solution)/shard_map/ppermute | solution.py:588
  132.4 17.9 %collective-permute-start.10 = (bf16[256,768]{1,0:T(8,128)(2,1)}, bf16[256,768]{1,0:T(8,128)(2,1)S(1)}, u32[]{:S(2)}, u32[]{:S(2)}) collective-permute-start(bf16[256,768]{1,0:T(8,128)(2,1)} %get-tuple-element.87), channel_id=1, source_target_pairs={{0,1},{1,0},{2,3},{3,2},{4,5},{5,4},{6,7},{7,6},{8,9},{9,8},{10,11... | collective-permute-start | bytes 1179656 | tf_op jit(solution)/shard_map/ppermute | solution.py:588
  134.2 17.3 %collective-permute-start.9 = (bf16[256,768]{1,0:T(8,128)(2,1)}, bf16[256,768]{1,0:T(8,128)(2,1)S(1)}, u32[]{:S(2)}, u32[]{:S(2)}) collective-permute-start(bf16[256,768]{1,0:T(8,128)(2,1)} %get-tuple-element.83), channel_id=1, source_target_pairs={{0,1},{1,0},{2,3},{3,2},{4,5},{5,4},{6,7},{7,6},{8,9},{9,8},{10,11... | collective-permute-start | bytes 1179656 | tf_op jit(solution)/shard_map/ppermute | solution.py:588
  152.2 220.9 %all-gather.2.cloned.1.call-start = ((), (), s32[]{:S(2)}) async-start(), calls=%async_computation.2 | async-start | bytes 10616832 | tf_op jit(solution)/shard_map/all_gather | solution.py:908
  152.7 19.3 %collective-permute-start.11 = (bf16[256,768]{1,0:T(8,128)(2,1)S(1)}, bf16[256,768]{1,0:T(8,128)(2,1)S(1)}, u32[]{:S(2)}, u32[]{:S(2)}) collective-permute-start(bf16[256,768]{1,0:T(8,128)(2,1)S(1)} %add_convert_fusion.4), channel_id=1, source_target_pairs={{0,2},{1,3},{2,0},{3,1},{4,6},{5,7},{6,4},{7,5},{8,10},{9,11},{10,... | collective-permute-start | bytes 1179656 | tf_op jit(solution)/shard_map/ppermute | solution.py:588
  177.2 21.8 %collective-permute-start.14 = (bf16[256,192]{1,0:T(8,128)(2,1)}, bf16[256,192]{1,0:T(8,128)(2,1)S(1)}, u32[]{:S(2)}, u32[]{:S(2)}) collective-permute-start(bf16[256,192]{1,0:T(8,128)(2,1)} %get-tuple-element.99), channel_id=1, source_target_pairs={{0,2},{1,3},{2,0},{3,1},{4,6},{5,7},{6,4},{7,5},{8,10},{9,11},{10,... | collective-permute-start | bytes 294920 | tf_op jit(solution)/shard_map/ppermute | solution.py:588
  180.6 18.4 %collective-permute-start.15 = (bf16[256,192]{1,0:T(8,128)(2,1)}, bf16[256,192]{1,0:T(8,128)(2,1)S(1)}, u32[]{:S(2)}, u32[]{:S(2)}) collective-permute-start(bf16[256,192]{1,0:T(8,128)(2,1)} %get-tuple-element.100), channel_id=1, source_target_pairs={{0,3},{1,2},{2,1},{3,0},{4,7},{5,6},{6,5},{7,4},{8,11},{9,10},{10,... | collective-permute-start | bytes 294920 | tf_op jit(solution)/shard_map/ppermute | solution.py:588
  181.6 35.3 %collective-permute-start.12 = (bf16[256,768]{1,0:T(8,128)(2,1)S(1)}, bf16[256,768]{1,0:T(8,128)(2,1)S(1)}, u32[]{:S(2)}, u32[]{:S(2)}) collective-permute-start(bf16[256,768]{1,0:T(8,128)(2,1)S(1)} %add_convert_fusion.3), channel_id=1, source_target_pairs={{0,2},{1,3},{2,0},{3,1},{4,6},{5,7},{6,4},{7,5},{8,10},{9,11},{10,... | collective-permute-start | bytes 1179656 | tf_op jit(solution)/shard_map/ppermute | solution.py:588
  216.9 13.6 %collective-permute-start.17 = (bf16[256,768]{1,0:T(8,128)(2,1)}, bf16[256,768]{1,0:T(8,128)(2,1)S(1)}, u32[]{:S(2)}, u32[]{:S(2)}) collective-permute-start(bf16[256,768]{1,0:T(8,128)(2,1)} %get-tuple-element.116), channel_id=1, source_target_pairs={{0,1},{1,0},{2,3},{3,2},{4,5},{5,4},{6,7},{7,6},{8,9},{9,8},{10,11... | collective-permute-start | bytes 1179656 | tf_op jit(solution)/shard_map/ppermute | solution.py:588
  220.3 15.5 %collective-permute-start.16 = (bf16[256,768]{1,0:T(8,128)(2,1)}, bf16[256,768]{1,0:T(8,128)(2,1)}, u32[]{:S(2)}, u32[]{:S(2)}) collective-permute-start(bf16[256,768]{1,0:T(8,128)(2,1)} %get-tuple-element.112), channel_id=1, source_target_pairs={{0,1},{1,0},{2,3},{3,2},{4,5},{5,4},{6,7},{7,6},{8,9},{9,8},{10,11... | collective-permute-start | bytes 1179656 | tf_op jit(solution)/shard_map/ppermute | solution.py:588
  236.8 21.2 %collective-permute-start.18 = (bf16[256,768]{1,0:T(8,128)(2,1)}, bf16[256,768]{1,0:T(8,128)(2,1)}, u32[]{:S(2)}, u32[]{:S(2)}) collective-permute-start(bf16[256,768]{1,0:T(8,128)(2,1)} %add_convert_fusion.2), channel_id=1, source_target_pairs={{0,2},{1,3},{2,0},{3,1},{4,6},{5,7},{6,4},{7,5},{8,10},{9,11},{10,... | collective-permute-start | bytes 1179656 | tf_op jit(solution)/shard_map/ppermute | solution.py:588
  261.3 24.1 %collective-permute-start.26 = (bf16[8,48,768]{2,1,0:T(8,128)(2,1)S(1)}, bf16[8,48,768]{2,1,0:T(8,128)(2,1)S(1)}, u32[]{:S(2)}, u32[]{:S(2)}) collective-permute-start(bf16[8,48,768]{2,1,0:T(8,128)(2,1)S(1)} %constant_dynamic-slice_fusion.1), channel_id=1, source_target_pairs={{0,8},{4,12},{8,0},{12,4},{16,24},{20,28},{24,16},{28,20},{1,9},{5... | collective-permute-start | bytes 1769480 | tf_op jit(solution)/shard_map/ppermute | solution.py:588
  262.8 22.7 %collective-permute-start.20 = (bf16[256,768]{1,0:T(8,128)(2,1)}, bf16[256,768]{1,0:T(8,128)(2,1)S(1)}, u32[]{:S(2)}, u32[]{:S(2)}) collective-permute-start(bf16[256,768]{1,0:T(8,128)(2,1)} %shard_map.222.refs_0_), channel_id=1, source_target_pairs={{0,2},{1,3},{2,0},{3,1},{4,6},{5,7},{6,4},{7,5},{8,10},{9,11},{10,... | collective-permute-start | bytes 1179656 | tf_op jit(solution)/shard_map/ppermute | solution.py:588
  285.6 14.5 %collective-permute-start.27 = (bf16[8,24,768]{2,1,0:T(8,128)(2,1)S(1)}, bf16[8,24,768]{2,1,0:T(8,128)(2,1)S(1)}, u32[]{:S(2)}, u32[]{:S(2)}) collective-permute-start(bf16[8,24,768]{2,1,0:T(8,128)(2,1)S(1)} %constant_dynamic-slice_fusion), channel_id=1, source_target_pairs={{0,16},{4,20},{8,24},{12,28},{16,0},{20,4},{24,8},{28,12},{1,17},{... | collective-permute-start | bytes 884744 | tf_op jit(solution)/shard_map/ppermute | solution.py:588
  300.2 8.9 %collective-permute-start.28 = (bf16[2,24,768]{2,1,0:T(8,128)(2,1)S(1)}, bf16[2,24,768]{2,1,0:T(8,128)(2,1)S(1)}, u32[]{:S(2)}, u32[]{:S(2)}) collective-permute-start(bf16[2,24,768]{2,1,0:T(8,128)(2,1)S(1)} %get-tuple-element.150), channel_id=1, source_target_pairs={{0,1},{1,0},{2,3},{3,2},{4,5},{5,4},{6,7},{7,6},{8,9},{9,8},{10,11... | collective-permute-start | bytes 221192 | tf_op jit(solution)/shard_map/ppermute | solution.py:588
  300.3 8.9 %collective-permute-start.29 = (bf16[2,24,768]{2,1,0:T(8,128)(2,1)S(1)}, bf16[2,24,768]{2,1,0:T(8,128)(2,1)S(1)}, u32[]{:S(2)}, u32[]{:S(2)}) collective-permute-start(bf16[2,24,768]{2,1,0:T(8,128)(2,1)S(1)} %get-tuple-element.152), channel_id=1, source_target_pairs={{0,2},{1,3},{2,0},{3,1},{4,6},{5,7},{6,4},{7,5},{8,10},{9,11},{10,... | collective-permute-start | bytes 221192 | tf_op jit(solution)/shard_map/ppermute | solution.py:588
  307.1 17.9 %collective-permute-start.24 = (bf16[256,768]{1,0:T(8,128)(2,1)S(1)}, bf16[256,768]{1,0:T(8,128)(2,1)S(1)}, u32[]{:S(2)}, u32[]{:S(2)}) collective-permute-start(bf16[256,768]{1,0:T(8,128)(2,1)S(1)} %copy-done.2), channel_id=1, source_target_pairs={{0,1},{1,0},{2,3},{3,2},{4,5},{5,4},{6,7},{7,6},{8,9},{9,8},{10,11... | collective-permute-start | bytes 1179656 | tf_op jit(solution)/shard_map/ppermute | solution.py:588
  307.1 18.1 %collective-permute-start.22 = (bf16[256,768]{1,0:T(8,128)(2,1)}, bf16[256,768]{1,0:T(8,128)(2,1)S(1)}, u32[]{:S(2)}, u32[]{:S(2)}) collective-permute-start(bf16[256,768]{1,0:T(8,128)(2,1)} %shard_map.218.refs_0_), channel_id=1, source_target_pairs={{0,2},{1,3},{2,0},{3,1},{4,6},{5,7},{6,4},{7,5},{8,10},{9,11},{10,... | collective-permute-start | bytes 1179656 | tf_op jit(solution)/shard_map/ppermute | solution.py:588
  309.2 22.5 %collective-permute-start.25 = (bf16[256,768]{1,0:T(8,128)(2,1)S(1)}, bf16[256,768]{1,0:T(8,128)(2,1)S(1)}, u32[]{:S(2)}, u32[]{:S(2)}) collective-permute-start(bf16[256,768]{1,0:T(8,128)(2,1)S(1)} %collective-permute-done.20.refs_2_), channel_id=1, source_target_pairs={{0,1},{1,0},{2,3},{3,2},{4,5},{5,4},{6,7},{7,6},{8,9},{9,8},{10,11... | collective-permute-start | bytes 1179656 | tf_op jit(solution)/shard_map/ppermute | solution.py:588
  337.3 7.8 %collective-permute-start.32 = (bf16[5,48,768]{2,1,0:T(8,128)(2,1)S(1)}, bf16[5,48,768]{2,1,0:T(8,128)(2,1)S(1)}, u32[]{:S(2)}, u32[]{:S(2)}) collective-permute-start(bf16[5,48,768]{2,1,0:T(8,128)(2,1)S(1)} %pad_maximum_fusion.3), channel_id=1, source_target_pairs={{0,8},{4,12},{8,0},{12,4},{16,24},{20,28},{24,16},{28,20},{1,9},{5... | collective-permute-start | bytes 1105928 | tf_op jit(solution)/shard_map/ppermute | solution.py:588
  345.3 23.4 %collective-permute-start.33 = (bf16[5,96,768]{2,1,0:T(8,128)(2,1)S(1)}, bf16[5,96,768]{2,1,0:T(8,128)(2,1)S(1)}, u32[]{:S(2)}, u32[]{:S(2)}) collective-permute-start(bf16[5,96,768]{2,1,0:T(8,128)(2,1)S(1)} %pad_maximum_fusion.1), channel_id=1, source_target_pairs={{0,4},{4,0},{8,12},{12,8},{16,20},{20,16},{24,28},{28,24},{1,5},{5... | collective-permute-start | bytes 2211848 | tf_op jit(solution)/shard_map/ppermute | solution.py:588
  345.4 12.0 %collective-permute-start.21 = (bf16[256,768]{1,0:T(8,128)(2,1)S(1)}, bf16[256,768]{1,0:T(8,128)(2,1)S(1)}, u32[]{:S(2)}, u32[]{:S(2)}) collective-permute-start(bf16[256,768]{1,0:T(8,128)(2,1)S(1)} %copy-done.1), channel_id=1, source_target_pairs={{0,1},{1,0},{2,3},{3,2},{4,5},{5,4},{6,7},{7,6},{8,9},{9,8},{10,11... | collective-permute-start | bytes 1179656 | tf_op jit(solution)/shard_map/ppermute | solution.py:588
  346.0 19.4 %collective-permute-start.23 = (bf16[256,768]{1,0:T(8,128)(2,1)}, bf16[256,768]{1,0:T(8,128)(2,1)S(1)}, u32[]{:S(2)}, u32[]{:S(2)}) collective-permute-start(bf16[256,768]{1,0:T(8,128)(2,1)} %copy-done.16), channel_id=1, source_target_pairs={{0,1},{1,0},{2,3},{3,2},{4,5},{5,4},{6,7},{7,6},{8,9},{9,8},{10,11... | collective-permute-start | bytes 1179656 | tf_op jit(solution)/shard_map/ppermute | solution.py:588
  (33 other events, 394.7 us)
Sparse Core Ops, SparseCore 0:
  151.6 77.5 reduce-scatter.1
  236.8 66.3 all-gather.1

commit v4 on v3

--- a/solution.py
+++ b/solution.py
@@ -602,7 +602,7 @@
         return [value] + [swap(value, axis, bit) for bit in range(1, count)]
     two = swap(value, axis, 2)
     one = swap(value, axis, 1)
-    return [value, one, two, swap(two, axis, 1)]
+    return [value, one, two, swap(after(two, one), axis, 1)]
 
 
 def reduce_near(parts, axis):
@@ -639,6 +639,10 @@
             [jnp.where(low, value, got), jnp.where(low, got, value)], axis=axis
         )
     return value
+
+
+def together(*values):
+    return lax.optimization_barrier(values)
 
 
 def after(value, *others):
@@ -691,8 +695,9 @@
         [tokens, gain_attn, w_qkv_t, segments, rel_bias.T, build_hot],
         flops=6 * 10**9, moved=8 * mib, with_index=False,
     )
+    att = after(att, *halves)
     atts = gather_parts(att, "tensor")
-    swapped = swap(jnp.stack(halves), "dp", 1)
+    swapped = swap(after(jnp.stack(halves), att), "dp", 1)
 
     full = lambda shape: pl.BlockSpec(shape, lambda e: (0,) * len(shape))
     per_expert = lambda shape: pl.BlockSpec((1,) + shape, lambda e: (e, 0, 0))
@@ -805,7 +810,7 @@
     grad_hidden, gh_low, ggain_two = back[shares:]
 
     if four:
-        moe_near = after(moe_near[0], gh_low), moe_near[1]
+        moe_near = after(moe_near[0], *go[1:]), moe_near[1]
         moe_got, _ = reduce_far(moe_parts, moe_near, "tensor")
     else:
         moe_got = [moe_parts[0], *moe_near]
@@ -878,24 +883,46 @@
         [idx, *gn_got, grad_hidden, tokens, gain_attn],
         moved=5 * mib,
     )[0]
-    gt_got = gather_parts(gt_share, "tensor")
+    bits = bits_of("dp")
+    if four:
+        keep, send = halves_of(late, 1, (place // bits[1]) % 2)
+        got = together(
+            swap(gt_share, "tensor", 2), swap(gt_share, "tensor", 1),
+            swap(after(send, gt_share), "dp", bits[1]),
+        )
+        gt_got = [gt_share, got[1], got[0]]
+        late = (keep.astype(F32) + got[2].astype(F32)).astype(BF16)
+        share_now = after(result_share, got[0])
+        keep, send = halves_of(late, 1, (place // bits[2]) % 2)
+        got = together(
+            swap(gt_got[2], "tensor", 1), swap(share_now, "tensor", 2),
+            swap(share_now, "tensor", 1), swap(send, "dp", bits[2]),
+        )
+        gt_got.append(got[0])
+        result_got = [result_share, got[2], got[1]]
+        late = (keep.astype(F32) + got[3].astype(F32)).astype(BF16)
+        for bit in bits[3:]:
+            late = halve(late, bit)
+    else:
+        gt_got = gather_parts(gt_share, "tensor")
+        result_got = gather_parts(result_share, "tensor")
+        for bit in bits[1:]:
+            late = halve(late, bit)
     grad_tokens = whole_call(
         functools.partial(place_kernel, PIECES, shares),
         [shaped((rows, width), F32)], [idx, *gt_got], moved=5 * mib,
     )[0]
 
-    result_got = gather_parts(after(result_share, gt_got[2]), "tensor")
+    sent = [swap(jnp.stack([late[4 + by], late[3]]), "tensor", by) for by in others]
+    if four:
+        *sent, last = together(*sent, swap(result_got[2], "tensor", 1))
+        result_got.append(last)
     result = whole_call(
         functools.partial(place_kernel, PIECES, shares),
         [shaped((rows, width), BF16)], [idx, *result_got], moved=3 * mib,
     )[0]
-
-    for level, bit in enumerate(bits_of("dp")[1:]):
-        late = halve(late, bit, gt_got[2] if level else gt_share)
-
     out_sum, small = late[4].astype(F32), [late[3]]
-    for by in others:
-        got = swap(jnp.stack([late[4 + by], late[3]]), "tensor", by)
+    for got in sent:
         out_sum = out_sum + got[0].astype(F32)
         small.append(got[1])
     small = [one.astype(F32) for one in small]
@@ -904,11 +931,12 @@
     late = jnp.concatenate(
         [late[:3], jnp.stack([small[0].astype(BF16), out_sum.astype(BF16)])], axis=0
     )
-    late = gather_back(after(late, *gt_got[1:], result_got[2]), "dp", 1)
+
     expert_rows = lax.all_gather(expert_rows, "dp", axis=0, tiled=True)
     expert_rows = expert_rows.reshape(experts, 2, width, width)
     grad_w_in = expert_rows[:, 0].astype(F32)
     grad_w_down = expert_rows[:, 1].astype(F32)
+    late = gather_back(after(late, grad_w_in, grad_w_down, grad_tokens), "dp", 1)
     grad_w_qkv = jnp.swapaxes(late[:3], 1, 2).astype(F32)
     grad_w_out = late[4].astype(F32)
     small = late[3].astype(F32)

time: 393 us -> 335 us (0.85)
  waiting for transfers between devices: 192 us -> 132 us
    ppermute x34, waiting for transfers between devices: 192 us -> 130 us  [swap(): return lax.ppermute(value, axis, [(i, i ^ bit) for i in range(count)])]
  transfers between devices with their start and end apart: 36 -> 36, of which waited for: 22 -> 21; matrix products, arithmetic and copies ran while one was open for 3% -> 2% of each run, Pallas kernels for 19% -> 26%
where the time goes in v4:
time: 335 us; the launch traced here: 334 us
  waiting for transfers between devices  132 us (39%)
  Pallas kernels  114 us (34%)
  starting transfers between devices  47.4 us (14%)
  other arithmetic  20.2 us (6%)
  between operations  14.5 us (4%)
  local copies, waits for them, and re-layouts  6.63 us (2%)
    ppermute x34, waiting for transfers between devices, swap(): return lax.ppermute(value, axis, [(i, i ^ bit) for i in range(count)])  130 us
    pallas_call x9, Pallas kernels, whole_call(): pl.pallas_call(kernel, out_shape=outs, in_specs=specs, out_specs=[VMEM] *...  52.7 us
    ppermute x34, starting transfers between devices, swap(): return lax.ppermute(value, axis, [(i, i ^ bit) for i in range(count)])  47.3 us
    pallas_call x1, Pallas kernels, body(): pl.pallas_call(functools.partial(moe_fwd_kernel, 0, PIECES, shares, exper...  25.7 us
    pallas_call x1, Pallas kernels, body(): pl.pallas_call(functools.partial(moe_bwd_kernel, 0, shares, experts), gri...  19.3 us
    pallas_call x1, Pallas kernels, body(): pl.pallas_call(functools.partial(moe_weights_kernel, PIECES), grid=(exper...  15.8 us
    convert_element_type x1, other arithmetic, body(): grad_w_down = expert_rows[:, 1].astype(F32)  12.4 us
  transfers between devices with their start and end apart: 36, of which 21 were waited for; matrix products, arithmetic and copies ran while one was open for 2% of the time, Pallas kernels for 26%

profile of v4, /device:TPU:0, one launch (start us, length us, event | category | flops | bytes accessed | tf_op | source)
XLA Modules:
  0.0 334.4 jit_solution(4987641922164318785)
XLA Ops:
  8.2 3.1 collective-permute-start
  11.3 2.6 collective-permute-start.1
  13.9 12.2 %shard_map.213 = (bf16[1024,768]{1,0:T(8,128)(2,1)}, bf16[3,1024,192]{2,1,0:T(8,128)(2,1)}, bf16[1024,192]{1,0:T(8,128)(2,1)}, bf16[1024,192]{1,0:T(8,128)(2,1)}...) custom-call(bf16[1024,768]{1,0:T(8,128)(2,1)} %refs_4_.5, ...), custom_call_target="tpu_custom_call" | custom-call | flops 6000000000 | bytes 8388608 | tf_op jit(solution)/shard_map/pallas_call | solution.py:575
  27.6 3.0 collective-permute-start.4
  30.7 19.8 %collective-permute-done.3.refs_1_ = bf16[1024,192]{1,0:T(8,128)(2,1)S(1)} collective-permute-done((bf16[1024,192]{1,0:T(8,128)(2,1)}, bf16[1024,192]{1,0:T(8,128)(2,1)S(1)}, u32[]{:S(2)}, u32[]{:S(2)}) %collective-permute-start.3) | collective-permute-done | bytes 393248 | tf_op jit(solution)/shard_map/ppermute | solution.py:588
  50.4 2.5 collective-permute-done.4.refs_2_
  55.0 8.8 %collective-permute-done.5.refs_3_ = bf16[1024,192]{1,0:T(8,128)(2,1)S(1)} collective-permute-done((bf16[1024,192]{1,0:T(8,128)(2,1)S(1)}, bf16[1024,192]{1,0:T(8,128)(2,1)S(1)}, u32[]{:S(2)}, u32[]{:S(2)}) %collective-permute-start.5) | collective-permute-done | bytes 393248 | tf_op jit(solution)/shard_map/ppermute | solution.py:588
  64.5 25.7 %shard_map.214 = (bf16[256,768]{1,0:T(8,128)(2,1)}, bf16[256,768]{1,0:T(8,128)(2,1)}, bf16[256,768]{1,0:T(8,128)(2,1)}, bf16[256,768]{1,0:T(8,128)(2,1)}, bf16[4...) custom-call(s32[2]{0:T(128)} %pad_add_fusion.idx, ...), custom_call_target="tpu_custom_call" | custom-call | flops 9663676416 | bytes 33554432 | tf_op jit(solution)/shard_map/pallas_call | solution.py:709
  92.3 19.3 %shard_map.215 = (bf16[256,768]{1,0:T(8,128)(2,1)}, bf16[256,768]{1,0:T(8,128)(2,1)}, bf16[256,768]{1,0:T(8,128)(2,1)}, bf16[256,768]{1,0:T(8,128)(2,1)}, f32[10...) custom-call(s32[2]{0:T(128)} %pad_add_fusion.idx, f32[1024,128]{1,0:T(8,128)} %get-tuple-element.93.refs_0_, ...), custom_call_target="tpu_custom_call" | custom-call | flops 9663676416 | bytes 27262976 | tf_op jit(solution)/shard_map/pallas_call | solution.py:753
  113.8 15.8 %shard_map.216 = (bf16[4,2,768,768]{3,2,1,0:T(8,128)(2,1)}, f32[8,768]{1,0:T(8,128)}) custom-call(bf16[1024,768]{1,0:T(8,128)(2,1)} %refs_5_.5, f32[1024,128]{1,0:T(8,128)} %get-tuple-element.93.refs_0_, f32[1024,128]{1,0:T(8,128)} %get-tuple-element.104.refs_1_, bf16[1024,768]{1,0:T(8,128)(2,1)} %get-tuple-element.105.refs_2_, ...), custom_call_target="tpu_custom_call" | custom-call | flops 9663676416 | bytes 27262976 | tf_op jit(solution)/shard_map/pallas_call | solution.py:778
  132.5 14.8 %collective-permute-done.11.refs_2_ = bf16[256,768]{1,0:T(8,128)(2,1)S(1)} collective-permute-done((bf16[256,768]{1,0:T(8,128)(2,1)S(1)}, bf16[256,768]{1,0:T(8,128)(2,1)S(1)}, u32[]{:S(2)}, u32[]{:S(2)}) %collective-permute-start.11) | collective-permute-done | bytes 393248 | tf_op jit(solution)/shard_map/ppermute | solution.py:588
  148.1 4.4 %shard_map.217 = (bf16[256,192]{1,0:T(8,128)(2,1)}, bf16[256,192]{1,0:T(8,128)(2,1)}, bf16[256,192]{1,0:T(8,128)(2,1)}, bf16[256,192]{1,0:T(8,128)(2,1)}, f32[25...) custom-call(s32[2]{0:T(128)} %pad_add_fusion.idx, bf16[256,768]{1,0:T(8,128)(2,1)} %get-tuple-element.97.refs_0_, ...), custom_call_target="tpu_custom_call" | custom-call | flops 300000000 | bytes 5242880 | tf_op jit(solution)/shard_map/pallas_call | solution.py:575
  152.4 2.7 collective-permute-start.13
  159.1 6.2 %collective-permute-done.13.refs_2_ = bf16[256,192]{1,0:T(8,128)(2,1)S(1)} collective-permute-done((bf16[256,192]{1,0:T(8,128)(2,1)}, bf16[256,192]{1,0:T(8,128)(2,1)S(1)}, u32[]{:S(2)}, u32[]{:S(2)}) %collective-permute-start.13) | collective-permute-done | bytes 98336 | tf_op jit(solution)/shard_map/ppermute | solution.py:588
  167.9 17.5 %shard_map.219 = (bf16[256,768]{1,0:T(8,128)(2,1)}, bf16[256,768]{1,0:T(8,128)(2,1)}, bf16[256,768]{1,0:T(8,128)(2,1)}, bf16[256,768]{1,0:T(8,128)(2,1)}, bf16[3...) custom-call(s32[2]{0:T(128)} %pad_add_fusion.idx, bf16[256,192]{1,0:T(8,128)(2,1)} %get-tuple-element.115.refs_0_, ...), custom_call_target="tpu_custom_call" | custom-call | flops 14000000000 | bytes 8388608 | tf_op jit(solution)/shard_map/pallas_call | solution.py:575
  187.5 3.2 shard_map.221
  190.6 4.1 %shard_map.220 = bf16[3,192,768]{2,1,0:T(8,128)(2,1)} custom-call(bf16[1024,768]{1,0:T(8,128)(2,1)} %get-tuple-element.132.refs_0_, bf16[3,1024,192]{2,1,0:T(8,128)(2,1)} %get-tuple-element.133.refs_1_), custom_call_target="tpu_custom_call" | custom-call | flops 1000000000 | bytes 4194304 | tf_op jit(solution)/shard_map/pallas_call | solution.py:575
  197.7 5.9 %collective-permute-done.16.refs_1_ = bf16[256,768]{1,0:T(8,128)(2,1)} collective-permute-done((bf16[256,768]{1,0:T(8,128)(2,1)}, bf16[256,768]{1,0:T(8,128)(2,1)}, u32[]{:S(2)}, u32[]{:S(2)}) %collective-permute-start.16) | collective-permute-done | bytes 393248 | tf_op jit(solution)/shard_map/ppermute | solution.py:588
  211.4 16.7 %collective-permute-done.18.refs_2_ = bf16[256,768]{1,0:T(8,128)(2,1)} collective-permute-done((bf16[256,768]{1,0:T(8,128)(2,1)}, bf16[256,768]{1,0:T(8,128)(2,1)}, u32[]{:S(2)}, u32[]{:S(2)}) %collective-permute-start.18) | collective-permute-done | bytes 393248 | tf_op jit(solution)/shard_map/ppermute | solution.py:588
  228.1 3.2 shard_map.222.refs_0_
  232.8 3.9 %collective-permute-start.21 = (bf16[256,768]{1,0:T(8,128)(2,1)}, bf16[256,768]{1,0:T(8,128)(2,1)S(1)}, u32[]{:S(2)}, u32[]{:S(2)}) collective-permute-start(bf16[256,768]{1,0:T(8,128)(2,1)} %shard_map.222.refs_0_), channel_id=1, source_target_pairs={{0,1},{1,0},{2,3},{3,2},{4,5},{5,4},{6,7},{7,6},{8,9},{9,8},{10,11... | collective-permute-start | bytes 1179656 | tf_op jit(solution)/shard_map/ppermute | solution.py:588
  239.1 13.8 %collective-permute-done.20.refs_2_ = bf16[256,768]{1,0:T(8,128)(2,1)S(1)} collective-permute-done((bf16[256,768]{1,0:T(8,128)(2,1)}, bf16[256,768]{1,0:T(8,128)(2,1)S(1)}, u32[]{:S(2)}, u32[]{:S(2)}) %collective-permute-start.20) | collective-permute-done | bytes 393248 | tf_op jit(solution)/shard_map/ppermute | solution.py:588
  254.4 3.5 %collective-permute-start.25 = (bf16[256,768]{1,0:T(8,128)(2,1)}, bf16[256,768]{1,0:T(8,128)(2,1)}, u32[]{:S(2)}, u32[]{:S(2)}) collective-permute-start(bf16[256,768]{1,0:T(8,128)(2,1)} %shard_map.218.refs_0_), channel_id=1, source_target_pairs={{0,1},{1,0},{2,3},{3,2},{4,5},{5,4},{6,7},{7,6},{8,9},{9,8},{10,11... | collective-permute-start | bytes 1179656 | tf_op jit(solution)/shard_map/ppermute | solution.py:588
  259.5 12.2 %collective-permute-done.26 = bf16[8,24,768]{2,1,0:T(8,128)(2,1)S(1)} collective-permute-done((bf16[8,24,768]{2,1,0:T(8,128)(2,1)S(1)}, bf16[8,24,768]{2,1,0:T(8,128)(2,1)S(1)}, u32[]{:S(2)}, u32[]{:S(2)}) %collective-permute-start.26) | collective-permute-done | bytes 294944 | tf_op jit(solution)/shard_map/ppermute | solution.py:588
  272.5 3.8 %collective-permute-done.25.refs_1_ = bf16[256,768]{1,0:T(8,128)(2,1)} collective-permute-done((bf16[256,768]{1,0:T(8,128)(2,1)}, bf16[256,768]{1,0:T(8,128)(2,1)}, u32[]{:S(2)}, u32[]{:S(2)}) %collective-permute-start.25) | collective-permute-done | bytes 393248 | tf_op jit(solution)/shard_map/ppermute | solution.py:588
  276.3 4.8 %collective-permute-done.23.refs_3_ = bf16[256,768]{1,0:T(8,128)(2,1)S(1)} collective-permute-done((bf16[256,768]{1,0:T(8,128)(2,1)S(1)}, bf16[256,768]{1,0:T(8,128)(2,1)S(1)}, u32[]{:S(2)}, u32[]{:S(2)}) %collective-permute-start.23) | collective-permute-done | bytes 393248 | tf_op jit(solution)/shard_map/ppermute | solution.py:588
  286.5 3.2 shard_map.224
  289.7 4.8 %collective-permute-done.27 = bf16[2,24,768]{2,1,0:T(8,128)(2,1)S(1)} collective-permute-done((bf16[2,24,768]{2,1,0:T(8,128)(2,1)S(1)}, bf16[2,24,768]{2,1,0:T(8,128)(2,1)S(1)}, u32[]{:S(2)}, u32[]{:S(2)}) %collective-permute-start.27) | collective-permute-done | bytes 73760 | tf_op jit(solution)/shard_map/ppermute | solution.py:588
  294.7 12.4 %fusion = (f32[4,768,768]{2,1,0:T(8,128)}, f32[4,768,768]{2,1,0:T(8,128)}) fusion(bf16[4,2,768,768]{3,2,1,0:T(8,128)(2,1)} %bitcast.36), kind=kLoop, calls=%fused_computation.1 | loop fusion | flops 4718592 | bytes 28311552 | tf_op jit(solution)/shard_map/convert_element_type | solution.py:938
  308.2 4.3 %collective-permute-done.31 = bf16[5,24,768]{2,1,0:T(8,128)(2,1)S(1)} collective-permute-done((bf16[5,24,768]{2,1,0:T(8,128)(2,1)S(1)}, bf16[5,24,768]{2,1,0:T(8,128)(2,1)S(1)}, u32[]{:S(2)}, u32[]{:S(2)}) %collective-permute-start.31) | collective-permute-done | bytes 184352 | tf_op jit(solution)/shard_map/ppermute | solution.py:588
  314.8 5.5 %collective-permute-done.32 = bf16[5,48,768]{2,1,0:T(8,128)(2,1)S(1)} collective-permute-done((bf16[5,48,768]{2,1,0:T(8,128)(2,1)S(1)}, bf16[5,48,768]{2,1,0:T(8,128)(2,1)S(1)}, u32[]{:S(2)}, u32[]{:S(2)}) %collective-permute-start.32) | collective-permute-done | bytes 368672 | tf_op jit(solution)/shard_map/ppermute | solution.py:588
  320.6 2.6 shard_map.223
  (133 shorter events, 53.7 us)
Async XLA Ops:
  7.2 199.5 %reduce-scatter.2.cloned.1.call-start = ((), (), s32[]{:S(2)}) async-start(), calls=%async_computation.1 | async-start | bytes 10616832 | tf_op jit(solution)/shard_map/reduce_scatter | solution.py:795
  8.2 17.8 %collective-permute-start = (bf16[96,768]{1,0:T(8,128)(2,1)S(1)}, bf16[96,768]{1,0:T(8,128)(2,1)S(1)}, u32[]{:S(2)}, u32[]{:S(2)}) collective-permute-start(bf16[96,768]{1,0:T(8,128)(2,1)S(1)} %constant_dynamic-slice_fusion.3), channel_id=1, source_target_pairs={{0,1},{1,0},{2,3},{3,2},{4,5},{5,4},{6,7},{7,6},{8,9},{9,8},{10,11... | collective-permute-start | bytes 442376 | tf_op jit(solution)/shard_map/ppermute | solution.py:588
  11.3 14.8 %collective-permute-start.1 = (bf16[96,768]{1,0:T(8,128)(2,1)S(1)}, bf16[96,768]{1,0:T(8,128)(2,1)S(1)}, u32[]{:S(2)}, u32[]{:S(2)}) collective-permute-start(bf16[96,768]{1,0:T(8,128)(2,1)S(1)} %constant_dynamic-slice_fusion.3), channel_id=1, source_target_pairs={{0,2},{1,3},{2,0},{3,1},{4,6},{5,7},{6,4},{7,5},{8,10},{9,11},{10,... | collective-permute-start | bytes 442376 | tf_op jit(solution)/shard_map/ppermute | solution.py:588
  13.8 12.2 %collective-permute-start.2 = (bf16[96,768]{1,0:T(8,128)(2,1)S(1)}, bf16[96,768]{1,0:T(8,128)(2,1)S(1)}, u32[]{:S(2)}, u32[]{:S(2)}) collective-permute-start(bf16[96,768]{1,0:T(8,128)(2,1)S(1)} %constant_dynamic-slice_fusion.3), channel_id=1, source_target_pairs={{0,3},{1,2},{2,1},{3,0},{4,7},{5,6},{6,5},{7,4},{8,11},{9,10},{10,... | collective-permute-start | bytes 442376 | tf_op jit(solution)/shard_map/ppermute | solution.py:588
  26.1 24.3 %collective-permute-start.3 = (bf16[1024,192]{1,0:T(8,128)(2,1)}, bf16[1024,192]{1,0:T(8,128)(2,1)S(1)}, u32[]{:S(2)}, u32[]{:S(2)}) collective-permute-start(bf16[1024,192]{1,0:T(8,128)(2,1)} %get-tuple-element.85.refs_0_), channel_id=1, source_target_pairs={{0,1},{1,0},{2,3},{3,2},{4,5},{5,4},{6,7},{7,6},{8,9},{9,8},{10,11... | collective-permute-start | bytes 1179656 | tf_op jit(solution)/shard_map/ppermute | solution.py:588
  27.6 25.4 %collective-permute-start.4 = (bf16[1024,192]{1,0:T(8,128)(2,1)}, bf16[1024,192]{1,0:T(8,128)(2,1)S(1)}, u32[]{:S(2)}, u32[]{:S(2)}) collective-permute-start(bf16[1024,192]{1,0:T(8,128)(2,1)} %get-tuple-element.85.refs_0_), channel_id=1, source_target_pairs={{0,2},{1,3},{2,0},{3,1},{4,6},{5,7},{6,4},{7,5},{8,10},{9,11},{10,... | collective-permute-start | bytes 1179656 | tf_op jit(solution)/shard_map/ppermute | solution.py:588
  30.6 24.4 %collective-permute-start.6 = (bf16[3,96,768]{2,1,0:T(8,128)(2,1)S(1)}, bf16[3,96,768]{2,1,0:T(8,128)(2,1)S(1)}, u32[]{:S(2)}, u32[]{:S(2)}) collective-permute-start(bf16[3,96,768]{2,1,0:T(8,128)(2,1)S(1)} %pad_maximum_fusion.2), channel_id=1, source_target_pairs={{0,4},{4,0},{8,12},{12,8},{16,20},{20,16},{24,28},{28,24},{1,5},{5... | collective-permute-start | bytes 1327112 | tf_op jit(solution)/shard_map/ppermute | solution.py:588
  53.0 10.8 %collective-permute-start.5 = (bf16[1024,192]{1,0:T(8,128)(2,1)S(1)}, bf16[1024,192]{1,0:T(8,128)(2,1)S(1)}, u32[]{:S(2)}, u32[]{:S(2)}) collective-permute-start(bf16[1024,192]{1,0:T(8,128)(2,1)S(1)} %collective-permute-done.4.refs_2_), channel_id=1, source_target_pairs={{0,1},{1,0},{2,3},{3,2},{4,5},{5,4},{6,7},{7,6},{8,9},{9,8},{10,11... | collective-permute-start | bytes 1179656 | tf_op jit(solution)/shard_map/ppermute | solution.py:588
  90.2 21.4 %collective-permute-start.7 = (bf16[256,768]{1,0:T(8,128)(2,1)}, bf16[256,768]{1,0:T(8,128)(2,1)S(1)}, u32[]{:S(2)}, u32[]{:S(2)}) collective-permute-start(bf16[256,768]{1,0:T(8,128)(2,1)} %get-tuple-element.90), channel_id=1, source_target_pairs={{0,1},{1,0},{2,3},{3,2},{4,5},{5,4},{6,7},{7,6},{8,9},{9,8},{10,11... | collective-permute-start | bytes 1179656 | tf_op jit(solution)/shard_map/ppermute | solution.py:588
  91.8 19.9 %collective-permute-start.8 = (bf16[256,768]{1,0:T(8,128)(2,1)}, bf16[256,768]{1,0:T(8,128)(2,1)S(1)}, u32[]{:S(2)}, u32[]{:S(2)}) collective-permute-start(bf16[256,768]{1,0:T(8,128)(2,1)} %get-tuple-element.92), channel_id=1, source_target_pairs={{0,1},{1,0},{2,3},{3,2},{4,5},{5,4},{6,7},{7,6},{8,9},{9,8},{10,11... | collective-permute-start | bytes 1179656 | tf_op jit(solution)/shard_map/ppermute | solution.py:588
  111.7 17.9 %collective-permute-start.10 = (bf16[256,768]{1,0:T(8,128)(2,1)}, bf16[256,768]{1,0:T(8,128)(2,1)S(1)}, u32[]{:S(2)}, u32[]{:S(2)}) collective-permute-start(bf16[256,768]{1,0:T(8,128)(2,1)} %get-tuple-element.103), channel_id=1, source_target_pairs={{0,1},{1,0},{2,3},{3,2},{4,5},{5,4},{6,7},{7,6},{8,9},{9,8},{10,11... | collective-permute-start | bytes 1179656 | tf_op jit(solution)/shard_map/ppermute | solution.py:588
  113.2 16.4 %collective-permute-start.9 = (bf16[256,768]{1,0:T(8,128)(2,1)}, bf16[256,768]{1,0:T(8,128)(2,1)S(1)}, u32[]{:S(2)}, u32[]{:S(2)}) collective-permute-start(bf16[256,768]{1,0:T(8,128)(2,1)} %get-tuple-element.99), channel_id=1, source_target_pairs={{0,1},{1,0},{2,3},{3,2},{4,5},{5,4},{6,7},{7,6},{8,9},{9,8},{10,11... | collective-permute-start | bytes 1179656 | tf_op jit(solution)/shard_map/ppermute | solution.py:588
  130.4 164.3 %all-gather.2.cloned.1.call-start = ((), (), s32[]{:S(2)}) async-start(), calls=%async_computation.2 | async-start | bytes 10616832 | tf_op jit(solution)/shard_map/all_gather | solution.py:935
  130.9 16.4 %collective-permute-start.11 = (bf16[256,768]{1,0:T(8,128)(2,1)S(1)}, bf16[256,768]{1,0:T(8,128)(2,1)S(1)}, u32[]{:S(2)}, u32[]{:S(2)}) collective-permute-start(bf16[256,768]{1,0:T(8,128)(2,1)S(1)} %add_convert_fusion.4), channel_id=1, source_target_pairs={{0,2},{1,3},{2,0},{3,1},{4,6},{5,7},{6,4},{7,5},{8,10},{9,11},{10,... | collective-permute-start | bytes 1179656 | tf_op jit(solution)/shard_map/ppermute | solution.py:588
  152.4 12.8 %collective-permute-start.13 = (bf16[256,192]{1,0:T(8,128)(2,1)}, bf16[256,192]{1,0:T(8,128)(2,1)S(1)}, u32[]{:S(2)}, u32[]{:S(2)}) collective-permute-start(bf16[256,192]{1,0:T(8,128)(2,1)} %get-tuple-element.112), channel_id=1, source_target_pairs={{0,2},{1,3},{2,0},{3,1},{4,6},{5,7},{6,4},{7,5},{8,10},{9,11},{10,... | collective-permute-start | bytes 294920 | tf_op jit(solution)/shard_map/ppermute | solution.py:588
  155.2 10.1 %collective-permute-start.14 = (bf16[256,192]{1,0:T(8,128)(2,1)}, bf16[256,192]{1,0:T(8,128)(2,1)S(1)}, u32[]{:S(2)}, u32[]{:S(2)}) collective-permute-start(bf16[256,192]{1,0:T(8,128)(2,1)} %get-tuple-element.113), channel_id=1, source_target_pairs={{0,3},{1,2},{2,1},{3,0},{4,7},{5,6},{6,5},{7,4},{8,11},{9,10},{10,... | collective-permute-start | bytes 294920 | tf_op jit(solution)/shard_map/ppermute | solution.py:588
  165.4 20.0 %collective-permute-start.15 = (bf16[256,768]{1,0:T(8,128)(2,1)S(1)}, bf16[256,768]{1,0:T(8,128)(2,1)S(1)}, u32[]{:S(2)}, u32[]{:S(2)}) collective-permute-start(bf16[256,768]{1,0:T(8,128)(2,1)S(1)} %add_convert_fusion.3), channel_id=1, source_target_pairs={{0,2},{1,3},{2,0},{3,1},{4,6},{5,7},{6,4},{7,5},{8,10},{9,11},{10,... | collective-permute-start | bytes 1179656 | tf_op jit(solution)/shard_map/ppermute | solution.py:588
  185.4 12.3 %collective-permute-start.17 = (bf16[256,768]{1,0:T(8,128)(2,1)}, bf16[256,768]{1,0:T(8,128)(2,1)S(1)}, u32[]{:S(2)}, u32[]{:S(2)}) collective-permute-start(bf16[256,768]{1,0:T(8,128)(2,1)} %get-tuple-element.131), channel_id=1, source_target_pairs={{0,1},{1,0},{2,3},{3,2},{4,5},{5,4},{6,7},{7,6},{8,9},{9,8},{10,11... | collective-permute-start | bytes 1179656 | tf_op jit(solution)/shard_map/ppermute | solution.py:588
  185.4 18.1 %collective-permute-start.16 = (bf16[256,768]{1,0:T(8,128)(2,1)}, bf16[256,768]{1,0:T(8,128)(2,1)}, u32[]{:S(2)}, u32[]{:S(2)}) collective-permute-start(bf16[256,768]{1,0:T(8,128)(2,1)} %get-tuple-element.127), channel_id=1, source_target_pairs={{0,1},{1,0},{2,3},{3,2},{4,5},{5,4},{6,7},{7,6},{8,9},{9,8},{10,11... | collective-permute-start | bytes 1179656 | tf_op jit(solution)/shard_map/ppermute | solution.py:588
  206.9 21.2 %collective-permute-start.18 = (bf16[256,768]{1,0:T(8,128)(2,1)}, bf16[256,768]{1,0:T(8,128)(2,1)}, u32[]{:S(2)}, u32[]{:S(2)}) collective-permute-start(bf16[256,768]{1,0:T(8,128)(2,1)} %add_convert_fusion.2), channel_id=1, source_target_pairs={{0,2},{1,3},{2,0},{3,1},{4,6},{5,7},{6,4},{7,5},{8,10},{9,11},{10,... | collective-permute-start | bytes 1179656 | tf_op jit(solution)/shard_map/ppermute | solution.py:588
  231.4 22.4 %collective-permute-start.22 = (bf16[8,48,768]{2,1,0:T(8,128)(2,1)S(1)}, bf16[8,48,768]{2,1,0:T(8,128)(2,1)S(1)}, u32[]{:S(2)}, u32[]{:S(2)}) collective-permute-start(bf16[8,48,768]{2,1,0:T(8,128)(2,1)S(1)} %constant_dynamic-slice_fusion.1), channel_id=1, source_target_pairs={{0,8},{4,12},{8,0},{12,4},{16,24},{20,28},{24,16},{28,20},{1,9},{5... | collective-permute-start | bytes 1769480 | tf_op jit(solution)/shard_map/ppermute | solution.py:588
  232.8 20.0 %collective-permute-start.20 = (bf16[256,768]{1,0:T(8,128)(2,1)}, bf16[256,768]{1,0:T(8,128)(2,1)S(1)}, u32[]{:S(2)}, u32[]{:S(2)}) collective-permute-start(bf16[256,768]{1,0:T(8,128)(2,1)} %shard_map.222.refs_0_), channel_id=1, source_target_pairs={{0,2},{1,3},{2,0},{3,1},{4,6},{5,7},{6,4},{7,5},{8,10},{9,11},{10,... | collective-permute-start | bytes 1179656 | tf_op jit(solution)/shard_map/ppermute | solution.py:588
  232.8 20.1 %collective-permute-start.21 = (bf16[256,768]{1,0:T(8,128)(2,1)}, bf16[256,768]{1,0:T(8,128)(2,1)S(1)}, u32[]{:S(2)}, u32[]{:S(2)}) collective-permute-start(bf16[256,768]{1,0:T(8,128)(2,1)} %shard_map.222.refs_0_), channel_id=1, source_target_pairs={{0,1},{1,0},{2,3},{3,2},{4,5},{5,4},{6,7},{7,6},{8,9},{9,8},{10,11... | collective-permute-start | bytes 1179656 | tf_op jit(solution)/shard_map/ppermute | solution.py:588
  253.7 18.8 %collective-permute-start.24 = (bf16[256,768]{1,0:T(8,128)(2,1)}, bf16[256,768]{1,0:T(8,128)(2,1)}, u32[]{:S(2)}, u32[]{:S(2)}) collective-permute-start(bf16[256,768]{1,0:T(8,128)(2,1)} %shard_map.218.refs_0_), channel_id=1, source_target_pairs={{0,2},{1,3},{2,0},{3,1},{4,6},{5,7},{6,4},{7,5},{8,10},{9,11},{10,... | collective-permute-start | bytes 1179656 | tf_op jit(solution)/shard_map/ppermute | solution.py:588
  254.4 21.9 %collective-permute-start.25 = (bf16[256,768]{1,0:T(8,128)(2,1)}, bf16[256,768]{1,0:T(8,128)(2,1)}, u32[]{:S(2)}, u32[]{:S(2)}) collective-permute-start(bf16[256,768]{1,0:T(8,128)(2,1)} %shard_map.218.refs_0_), channel_id=1, source_target_pairs={{0,1},{1,0},{2,3},{3,2},{4,5},{5,4},{6,7},{7,6},{8,9},{9,8},{10,11... | collective-permute-start | bytes 1179656 | tf_op jit(solution)/shard_map/ppermute | solution.py:588
  257.9 23.2 %collective-permute-start.23 = (bf16[256,768]{1,0:T(8,128)(2,1)S(1)}, bf16[256,768]{1,0:T(8,128)(2,1)S(1)}, u32[]{:S(2)}, u32[]{:S(2)}) collective-permute-start(bf16[256,768]{1,0:T(8,128)(2,1)S(1)} %collective-permute-done.20.refs_2_), channel_id=1, source_target_pairs={{0,1},{1,0},{2,3},{3,2},{4,5},{5,4},{6,7},{7,6},{8,9},{9,8},{10,11... | collective-permute-start | bytes 1179656 | tf_op jit(solution)/shard_map/ppermute | solution.py:588
  258.1 13.6 %collective-permute-start.26 = (bf16[8,24,768]{2,1,0:T(8,128)(2,1)S(1)}, bf16[8,24,768]{2,1,0:T(8,128)(2,1)S(1)}, u32[]{:S(2)}, u32[]{:S(2)}) collective-permute-start(bf16[8,24,768]{2,1,0:T(8,128)(2,1)S(1)} %constant_dynamic-slice_fusion), channel_id=1, source_target_pairs={{0,16},{4,20},{8,24},{12,28},{16,0},{20,4},{24,8},{28,12},{1,17},{... | collective-permute-start | bytes 884744 | tf_op jit(solution)/shard_map/ppermute | solution.py:588
  281.1 13.4 %collective-permute-start.30 = (bf16[256,768]{1,0:T(8,128)(2,1)}, bf16[256,768]{1,0:T(8,128)(2,1)S(1)}, u32[]{:S(2)}, u32[]{:S(2)}) collective-permute-start(bf16[256,768]{1,0:T(8,128)(2,1)} %collective-permute-done.24.refs_2_), channel_id=1, source_target_pairs={{0,1},{1,0},{2,3},{3,2},{4,5},{5,4},{6,7},{7,6},{8,9},{9,8},{10,11... | collective-permute-start | bytes 1179656 | tf_op jit(solution)/shard_map/ppermute | solution.py:588
  282.0 12.5 %collective-permute-start.27 = (bf16[2,24,768]{2,1,0:T(8,128)(2,1)S(1)}, bf16[2,24,768]{2,1,0:T(8,128)(2,1)S(1)}, u32[]{:S(2)}, u32[]{:S(2)}) collective-permute-start(bf16[2,24,768]{2,1,0:T(8,128)(2,1)S(1)} %get-tuple-element.178), channel_id=1, source_target_pairs={{0,1},{1,0},{2,3},{3,2},{4,5},{5,4},{6,7},{7,6},{8,9},{9,8},{10,11... | collective-permute-start | bytes 221192 | tf_op jit(solution)/shard_map/ppermute | solution.py:588
  283.4 11.1 %collective-permute-start.28 = (bf16[2,24,768]{2,1,0:T(8,128)(2,1)S(1)}, bf16[2,24,768]{2,1,0:T(8,128)(2,1)S(1)}, u32[]{:S(2)}, u32[]{:S(2)}) collective-permute-start(bf16[2,24,768]{2,1,0:T(8,128)(2,1)S(1)} %get-tuple-element.177), channel_id=1, source_target_pairs={{0,2},{1,3},{2,0},{3,1},{4,6},{5,7},{6,4},{7,5},{8,10},{9,11},{10,... | collective-permute-start | bytes 221192 | tf_op jit(solution)/shard_map/ppermute | solution.py:588
  284.3 10.2 %collective-permute-start.29 = (bf16[2,24,768]{2,1,0:T(8,128)(2,1)S(1)}, bf16[2,24,768]{2,1,0:T(8,128)(2,1)S(1)}, u32[]{:S(2)}, u32[]{:S(2)}) collective-permute-start(bf16[2,24,768]{2,1,0:T(8,128)(2,1)S(1)} %get-tuple-element.176), channel_id=1, source_target_pairs={{0,3},{1,2},{2,1},{3,0},{4,7},{5,6},{6,5},{7,4},{8,11},{9,10},{10,... | collective-permute-start | bytes 221192 | tf_op jit(solution)/shard_map/ppermute | solution.py:588
  312.6 7.7 %collective-permute-start.32 = (bf16[5,48,768]{2,1,0:T(8,128)(2,1)S(1)}, bf16[5,48,768]{2,1,0:T(8,128)(2,1)S(1)}, u32[]{:S(2)}, u32[]{:S(2)}) collective-permute-start(bf16[5,48,768]{2,1,0:T(8,128)(2,1)S(1)} %pad_maximum_fusion.3), channel_id=1, source_target_pairs={{0,8},{4,12},{8,0},{12,4},{16,24},{20,28},{24,16},{28,20},{1,9},{5... | collective-permute-start | bytes 1105928 | tf_op jit(solution)/shard_map/ppermute | solution.py:588
  (28 other events, 354.2 us)
Sparse Core Ops, SparseCore 0:
  129.8 76.8 reduce-scatter.1
  208.6 64.6 all-gather.1

commit v5 on v3

--- a/solution.py
+++ b/solution.py
@@ -559,7 +559,7 @@
             out[pl.ds(start, share), :] = got.astype(out.dtype)
 
 
-ROWS = 512
+ROWS = 1024
 PIECES = 1
 
 SMEM = pl.BlockSpec(memory_space=pltpu.SMEM)
@@ -602,7 +602,7 @@
         return [value] + [swap(value, axis, bit) for bit in range(1, count)]
     two = swap(value, axis, 2)
     one = swap(value, axis, 1)
-    return [value, one, two, swap(two, axis, 1)]
+    return [value, one, two, swap(after(two, one), axis, 1)]
 
 
 def reduce_near(parts, axis):
@@ -639,6 +639,10 @@
             [jnp.where(low, value, got), jnp.where(low, got, value)], axis=axis
         )
     return value
+
+
+def together(*values):
+    return lax.optimization_barrier(values)
 
 
 def after(value, *others):
@@ -691,8 +695,9 @@
         [tokens, gain_attn, w_qkv_t, segments, rel_bias.T, build_hot],
         flops=6 * 10**9, moved=8 * mib, with_index=False,
     )
+    att = after(att, *halves)
     atts = gather_parts(att, "tensor")
-    swapped = swap(jnp.stack(halves), "dp", 1)
+    swapped = swap(after(jnp.stack(halves), att), "dp", 1)
 
     full = lambda shape: pl.BlockSpec(shape, lambda e: (0,) * len(shape))
     per_expert = lambda shape: pl.BlockSpec((1,) + shape, lambda e: (e, 0, 0))
@@ -805,7 +810,7 @@
     grad_hidden, gh_low, ggain_two = back[shares:]
 
     if four:
-        moe_near = after(moe_near[0], gh_low), moe_near[1]
+        moe_near = after(moe_near[0], *go[1:]), moe_near[1]
         moe_got, _ = reduce_far(moe_parts, moe_near, "tensor")
     else:
         moe_got = [moe_parts[0], *moe_near]
@@ -868,6 +873,7 @@
         return (keep.astype(F32) + got.astype(F32)).astype(BF16)
 
     late = after(late, mark)
+    bits = bits_of("dp")
     late = halve(late, 1)
     grad_hidden = after(grad_hidden, late)
 
@@ -878,37 +884,65 @@
         [idx, *gn_got, grad_hidden, tokens, gain_attn],
         moved=5 * mib,
     )[0]
-    gt_got = gather_parts(gt_share, "tensor")
+    keep, send = halves_of(late, 1, (place // bits[1]) % 2)
+    two, one, got = together(
+        swap(gt_share, "tensor", 2), swap(gt_share, "tensor", 1),
+        swap(after(send, gt_share), "dp", bits[1]),
+    )
+    late = (keep.astype(F32) + got.astype(F32)).astype(BF16)
+    keep, send = halves_of(late, 1, (place // bits[2]) % 2)
+    share_now = after(result_share, two)
+    three, result_two, result_one, got = together(
+        swap(two, "tensor", 1), swap(share_now, "tensor", 2), swap(share_now, "tensor", 1),
+        swap(send, "dp", bits[2]),
+    )
+    late = (keep.astype(F32) + got.astype(F32)).astype(BF16)
+    for bit in bits[3:]:
+        late = halve(late, bit)
     grad_tokens = whole_call(
         functools.partial(place_kernel, PIECES, shares),
-        [shaped((rows, width), F32)], [idx, *gt_got], moved=5 * mib,
+        [shaped((rows, width), F32)], [idx, gt_share, one, two, three], moved=5 * mib,
     )[0]
 
-    result_got = gather_parts(after(result_share, gt_got[2]), "tensor")
-    result = whole_call(
-        functools.partial(place_kernel, PIECES, shares),
-        [shaped((rows, width), BF16)], [idx, *result_got], moved=3 * mib,
-    )[0]
-
-    for level, bit in enumerate(bits_of("dp")[1:]):
-        late = halve(late, bit, gt_got[2] if level else gt_share)
-
+    *sent, _ = together(
+        *[swap(jnp.stack([late[4 + by], late[3]]), "tensor", by) for by in others], grad_tokens
+    )
     out_sum, small = late[4].astype(F32), [late[3]]
-    for by in others:
-        got = swap(jnp.stack([late[4 + by], late[3]]), "tensor", by)
+    for got in sent:
         out_sum = out_sum + got[0].astype(F32)
         small.append(got[1])
-    small = [one.astype(F32) for one in small]
+    small = [part.astype(F32) for part in small]
     while len(small) > 1:
         small = [small[at] + small[at + 1] for at in range(0, len(small), 2)]
     late = jnp.concatenate(
         [late[:3], jnp.stack([small[0].astype(BF16), out_sum.astype(BF16)])], axis=0
     )
-    late = gather_back(after(late, *gt_got[1:], result_got[2]), "dp", 1)
+
     expert_rows = lax.all_gather(expert_rows, "dp", axis=0, tiled=True)
-    expert_rows = expert_rows.reshape(experts, 2, width, width)
-    grad_w_in = expert_rows[:, 0].astype(F32)
-    grad_w_down = expert_rows[:, 1].astype(F32)
+
+    def joined(value, got, bit):
+        low = (place // bit) % 2 == 0
+        return jnp.concatenate([jnp.where(low, value, got), jnp.where(low, got, value)], axis=1)
+
+    for bit in reversed(bits[3:]):
+        late = joined(late, swap(late, "dp", bit), bit)
+    got, result_three = together(
+        swap(late, "dp", bits[2]), swap(result_two, "tensor", 1)
+    )
+    late = joined(late, got, bits[2])
+    grad_w_in = expert_rows.reshape(experts, 2, width, width)[:, 0].astype(F32)
+    got = after(swap(late, "dp", bits[1]), grad_w_in)
+    late = joined(late, got, bits[1])
+    expert_rows = after(expert_rows, got)
+    grad_w_down = expert_rows.reshape(experts, 2, width, width)[:, 1].astype(F32)
+    result = whole_call(
+        functools.partial(place_kernel, PIECES, shares),
+        [shaped((rows, width), BF16)],
+        [idx, result_share, result_one, result_two, result_three],
+        moved=3 * mib,
+    )[0]
+    got = after(swap(late, "dp", bits[0]), grad_w_down, result)
+    late = joined(late, got, bits[0])
     grad_w_qkv = jnp.swapaxes(late[:3], 1, 2).astype(F32)
     grad_w_out = late[4].astype(F32)
     small = late[3].astype(F32)

time: 393 us -> 328 us (0.83)
  waiting for transfers between devices: 192 us -> 124 us
    ppermute x34, waiting for transfers between devices: 192 us -> 122 us  [swap(): return lax.ppermute(value, axis, [(i, i ^ bit) for i in range(count)])]
    convert_element_type x1 -> x4, other arithmetic: 12.3 us -> 14 us  [the longest x1 6.9 us: body(): grad_w_in = expert_rows.reshape(experts, 2, width, width)[:, 0].astype(F32)]
  transfers between devices with their start and end apart: 36 -> 36, of which waited for: 22 -> 20; matrix products, arithmetic and copies ran while one was open for 3% -> 6% of each run, Pallas kernels for 19% -> 27%
where the time goes in v5:
time: 328 us
  waiting for transfers between devices  124 us (38%)
  Pallas kernels  114 us (35%)
  starting transfers between devices  46.8 us (14%)
  other arithmetic  21.5 us (7%)
  between operations  14.5 us (4%)
  local copies, waits for them, and re-layouts  6.64 us (2%)
    ppermute x34, waiting for transfers between devices, swap(): return lax.ppermute(value, axis, [(i, i ^ bit) for i in range(count)])  122 us
    pallas_call x9, Pallas kernels, whole_call(): pl.pallas_call(kernel, out_shape=outs, in_specs=specs, out_specs=[VMEM] *...  52.7 us
    ppermute x34, starting transfers between devices, swap(): return lax.ppermute(value, axis, [(i, i ^ bit) for i in range(count)])  46.8 us
    pallas_call x1, Pallas kernels, body(): pl.pallas_call(functools.partial(moe_fwd_kernel, 0, PIECES, shares, exper...  26.3 us
    pallas_call x1, Pallas kernels, body(): pl.pallas_call(functools.partial(moe_bwd_kernel, 0, shares, experts), gri...  19.3 us
    pallas_call x1, Pallas kernels, body(): pl.pallas_call(functools.partial(moe_weights_kernel, PIECES), grid=(exper...  15.9 us
    convert_element_type x1, other arithmetic, body(): grad_w_in = expert_rows.reshape(experts, 2, width, width)[:, 0].astype(F32)  6.9 us
    convert_element_type x1, other arithmetic, body(): expert_rows.reshape(experts, 2, width, width)[:, 1].astype(F32)  6.9 us
  transfers between devices with their start and end apart: 36, of which 20 were waited for; matrix products, arithmetic and copies ran while one was open for 6% of the time, Pallas kernels for 27%

profile of v5, /device:TPU:0, one launch (start us, length us, event | category | flops | bytes accessed | tf_op | source)
XLA Modules:
  0.0 327.6 jit_solution(12802323590440632317)
XLA Ops:
  8.2 3.1 collective-permute-start
  11.3 2.6 collective-permute-start.1
  13.9 12.2 %shard_map.213 = (bf16[1024,768]{1,0:T(8,128)(2,1)}, bf16[3,1024,192]{2,1,0:T(8,128)(2,1)}, bf16[1024,192]{1,0:T(8,128)(2,1)}, bf16[1024,192]{1,0:T(8,128)(2,1)}...) custom-call(bf16[1024,768]{1,0:T(8,128)(2,1)} %refs_4_.5, ...), custom_call_target="tpu_custom_call" | custom-call | flops 6000000000 | bytes 8388608 | tf_op jit(solution)/shard_map/pallas_call | solution.py:575
  27.6 3.0 collective-permute-start.4
  30.7 19.8 %collective-permute-done.3.refs_1_ = bf16[1024,192]{1,0:T(8,128)(2,1)S(1)} collective-permute-done((bf16[1024,192]{1,0:T(8,128)(2,1)}, bf16[1024,192]{1,0:T(8,128)(2,1)S(1)}, u32[]{:S(2)}, u32[]{:S(2)}) %collective-permute-start.3) | collective-permute-done | bytes 393248 | tf_op jit(solution)/shard_map/ppermute | solution.py:588
  50.4 2.5 collective-permute-done.4.refs_2_
  54.9 8.9 %collective-permute-done.5.refs_3_ = bf16[1024,192]{1,0:T(8,128)(2,1)S(1)} collective-permute-done((bf16[1024,192]{1,0:T(8,128)(2,1)S(1)}, bf16[1024,192]{1,0:T(8,128)(2,1)S(1)}, u32[]{:S(2)}, u32[]{:S(2)}) %collective-permute-start.5) | collective-permute-done | bytes 393248 | tf_op jit(solution)/shard_map/ppermute | solution.py:588
  64.5 26.3 %shard_map.214 = (bf16[256,768]{1,0:T(8,128)(2,1)}, bf16[256,768]{1,0:T(8,128)(2,1)}, bf16[256,768]{1,0:T(8,128)(2,1)}, bf16[256,768]{1,0:T(8,128)(2,1)}, bf16[4...) custom-call(s32[2]{0:T(128)} %pad_add_fusion.idx, ...), custom_call_target="tpu_custom_call" | custom-call | flops 9663676416 | bytes 33554432 | tf_op jit(solution)/shard_map/pallas_call | solution.py:709
  93.0 19.3 %shard_map.215 = (bf16[256,768]{1,0:T(8,128)(2,1)}, bf16[256,768]{1,0:T(8,128)(2,1)}, bf16[256,768]{1,0:T(8,128)(2,1)}, bf16[256,768]{1,0:T(8,128)(2,1)}, f32[10...) custom-call(s32[2]{0:T(128)} %pad_add_fusion.idx, f32[1024,128]{1,0:T(8,128)} %get-tuple-element.96.refs_0_, ...), custom_call_target="tpu_custom_call" | custom-call | flops 9663676416 | bytes 27262976 | tf_op jit(solution)/shard_map/pallas_call | solution.py:753
  114.4 15.9 %shard_map.216 = (bf16[4,2,768,768]{3,2,1,0:T(8,128)(2,1)}, f32[8,768]{1,0:T(8,128)}) custom-call(bf16[1024,768]{1,0:T(8,128)(2,1)} %refs_5_.5, f32[1024,128]{1,0:T(8,128)} %get-tuple-element.96.refs_0_, f32[1024,128]{1,0:T(8,128)} %get-tuple-element.107.refs_1_, bf16[1024,768]{1,0:T(8,128)(2,1)} %get-tuple-element.108.refs_2_, ...), custom_call_target="tpu_custom_call" | custom-call | flops 9663676416 | bytes 27262976 | tf_op jit(solution)/shard_map/pallas_call | solution.py:778
  133.1 14.8 %collective-permute-done.11.refs_2_ = bf16[256,768]{1,0:T(8,128)(2,1)S(1)} collective-permute-done((bf16[256,768]{1,0:T(8,128)(2,1)S(1)}, bf16[256,768]{1,0:T(8,128)(2,1)S(1)}, u32[]{:S(2)}, u32[]{:S(2)}) %collective-permute-start.11) | collective-permute-done | bytes 393248 | tf_op jit(solution)/shard_map/ppermute | solution.py:588
  148.7 4.4 %shard_map.217 = (bf16[256,192]{1,0:T(8,128)(2,1)}, bf16[256,192]{1,0:T(8,128)(2,1)}, bf16[256,192]{1,0:T(8,128)(2,1)}, bf16[256,192]{1,0:T(8,128)(2,1)}, f32[25...) custom-call(s32[2]{0:T(128)} %pad_add_fusion.idx, bf16[256,768]{1,0:T(8,128)(2,1)} %get-tuple-element.100.refs_0_, ...), custom_call_target="tpu_custom_call" | custom-call | flops 300000000 | bytes 5242880 | tf_op jit(solution)/shard_map/pallas_call | solution.py:575
  153.0 2.7 collective-permute-start.13
  159.7 6.2 %collective-permute-done.13.refs_2_ = bf16[256,192]{1,0:T(8,128)(2,1)S(1)} collective-permute-done((bf16[256,192]{1,0:T(8,128)(2,1)}, bf16[256,192]{1,0:T(8,128)(2,1)S(1)}, u32[]{:S(2)}, u32[]{:S(2)}) %collective-permute-start.13) | collective-permute-done | bytes 98336 | tf_op jit(solution)/shard_map/ppermute | solution.py:588
  168.5 17.4 %shard_map.219 = (bf16[256,768]{1,0:T(8,128)(2,1)}, bf16[256,768]{1,0:T(8,128)(2,1)}, bf16[256,768]{1,0:T(8,128)(2,1)}, bf16[256,768]{1,0:T(8,128)(2,1)}, bf16[3...) custom-call(s32[2]{0:T(128)} %pad_add_fusion.idx, bf16[256,192]{1,0:T(8,128)(2,1)} %get-tuple-element.118.refs_0_, ...), custom_call_target="tpu_custom_call" | custom-call | flops 14000000000 | bytes 8388608 | tf_op jit(solution)/shard_map/pallas_call | solution.py:575
  188.0 3.2 shard_map.221
  191.2 4.1 %shard_map.220 = bf16[3,192,768]{2,1,0:T(8,128)(2,1)} custom-call(bf16[1024,768]{1,0:T(8,128)(2,1)} %get-tuple-element.135.refs_0_, bf16[3,1024,192]{2,1,0:T(8,128)(2,1)} %get-tuple-element.136.refs_1_), custom_call_target="tpu_custom_call" | custom-call | flops 1000000000 | bytes 4194304 | tf_op jit(solution)/shard_map/pallas_call | solution.py:575
  198.2 5.9 %collective-permute-done.16.refs_1_ = bf16[256,768]{1,0:T(8,128)(2,1)} collective-permute-done((bf16[256,768]{1,0:T(8,128)(2,1)}, bf16[256,768]{1,0:T(8,128)(2,1)}, u32[]{:S(2)}, u32[]{:S(2)}) %collective-permute-start.16) | collective-permute-done | bytes 393248 | tf_op jit(solution)/shard_map/ppermute | solution.py:588
  207.5 2.5 collective-permute-start.18
  212.0 16.7 %collective-permute-done.18.refs_2_ = bf16[256,768]{1,0:T(8,128)(2,1)} collective-permute-done((bf16[256,768]{1,0:T(8,128)(2,1)}, bf16[256,768]{1,0:T(8,128)(2,1)}, u32[]{:S(2)}, u32[]{:S(2)}) %collective-permute-start.18) | collective-permute-done | bytes 393248 | tf_op jit(solution)/shard_map/ppermute | solution.py:588
  228.7 3.2 shard_map.222.refs_0_
  233.4 3.9 %collective-permute-start.21 = (bf16[256,768]{1,0:T(8,128)(2,1)}, bf16[256,768]{1,0:T(8,128)(2,1)S(1)}, u32[]{:S(2)}, u32[]{:S(2)}) collective-permute-start(bf16[256,768]{1,0:T(8,128)(2,1)} %shard_map.222.refs_0_), channel_id=1, source_target_pairs={{0,1},{1,0},{2,3},{3,2},{4,5},{5,4},{6,7},{7,6},{8,9},{9,8},{10,11... | collective-permute-start | bytes 1179656 | tf_op jit(solution)/shard_map/ppermute | solution.py:588
  239.6 13.8 %collective-permute-done.20.refs_2_ = bf16[256,768]{1,0:T(8,128)(2,1)S(1)} collective-permute-done((bf16[256,768]{1,0:T(8,128)(2,1)}, bf16[256,768]{1,0:T(8,128)(2,1)S(1)}, u32[]{:S(2)}, u32[]{:S(2)}) %collective-permute-start.20) | collective-permute-done | bytes 393248 | tf_op jit(solution)/shard_map/ppermute | solution.py:588
  255.0 3.5 %collective-permute-start.25 = (bf16[256,768]{1,0:T(8,128)(2,1)}, bf16[256,768]{1,0:T(8,128)(2,1)}, u32[]{:S(2)}, u32[]{:S(2)}) collective-permute-start(bf16[256,768]{1,0:T(8,128)(2,1)} %shard_map.218.refs_0_), channel_id=1, source_target_pairs={{0,1},{1,0},{2,3},{3,2},{4,5},{5,4},{6,7},{7,6},{8,9},{9,8},{10,11... | collective-permute-start | bytes 1179656 | tf_op jit(solution)/shard_map/ppermute | solution.py:588
  260.0 12.2 %collective-permute-done.26 = bf16[8,24,768]{2,1,0:T(8,128)(2,1)S(1)} collective-permute-done((bf16[8,24,768]{2,1,0:T(8,128)(2,1)S(1)}, bf16[8,24,768]{2,1,0:T(8,128)(2,1)S(1)}, u32[]{:S(2)}, u32[]{:S(2)}) %collective-permute-start.26) | collective-permute-done | bytes 294944 | tf_op jit(solution)/shard_map/ppermute | solution.py:588
  273.1 3.8 %collective-permute-done.25.refs_1_ = bf16[256,768]{1,0:T(8,128)(2,1)} collective-permute-done((bf16[256,768]{1,0:T(8,128)(2,1)}, bf16[256,768]{1,0:T(8,128)(2,1)}, u32[]{:S(2)}, u32[]{:S(2)}) %collective-permute-start.25) | collective-permute-done | bytes 393248 | tf_op jit(solution)/shard_map/ppermute | solution.py:588
  276.9 4.8 %collective-permute-done.23.refs_3_ = bf16[256,768]{1,0:T(8,128)(2,1)S(1)} collective-permute-done((bf16[256,768]{1,0:T(8,128)(2,1)S(1)}, bf16[256,768]{1,0:T(8,128)(2,1)S(1)}, u32[]{:S(2)}, u32[]{:S(2)}) %collective-permute-start.23) | collective-permute-done | bytes 393248 | tf_op jit(solution)/shard_map/ppermute | solution.py:588
  286.3 3.2 shard_map.223
  293.1 4.3 %collective-permute-done.30 = bf16[5,24,768]{2,1,0:T(8,128)(2,1)S(1)} collective-permute-done((bf16[5,24,768]{2,1,0:T(8,128)(2,1)S(1)}, bf16[5,24,768]{2,1,0:T(8,128)(2,1)S(1)}, u32[]{:S(2)}, u32[]{:S(2)}) %collective-permute-start.30) | collective-permute-done | bytes 184352 | tf_op jit(solution)/shard_map/ppermute | solution.py:588
  299.7 6.9 %fusion.1 = f32[4,768,768]{2,1,0:T(8,128)} fusion(bf16[4,2,768,768]{3,2,1,0:T(8,128)(2,1)} %bitcast.37), kind=kLoop, calls=%fused_computation.3 | loop fusion | flops 2359296 | bytes 14155776 | tf_op jit(solution)/shard_map/convert_element_type | solution.py:933
  306.9 2.6 shard_map.224
  309.5 6.9 %fusion = f32[4,768,768]{2,1,0:T(8,128)} fusion(bf16[4,2,768,768]{3,2,1,0:T(8,128)(2,1)} %bitcast.38), kind=kLoop, calls=%fused_computation.1 | loop fusion | flops 2359296 | bytes 14155776 | tf_op jit(solution)/shard_map/convert_element_type | solution.py:937
  (134 shorter events, 52.8 us)
Async XLA Ops:
  7.2 200.1 %reduce-scatter.2.cloned.1.call-start = ((), (), s32[]{:S(2)}) async-start(), calls=%async_computation.1 | async-start | bytes 10616832 | tf_op jit(solution)/shard_map/reduce_scatter | solution.py:795
  8.2 17.9 %collective-permute-start = (bf16[96,768]{1,0:T(8,128)(2,1)S(1)}, bf16[96,768]{1,0:T(8,128)(2,1)S(1)}, u32[]{:S(2)}, u32[]{:S(2)}) collective-permute-start(bf16[96,768]{1,0:T(8,128)(2,1)S(1)} %constant_dynamic-slice_fusion.3), channel_id=1, source_target_pairs={{0,1},{1,0},{2,3},{3,2},{4,5},{5,4},{6,7},{7,6},{8,9},{9,8},{10,11... | collective-permute-start | bytes 442376 | tf_op jit(solution)/shard_map/ppermute | solution.py:588
  11.3 14.8 %collective-permute-start.1 = (bf16[96,768]{1,0:T(8,128)(2,1)S(1)}, bf16[96,768]{1,0:T(8,128)(2,1)S(1)}, u32[]{:S(2)}, u32[]{:S(2)}) collective-permute-start(bf16[96,768]{1,0:T(8,128)(2,1)S(1)} %constant_dynamic-slice_fusion.3), channel_id=1, source_target_pairs={{0,2},{1,3},{2,0},{3,1},{4,6},{5,7},{6,4},{7,5},{8,10},{9,11},{10,... | collective-permute-start | bytes 442376 | tf_op jit(solution)/shard_map/ppermute | solution.py:588
  13.8 12.2 %collective-permute-start.2 = (bf16[96,768]{1,0:T(8,128)(2,1)S(1)}, bf16[96,768]{1,0:T(8,128)(2,1)S(1)}, u32[]{:S(2)}, u32[]{:S(2)}) collective-permute-start(bf16[96,768]{1,0:T(8,128)(2,1)S(1)} %constant_dynamic-slice_fusion.3), channel_id=1, source_target_pairs={{0,3},{1,2},{2,1},{3,0},{4,7},{5,6},{6,5},{7,4},{8,11},{9,10},{10,... | collective-permute-start | bytes 442376 | tf_op jit(solution)/shard_map/ppermute | solution.py:588
  26.1 24.3 %collective-permute-start.3 = (bf16[1024,192]{1,0:T(8,128)(2,1)}, bf16[1024,192]{1,0:T(8,128)(2,1)S(1)}, u32[]{:S(2)}, u32[]{:S(2)}) collective-permute-start(bf16[1024,192]{1,0:T(8,128)(2,1)} %get-tuple-element.88.refs_0_), channel_id=1, source_target_pairs={{0,1},{1,0},{2,3},{3,2},{4,5},{5,4},{6,7},{7,6},{8,9},{9,8},{10,11... | collective-permute-start | bytes 1179656 | tf_op jit(solution)/shard_map/ppermute | solution.py:588
  27.6 25.4 %collective-permute-start.4 = (bf16[1024,192]{1,0:T(8,128)(2,1)}, bf16[1024,192]{1,0:T(8,128)(2,1)S(1)}, u32[]{:S(2)}, u32[]{:S(2)}) collective-permute-start(bf16[1024,192]{1,0:T(8,128)(2,1)} %get-tuple-element.88.refs_0_), channel_id=1, source_target_pairs={{0,2},{1,3},{2,0},{3,1},{4,6},{5,7},{6,4},{7,5},{8,10},{9,11},{10,... | collective-permute-start | bytes 1179656 | tf_op jit(solution)/shard_map/ppermute | solution.py:588
  30.6 24.3 %collective-permute-start.6 = (bf16[3,96,768]{2,1,0:T(8,128)(2,1)S(1)}, bf16[3,96,768]{2,1,0:T(8,128)(2,1)S(1)}, u32[]{:S(2)}, u32[]{:S(2)}) collective-permute-start(bf16[3,96,768]{2,1,0:T(8,128)(2,1)S(1)} %pad_maximum_fusion.2), channel_id=1, source_target_pairs={{0,4},{4,0},{8,12},{12,8},{16,20},{20,16},{24,28},{28,24},{1,5},{5... | collective-permute-start | bytes 1327112 | tf_op jit(solution)/shard_map/ppermute | solution.py:588
  53.0 10.8 %collective-permute-start.5 = (bf16[1024,192]{1,0:T(8,128)(2,1)S(1)}, bf16[1024,192]{1,0:T(8,128)(2,1)S(1)}, u32[]{:S(2)}, u32[]{:S(2)}) collective-permute-start(bf16[1024,192]{1,0:T(8,128)(2,1)S(1)} %collective-permute-done.4.refs_2_), channel_id=1, source_target_pairs={{0,1},{1,0},{2,3},{3,2},{4,5},{5,4},{6,7},{7,6},{8,9},{9,8},{10,11... | collective-permute-start | bytes 1179656 | tf_op jit(solution)/shard_map/ppermute | solution.py:588
  90.9 21.4 %collective-permute-start.7 = (bf16[256,768]{1,0:T(8,128)(2,1)}, bf16[256,768]{1,0:T(8,128)(2,1)S(1)}, u32[]{:S(2)}, u32[]{:S(2)}) collective-permute-start(bf16[256,768]{1,0:T(8,128)(2,1)} %get-tuple-element.93), channel_id=1, source_target_pairs={{0,1},{1,0},{2,3},{3,2},{4,5},{5,4},{6,7},{7,6},{8,9},{9,8},{10,11... | collective-permute-start | bytes 1179656 | tf_op jit(solution)/shard_map/ppermute | solution.py:588
  92.4 19.8 %collective-permute-start.8 = (bf16[256,768]{1,0:T(8,128)(2,1)}, bf16[256,768]{1,0:T(8,128)(2,1)S(1)}, u32[]{:S(2)}, u32[]{:S(2)}) collective-permute-start(bf16[256,768]{1,0:T(8,128)(2,1)} %get-tuple-element.95), channel_id=1, source_target_pairs={{0,1},{1,0},{2,3},{3,2},{4,5},{5,4},{6,7},{7,6},{8,9},{9,8},{10,11... | collective-permute-start | bytes 1179656 | tf_op jit(solution)/shard_map/ppermute | solution.py:588
  112.3 17.9 %collective-permute-start.10 = (bf16[256,768]{1,0:T(8,128)(2,1)}, bf16[256,768]{1,0:T(8,128)(2,1)S(1)}, u32[]{:S(2)}, u32[]{:S(2)}) collective-permute-start(bf16[256,768]{1,0:T(8,128)(2,1)} %get-tuple-element.106), channel_id=1, source_target_pairs={{0,1},{1,0},{2,3},{3,2},{4,5},{5,4},{6,7},{7,6},{8,9},{9,8},{10,11... | collective-permute-start | bytes 1179656 | tf_op jit(solution)/shard_map/ppermute | solution.py:588
  113.8 16.4 %collective-permute-start.9 = (bf16[256,768]{1,0:T(8,128)(2,1)}, bf16[256,768]{1,0:T(8,128)(2,1)S(1)}, u32[]{:S(2)}, u32[]{:S(2)}) collective-permute-start(bf16[256,768]{1,0:T(8,128)(2,1)} %get-tuple-element.102), channel_id=1, source_target_pairs={{0,1},{1,0},{2,3},{3,2},{4,5},{5,4},{6,7},{7,6},{8,9},{9,8},{10,11... | collective-permute-start | bytes 1179656 | tf_op jit(solution)/shard_map/ppermute | solution.py:588
  131.0 168.8 %all-gather.2.cloned.1.call-start = ((), (), s32[]{:S(2)}) async-start(), calls=%async_computation.2 | async-start | bytes 10616832 | tf_op jit(solution)/shard_map/all_gather | solution.py:921
  131.5 16.4 %collective-permute-start.11 = (bf16[256,768]{1,0:T(8,128)(2,1)S(1)}, bf16[256,768]{1,0:T(8,128)(2,1)S(1)}, u32[]{:S(2)}, u32[]{:S(2)}) collective-permute-start(bf16[256,768]{1,0:T(8,128)(2,1)S(1)} %add_convert_fusion.4), channel_id=1, source_target_pairs={{0,2},{1,3},{2,0},{3,1},{4,6},{5,7},{6,4},{7,5},{8,10},{9,11},{10,... | collective-permute-start | bytes 1179656 | tf_op jit(solution)/shard_map/ppermute | solution.py:588
  153.0 12.8 %collective-permute-start.13 = (bf16[256,192]{1,0:T(8,128)(2,1)}, bf16[256,192]{1,0:T(8,128)(2,1)S(1)}, u32[]{:S(2)}, u32[]{:S(2)}) collective-permute-start(bf16[256,192]{1,0:T(8,128)(2,1)} %get-tuple-element.115), channel_id=1, source_target_pairs={{0,2},{1,3},{2,0},{3,1},{4,6},{5,7},{6,4},{7,5},{8,10},{9,11},{10,... | collective-permute-start | bytes 294920 | tf_op jit(solution)/shard_map/ppermute | solution.py:588
  155.7 10.1 %collective-permute-start.14 = (bf16[256,192]{1,0:T(8,128)(2,1)}, bf16[256,192]{1,0:T(8,128)(2,1)S(1)}, u32[]{:S(2)}, u32[]{:S(2)}) collective-permute-start(bf16[256,192]{1,0:T(8,128)(2,1)} %get-tuple-element.116), channel_id=1, source_target_pairs={{0,3},{1,2},{2,1},{3,0},{4,7},{5,6},{6,5},{7,4},{8,11},{9,10},{10,... | collective-permute-start | bytes 294920 | tf_op jit(solution)/shard_map/ppermute | solution.py:588
  166.0 19.9 %collective-permute-start.15 = (bf16[256,768]{1,0:T(8,128)(2,1)S(1)}, bf16[256,768]{1,0:T(8,128)(2,1)S(1)}, u32[]{:S(2)}, u32[]{:S(2)}) collective-permute-start(bf16[256,768]{1,0:T(8,128)(2,1)S(1)} %add_convert_fusion.3), channel_id=1, source_target_pairs={{0,2},{1,3},{2,0},{3,1},{4,6},{5,7},{6,4},{7,5},{8,10},{9,11},{10,... | collective-permute-start | bytes 1179656 | tf_op jit(solution)/shard_map/ppermute | solution.py:588
  185.9 12.3 %collective-permute-start.17 = (bf16[256,768]{1,0:T(8,128)(2,1)}, bf16[256,768]{1,0:T(8,128)(2,1)S(1)}, u32[]{:S(2)}, u32[]{:S(2)}) collective-permute-start(bf16[256,768]{1,0:T(8,128)(2,1)} %get-tuple-element.134), channel_id=1, source_target_pairs={{0,1},{1,0},{2,3},{3,2},{4,5},{5,4},{6,7},{7,6},{8,9},{9,8},{10,11... | collective-permute-start | bytes 1179656 | tf_op jit(solution)/shard_map/ppermute | solution.py:588
  186.0 18.1 %collective-permute-start.16 = (bf16[256,768]{1,0:T(8,128)(2,1)}, bf16[256,768]{1,0:T(8,128)(2,1)}, u32[]{:S(2)}, u32[]{:S(2)}) collective-permute-start(bf16[256,768]{1,0:T(8,128)(2,1)} %get-tuple-element.130), channel_id=1, source_target_pairs={{0,1},{1,0},{2,3},{3,2},{4,5},{5,4},{6,7},{7,6},{8,9},{9,8},{10,11... | collective-permute-start | bytes 1179656 | tf_op jit(solution)/shard_map/ppermute | solution.py:588
  207.5 21.2 %collective-permute-start.18 = (bf16[256,768]{1,0:T(8,128)(2,1)}, bf16[256,768]{1,0:T(8,128)(2,1)}, u32[]{:S(2)}, u32[]{:S(2)}) collective-permute-start(bf16[256,768]{1,0:T(8,128)(2,1)} %add_convert_fusion.2), channel_id=1, source_target_pairs={{0,2},{1,3},{2,0},{3,1},{4,6},{5,7},{6,4},{7,5},{8,10},{9,11},{10,... | collective-permute-start | bytes 1179656 | tf_op jit(solution)/shard_map/ppermute | solution.py:588
  231.9 22.4 %collective-permute-start.22 = (bf16[8,48,768]{2,1,0:T(8,128)(2,1)S(1)}, bf16[8,48,768]{2,1,0:T(8,128)(2,1)S(1)}, u32[]{:S(2)}, u32[]{:S(2)}) collective-permute-start(bf16[8,48,768]{2,1,0:T(8,128)(2,1)S(1)} %constant_dynamic-slice_fusion.1), channel_id=1, source_target_pairs={{0,8},{4,12},{8,0},{12,4},{16,24},{20,28},{24,16},{28,20},{1,9},{5... | collective-permute-start | bytes 1769480 | tf_op jit(solution)/shard_map/ppermute | solution.py:588
  233.4 20.0 %collective-permute-start.20 = (bf16[256,768]{1,0:T(8,128)(2,1)}, bf16[256,768]{1,0:T(8,128)(2,1)S(1)}, u32[]{:S(2)}, u32[]{:S(2)}) collective-permute-start(bf16[256,768]{1,0:T(8,128)(2,1)} %shard_map.222.refs_0_), channel_id=1, source_target_pairs={{0,2},{1,3},{2,0},{3,1},{4,6},{5,7},{6,4},{7,5},{8,10},{9,11},{10,... | collective-permute-start | bytes 1179656 | tf_op jit(solution)/shard_map/ppermute | solution.py:588
  233.4 20.1 %collective-permute-start.21 = (bf16[256,768]{1,0:T(8,128)(2,1)}, bf16[256,768]{1,0:T(8,128)(2,1)S(1)}, u32[]{:S(2)}, u32[]{:S(2)}) collective-permute-start(bf16[256,768]{1,0:T(8,128)(2,1)} %shard_map.222.refs_0_), channel_id=1, source_target_pairs={{0,1},{1,0},{2,3},{3,2},{4,5},{5,4},{6,7},{7,6},{8,9},{9,8},{10,11... | collective-permute-start | bytes 1179656 | tf_op jit(solution)/shard_map/ppermute | solution.py:588
  254.3 18.8 %collective-permute-start.24 = (bf16[256,768]{1,0:T(8,128)(2,1)}, bf16[256,768]{1,0:T(8,128)(2,1)}, u32[]{:S(2)}, u32[]{:S(2)}) collective-permute-start(bf16[256,768]{1,0:T(8,128)(2,1)} %shard_map.218.refs_0_), channel_id=1, source_target_pairs={{0,2},{1,3},{2,0},{3,1},{4,6},{5,7},{6,4},{7,5},{8,10},{9,11},{10,... | collective-permute-start | bytes 1179656 | tf_op jit(solution)/shard_map/ppermute | solution.py:588
  255.0 21.9 %collective-permute-start.25 = (bf16[256,768]{1,0:T(8,128)(2,1)}, bf16[256,768]{1,0:T(8,128)(2,1)}, u32[]{:S(2)}, u32[]{:S(2)}) collective-permute-start(bf16[256,768]{1,0:T(8,128)(2,1)} %shard_map.218.refs_0_), channel_id=1, source_target_pairs={{0,1},{1,0},{2,3},{3,2},{4,5},{5,4},{6,7},{7,6},{8,9},{9,8},{10,11... | collective-permute-start | bytes 1179656 | tf_op jit(solution)/shard_map/ppermute | solution.py:588
  258.5 23.1 %collective-permute-start.23 = (bf16[256,768]{1,0:T(8,128)(2,1)S(1)}, bf16[256,768]{1,0:T(8,128)(2,1)S(1)}, u32[]{:S(2)}, u32[]{:S(2)}) collective-permute-start(bf16[256,768]{1,0:T(8,128)(2,1)S(1)} %collective-permute-done.20.refs_2_), channel_id=1, source_target_pairs={{0,1},{1,0},{2,3},{3,2},{4,5},{5,4},{6,7},{7,6},{8,9},{9,8},{10,11... | collective-permute-start | bytes 1179656 | tf_op jit(solution)/shard_map/ppermute | solution.py:588
  258.7 13.5 %collective-permute-start.26 = (bf16[8,24,768]{2,1,0:T(8,128)(2,1)S(1)}, bf16[8,24,768]{2,1,0:T(8,128)(2,1)S(1)}, u32[]{:S(2)}, u32[]{:S(2)}) collective-permute-start(bf16[8,24,768]{2,1,0:T(8,128)(2,1)S(1)} %constant_dynamic-slice_fusion), channel_id=1, source_target_pairs={{0,16},{4,20},{8,24},{12,28},{16,0},{20,4},{24,8},{28,12},{1,17},{... | collective-permute-start | bytes 884744 | tf_op jit(solution)/shard_map/ppermute | solution.py:588
  281.8 7.8 %collective-permute-start.27 = (bf16[2,24,768]{2,1,0:T(8,128)(2,1)S(1)}, bf16[2,24,768]{2,1,0:T(8,128)(2,1)S(1)}, u32[]{:S(2)}, u32[]{:S(2)}) collective-permute-start(bf16[2,24,768]{2,1,0:T(8,128)(2,1)S(1)} %get-tuple-element.181), channel_id=1, source_target_pairs={{0,1},{1,0},{2,3},{3,2},{4,5},{5,4},{6,7},{7,6},{8,9},{9,8},{10,11... | collective-permute-start | bytes 221192 | tf_op jit(solution)/shard_map/ppermute | solution.py:588
  284.8 7.0 %collective-permute-start.29 = (bf16[2,24,768]{2,1,0:T(8,128)(2,1)S(1)}, bf16[2,24,768]{2,1,0:T(8,128)(2,1)S(1)}, u32[]{:S(2)}, u32[]{:S(2)}) collective-permute-start(bf16[2,24,768]{2,1,0:T(8,128)(2,1)S(1)} %get-tuple-element.180), channel_id=1, source_target_pairs={{0,3},{1,2},{2,1},{3,0},{4,7},{5,6},{6,5},{7,4},{8,11},{9,10},{10,... | collective-permute-start | bytes 221192 | tf_op jit(solution)/shard_map/ppermute | solution.py:588
  286.3 11.2 %collective-permute-start.31 = (bf16[256,768]{1,0:T(8,128)(2,1)}, bf16[256,768]{1,0:T(8,128)(2,1)S(1)}, u32[]{:S(2)}, u32[]{:S(2)}) collective-permute-start(bf16[256,768]{1,0:T(8,128)(2,1)} %collective-permute-done.24.refs_2_), channel_id=1, source_target_pairs={{0,1},{1,0},{2,3},{3,2},{4,5},{5,4},{6,7},{7,6},{8,9},{9,8},{10,11... | collective-permute-start | bytes 1179656 | tf_op jit(solution)/shard_map/ppermute | solution.py:588
  297.5 9.1 %collective-permute-start.32 = (bf16[5,48,768]{2,1,0:T(8,128)(2,1)S(1)}, bf16[5,48,768]{2,1,0:T(8,128)(2,1)S(1)}, u32[]{:S(2)}, u32[]{:S(2)}) collective-permute-start(bf16[5,48,768]{2,1,0:T(8,128)(2,1)S(1)} %pad_maximum_fusion.3), channel_id=1, source_target_pairs={{0,8},{4,12},{8,0},{12,4},{16,24},{20,28},{24,16},{28,20},{1,9},{5... | collective-permute-start | bytes 1105928 | tf_op jit(solution)/shard_map/ppermute | solution.py:588
  306.8 9.6 %collective-permute-start.33 = (bf16[5,96,768]{2,1,0:T(8,128)(2,1)S(1)}, bf16[5,96,768]{2,1,0:T(8,128)(2,1)S(1)}, u32[]{:S(2)}, u32[]{:S(2)}) collective-permute-start(bf16[5,96,768]{2,1,0:T(8,128)(2,1)S(1)} %pad_maximum_fusion.1), channel_id=1, source_target_pairs={{0,4},{4,0},{8,12},{12,8},{16,20},{20,16},{24,28},{28,24},{1,5},{5... | collective-permute-start | bytes 2211848 | tf_op jit(solution)/shard_map/ppermute | solution.py:588
  (28 other events, 353.1 us)
Sparse Core Ops, SparseCore 0:
  130.4 76.8 reduce-scatter.1
  209.2 64.6 all-gather.1

commit v6 on v5

--- a/solution.py
+++ b/solution.py
@@ -559,7 +559,7 @@
             out[pl.ds(start, share), :] = got.astype(out.dtype)
 
 
-ROWS = 1024
+ROWS = 512
 PIECES = 1
 
 SMEM = pl.BlockSpec(memory_space=pltpu.SMEM)
@@ -808,6 +808,13 @@
     )
     go = exchange(back[:shares], "tensor")
     grad_hidden, gh_low, ggain_two = back[shares:]
+    w_out_rows = whole_call(
+        functools.partial(w_out_back_kernel, PIECES, shares),
+        [shaped((shares, features, width), BF16)],
+        [idx, *atts, gh_low],
+        flops=3 * 10**8, moved=4 * mib,
+    )[0]
+    go[1:] = after(go[1], w_out_rows), *go[2:]
 
     if four:
         moe_near = after(moe_near[0], *go[1:]), moe_near[1]
@@ -850,12 +857,6 @@
         [normed_one, gproj],
         flops=10**9, moved=4 * mib, with_index=False,
     )[0]
-    w_out_rows = whole_call(
-        functools.partial(w_out_back_kernel, PIECES, shares),
-        [shaped((shares, features, width), BF16)],
-        [idx, *atts, after(gh_low, gproj)],
-        flops=3 * 10**8, moved=4 * mib,
-    )[0]
     late = jnp.concatenate([qkv_rows, misc[None], w_out_rows], axis=0)
     if four:
         near = reduce_near(gn_parts, "tensor")
@@ -872,10 +873,10 @@
         got = swap(after(send, *ready), "dp", bit)
         return (keep.astype(F32) + got.astype(F32)).astype(BF16)
 
-    late = after(late, mark)
     bits = bits_of("dp")
     late = halve(late, 1)
-    grad_hidden = after(grad_hidden, late)
+    keep, send = halves_of(late, 1, (place // bits[1]) % 2)
+    got = swap(send[:4], "dp", bits[1]), swap(send[4:], "dp", bits[1])
 
     expert_rows = after(expert_rows, mark)
     gt_share = whole_call(
@@ -884,28 +885,21 @@
         [idx, *gn_got, grad_hidden, tokens, gain_attn],
         moved=5 * mib,
     )[0]
-    keep, send = halves_of(late, 1, (place // bits[1]) % 2)
-    two, one, got = together(
-        swap(gt_share, "tensor", 2), swap(gt_share, "tensor", 1),
-        swap(after(send, gt_share), "dp", bits[1]),
-    )
+    gt_now, result_share, *got = together(gt_share, result_share, *got)
+    got = jnp.concatenate(got, axis=0)
     late = (keep.astype(F32) + got.astype(F32)).astype(BF16)
     keep, send = halves_of(late, 1, (place // bits[2]) % 2)
-    share_now = after(result_share, two)
-    three, result_two, result_one, got = together(
-        swap(two, "tensor", 1), swap(share_now, "tensor", 2), swap(share_now, "tensor", 1),
-        swap(send, "dp", bits[2]),
+    two, one, got = together(
+        swap(gt_now, "tensor", 2), swap(gt_now, "tensor", 1), swap(send, "dp", bits[2])
     )
     late = (keep.astype(F32) + got.astype(F32)).astype(BF16)
     for bit in bits[3:]:
         late = halve(late, bit)
-    grad_tokens = whole_call(
-        functools.partial(place_kernel, PIECES, shares),
-        [shaped((rows, width), F32)], [idx, gt_share, one, two, three], moved=5 * mib,
-    )[0]
-
-    *sent, _ = together(
-        *[swap(jnp.stack([late[4 + by], late[3]]), "tensor", by) for by in others], grad_tokens
+
+    sent = together(*[swap(jnp.stack([late[4 + by], late[3]]), "tensor", by) for by in others])
+    share_now = after(result_share, two)
+    three, result_two, result_one = (
+        swap(two, "tensor", 1), swap(share_now, "tensor", 2), swap(share_now, "tensor", 1)
     )
     out_sum, small = late[4].astype(F32), [late[3]]
     for got in sent:
@@ -926,12 +920,18 @@
 
     for bit in reversed(bits[3:]):
         late = joined(late, swap(late, "dp", bit), bit)
-    got, result_three = together(
-        swap(late, "dp", bits[2]), swap(result_two, "tensor", 1)
+    got, three, result_two, result_one = together(
+        swap(late, "dp", bits[2]), three, result_two, result_one
     )
     late = joined(late, got, bits[2])
+    grad_tokens = whole_call(
+        functools.partial(place_kernel, PIECES, shares),
+        [shaped((rows, width), F32)], [idx, gt_share, one, two, three], moved=5 * mib,
+    )[0]
     grad_w_in = expert_rows.reshape(experts, 2, width, width)[:, 0].astype(F32)
-    got = after(swap(late, "dp", bits[1]), grad_w_in)
+    got, result_three, _, _ = together(
+        swap(late, "dp", bits[1]), swap(result_two, "tensor", 1), grad_w_in, grad_tokens
+    )
     late = joined(late, got, bits[1])
     expert_rows = after(expert_rows, got)
     grad_w_down = expert_rows.reshape(experts, 2, width, width)[:, 1].astype(F32)

time: 328 us -> 323 us (0.985)
  waiting for transfers between devices: 124 us -> 119 us
    ppermute x34 -> x35, waiting for transfers between devices: 122 us -> 117 us  [swap(): return lax.ppermute(value, axis, [(i, i ^ bit) for i in range(count)])]
    ppermute x34 -> x35, starting transfers between devices: 46.8 us -> 46.9 us  [swap(): return lax.ppermute(value, axis, [(i, i ^ bit) for i in range(count)])]
  transfers between devices with their start and end apart: 36 -> 37, of which waited for: 20 -> 18; matrix products, arithmetic and copies ran while one was open for 6% -> 6% of each run, Pallas kernels for 27% -> 27%
where the time goes in v6:
time: 323 us
  waiting for transfers between devices  119 us (37%)
  Pallas kernels  114 us (35%)
  starting transfers between devices  46.9 us (15%)
  other arithmetic  21.6 us (7%)
  between operations  14.5 us (4%)
  local copies, waits for them, and re-layouts  7.14 us (2%)
    ppermute x35, waiting for transfers between devices, swap(): return lax.ppermute(value, axis, [(i, i ^ bit) for i in range(count)])  117 us
    pallas_call x9, Pallas kernels, whole_call(): pl.pallas_call(kernel, out_shape=outs, in_specs=specs, out_specs=[VMEM] *...  52.7 us
    ppermute x35, starting transfers between devices, swap(): return lax.ppermute(value, axis, [(i, i ^ bit) for i in range(count)])  46.9 us
    pallas_call x1, Pallas kernels, body(): pl.pallas_call(functools.partial(moe_fwd_kernel, 0, PIECES, shares, exper...  25.7 us
    pallas_call x1, Pallas kernels, body(): pl.pallas_call(functools.partial(moe_bwd_kernel, 0, shares, experts), gri...  19.3 us
    pallas_call x1, Pallas kernels, body(): pl.pallas_call(functools.partial(moe_weights_kernel, PIECES), grid=(exper...  15.9 us
    convert_element_type x1, other arithmetic, body(): grad_w_in = expert_rows.reshape(experts, 2, width, width)[:, 0].astype(F32)  6.9 us
    convert_element_type x1, other arithmetic, body(): expert_rows.reshape(experts, 2, width, width)[:, 1].astype(F32)  6.9 us
  transfers between devices with their start and end apart: 37, of which 18 were waited for; matrix products, arithmetic and copies ran while one was open for 6% of the time, Pallas kernels for 27%

profile of v6, /device:TPU:0, one launch (start us, length us, event | category | flops | bytes accessed | tf_op | source)
XLA Modules:
  0.0 322.9 jit_solution(7246355243717215503)
XLA Ops:
  8.2 3.1 collective-permute-start
  11.3 2.6 collective-permute-start.1
  13.9 12.2 %shard_map.213 = (bf16[1024,768]{1,0:T(8,128)(2,1)}, bf16[3,1024,192]{2,1,0:T(8,128)(2,1)}, bf16[1024,192]{1,0:T(8,128)(2,1)}, bf16[1024,192]{1,0:T(8,128)(2,1)}...) custom-call(bf16[1024,768]{1,0:T(8,128)(2,1)} %refs_4_.5, ...), custom_call_target="tpu_custom_call" | custom-call | flops 6000000000 | bytes 8388608 | tf_op jit(solution)/shard_map/pallas_call | solution.py:575
  27.6 3.0 collective-permute-start.4
  30.6 19.8 %collective-permute-done.3.refs_1_ = bf16[1024,192]{1,0:T(8,128)(2,1)S(1)} collective-permute-done((bf16[1024,192]{1,0:T(8,128)(2,1)}, bf16[1024,192]{1,0:T(8,128)(2,1)S(1)}, u32[]{:S(2)}, u32[]{:S(2)}) %collective-permute-start.3) | collective-permute-done | bytes 393248 | tf_op jit(solution)/shard_map/ppermute | solution.py:588
  54.9 8.8 %collective-permute-done.5.refs_3_ = bf16[1024,192]{1,0:T(8,128)(2,1)S(1)} collective-permute-done((bf16[1024,192]{1,0:T(8,128)(2,1)S(1)}, bf16[1024,192]{1,0:T(8,128)(2,1)S(1)}, u32[]{:S(2)}, u32[]{:S(2)}) %collective-permute-start.5) | collective-permute-done | bytes 393248 | tf_op jit(solution)/shard_map/ppermute | solution.py:588
  64.5 25.7 %shard_map.214 = (bf16[256,768]{1,0:T(8,128)(2,1)}, bf16[256,768]{1,0:T(8,128)(2,1)}, bf16[256,768]{1,0:T(8,128)(2,1)}, bf16[256,768]{1,0:T(8,128)(2,1)}, bf16[4...) custom-call(s32[2]{0:T(128)} %pad_add_fusion.idx, ...), custom_call_target="tpu_custom_call" | custom-call | flops 9663676416 | bytes 33554432 | tf_op jit(solution)/shard_map/pallas_call | solution.py:709
  92.3 19.3 %shard_map.215 = (bf16[256,768]{1,0:T(8,128)(2,1)}, bf16[256,768]{1,0:T(8,128)(2,1)}, bf16[256,768]{1,0:T(8,128)(2,1)}, bf16[256,768]{1,0:T(8,128)(2,1)}, f32[10...) custom-call(s32[2]{0:T(128)} %pad_add_fusion.idx, f32[1024,128]{1,0:T(8,128)} %get-tuple-element.91.refs_0_, ...), custom_call_target="tpu_custom_call" | custom-call | flops 9663676416 | bytes 27262976 | tf_op jit(solution)/shard_map/pallas_call | solution.py:753
  113.8 15.9 %shard_map.216 = (bf16[4,2,768,768]{3,2,1,0:T(8,128)(2,1)}, f32[8,768]{1,0:T(8,128)}) custom-call(bf16[1024,768]{1,0:T(8,128)(2,1)} %refs_5_.5, f32[1024,128]{1,0:T(8,128)} %get-tuple-element.91.refs_0_, f32[1024,128]{1,0:T(8,128)} %get-tuple-element.104.refs_1_, bf16[1024,768]{1,0:T(8,128)(2,1)} %get-tuple-element.105.refs_2_, ...), custom_call_target="tpu_custom_call" | custom-call | flops 9663676416 | bytes 27262976 | tf_op jit(solution)/shard_map/pallas_call | solution.py:778
  132.5 14.8 %collective-permute-done.11.refs_2_ = bf16[256,768]{1,0:T(8,128)(2,1)S(1)} collective-permute-done((bf16[256,768]{1,0:T(8,128)(2,1)S(1)}, bf16[256,768]{1,0:T(8,128)(2,1)S(1)}, u32[]{:S(2)}, u32[]{:S(2)}) %collective-permute-start.11) | collective-permute-done | bytes 393248 | tf_op jit(solution)/shard_map/ppermute | solution.py:588
  148.1 4.3 %shard_map.217 = (bf16[256,192]{1,0:T(8,128)(2,1)}, bf16[256,192]{1,0:T(8,128)(2,1)}, bf16[256,192]{1,0:T(8,128)(2,1)}, bf16[256,192]{1,0:T(8,128)(2,1)}, f32[25...) custom-call(s32[2]{0:T(128)} %pad_add_fusion.idx, bf16[256,768]{1,0:T(8,128)(2,1)} %get-tuple-element.97.refs_0_, ...), custom_call_target="tpu_custom_call" | custom-call | flops 300000000 | bytes 5242880 | tf_op jit(solution)/shard_map/pallas_call | solution.py:575
  152.4 2.7 collective-permute-start.13
  156.8 3.3 %shard_map.218 = bf16[4,192,768]{2,1,0:T(8,128)(2,1)} custom-call(s32[2]{0:T(128)} %pad_add_fusion.idx, bf16[1024,192]{1,0:T(8,128)(2,1)} %get-tuple-element.88.refs_0_, bf16[1024,192]{1,0:T(8,128)(2,1)} %copy-done.2, bf16[1024,192]{1,0:T(8,128)(2,1)} %copy-done.3, bf16[1024,192]{1,0:T(8,128)(2,1)} %copy-done.4, bf16[256,768]{1,0:T(8,128)(2,1)} %get-tuple-element.114.refs_4_), custom_call_target="tpu_custom_call" | custom-call | flops 300000000 | bytes 4194304 | tf_op jit(solution)/shard_map/pallas_call | solution.py:575
  160.1 5.2 %collective-permute-done.13.refs_2_ = bf16[256,192]{1,0:T(8,128)(2,1)S(1)} collective-permute-done((bf16[256,192]{1,0:T(8,128)(2,1)}, bf16[256,192]{1,0:T(8,128)(2,1)S(1)}, u32[]{:S(2)}, u32[]{:S(2)}) %collective-permute-start.13) | collective-permute-done | bytes 98336 | tf_op jit(solution)/shard_map/ppermute | solution.py:588
  167.9 17.4 %shard_map.219 = (bf16[256,768]{1,0:T(8,128)(2,1)}, bf16[256,768]{1,0:T(8,128)(2,1)}, bf16[256,768]{1,0:T(8,128)(2,1)}, bf16[256,768]{1,0:T(8,128)(2,1)}, bf16[3...) custom-call(s32[2]{0:T(128)} %pad_add_fusion.idx, bf16[256,192]{1,0:T(8,128)(2,1)} %get-tuple-element.112.refs_0_, ...), custom_call_target="tpu_custom_call" | custom-call | flops 14000000000 | bytes 8388608 | tf_op jit(solution)/shard_map/pallas_call | solution.py:575
  187.4 4.1 %shard_map.220 = bf16[3,192,768]{2,1,0:T(8,128)(2,1)} custom-call(bf16[1024,768]{1,0:T(8,128)(2,1)} %get-tuple-element.136.refs_0_, bf16[3,1024,192]{2,1,0:T(8,128)(2,1)} %get-tuple-element.137.refs_1_), custom_call_target="tpu_custom_call" | custom-call | flops 1000000000 | bytes 4194304 | tf_op jit(solution)/shard_map/pallas_call | solution.py:575
  192.9 4.7 %collective-permute-done.17 = bf16[256,768]{1,0:T(8,128)(2,1)S(1)} collective-permute-done((bf16[256,768]{1,0:T(8,128)(2,1)}, bf16[256,768]{1,0:T(8,128)(2,1)S(1)}, u32[]{:S(2)}, u32[]{:S(2)}) %collective-permute-start.17) | collective-permute-done | bytes 393248 | tf_op jit(solution)/shard_map/ppermute | solution.py:588
  197.6 5.9 %collective-permute-done.16.refs_1_ = bf16[256,768]{1,0:T(8,128)(2,1)} collective-permute-done((bf16[256,768]{1,0:T(8,128)(2,1)}, bf16[256,768]{1,0:T(8,128)(2,1)}, u32[]{:S(2)}, u32[]{:S(2)}) %collective-permute-start.16) | collective-permute-done | bytes 393248 | tf_op jit(solution)/shard_map/ppermute | solution.py:588
  216.1 12.0 %collective-permute-done.18.refs_2_ = bf16[256,768]{1,0:T(8,128)(2,1)} collective-permute-done((bf16[256,768]{1,0:T(8,128)(2,1)}, bf16[256,768]{1,0:T(8,128)(2,1)}, u32[]{:S(2)}, u32[]{:S(2)}) %collective-permute-start.18) | collective-permute-done | bytes 393248 | tf_op jit(solution)/shard_map/ppermute | solution.py:588
  228.1 3.2 shard_map.221.refs_0_
  231.3 4.0 %collective-permute-done.21 = bf16[4,48,768]{2,1,0:T(8,128)(2,1)S(1)} collective-permute-done((bf16[4,48,768]{2,1,0:T(8,128)(2,1)S(1)}, bf16[4,48,768]{2,1,0:T(8,128)(2,1)S(1)}, u32[]{:S(2)}, u32[]{:S(2)}) %collective-permute-start.21) | collective-permute-done | bytes 294944 | tf_op jit(solution)/shard_map/ppermute | solution.py:588
  240.7 5.5 %collective-permute-done.24 = bf16[8,24,768]{2,1,0:T(8,128)(2,1)S(1)} collective-permute-done((bf16[8,24,768]{2,1,0:T(8,128)(2,1)S(1)}, bf16[8,24,768]{2,1,0:T(8,128)(2,1)S(1)}, u32[]{:S(2)}, u32[]{:S(2)}) %collective-permute-start.24) | collective-permute-done | bytes 294944 | tf_op jit(solution)/shard_map/ppermute | solution.py:588
  246.2 7.6 %collective-permute-done.22.refs_2_ = bf16[256,768]{1,0:T(8,128)(2,1)S(1)} collective-permute-done((bf16[256,768]{1,0:T(8,128)(2,1)}, bf16[256,768]{1,0:T(8,128)(2,1)S(1)}, u32[]{:S(2)}, u32[]{:S(2)}) %collective-permute-start.22) | collective-permute-done | bytes 393248 | tf_op jit(solution)/shard_map/ppermute | solution.py:588
  259.3 2.8 collective-permute-start.31
  262.2 9.8 %collective-permute-done.26 = bf16[2,24,768]{2,1,0:T(8,128)(2,1)S(1)} collective-permute-done((bf16[2,24,768]{2,1,0:T(8,128)(2,1)S(1)}, bf16[2,24,768]{2,1,0:T(8,128)(2,1)S(1)}, u32[]{:S(2)}, u32[]{:S(2)}) %collective-permute-start.26) | collective-permute-done | bytes 73760 | tf_op jit(solution)/shard_map/ppermute | solution.py:588
  273.4 4.3 %collective-permute-done.28 = bf16[5,24,768]{2,1,0:T(8,128)(2,1)S(1)} collective-permute-done((bf16[5,24,768]{2,1,0:T(8,128)(2,1)S(1)}, bf16[5,24,768]{2,1,0:T(8,128)(2,1)S(1)}, u32[]{:S(2)}, u32[]{:S(2)}) %collective-permute-start.28) | collective-permute-done | bytes 184352 | tf_op jit(solution)/shard_map/ppermute | solution.py:588
  277.7 4.1 %collective-permute-done.30.refs_2_ = bf16[256,768]{1,0:T(8,128)(2,1)S(1)} collective-permute-done((bf16[256,768]{1,0:T(8,128)(2,1)S(1)}, bf16[256,768]{1,0:T(8,128)(2,1)S(1)}, u32[]{:S(2)}, u32[]{:S(2)}) %collective-permute-start.30) | collective-permute-done | bytes 393248 | tf_op jit(solution)/shard_map/ppermute | solution.py:588
  281.8 7.2 %collective-permute-done.29.refs_3_ = bf16[256,768]{1,0:T(8,128)(2,1)S(1)} collective-permute-done((bf16[256,768]{1,0:T(8,128)(2,1)S(1)}, bf16[256,768]{1,0:T(8,128)(2,1)S(1)}, u32[]{:S(2)}, u32[]{:S(2)}) %collective-permute-start.29) | collective-permute-done | bytes 393248 | tf_op jit(solution)/shard_map/ppermute | solution.py:588
  291.2 3.2 %shard_map.223 = f32[1024,768]{1,0:T(8,128)} custom-call(s32[2]{0:T(128)} %pad_add_fusion.idx, bf16[256,768]{1,0:T(8,128)(2,1)} %shard_map.221.refs_0_, bf16[256,768]{1,0:T(8,128)(2,1)} %copy-done.8, bf16[256,768]{1,0:T(8,128)(2,1)} %copy-done.7, bf16[256,768]{1,0:T(8,128)(2,1)} %copy-done.9), custom_call_target="tpu_custom_call" | custom-call | bytes 5242880 | tf_op jit(solution)/shard_map/pallas_call | solution.py:575
  294.5 6.9 %fusion.1 = f32[4,768,768]{2,1,0:T(8,128)} fusion(bf16[4,2,768,768]{3,2,1,0:T(8,128)(2,1)} %bitcast.37), kind=kLoop, calls=%fused_computation.3 | loop fusion | flops 2359296 | bytes 14155776 | tf_op jit(solution)/shard_map/convert_element_type | solution.py:931
  302.2 2.6 shard_map.224
  304.8 6.9 %fusion = f32[4,768,768]{2,1,0:T(8,128)} fusion(bf16[4,2,768,768]{3,2,1,0:T(8,128)(2,1)} %bitcast.38), kind=kLoop, calls=%fused_computation.1 | loop fusion | flops 2359296 | bytes 14155776 | tf_op jit(solution)/shard_map/convert_element_type | solution.py:937
  (142 shorter events, 55.6 us)
Async XLA Ops:
  7.2 199.6 %reduce-scatter.2.cloned.1.call-start = ((), (), s32[]{:S(2)}) async-start(), calls=%async_computation.1 | async-start | bytes 10616832 | tf_op jit(solution)/shard_map/reduce_scatter | solution.py:795
  8.2 17.8 %collective-permute-start = (bf16[96,768]{1,0:T(8,128)(2,1)S(1)}, bf16[96,768]{1,0:T(8,128)(2,1)S(1)}, u32[]{:S(2)}, u32[]{:S(2)}) collective-permute-start(bf16[96,768]{1,0:T(8,128)(2,1)S(1)} %constant_dynamic-slice_fusion.4), channel_id=1, source_target_pairs={{0,1},{1,0},{2,3},{3,2},{4,5},{5,4},{6,7},{7,6},{8,9},{9,8},{10,11... | collective-permute-start | bytes 442376 | tf_op jit(solution)/shard_map/ppermute | solution.py:588
  11.3 14.8 %collective-permute-start.1 = (bf16[96,768]{1,0:T(8,128)(2,1)S(1)}, bf16[96,768]{1,0:T(8,128)(2,1)S(1)}, u32[]{:S(2)}, u32[]{:S(2)}) collective-permute-start(bf16[96,768]{1,0:T(8,128)(2,1)S(1)} %constant_dynamic-slice_fusion.4), channel_id=1, source_target_pairs={{0,2},{1,3},{2,0},{3,1},{4,6},{5,7},{6,4},{7,5},{8,10},{9,11},{10,... | collective-permute-start | bytes 442376 | tf_op jit(solution)/shard_map/ppermute | solution.py:588
  13.8 12.2 %collective-permute-start.2 = (bf16[96,768]{1,0:T(8,128)(2,1)S(1)}, bf16[96,768]{1,0:T(8,128)(2,1)S(1)}, u32[]{:S(2)}, u32[]{:S(2)}) collective-permute-start(bf16[96,768]{1,0:T(8,128)(2,1)S(1)} %constant_dynamic-slice_fusion.4), channel_id=1, source_target_pairs={{0,3},{1,2},{2,1},{3,0},{4,7},{5,6},{6,5},{7,4},{8,11},{9,10},{10,... | collective-permute-start | bytes 442376 | tf_op jit(solution)/shard_map/ppermute | solution.py:588
  26.1 24.3 %collective-permute-start.3 = (bf16[1024,192]{1,0:T(8,128)(2,1)}, bf16[1024,192]{1,0:T(8,128)(2,1)S(1)}, u32[]{:S(2)}, u32[]{:S(2)}) collective-permute-start(bf16[1024,192]{1,0:T(8,128)(2,1)} %get-tuple-element.88.refs_0_), channel_id=1, source_target_pairs={{0,1},{1,0},{2,3},{3,2},{4,5},{5,4},{6,7},{7,6},{8,9},{9,8},{10,11... | collective-permute-start | bytes 1179656 | tf_op jit(solution)/shard_map/ppermute | solution.py:588
  27.6 25.4 %collective-permute-start.4 = (bf16[1024,192]{1,0:T(8,128)(2,1)}, bf16[1024,192]{1,0:T(8,128)(2,1)S(1)}, u32[]{:S(2)}, u32[]{:S(2)}) collective-permute-start(bf16[1024,192]{1,0:T(8,128)(2,1)} %get-tuple-element.88.refs_0_), channel_id=1, source_target_pairs={{0,2},{1,3},{2,0},{3,1},{4,6},{5,7},{6,4},{7,5},{8,10},{9,11},{10,... | collective-permute-start | bytes 1179656 | tf_op jit(solution)/shard_map/ppermute | solution.py:588
  30.6 24.4 %collective-permute-start.6 = (bf16[3,96,768]{2,1,0:T(8,128)(2,1)S(1)}, bf16[3,96,768]{2,1,0:T(8,128)(2,1)S(1)}, u32[]{:S(2)}, u32[]{:S(2)}) collective-permute-start(bf16[3,96,768]{2,1,0:T(8,128)(2,1)S(1)} %pad_maximum_fusion.2), channel_id=1, source_target_pairs={{0,4},{4,0},{8,12},{12,8},{16,20},{20,16},{24,28},{28,24},{1,5},{5... | collective-permute-start | bytes 1327112 | tf_op jit(solution)/shard_map/ppermute | solution.py:588
  52.9 10.8 %collective-permute-start.5 = (bf16[1024,192]{1,0:T(8,128)(2,1)S(1)}, bf16[1024,192]{1,0:T(8,128)(2,1)S(1)}, u32[]{:S(2)}, u32[]{:S(2)}) collective-permute-start(bf16[1024,192]{1,0:T(8,128)(2,1)S(1)} %collective-permute-done.4.refs_2_), channel_id=1, source_target_pairs={{0,1},{1,0},{2,3},{3,2},{4,5},{5,4},{6,7},{7,6},{8,9},{9,8},{10,11... | collective-permute-start | bytes 1179656 | tf_op jit(solution)/shard_map/ppermute | solution.py:588
  90.2 21.4 %collective-permute-start.7 = (bf16[256,768]{1,0:T(8,128)(2,1)}, bf16[256,768]{1,0:T(8,128)(2,1)S(1)}, u32[]{:S(2)}, u32[]{:S(2)}) collective-permute-start(bf16[256,768]{1,0:T(8,128)(2,1)} %get-tuple-element.95), channel_id=1, source_target_pairs={{0,1},{1,0},{2,3},{3,2},{4,5},{5,4},{6,7},{7,6},{8,9},{9,8},{10,11... | collective-permute-start | bytes 1179656 | tf_op jit(solution)/shard_map/ppermute | solution.py:588
  91.8 19.9 %collective-permute-start.8 = (bf16[256,768]{1,0:T(8,128)(2,1)}, bf16[256,768]{1,0:T(8,128)(2,1)S(1)}, u32[]{:S(2)}, u32[]{:S(2)}) collective-permute-start(bf16[256,768]{1,0:T(8,128)(2,1)} %get-tuple-element.96), channel_id=1, source_target_pairs={{0,1},{1,0},{2,3},{3,2},{4,5},{5,4},{6,7},{7,6},{8,9},{9,8},{10,11... | collective-permute-start | bytes 1179656 | tf_op jit(solution)/shard_map/ppermute | solution.py:588
  111.7 18.0 %collective-permute-start.10 = (bf16[256,768]{1,0:T(8,128)(2,1)}, bf16[256,768]{1,0:T(8,128)(2,1)S(1)}, u32[]{:S(2)}, u32[]{:S(2)}) collective-permute-start(bf16[256,768]{1,0:T(8,128)(2,1)} %get-tuple-element.103), channel_id=1, source_target_pairs={{0,1},{1,0},{2,3},{3,2},{4,5},{5,4},{6,7},{7,6},{8,9},{9,8},{10,11... | collective-permute-start | bytes 1179656 | tf_op jit(solution)/shard_map/ppermute | solution.py:588
  113.2 16.4 %collective-permute-start.9 = (bf16[256,768]{1,0:T(8,128)(2,1)}, bf16[256,768]{1,0:T(8,128)(2,1)S(1)}, u32[]{:S(2)}, u32[]{:S(2)}) collective-permute-start(bf16[256,768]{1,0:T(8,128)(2,1)} %get-tuple-element.99), channel_id=1, source_target_pairs={{0,1},{1,0},{2,3},{3,2},{4,5},{5,4},{6,7},{7,6},{8,9},{9,8},{10,11... | collective-permute-start | bytes 1179656 | tf_op jit(solution)/shard_map/ppermute | solution.py:588
  130.4 164.1 %all-gather.2.cloned.1.call-start = ((), (), s32[]{:S(2)}) async-start(), calls=%async_computation.2 | async-start | bytes 10616832 | tf_op jit(solution)/shard_map/all_gather | solution.py:915
  130.9 16.4 %collective-permute-start.11 = (bf16[256,768]{1,0:T(8,128)(2,1)S(1)}, bf16[256,768]{1,0:T(8,128)(2,1)S(1)}, u32[]{:S(2)}, u32[]{:S(2)}) collective-permute-start(bf16[256,768]{1,0:T(8,128)(2,1)S(1)} %add_convert_fusion.4), channel_id=1, source_target_pairs={{0,2},{1,3},{2,0},{3,1},{4,6},{5,7},{6,4},{7,5},{8,10},{9,11},{10,... | collective-permute-start | bytes 1179656 | tf_op jit(solution)/shard_map/ppermute | solution.py:588
  152.4 12.8 %collective-permute-start.13 = (bf16[256,192]{1,0:T(8,128)(2,1)}, bf16[256,192]{1,0:T(8,128)(2,1)S(1)}, u32[]{:S(2)}, u32[]{:S(2)}) collective-permute-start(bf16[256,192]{1,0:T(8,128)(2,1)} %get-tuple-element.116), channel_id=1, source_target_pairs={{0,2},{1,3},{2,0},{3,1},{4,6},{5,7},{6,4},{7,5},{8,10},{9,11},{10,... | collective-permute-start | bytes 294920 | tf_op jit(solution)/shard_map/ppermute | solution.py:588
  155.1 10.1 %collective-permute-start.14 = (bf16[256,192]{1,0:T(8,128)(2,1)}, bf16[256,192]{1,0:T(8,128)(2,1)S(1)}, u32[]{:S(2)}, u32[]{:S(2)}) collective-permute-start(bf16[256,192]{1,0:T(8,128)(2,1)} %get-tuple-element.117), channel_id=1, source_target_pairs={{0,3},{1,2},{2,1},{3,0},{4,7},{5,6},{6,5},{7,4},{8,11},{9,10},{10,... | collective-permute-start | bytes 294920 | tf_op jit(solution)/shard_map/ppermute | solution.py:588
  165.3 20.0 %collective-permute-start.15 = (bf16[256,768]{1,0:T(8,128)(2,1)S(1)}, bf16[256,768]{1,0:T(8,128)(2,1)S(1)}, u32[]{:S(2)}, u32[]{:S(2)}) collective-permute-start(bf16[256,768]{1,0:T(8,128)(2,1)S(1)} %add_convert_fusion.3), channel_id=1, source_target_pairs={{0,2},{1,3},{2,0},{3,1},{4,6},{5,7},{6,4},{7,5},{8,10},{9,11},{10,... | collective-permute-start | bytes 1179656 | tf_op jit(solution)/shard_map/ppermute | solution.py:588
  185.3 12.3 %collective-permute-start.17 = (bf16[256,768]{1,0:T(8,128)(2,1)}, bf16[256,768]{1,0:T(8,128)(2,1)S(1)}, u32[]{:S(2)}, u32[]{:S(2)}) collective-permute-start(bf16[256,768]{1,0:T(8,128)(2,1)} %get-tuple-element.135), channel_id=1, source_target_pairs={{0,1},{1,0},{2,3},{3,2},{4,5},{5,4},{6,7},{7,6},{8,9},{9,8},{10,11... | collective-permute-start | bytes 1179656 | tf_op jit(solution)/shard_map/ppermute | solution.py:588
  185.4 18.1 %collective-permute-start.16 = (bf16[256,768]{1,0:T(8,128)(2,1)}, bf16[256,768]{1,0:T(8,128)(2,1)}, u32[]{:S(2)}, u32[]{:S(2)}) collective-permute-start(bf16[256,768]{1,0:T(8,128)(2,1)} %get-tuple-element.131), channel_id=1, source_target_pairs={{0,1},{1,0},{2,3},{3,2},{4,5},{5,4},{6,7},{7,6},{8,9},{9,8},{10,11... | collective-permute-start | bytes 1179656 | tf_op jit(solution)/shard_map/ppermute | solution.py:588
  207.0 21.1 %collective-permute-start.18 = (bf16[256,768]{1,0:T(8,128)(2,1)}, bf16[256,768]{1,0:T(8,128)(2,1)}, u32[]{:S(2)}, u32[]{:S(2)}) collective-permute-start(bf16[256,768]{1,0:T(8,128)(2,1)} %add_convert_fusion.2), channel_id=1, source_target_pairs={{0,2},{1,3},{2,0},{3,1},{4,6},{5,7},{6,4},{7,5},{8,10},{9,11},{10,... | collective-permute-start | bytes 1179656 | tf_op jit(solution)/shard_map/ppermute | solution.py:588
  211.5 19.8 %collective-permute-start.20 = (bf16[4,48,768]{2,1,0:T(8,128)(2,1)S(1)}, bf16[4,48,768]{2,1,0:T(8,128)(2,1)S(1)}, u32[]{:S(2)}, u32[]{:S(2)}) collective-permute-start(bf16[4,48,768]{2,1,0:T(8,128)(2,1)S(1)} %get-tuple-element.171), channel_id=1, source_target_pairs={{0,8},{4,12},{8,0},{12,4},{16,24},{20,28},{24,16},{28,20},{1,9},{5... | collective-permute-start | bytes 884744 | tf_op jit(solution)/shard_map/ppermute | solution.py:588
  212.9 22.4 %collective-permute-start.21 = (bf16[4,48,768]{2,1,0:T(8,128)(2,1)S(1)}, bf16[4,48,768]{2,1,0:T(8,128)(2,1)S(1)}, u32[]{:S(2)}, u32[]{:S(2)}) collective-permute-start(bf16[4,48,768]{2,1,0:T(8,128)(2,1)S(1)} %get-tuple-element.170), channel_id=1, source_target_pairs={{0,8},{4,12},{8,0},{12,4},{16,24},{20,28},{24,16},{28,20},{1,9},{5... | collective-permute-start | bytes 884744 | tf_op jit(solution)/shard_map/ppermute | solution.py:588
  235.3 18.5 %collective-permute-start.22 = (bf16[256,768]{1,0:T(8,128)(2,1)}, bf16[256,768]{1,0:T(8,128)(2,1)S(1)}, u32[]{:S(2)}, u32[]{:S(2)}) collective-permute-start(bf16[256,768]{1,0:T(8,128)(2,1)} %shard_map.221.refs_0_), channel_id=1, source_target_pairs={{0,2},{1,3},{2,0},{3,1},{4,6},{5,7},{6,4},{7,5},{8,10},{9,11},{10,... | collective-permute-start | bytes 1179656 | tf_op jit(solution)/shard_map/ppermute | solution.py:588
  237.7 16.2 %collective-permute-start.23 = (bf16[256,768]{1,0:T(8,128)(2,1)}, bf16[256,768]{1,0:T(8,128)(2,1)S(1)}, u32[]{:S(2)}, u32[]{:S(2)}) collective-permute-start(bf16[256,768]{1,0:T(8,128)(2,1)} %shard_map.221.refs_0_), channel_id=1, source_target_pairs={{0,1},{1,0},{2,3},{3,2},{4,5},{5,4},{6,7},{7,6},{8,9},{9,8},{10,11... | collective-permute-start | bytes 1179656 | tf_op jit(solution)/shard_map/ppermute | solution.py:588
  255.4 16.6 %collective-permute-start.26 = (bf16[2,24,768]{2,1,0:T(8,128)(2,1)S(1)}, bf16[2,24,768]{2,1,0:T(8,128)(2,1)S(1)}, u32[]{:S(2)}, u32[]{:S(2)}) collective-permute-start(bf16[2,24,768]{2,1,0:T(8,128)(2,1)S(1)} %get-tuple-element.184), channel_id=1, source_target_pairs={{0,2},{1,3},{2,0},{3,1},{4,6},{5,7},{6,4},{7,5},{8,10},{9,11},{10,... | collective-permute-start | bytes 221192 | tf_op jit(solution)/shard_map/ppermute | solution.py:588
  257.7 14.3 %collective-permute-start.27 = (bf16[2,24,768]{2,1,0:T(8,128)(2,1)S(1)}, bf16[2,24,768]{2,1,0:T(8,128)(2,1)S(1)}, u32[]{:S(2)}, u32[]{:S(2)}) collective-permute-start(bf16[2,24,768]{2,1,0:T(8,128)(2,1)S(1)} %get-tuple-element.182), channel_id=1, source_target_pairs={{0,3},{1,2},{2,1},{3,0},{4,7},{5,6},{6,5},{7,4},{8,11},{9,10},{10,... | collective-permute-start | bytes 221192 | tf_op jit(solution)/shard_map/ppermute | solution.py:588
  258.4 23.3 %collective-permute-start.30 = (bf16[256,768]{1,0:T(8,128)(2,1)S(1)}, bf16[256,768]{1,0:T(8,128)(2,1)S(1)}, u32[]{:S(2)}, u32[]{:S(2)}) collective-permute-start(bf16[256,768]{1,0:T(8,128)(2,1)S(1)} %copy-done.1), channel_id=1, source_target_pairs={{0,2},{1,3},{2,0},{3,1},{4,6},{5,7},{6,4},{7,5},{8,10},{9,11},{10,... | collective-permute-start | bytes 1179656 | tf_op jit(solution)/shard_map/ppermute | solution.py:588
  259.3 22.5 %collective-permute-start.31 = (bf16[256,768]{1,0:T(8,128)(2,1)S(1)}, bf16[256,768]{1,0:T(8,128)(2,1)S(1)}, u32[]{:S(2)}, u32[]{:S(2)}) collective-permute-start(bf16[256,768]{1,0:T(8,128)(2,1)S(1)} %copy-done.1), channel_id=1, source_target_pairs={{0,1},{1,0},{2,3},{3,2},{4,5},{5,4},{6,7},{7,6},{8,9},{9,8},{10,11... | collective-permute-start | bytes 1179656 | tf_op jit(solution)/shard_map/ppermute | solution.py:588
  262.1 26.8 %collective-permute-start.29 = (bf16[256,768]{1,0:T(8,128)(2,1)S(1)}, bf16[256,768]{1,0:T(8,128)(2,1)S(1)}, u32[]{:S(2)}, u32[]{:S(2)}) collective-permute-start(bf16[256,768]{1,0:T(8,128)(2,1)S(1)} %collective-permute-done.22.refs_2_), channel_id=1, source_target_pairs={{0,1},{1,0},{2,3},{3,2},{4,5},{5,4},{6,7},{7,6},{8,9},{9,8},{10,11... | collective-permute-start | bytes 1179656 | tf_op jit(solution)/shard_map/ppermute | solution.py:588
  289.0 12.4 %collective-permute-start.32 = (bf16[5,48,768]{2,1,0:T(8,128)(2,1)S(1)}, bf16[5,48,768]{2,1,0:T(8,128)(2,1)S(1)}, u32[]{:S(2)}, u32[]{:S(2)}) collective-permute-start(bf16[5,48,768]{2,1,0:T(8,128)(2,1)S(1)} %pad_maximum_fusion.3), channel_id=1, source_target_pairs={{0,8},{4,12},{8,0},{12,4},{16,24},{20,28},{24,16},{28,20},{1,9},{5... | collective-permute-start | bytes 1105928 | tf_op jit(solution)/shard_map/ppermute | solution.py:588
  291.2 10.2 %collective-permute-start.33 = (bf16[256,768]{1,0:T(8,128)(2,1)S(1)}, bf16[256,768]{1,0:T(8,128)(2,1)S(1)}, u32[]{:S(2)}, u32[]{:S(2)}) collective-permute-start(bf16[256,768]{1,0:T(8,128)(2,1)S(1)} %collective-permute-done.30.refs_2_), channel_id=1, source_target_pairs={{0,1},{1,0},{2,3},{3,2},{4,5},{5,4},{6,7},{7,6},{8,9},{9,8},{10,11... | collective-permute-start | bytes 1179656 | tf_op jit(solution)/shard_map/ppermute | solution.py:588
  301.6 10.1 %collective-permute-start.34 = (bf16[5,96,768]{2,1,0:T(8,128)(2,1)S(1)}, bf16[5,96,768]{2,1,0:T(8,128)(2,1)S(1)}, u32[]{:S(2)}, u32[]{:S(2)}) collective-permute-start(bf16[5,96,768]{2,1,0:T(8,128)(2,1)S(1)} %pad_maximum_fusion.1), channel_id=1, source_target_pairs={{0,4},{4,0},{8,12},{12,8},{16,20},{20,16},{24,28},{28,24},{1,5},{5... | collective-permute-start | bytes 2211848 | tf_op jit(solution)/shard_map/ppermute | solution.py:588
  (32 other events, 407.8 us)
Sparse Core Ops, SparseCore 0:
  129.8 76.8 reduce-scatter.1
  208.6 67.9 all-gather.1

commit v7 on v6

--- a/solution.py
+++ b/solution.py
@@ -885,7 +885,8 @@
         [idx, *gn_got, grad_hidden, tokens, gain_attn],
         moved=5 * mib,
     )[0]
-    gt_now, result_share, *got = together(gt_share, result_share, *got)
+    result_one = swap(after(result_share, mark), "tensor", 1)
+    gt_now, result_one, *got = together(gt_share, result_one, *got)
     got = jnp.concatenate(got, axis=0)
     late = (keep.astype(F32) + got.astype(F32)).astype(BF16)
     keep, send = halves_of(late, 1, (place // bits[2]) % 2)
@@ -897,10 +898,8 @@
         late = halve(late, bit)
 
     sent = together(*[swap(jnp.stack([late[4 + by], late[3]]), "tensor", by) for by in others])
-    share_now = after(result_share, two)
-    three, result_two, result_one = (
-        swap(two, "tensor", 1), swap(share_now, "tensor", 2), swap(share_now, "tensor", 1)
-    )
+    three = swap(two, "tensor", 1)
+    result_two = swap(after(result_share, two), "tensor", 2)
     out_sum, small = late[4].astype(F32), [late[3]]
     for got in sent:
         out_sum = out_sum + got[0].astype(F32)
@@ -920,17 +919,15 @@
 
     for bit in reversed(bits[3:]):
         late = joined(late, swap(late, "dp", bit), bit)
-    got, three, result_two, result_one = together(
-        swap(late, "dp", bits[2]), three, result_two, result_one
-    )
-    late = joined(late, got, bits[2])
     grad_tokens = whole_call(
         functools.partial(place_kernel, PIECES, shares),
         [shaped((rows, width), F32)], [idx, gt_share, one, two, three], moved=5 * mib,
     )[0]
+    got, _, result_two = together(swap(late, "dp", bits[2]), grad_tokens, result_two)
+    late = joined(late, got, bits[2])
     grad_w_in = expert_rows.reshape(experts, 2, width, width)[:, 0].astype(F32)
-    got, result_three, _, _ = together(
-        swap(late, "dp", bits[1]), swap(result_two, "tensor", 1), grad_w_in, grad_tokens
+    got, _, result_three = together(
+        swap(late, "dp", bits[1]), grad_w_in, swap(result_two, "tensor", 1)
     )
     late = joined(late, got, bits[1])
     expert_rows = after(expert_rows, got)

time: 323 us -> 319 us (0.988)
  starting transfers between devices: 46.9 us -> 41.3 us
    ppermute x35, starting transfers between devices: 46.9 us -> 41.3 us  [swap(): return lax.ppermute(value, axis, [(i, i ^ bit) for i in range(count)])]
  transfers between devices with their start and end apart: 37 -> 37, of which waited for: 18 -> 18; matrix products, arithmetic and copies ran while one was open for 6% -> 6% of each run, Pallas kernels for 27% -> 28%
where the time goes in v7:
time: 319 us
  waiting for transfers between devices  120 us (38%)
  Pallas kernels  114 us (36%)
  starting transfers between devices  41.3 us (13%)
  other arithmetic  21.6 us (7%)
  between operations  14.5 us (5%)
  local copies, waits for them, and re-layouts  7.84 us (2%)
    ppermute x35, waiting for transfers between devices, swap(): return lax.ppermute(value, axis, [(i, i ^ bit) for i in range(count)])  118 us
    pallas_call x9, Pallas kernels, whole_call(): pl.pallas_call(kernel, out_shape=outs, in_specs=specs, out_specs=[VMEM] *...  52.7 us
    ppermute x35, starting transfers between devices, swap(): return lax.ppermute(value, axis, [(i, i ^ bit) for i in range(count)])  41.3 us
    pallas_call x1, Pallas kernels, body(): pl.pallas_call(functools.partial(moe_fwd_kernel, 0, PIECES, shares, exper...  25.7 us
    pallas_call x1, Pallas kernels, body(): pl.pallas_call(functools.partial(moe_bwd_kernel, 0, shares, experts), gri...  19.3 us
    pallas_call x1, Pallas kernels, body(): pl.pallas_call(functools.partial(moe_weights_kernel, PIECES), grid=(exper...  15.8 us
    convert_element_type x1, other arithmetic, body(): grad_w_in = expert_rows.reshape(experts, 2, width, width)[:, 0].astype(F32)  6.9 us
    convert_element_type x1, other arithmetic, body(): expert_rows.reshape(experts, 2, width, width)[:, 1].astype(F32)  6.9 us
  transfers between devices with their start and end apart: 37, of which 18 were waited for; matrix products, arithmetic and copies ran while one was open for 6% of the time, Pallas kernels for 28%

profile of v7, /device:TPU:0, one launch (start us, length us, event | category | flops | bytes accessed | tf_op | source)
XLA Modules:
  0.0 318.8 jit_solution(2445484379988209803)
XLA Ops:
  8.2 3.1 collective-permute-start
  11.3 2.6 collective-permute-start.1
  13.9 12.2 %shard_map.213 = (bf16[1024,768]{1,0:T(8,128)(2,1)}, bf16[3,1024,192]{2,1,0:T(8,128)(2,1)}, bf16[1024,192]{1,0:T(8,128)(2,1)}, bf16[1024,192]{1,0:T(8,128)(2,1)}...) custom-call(bf16[1024,768]{1,0:T(8,128)(2,1)} %refs_4_.5, ...), custom_call_target="tpu_custom_call" | custom-call | flops 6000000000 | bytes 8388608 | tf_op jit(solution)/shard_map/pallas_call | solution.py:575
  27.6 3.0 collective-permute-start.4
  30.7 19.8 %collective-permute-done.3.refs_1_ = bf16[1024,192]{1,0:T(8,128)(2,1)S(1)} collective-permute-done((bf16[1024,192]{1,0:T(8,128)(2,1)}, bf16[1024,192]{1,0:T(8,128)(2,1)S(1)}, u32[]{:S(2)}, u32[]{:S(2)}) %collective-permute-start.3) | collective-permute-done | bytes 393248 | tf_op jit(solution)/shard_map/ppermute | solution.py:588
  50.4 2.5 collective-permute-done.4.refs_2_
  55.0 8.8 %collective-permute-done.5.refs_3_ = bf16[1024,192]{1,0:T(8,128)(2,1)S(1)} collective-permute-done((bf16[1024,192]{1,0:T(8,128)(2,1)S(1)}, bf16[1024,192]{1,0:T(8,128)(2,1)S(1)}, u32[]{:S(2)}, u32[]{:S(2)}) %collective-permute-start.5) | collective-permute-done | bytes 393248 | tf_op jit(solution)/shard_map/ppermute | solution.py:588
  64.5 25.7 %shard_map.214 = (bf16[256,768]{1,0:T(8,128)(2,1)}, bf16[256,768]{1,0:T(8,128)(2,1)}, bf16[256,768]{1,0:T(8,128)(2,1)}, bf16[256,768]{1,0:T(8,128)(2,1)}, bf16[4...) custom-call(s32[2]{0:T(128)} %pad_add_fusion.idx, ...), custom_call_target="tpu_custom_call" | custom-call | flops 9663676416 | bytes 33554432 | tf_op jit(solution)/shard_map/pallas_call | solution.py:709
  92.3 19.3 %shard_map.215 = (bf16[256,768]{1,0:T(8,128)(2,1)}, bf16[256,768]{1,0:T(8,128)(2,1)}, bf16[256,768]{1,0:T(8,128)(2,1)}, bf16[256,768]{1,0:T(8,128)(2,1)}, f32[10...) custom-call(s32[2]{0:T(128)} %pad_add_fusion.idx, f32[1024,128]{1,0:T(8,128)} %get-tuple-element.95.refs_0_, ...), custom_call_target="tpu_custom_call" | custom-call | flops 9663676416 | bytes 27262976 | tf_op jit(solution)/shard_map/pallas_call | solution.py:753
  113.8 15.8 %shard_map.216 = (bf16[4,2,768,768]{3,2,1,0:T(8,128)(2,1)}, f32[8,768]{1,0:T(8,128)}) custom-call(bf16[1024,768]{1,0:T(8,128)(2,1)} %refs_5_.5, f32[1024,128]{1,0:T(8,128)} %get-tuple-element.95.refs_0_, f32[1024,128]{1,0:T(8,128)} %get-tuple-element.106.refs_1_, bf16[1024,768]{1,0:T(8,128)(2,1)} %get-tuple-element.107.refs_2_, ...), custom_call_target="tpu_custom_call" | custom-call | flops 9663676416 | bytes 27262976 | tf_op jit(solution)/shard_map/pallas_call | solution.py:778
  132.5 14.9 %collective-permute-done.11.refs_2_ = bf16[256,768]{1,0:T(8,128)(2,1)S(1)} collective-permute-done((bf16[256,768]{1,0:T(8,128)(2,1)S(1)}, bf16[256,768]{1,0:T(8,128)(2,1)S(1)}, u32[]{:S(2)}, u32[]{:S(2)}) %collective-permute-start.11) | collective-permute-done | bytes 393248 | tf_op jit(solution)/shard_map/ppermute | solution.py:588
  148.1 4.3 %shard_map.217 = (bf16[256,192]{1,0:T(8,128)(2,1)}, bf16[256,192]{1,0:T(8,128)(2,1)}, bf16[256,192]{1,0:T(8,128)(2,1)}, bf16[256,192]{1,0:T(8,128)(2,1)}, f32[25...) custom-call(s32[2]{0:T(128)} %pad_add_fusion.idx, bf16[256,768]{1,0:T(8,128)(2,1)} %get-tuple-element.99.refs_0_, ...), custom_call_target="tpu_custom_call" | custom-call | flops 300000000 | bytes 5242880 | tf_op jit(solution)/shard_map/pallas_call | solution.py:575
  152.4 2.7 collective-permute-start.13
  156.8 3.3 %shard_map.218 = bf16[4,192,768]{2,1,0:T(8,128)(2,1)} custom-call(s32[2]{0:T(128)} %pad_add_fusion.idx, bf16[1024,192]{1,0:T(8,128)(2,1)} %get-tuple-element.87.refs_0_, bf16[1024,192]{1,0:T(8,128)(2,1)} %copy-done.2, bf16[1024,192]{1,0:T(8,128)(2,1)} %copy-done.3, bf16[1024,192]{1,0:T(8,128)(2,1)} %copy-done.4, bf16[256,768]{1,0:T(8,128)(2,1)} %get-tuple-element.114.refs_4_), custom_call_target="tpu_custom_call" | custom-call | flops 300000000 | bytes 4194304 | tf_op jit(solution)/shard_map/pallas_call | solution.py:575
  160.1 5.2 %collective-permute-done.13.refs_2_ = bf16[256,192]{1,0:T(8,128)(2,1)S(1)} collective-permute-done((bf16[256,192]{1,0:T(8,128)(2,1)}, bf16[256,192]{1,0:T(8,128)(2,1)S(1)}, u32[]{:S(2)}, u32[]{:S(2)}) %collective-permute-start.13) | collective-permute-done | bytes 98336 | tf_op jit(solution)/shard_map/ppermute | solution.py:588
  167.9 17.4 %shard_map.220 = (bf16[256,768]{1,0:T(8,128)(2,1)}, bf16[256,768]{1,0:T(8,128)(2,1)}, bf16[256,768]{1,0:T(8,128)(2,1)}, bf16[256,768]{1,0:T(8,128)(2,1)}, bf16[3...) custom-call(s32[2]{0:T(128)} %pad_add_fusion.idx, bf16[256,192]{1,0:T(8,128)(2,1)} %get-tuple-element.119.refs_0_, ...), custom_call_target="tpu_custom_call" | custom-call | flops 14000000000 | bytes 8388608 | tf_op jit(solution)/shard_map/pallas_call | solution.py:575
  187.4 4.1 %shard_map.221 = bf16[3,192,768]{2,1,0:T(8,128)(2,1)} custom-call(bf16[1024,768]{1,0:T(8,128)(2,1)} %get-tuple-element.136.refs_0_, bf16[3,1024,192]{2,1,0:T(8,128)(2,1)} %get-tuple-element.137.refs_1_), custom_call_target="tpu_custom_call" | custom-call | flops 1000000000 | bytes 4194304 | tf_op jit(solution)/shard_map/pallas_call | solution.py:575
  192.9 4.7 %collective-permute-done.17 = bf16[256,768]{1,0:T(8,128)(2,1)S(1)} collective-permute-done((bf16[256,768]{1,0:T(8,128)(2,1)}, bf16[256,768]{1,0:T(8,128)(2,1)S(1)}, u32[]{:S(2)}, u32[]{:S(2)}) %collective-permute-start.17) | collective-permute-done | bytes 393248 | tf_op jit(solution)/shard_map/ppermute | solution.py:588
  197.6 5.9 %collective-permute-done.16.refs_1_ = bf16[256,768]{1,0:T(8,128)(2,1)} collective-permute-done((bf16[256,768]{1,0:T(8,128)(2,1)}, bf16[256,768]{1,0:T(8,128)(2,1)}, u32[]{:S(2)}, u32[]{:S(2)}) %collective-permute-start.16) | collective-permute-done | bytes 393248 | tf_op jit(solution)/shard_map/ppermute | solution.py:588
  216.9 13.6 %collective-permute-done.18.refs_2_ = bf16[256,768]{1,0:T(8,128)(2,1)} collective-permute-done((bf16[256,768]{1,0:T(8,128)(2,1)}, bf16[256,768]{1,0:T(8,128)(2,1)}, u32[]{:S(2)}, u32[]{:S(2)}) %collective-permute-start.18) | collective-permute-done | bytes 393248 | tf_op jit(solution)/shard_map/ppermute | solution.py:588
  230.6 3.2 %shard_map.222.refs_0_ = bf16[256,768]{1,0:T(8,128)(2,1)} custom-call(s32[2]{0:T(128)} %pad_add_fusion.idx, bf16[256,768]{1,0:T(8,128)(2,1)} %get-tuple-element.129.refs_0_, bf16[256,768]{1,0:T(8,128)(2,1)} %collective-permute-done.16.refs_1_, bf16[256,768]{1,0:T(8,128)(2,1)} %collective-permute-done.18.refs_2_, f32[256,768]{1,0:T(8,128)} %get-tuple-element.140.refs_3_, ...), custom_call_target="tpu_custom_call" | custom-call | bytes 5242880 | tf_op jit(solution)/shard_map/pallas_call | solution.py:575
  233.8 8.2 %collective-permute-done.22 = bf16[4,48,768]{2,1,0:T(8,128)(2,1)S(1)} collective-permute-done((bf16[4,48,768]{2,1,0:T(8,128)(2,1)S(1)}, bf16[4,48,768]{2,1,0:T(8,128)(2,1)S(1)}, u32[]{:S(2)}, u32[]{:S(2)}) %collective-permute-start.22) | collective-permute-done | bytes 294944 | tf_op jit(solution)/shard_map/ppermute | solution.py:588
  243.4 8.7 %collective-permute-done.25 = bf16[8,24,768]{2,1,0:T(8,128)(2,1)S(1)} collective-permute-done((bf16[8,24,768]{2,1,0:T(8,128)(2,1)S(1)}, bf16[8,24,768]{2,1,0:T(8,128)(2,1)S(1)}, u32[]{:S(2)}, u32[]{:S(2)}) %collective-permute-start.25) | collective-permute-done | bytes 294944 | tf_op jit(solution)/shard_map/ppermute | solution.py:588
  252.2 6.3 %collective-permute-done.23.refs_2_ = bf16[256,768]{1,0:T(8,128)(2,1)S(1)} collective-permute-done((bf16[256,768]{1,0:T(8,128)(2,1)}, bf16[256,768]{1,0:T(8,128)(2,1)S(1)}, u32[]{:S(2)}, u32[]{:S(2)}) %collective-permute-start.23) | collective-permute-done | bytes 393248 | tf_op jit(solution)/shard_map/ppermute | solution.py:588
  259.6 3.9 %collective-permute-start.28 = (bf16[2,24,768]{2,1,0:T(8,128)(2,1)S(1)}, bf16[2,24,768]{2,1,0:T(8,128)(2,1)S(1)}, u32[]{:S(2)}, u32[]{:S(2)}) collective-permute-start(bf16[2,24,768]{2,1,0:T(8,128)(2,1)S(1)} %get-tuple-element.180), channel_id=1, source_target_pairs={{0,3},{1,2},{2,1},{3,0},{4,7},{5,6},{6,5},{7,4},{8,11},{9,10},{10,... | collective-permute-start | bytes 221192 | tf_op jit(solution)/shard_map/ppermute | solution.py:588
  264.2 3.3 %collective-permute-done.27 = bf16[2,24,768]{2,1,0:T(8,128)(2,1)S(1)} collective-permute-done((bf16[2,24,768]{2,1,0:T(8,128)(2,1)S(1)}, bf16[2,24,768]{2,1,0:T(8,128)(2,1)S(1)}, u32[]{:S(2)}, u32[]{:S(2)}) %collective-permute-start.27) | collective-permute-done | bytes 73760 | tf_op jit(solution)/shard_map/ppermute | solution.py:588
  269.3 11.8 %collective-permute-done.30.refs_3_ = bf16[256,768]{1,0:T(8,128)(2,1)S(1)} collective-permute-done((bf16[256,768]{1,0:T(8,128)(2,1)S(1)}, bf16[256,768]{1,0:T(8,128)(2,1)S(1)}, u32[]{:S(2)}, u32[]{:S(2)}) %collective-permute-start.30) | collective-permute-done | bytes 393248 | tf_op jit(solution)/shard_map/ppermute | solution.py:588
  281.9 3.2 %shard_map.223 = f32[1024,768]{1,0:T(8,128)} custom-call(s32[2]{0:T(128)} %pad_add_fusion.idx, bf16[256,768]{1,0:T(8,128)(2,1)} %shard_map.222.refs_0_, bf16[256,768]{1,0:T(8,128)(2,1)} %copy-done.8, bf16[256,768]{1,0:T(8,128)(2,1)} %copy-done.7, bf16[256,768]{1,0:T(8,128)(2,1)} %copy-done.10), custom_call_target="tpu_custom_call" | custom-call | bytes 5242880 | tf_op jit(solution)/shard_map/pallas_call | solution.py:575
  285.2 2.6 collective-permute-start.32
  287.8 6.9 %fusion.1 = f32[4,768,768]{2,1,0:T(8,128)} fusion(bf16[4,2,768,768]{3,2,1,0:T(8,128)(2,1)} %bitcast.37), kind=kLoop, calls=%fused_computation.3 | loop fusion | flops 2359296 | bytes 14155776 | tf_op jit(solution)/shard_map/convert_element_type | solution.py:928
  298.1 2.6 shard_map.224
  300.8 6.9 %fusion = f32[4,768,768]{2,1,0:T(8,128)} fusion(bf16[4,2,768,768]{3,2,1,0:T(8,128)(2,1)} %bitcast.38), kind=kLoop, calls=%fused_computation.1 | loop fusion | flops 2359296 | bytes 14155776 | tf_op jit(solution)/shard_map/convert_element_type | solution.py:934
  (140 shorter events, 48.0 us)
Async XLA Ops:
  7.2 199.5 %reduce-scatter.2.cloned.1.call-start = ((), (), s32[]{:S(2)}) async-start(), calls=%async_computation.1 | async-start | bytes 10616832 | tf_op jit(solution)/shard_map/reduce_scatter | solution.py:795
  8.2 17.9 %collective-permute-start = (bf16[96,768]{1,0:T(8,128)(2,1)S(1)}, bf16[96,768]{1,0:T(8,128)(2,1)S(1)}, u32[]{:S(2)}, u32[]{:S(2)}) collective-permute-start(bf16[96,768]{1,0:T(8,128)(2,1)S(1)} %constant_dynamic-slice_fusion.4), channel_id=1, source_target_pairs={{0,1},{1,0},{2,3},{3,2},{4,5},{5,4},{6,7},{7,6},{8,9},{9,8},{10,11... | collective-permute-start | bytes 442376 | tf_op jit(solution)/shard_map/ppermute | solution.py:588
  11.3 14.8 %collective-permute-start.1 = (bf16[96,768]{1,0:T(8,128)(2,1)S(1)}, bf16[96,768]{1,0:T(8,128)(2,1)S(1)}, u32[]{:S(2)}, u32[]{:S(2)}) collective-permute-start(bf16[96,768]{1,0:T(8,128)(2,1)S(1)} %constant_dynamic-slice_fusion.4), channel_id=1, source_target_pairs={{0,2},{1,3},{2,0},{3,1},{4,6},{5,7},{6,4},{7,5},{8,10},{9,11},{10,... | collective-permute-start | bytes 442376 | tf_op jit(solution)/shard_map/ppermute | solution.py:588
  13.8 12.2 %collective-permute-start.2 = (bf16[96,768]{1,0:T(8,128)(2,1)S(1)}, bf16[96,768]{1,0:T(8,128)(2,1)S(1)}, u32[]{:S(2)}, u32[]{:S(2)}) collective-permute-start(bf16[96,768]{1,0:T(8,128)(2,1)S(1)} %constant_dynamic-slice_fusion.4), channel_id=1, source_target_pairs={{0,3},{1,2},{2,1},{3,0},{4,7},{5,6},{6,5},{7,4},{8,11},{9,10},{10,... | collective-permute-start | bytes 442376 | tf_op jit(solution)/shard_map/ppermute | solution.py:588
  26.1 24.3 %collective-permute-start.3 = (bf16[1024,192]{1,0:T(8,128)(2,1)}, bf16[1024,192]{1,0:T(8,128)(2,1)S(1)}, u32[]{:S(2)}, u32[]{:S(2)}) collective-permute-start(bf16[1024,192]{1,0:T(8,128)(2,1)} %get-tuple-element.87.refs_0_), channel_id=1, source_target_pairs={{0,1},{1,0},{2,3},{3,2},{4,5},{5,4},{6,7},{7,6},{8,9},{9,8},{10,11... | collective-permute-start | bytes 1179656 | tf_op jit(solution)/shard_map/ppermute | solution.py:588
  27.6 25.4 %collective-permute-start.4 = (bf16[1024,192]{1,0:T(8,128)(2,1)}, bf16[1024,192]{1,0:T(8,128)(2,1)S(1)}, u32[]{:S(2)}, u32[]{:S(2)}) collective-permute-start(bf16[1024,192]{1,0:T(8,128)(2,1)} %get-tuple-element.87.refs_0_), channel_id=1, source_target_pairs={{0,2},{1,3},{2,0},{3,1},{4,6},{5,7},{6,4},{7,5},{8,10},{9,11},{10,... | collective-permute-start | bytes 1179656 | tf_op jit(solution)/shard_map/ppermute | solution.py:588
  30.6 24.4 %collective-permute-start.6 = (bf16[3,96,768]{2,1,0:T(8,128)(2,1)S(1)}, bf16[3,96,768]{2,1,0:T(8,128)(2,1)S(1)}, u32[]{:S(2)}, u32[]{:S(2)}) collective-permute-start(bf16[3,96,768]{2,1,0:T(8,128)(2,1)S(1)} %pad_maximum_fusion.2), channel_id=1, source_target_pairs={{0,4},{4,0},{8,12},{12,8},{16,20},{20,16},{24,28},{28,24},{1,5},{5... | collective-permute-start | bytes 1327112 | tf_op jit(solution)/shard_map/ppermute | solution.py:588
  53.0 10.8 %collective-permute-start.5 = (bf16[1024,192]{1,0:T(8,128)(2,1)S(1)}, bf16[1024,192]{1,0:T(8,128)(2,1)S(1)}, u32[]{:S(2)}, u32[]{:S(2)}) collective-permute-start(bf16[1024,192]{1,0:T(8,128)(2,1)S(1)} %collective-permute-done.4.refs_2_), channel_id=1, source_target_pairs={{0,1},{1,0},{2,3},{3,2},{4,5},{5,4},{6,7},{7,6},{8,9},{9,8},{10,11... | collective-permute-start | bytes 1179656 | tf_op jit(solution)/shard_map/ppermute | solution.py:588
  90.2 21.4 %collective-permute-start.7 = (bf16[256,768]{1,0:T(8,128)(2,1)}, bf16[256,768]{1,0:T(8,128)(2,1)S(1)}, u32[]{:S(2)}, u32[]{:S(2)}) collective-permute-start(bf16[256,768]{1,0:T(8,128)(2,1)} %get-tuple-element.92), channel_id=1, source_target_pairs={{0,1},{1,0},{2,3},{3,2},{4,5},{5,4},{6,7},{7,6},{8,9},{9,8},{10,11... | collective-permute-start | bytes 1179656 | tf_op jit(solution)/shard_map/ppermute | solution.py:588
  91.8 19.9 %collective-permute-start.8 = (bf16[256,768]{1,0:T(8,128)(2,1)}, bf16[256,768]{1,0:T(8,128)(2,1)S(1)}, u32[]{:S(2)}, u32[]{:S(2)}) collective-permute-start(bf16[256,768]{1,0:T(8,128)(2,1)} %get-tuple-element.94), channel_id=1, source_target_pairs={{0,1},{1,0},{2,3},{3,2},{4,5},{5,4},{6,7},{7,6},{8,9},{9,8},{10,11... | collective-permute-start | bytes 1179656 | tf_op jit(solution)/shard_map/ppermute | solution.py:588
  111.7 17.9 %collective-permute-start.10 = (bf16[256,768]{1,0:T(8,128)(2,1)}, bf16[256,768]{1,0:T(8,128)(2,1)S(1)}, u32[]{:S(2)}, u32[]{:S(2)}) collective-permute-start(bf16[256,768]{1,0:T(8,128)(2,1)} %get-tuple-element.105), channel_id=1, source_target_pairs={{0,1},{1,0},{2,3},{3,2},{4,5},{5,4},{6,7},{7,6},{8,9},{9,8},{10,11... | collective-permute-start | bytes 1179656 | tf_op jit(solution)/shard_map/ppermute | solution.py:588
  113.2 16.4 %collective-permute-start.9 = (bf16[256,768]{1,0:T(8,128)(2,1)}, bf16[256,768]{1,0:T(8,128)(2,1)S(1)}, u32[]{:S(2)}, u32[]{:S(2)}) collective-permute-start(bf16[256,768]{1,0:T(8,128)(2,1)} %get-tuple-element.101), channel_id=1, source_target_pairs={{0,1},{1,0},{2,3},{3,2},{4,5},{5,4},{6,7},{7,6},{8,9},{9,8},{10,11... | collective-permute-start | bytes 1179656 | tf_op jit(solution)/shard_map/ppermute | solution.py:588
  130.4 157.4 %all-gather.2.cloned.1.call-start = ((), (), s32[]{:S(2)}) async-start(), calls=%async_computation.2 | async-start | bytes 10616832 | tf_op jit(solution)/shard_map/all_gather | solution.py:914
  130.9 16.4 %collective-permute-start.11 = (bf16[256,768]{1,0:T(8,128)(2,1)S(1)}, bf16[256,768]{1,0:T(8,128)(2,1)S(1)}, u32[]{:S(2)}, u32[]{:S(2)}) collective-permute-start(bf16[256,768]{1,0:T(8,128)(2,1)S(1)} %add_convert_fusion.4), channel_id=1, source_target_pairs={{0,2},{1,3},{2,0},{3,1},{4,6},{5,7},{6,4},{7,5},{8,10},{9,11},{10,... | collective-permute-start | bytes 1179656 | tf_op jit(solution)/shard_map/ppermute | solution.py:588
  152.4 12.8 %collective-permute-start.13 = (bf16[256,192]{1,0:T(8,128)(2,1)}, bf16[256,192]{1,0:T(8,128)(2,1)S(1)}, u32[]{:S(2)}, u32[]{:S(2)}) collective-permute-start(bf16[256,192]{1,0:T(8,128)(2,1)} %get-tuple-element.116), channel_id=1, source_target_pairs={{0,2},{1,3},{2,0},{3,1},{4,6},{5,7},{6,4},{7,5},{8,10},{9,11},{10,... | collective-permute-start | bytes 294920 | tf_op jit(solution)/shard_map/ppermute | solution.py:588
  155.1 10.1 %collective-permute-start.14 = (bf16[256,192]{1,0:T(8,128)(2,1)}, bf16[256,192]{1,0:T(8,128)(2,1)S(1)}, u32[]{:S(2)}, u32[]{:S(2)}) collective-permute-start(bf16[256,192]{1,0:T(8,128)(2,1)} %get-tuple-element.117), channel_id=1, source_target_pairs={{0,3},{1,2},{2,1},{3,0},{4,7},{5,6},{6,5},{7,4},{8,11},{9,10},{10,... | collective-permute-start | bytes 294920 | tf_op jit(solution)/shard_map/ppermute | solution.py:588
  165.3 19.9 %collective-permute-start.15 = (bf16[256,768]{1,0:T(8,128)(2,1)S(1)}, bf16[256,768]{1,0:T(8,128)(2,1)S(1)}, u32[]{:S(2)}, u32[]{:S(2)}) collective-permute-start(bf16[256,768]{1,0:T(8,128)(2,1)S(1)} %add_convert_fusion.3), channel_id=1, source_target_pairs={{0,2},{1,3},{2,0},{3,1},{4,6},{5,7},{6,4},{7,5},{8,10},{9,11},{10,... | collective-permute-start | bytes 1179656 | tf_op jit(solution)/shard_map/ppermute | solution.py:588
  185.3 12.3 %collective-permute-start.17 = (bf16[256,768]{1,0:T(8,128)(2,1)}, bf16[256,768]{1,0:T(8,128)(2,1)S(1)}, u32[]{:S(2)}, u32[]{:S(2)}) collective-permute-start(bf16[256,768]{1,0:T(8,128)(2,1)} %get-tuple-element.135), channel_id=1, source_target_pairs={{0,1},{1,0},{2,3},{3,2},{4,5},{5,4},{6,7},{7,6},{8,9},{9,8},{10,11... | collective-permute-start | bytes 1179656 | tf_op jit(solution)/shard_map/ppermute | solution.py:588
  185.4 18.1 %collective-permute-start.16 = (bf16[256,768]{1,0:T(8,128)(2,1)}, bf16[256,768]{1,0:T(8,128)(2,1)}, u32[]{:S(2)}, u32[]{:S(2)}) collective-permute-start(bf16[256,768]{1,0:T(8,128)(2,1)} %get-tuple-element.131), channel_id=1, source_target_pairs={{0,1},{1,0},{2,3},{3,2},{4,5},{5,4},{6,7},{7,6},{8,9},{9,8},{10,11... | collective-permute-start | bytes 1179656 | tf_op jit(solution)/shard_map/ppermute | solution.py:588
  209.4 21.2 %collective-permute-start.18 = (bf16[256,768]{1,0:T(8,128)(2,1)}, bf16[256,768]{1,0:T(8,128)(2,1)}, u32[]{:S(2)}, u32[]{:S(2)}) collective-permute-start(bf16[256,768]{1,0:T(8,128)(2,1)} %add_convert_fusion.2), channel_id=1, source_target_pairs={{0,2},{1,3},{2,0},{3,1},{4,6},{5,7},{6,4},{7,5},{8,10},{9,11},{10,... | collective-permute-start | bytes 1179656 | tf_op jit(solution)/shard_map/ppermute | solution.py:588
  211.7 22.0 %collective-permute-start.19 = (bf16[256,768]{1,0:T(8,128)(2,1)}, bf16[256,768]{1,0:T(8,128)(2,1)}, u32[]{:S(2)}, u32[]{:S(2)}) collective-permute-start(bf16[256,768]{1,0:T(8,128)(2,1)} %shard_map.219.refs_0_), channel_id=1, source_target_pairs={{0,1},{1,0},{2,3},{3,2},{4,5},{5,4},{6,7},{7,6},{8,9},{9,8},{10,11... | collective-permute-start | bytes 1179656 | tf_op jit(solution)/shard_map/ppermute | solution.py:588
  214.9 18.9 %collective-permute-start.21 = (bf16[4,48,768]{2,1,0:T(8,128)(2,1)S(1)}, bf16[4,48,768]{2,1,0:T(8,128)(2,1)S(1)}, u32[]{:S(2)}, u32[]{:S(2)}) collective-permute-start(bf16[4,48,768]{2,1,0:T(8,128)(2,1)S(1)} %get-tuple-element.169), channel_id=1, source_target_pairs={{0,8},{4,12},{8,0},{12,4},{16,24},{20,28},{24,16},{28,20},{1,9},{5... | collective-permute-start | bytes 884744 | tf_op jit(solution)/shard_map/ppermute | solution.py:588
  216.3 25.7 %collective-permute-start.22 = (bf16[4,48,768]{2,1,0:T(8,128)(2,1)S(1)}, bf16[4,48,768]{2,1,0:T(8,128)(2,1)S(1)}, u32[]{:S(2)}, u32[]{:S(2)}) collective-permute-start(bf16[4,48,768]{2,1,0:T(8,128)(2,1)S(1)} %get-tuple-element.168), channel_id=1, source_target_pairs={{0,8},{4,12},{8,0},{12,4},{16,24},{20,28},{24,16},{28,20},{1,9},{5... | collective-permute-start | bytes 884744 | tf_op jit(solution)/shard_map/ppermute | solution.py:588
  242.0 16.5 %collective-permute-start.23 = (bf16[256,768]{1,0:T(8,128)(2,1)}, bf16[256,768]{1,0:T(8,128)(2,1)S(1)}, u32[]{:S(2)}, u32[]{:S(2)}) collective-permute-start(bf16[256,768]{1,0:T(8,128)(2,1)} %shard_map.222.refs_0_), channel_id=1, source_target_pairs={{0,2},{1,3},{2,0},{3,1},{4,6},{5,7},{6,4},{7,5},{8,10},{9,11},{10,... | collective-permute-start | bytes 1179656 | tf_op jit(solution)/shard_map/ppermute | solution.py:588
  242.0 16.9 %collective-permute-start.24 = (bf16[256,768]{1,0:T(8,128)(2,1)}, bf16[256,768]{1,0:T(8,128)(2,1)S(1)}, u32[]{:S(2)}, u32[]{:S(2)}) collective-permute-start(bf16[256,768]{1,0:T(8,128)(2,1)} %shard_map.222.refs_0_), channel_id=1, source_target_pairs={{0,1},{1,0},{2,3},{3,2},{4,5},{5,4},{6,7},{7,6},{8,9},{9,8},{10,11... | collective-permute-start | bytes 1179656 | tf_op jit(solution)/shard_map/ppermute | solution.py:588
  242.2 10.0 %collective-permute-start.25 = (bf16[8,24,768]{2,1,0:T(8,128)(2,1)S(1)}, bf16[8,24,768]{2,1,0:T(8,128)(2,1)S(1)}, u32[]{:S(2)}, u32[]{:S(2)}) collective-permute-start(bf16[8,24,768]{2,1,0:T(8,128)(2,1)S(1)} %constant_dynamic-slice_fusion.1), channel_id=1, source_target_pairs={{0,16},{4,20},{8,24},{12,28},{16,0},{20,4},{24,8},{28,12},{1,17},{... | collective-permute-start | bytes 884744 | tf_op jit(solution)/shard_map/ppermute | solution.py:588
  263.5 17.6 %collective-permute-start.30 = (bf16[256,768]{1,0:T(8,128)(2,1)S(1)}, bf16[256,768]{1,0:T(8,128)(2,1)S(1)}, u32[]{:S(2)}, u32[]{:S(2)}) collective-permute-start(bf16[256,768]{1,0:T(8,128)(2,1)S(1)} %collective-permute-done.23.refs_2_), channel_id=1, source_target_pairs={{0,1},{1,0},{2,3},{3,2},{4,5},{5,4},{6,7},{7,6},{8,9},{9,8},{10,11... | collective-permute-start | bytes 1179656 | tf_op jit(solution)/shard_map/ppermute | solution.py:588
  263.5 21.6 %collective-permute-start.31 = (bf16[256,768]{1,0:T(8,128)(2,1)S(1)}, bf16[256,768]{1,0:T(8,128)(2,1)S(1)}, u32[]{:S(2)}, u32[]{:S(2)}) collective-permute-start(bf16[256,768]{1,0:T(8,128)(2,1)S(1)} %copy-done.1), channel_id=1, source_target_pairs={{0,2},{1,3},{2,0},{3,1},{4,6},{5,7},{6,4},{7,5},{8,10},{9,11},{10,... | collective-permute-start | bytes 1179656 | tf_op jit(solution)/shard_map/ppermute | solution.py:588
  268.4 16.8 %collective-permute-start.29 = (bf16[5,24,768]{2,1,0:T(8,128)(2,1)S(1)}, bf16[5,24,768]{2,1,0:T(8,128)(2,1)S(1)}, u32[]{:S(2)}, u32[]{:S(2)}) collective-permute-start(bf16[5,24,768]{2,1,0:T(8,128)(2,1)S(1)} %pad_maximum_fusion.5), channel_id=1, source_target_pairs={{0,16},{4,20},{8,24},{12,28},{16,0},{20,4},{24,8},{28,12},{1,17},{... | collective-permute-start | bytes 552968 | tf_op jit(solution)/shard_map/ppermute | solution.py:588
  285.2 10.2 %collective-permute-start.32 = (bf16[5,48,768]{2,1,0:T(8,128)(2,1)S(1)}, bf16[5,48,768]{2,1,0:T(8,128)(2,1)S(1)}, u32[]{:S(2)}, u32[]{:S(2)}) collective-permute-start(bf16[5,48,768]{2,1,0:T(8,128)(2,1)S(1)} %pad_maximum_fusion.3), channel_id=1, source_target_pairs={{0,8},{4,12},{8,0},{12,4},{16,24},{20,28},{24,16},{28,20},{1,9},{5... | collective-permute-start | bytes 1105928 | tf_op jit(solution)/shard_map/ppermute | solution.py:588
  287.8 9.6 %collective-permute-start.33 = (bf16[256,768]{1,0:T(8,128)(2,1)S(1)}, bf16[256,768]{1,0:T(8,128)(2,1)S(1)}, u32[]{:S(2)}, u32[]{:S(2)}) collective-permute-start(bf16[256,768]{1,0:T(8,128)(2,1)S(1)} %collective-permute-done.31.refs_2_), channel_id=1, source_target_pairs={{0,1},{1,0},{2,3},{3,2},{4,5},{5,4},{6,7},{7,6},{8,9},{9,8},{10,11... | collective-permute-start | bytes 1179656 | tf_op jit(solution)/shard_map/ppermute | solution.py:588
  297.6 10.1 %collective-permute-start.34 = (bf16[5,96,768]{2,1,0:T(8,128)(2,1)S(1)}, bf16[5,96,768]{2,1,0:T(8,128)(2,1)S(1)}, u32[]{:S(2)}, u32[]{:S(2)}) collective-permute-start(bf16[5,96,768]{2,1,0:T(8,128)(2,1)S(1)} %pad_maximum_fusion.1), channel_id=1, source_target_pairs={{0,4},{4,0},{8,12},{12,8},{16,20},{20,16},{24,28},{28,24},{1,5},{5... | collective-permute-start | bytes 2211848 | tf_op jit(solution)/shard_map/ppermute | solution.py:588
  (31 other events, 363.8 us)
Sparse Core Ops, SparseCore 0:
  129.8 76.8 reduce-scatter.1
  208.6 71.5 all-gather.1

commit v8 on v7

--- a/solution.py
+++ b/solution.py
@@ -875,10 +875,9 @@
 
     bits = bits_of("dp")
     late = halve(late, 1)
-    keep, send = halves_of(late, 1, (place // bits[1]) % 2)
-    got = swap(send[:4], "dp", bits[1]), swap(send[4:], "dp", bits[1])
 
     expert_rows = after(expert_rows, mark)
+    grad_hidden = after(grad_hidden, late)
     gt_share = whole_call(
         functools.partial(input_back_kernel, PIECES, len(gn_got)),
         [shaped((share, width), BF16)],
@@ -886,20 +885,27 @@
         moved=5 * mib,
     )[0]
     result_one = swap(after(result_share, mark), "tensor", 1)
-    gt_now, result_one, *got = together(gt_share, result_one, *got)
-    got = jnp.concatenate(got, axis=0)
+    gt_now, result_one = together(gt_share, result_one)
+    keep, send = halves_of(late, 1, (place // bits[1]) % 2)
+    two, one, got = together(
+        swap(gt_now, "tensor", 2), swap(gt_now, "tensor", 1),
+        swap(after(send, gt_share), "dp", bits[1]),
+    )
     late = (keep.astype(F32) + got.astype(F32)).astype(BF16)
     keep, send = halves_of(late, 1, (place // bits[2]) % 2)
-    two, one, got = together(
-        swap(gt_now, "tensor", 2), swap(gt_now, "tensor", 1), swap(send, "dp", bits[2])
-    )
+    three, got = together(swap(two, "tensor", 1), swap(send, "dp", bits[2]))
     late = (keep.astype(F32) + got.astype(F32)).astype(BF16)
     for bit in bits[3:]:
         late = halve(late, bit)
-
-    sent = together(*[swap(jnp.stack([late[4 + by], late[3]]), "tensor", by) for by in others])
-    three = swap(two, "tensor", 1)
-    result_two = swap(after(result_share, two), "tensor", 2)
+    grad_tokens = whole_call(
+        functools.partial(place_kernel, PIECES, shares),
+        [shaped((rows, width), F32)], [idx, gt_share, one, two, three], moved=5 * mib,
+    )[0]
+
+    *sent, result_two, _ = together(
+        *[swap(jnp.stack([late[4 + by], late[3]]), "tensor", by) for by in others],
+        swap(after(result_share, two), "tensor", 2), grad_tokens,
+    )
     out_sum, small = late[4].astype(F32), [late[3]]
     for got in sent:
         out_sum = out_sum + got[0].astype(F32)
@@ -919,12 +925,7 @@
 
     for bit in reversed(bits[3:]):
         late = joined(late, swap(late, "dp", bit), bit)
-    grad_tokens = whole_call(
-        functools.partial(place_kernel, PIECES, shares),
-        [shaped((rows, width), F32)], [idx, gt_share, one, two, three], moved=5 * mib,
-    )[0]
-    got, _, result_two = together(swap(late, "dp", bits[2]), grad_tokens, result_two)
-    late = joined(late, got, bits[2])
+    late = joined(late, swap(late, "dp", bits[2]), bits[2])
     grad_w_in = expert_rows.reshape(experts, 2, width, width)[:, 0].astype(F32)
     got, _, result_three = together(
         swap(late, "dp", bits[1]), grad_w_in, swap(result_two, "tensor", 1)

time: 319 us -> 317 us (level)
  waiting for transfers between devices: 120 us -> 110 us
  starting transfers between devices: 41.3 us -> 48.9 us
    ppermute x35 -> x34, waiting for transfers between devices: 118 us -> 107 us  [swap(): return lax.ppermute(value, axis, [(i, i ^ bit) for i in range(count)])]
    ppermute x35 -> x34, starting transfers between devices: 41.3 us -> 48.9 us  [swap(): return lax.ppermute(value, axis, [(i, i ^ bit) for i in range(count)])]
  transfers between devices with their start and end apart: 37 -> 36, of which waited for: 18 -> 16; matrix products, arithmetic and copies ran while one was open for 6% -> 6% of each run, Pallas kernels for 28% -> 28%
where the time goes in v8:
time: 317 us; the launch traced here: 316 us
  Pallas kernels  114 us (36%)
  waiting for transfers between devices  110 us (35%)
  starting transfers between devices  48.9 us (15%)
  other arithmetic  21.5 us (7%)
  between operations  14.5 us (5%)
  local copies, waits for them, and re-layouts  7.84 us (2%)
    ppermute x34, waiting for transfers between devices, swap(): return lax.ppermute(value, axis, [(i, i ^ bit) for i in range(count)])  107 us
    pallas_call x9, Pallas kernels, whole_call(): pl.pallas_call(kernel, out_shape=outs, in_specs=specs, out_specs=[VMEM] *...  52.7 us
    ppermute x34, starting transfers between devices, swap(): return lax.ppermute(value, axis, [(i, i ^ bit) for i in range(count)])  48.9 us
    pallas_call x1, Pallas kernels, body(): pl.pallas_call(functools.partial(moe_fwd_kernel, 0, PIECES, shares, exper...  25.7 us
    pallas_call x1, Pallas kernels, body(): pl.pallas_call(functools.partial(moe_bwd_kernel, 0, shares, experts), gri...  19.3 us
    pallas_call x1, Pallas kernels, body(): pl.pallas_call(functools.partial(moe_weights_kernel, PIECES), grid=(exper...  15.8 us
    convert_element_type x1, other arithmetic, body(): grad_w_in = expert_rows.reshape(experts, 2, width, width)[:, 0].astype(F32)  6.9 us
    convert_element_type x1, other arithmetic, body(): expert_rows.reshape(experts, 2, width, width)[:, 1].astype(F32)  6.9 us
  transfers between devices with their start and end apart: 36, of which 16 were waited for; matrix products, arithmetic and copies ran while one was open for 6% of the time, Pallas kernels for 28%

profile of v8, /device:TPU:0, one launch (start us, length us, event | category | flops | bytes accessed | tf_op | source)
XLA Modules:
  0.0 316.1 jit_solution(9136208629206789784)
XLA Ops:
  8.2 3.1 collective-permute-start
  11.3 2.6 collective-permute-start.1
  13.9 12.2 %shard_map.213 = (bf16[1024,768]{1,0:T(8,128)(2,1)}, bf16[3,1024,192]{2,1,0:T(8,128)(2,1)}, bf16[1024,192]{1,0:T(8,128)(2,1)}, bf16[1024,192]{1,0:T(8,128)(2,1)}...) custom-call(bf16[1024,768]{1,0:T(8,128)(2,1)} %refs_4_.5, ...), custom_call_target="tpu_custom_call" | custom-call | flops 6000000000 | bytes 8388608 | tf_op jit(solution)/shard_map/pallas_call | solution.py:575
  27.6 3.0 collective-permute-start.4
  30.6 19.8 %collective-permute-done.3.refs_1_ = bf16[1024,192]{1,0:T(8,128)(2,1)S(1)} collective-permute-done((bf16[1024,192]{1,0:T(8,128)(2,1)}, bf16[1024,192]{1,0:T(8,128)(2,1)S(1)}, u32[]{:S(2)}, u32[]{:S(2)}) %collective-permute-start.3) | collective-permute-done | bytes 393248 | tf_op jit(solution)/shard_map/ppermute | solution.py:588
  50.4 2.5 collective-permute-done.4.refs_2_
  54.9 8.8 %collective-permute-done.5.refs_3_ = bf16[1024,192]{1,0:T(8,128)(2,1)S(1)} collective-permute-done((bf16[1024,192]{1,0:T(8,128)(2,1)S(1)}, bf16[1024,192]{1,0:T(8,128)(2,1)S(1)}, u32[]{:S(2)}, u32[]{:S(2)}) %collective-permute-start.5) | collective-permute-done | bytes 393248 | tf_op jit(solution)/shard_map/ppermute | solution.py:588
  64.5 25.7 %shard_map.214 = (bf16[256,768]{1,0:T(8,128)(2,1)}, bf16[256,768]{1,0:T(8,128)(2,1)}, bf16[256,768]{1,0:T(8,128)(2,1)}, bf16[256,768]{1,0:T(8,128)(2,1)}, bf16[4...) custom-call(s32[2]{0:T(128)} %pad_add_fusion.idx, ...), custom_call_target="tpu_custom_call" | custom-call | flops 9663676416 | bytes 33554432 | tf_op jit(solution)/shard_map/pallas_call | solution.py:709
  92.3 19.3 %shard_map.215 = (bf16[256,768]{1,0:T(8,128)(2,1)}, bf16[256,768]{1,0:T(8,128)(2,1)}, bf16[256,768]{1,0:T(8,128)(2,1)}, bf16[256,768]{1,0:T(8,128)(2,1)}, f32[10...) custom-call(s32[2]{0:T(128)} %pad_add_fusion.idx, f32[1024,128]{1,0:T(8,128)} %get-tuple-element.96.refs_0_, ...), custom_call_target="tpu_custom_call" | custom-call | flops 9663676416 | bytes 27262976 | tf_op jit(solution)/shard_map/pallas_call | solution.py:753
  113.7 15.8 %shard_map.216 = (bf16[4,2,768,768]{3,2,1,0:T(8,128)(2,1)}, f32[8,768]{1,0:T(8,128)}) custom-call(bf16[1024,768]{1,0:T(8,128)(2,1)} %refs_5_.5, f32[1024,128]{1,0:T(8,128)} %get-tuple-element.96.refs_0_, f32[1024,128]{1,0:T(8,128)} %get-tuple-element.107.refs_1_, bf16[1024,768]{1,0:T(8,128)(2,1)} %get-tuple-element.108.refs_2_, ...), custom_call_target="tpu_custom_call" | custom-call | flops 9663676416 | bytes 27262976 | tf_op jit(solution)/shard_map/pallas_call | solution.py:778
  132.5 14.8 %collective-permute-done.11.refs_2_ = bf16[256,768]{1,0:T(8,128)(2,1)S(1)} collective-permute-done((bf16[256,768]{1,0:T(8,128)(2,1)S(1)}, bf16[256,768]{1,0:T(8,128)(2,1)S(1)}, u32[]{:S(2)}, u32[]{:S(2)}) %collective-permute-start.11) | collective-permute-done | bytes 393248 | tf_op jit(solution)/shard_map/ppermute | solution.py:588
  148.1 4.3 %shard_map.217 = (bf16[256,192]{1,0:T(8,128)(2,1)}, bf16[256,192]{1,0:T(8,128)(2,1)}, bf16[256,192]{1,0:T(8,128)(2,1)}, bf16[256,192]{1,0:T(8,128)(2,1)}, f32[25...) custom-call(s32[2]{0:T(128)} %pad_add_fusion.idx, bf16[256,768]{1,0:T(8,128)(2,1)} %get-tuple-element.100.refs_0_, ...), custom_call_target="tpu_custom_call" | custom-call | flops 300000000 | bytes 5242880 | tf_op jit(solution)/shard_map/pallas_call | solution.py:575
  152.4 2.7 collective-permute-start.13
  156.8 3.3 %shard_map.218 = bf16[4,192,768]{2,1,0:T(8,128)(2,1)} custom-call(s32[2]{0:T(128)} %pad_add_fusion.idx, bf16[1024,192]{1,0:T(8,128)(2,1)} %get-tuple-element.88.refs_0_, bf16[1024,192]{1,0:T(8,128)(2,1)} %copy-done.2, bf16[1024,192]{1,0:T(8,128)(2,1)} %copy-done.3, bf16[1024,192]{1,0:T(8,128)(2,1)} %copy-done.4, bf16[256,768]{1,0:T(8,128)(2,1)} %get-tuple-element.115.refs_4_), custom_call_target="tpu_custom_call" | custom-call | flops 300000000 | bytes 4194304 | tf_op jit(solution)/shard_map/pallas_call | solution.py:575
  160.1 5.2 %collective-permute-done.13.refs_2_ = bf16[256,192]{1,0:T(8,128)(2,1)S(1)} collective-permute-done((bf16[256,192]{1,0:T(8,128)(2,1)}, bf16[256,192]{1,0:T(8,128)(2,1)S(1)}, u32[]{:S(2)}, u32[]{:S(2)}) %collective-permute-start.13) | collective-permute-done | bytes 98336 | tf_op jit(solution)/shard_map/ppermute | solution.py:588
  165.4 2.5 collective-permute-start.15
  167.9 17.5 %shard_map.220 = (bf16[256,768]{1,0:T(8,128)(2,1)}, bf16[256,768]{1,0:T(8,128)(2,1)}, bf16[256,768]{1,0:T(8,128)(2,1)}, bf16[256,768]{1,0:T(8,128)(2,1)}, bf16[3...) custom-call(s32[2]{0:T(128)} %pad_add_fusion.idx, bf16[256,192]{1,0:T(8,128)(2,1)} %get-tuple-element.120.refs_0_, ...), custom_call_target="tpu_custom_call" | custom-call | flops 14000000000 | bytes 8388608 | tf_op jit(solution)/shard_map/pallas_call | solution.py:575
  187.4 4.1 %shard_map.221 = bf16[3,192,768]{2,1,0:T(8,128)(2,1)} custom-call(bf16[1024,768]{1,0:T(8,128)(2,1)} %get-tuple-element.137.refs_0_, bf16[3,1024,192]{2,1,0:T(8,128)(2,1)} %get-tuple-element.138.refs_1_), custom_call_target="tpu_custom_call" | custom-call | flops 1000000000 | bytes 4194304 | tf_op jit(solution)/shard_map/pallas_call | solution.py:575
  193.0 4.7 %collective-permute-done.17 = bf16[256,768]{1,0:T(8,128)(2,1)S(1)} collective-permute-done((bf16[256,768]{1,0:T(8,128)(2,1)}, bf16[256,768]{1,0:T(8,128)(2,1)S(1)}, u32[]{:S(2)}, u32[]{:S(2)}) %collective-permute-start.17) | collective-permute-done | bytes 393248 | tf_op jit(solution)/shard_map/ppermute | solution.py:588
  197.7 5.9 %collective-permute-done.16.refs_1_ = bf16[256,768]{1,0:T(8,128)(2,1)} collective-permute-done((bf16[256,768]{1,0:T(8,128)(2,1)}, bf16[256,768]{1,0:T(8,128)(2,1)}, u32[]{:S(2)}, u32[]{:S(2)}) %collective-permute-start.16) | collective-permute-done | bytes 393248 | tf_op jit(solution)/shard_map/ppermute | solution.py:588
  206.9 2.5 collective-permute-start.18
  214.8 13.4 %collective-permute-done.18.refs_2_ = bf16[256,768]{1,0:T(8,128)(2,1)} collective-permute-done((bf16[256,768]{1,0:T(8,128)(2,1)}, bf16[256,768]{1,0:T(8,128)(2,1)}, u32[]{:S(2)}, u32[]{:S(2)}) %collective-permute-start.18) | collective-permute-done | bytes 393248 | tf_op jit(solution)/shard_map/ppermute | solution.py:588
  228.2 3.2 %shard_map.222.refs_0_ = bf16[256,768]{1,0:T(8,128)(2,1)} custom-call(s32[2]{0:T(128)} %pad_add_fusion.idx, bf16[256,768]{1,0:T(8,128)(2,1)} %get-tuple-element.130.refs_0_, bf16[256,768]{1,0:T(8,128)(2,1)} %collective-permute-done.16.refs_1_, bf16[256,768]{1,0:T(8,128)(2,1)} %collective-permute-done.18.refs_2_, f32[256,768]{1,0:T(8,128)} %get-tuple-element.142.refs_3_, ...), custom_call_target="tpu_custom_call" | custom-call | bytes 5242880 | tf_op jit(solution)/shard_map/pallas_call | solution.py:575
  233.6 3.9 %collective-permute-start.22 = (bf16[256,768]{1,0:T(8,128)(2,1)}, bf16[256,768]{1,0:T(8,128)(2,1)S(1)}, u32[]{:S(2)}, u32[]{:S(2)}) collective-permute-start(bf16[256,768]{1,0:T(8,128)(2,1)} %shard_map.222.refs_0_), channel_id=1, source_target_pairs={{0,1},{1,0},{2,3},{3,2},{4,5},{5,4},{6,7},{7,6},{8,9},{9,8},{10,11... | collective-permute-start | bytes 1179656 | tf_op jit(solution)/shard_map/ppermute | solution.py:588
  237.5 16.1 %collective-permute-done.21.refs_2_ = bf16[256,768]{1,0:T(8,128)(2,1)S(1)} collective-permute-done((bf16[256,768]{1,0:T(8,128)(2,1)}, bf16[256,768]{1,0:T(8,128)(2,1)S(1)}, u32[]{:S(2)}, u32[]{:S(2)}) %collective-permute-start.21) | collective-permute-done | bytes 393248 | tf_op jit(solution)/shard_map/ppermute | solution.py:588
  255.4 4.2 %collective-permute-start.29 = (bf16[256,768]{1,0:T(8,128)(2,1)S(1)}, bf16[256,768]{1,0:T(8,128)(2,1)S(1)}, u32[]{:S(2)}, u32[]{:S(2)}) collective-permute-start(bf16[256,768]{1,0:T(8,128)(2,1)S(1)} %copy-done.1), channel_id=1, source_target_pairs={{0,2},{1,3},{2,0},{3,1},{4,6},{5,7},{6,4},{7,5},{8,10},{9,11},{10,... | collective-permute-start | bytes 1179656 | tf_op jit(solution)/shard_map/ppermute | solution.py:588
  259.6 9.9 %collective-permute-done.25 = bf16[8,24,768]{2,1,0:T(8,128)(2,1)S(1)} collective-permute-done((bf16[8,24,768]{2,1,0:T(8,128)(2,1)S(1)}, bf16[8,24,768]{2,1,0:T(8,128)(2,1)S(1)}, u32[]{:S(2)}, u32[]{:S(2)}) %collective-permute-start.25) | collective-permute-done | bytes 294944 | tf_op jit(solution)/shard_map/ppermute | solution.py:588
  276.0 3.2 %shard_map.223 = f32[1024,768]{1,0:T(8,128)} custom-call(s32[2]{0:T(128)} %pad_add_fusion.idx, bf16[256,768]{1,0:T(8,128)(2,1)} %shard_map.222.refs_0_, bf16[256,768]{1,0:T(8,128)(2,1)} %copy-done.7, bf16[256,768]{1,0:T(8,128)(2,1)} %copy-done.6, bf16[256,768]{1,0:T(8,128)(2,1)} %collective-permute-done.24.refs_3_), custom_call_target="tpu_custom_call" | custom-call | bytes 5242880 | tf_op jit(solution)/shard_map/pallas_call | solution.py:575
  282.4 3.3 %collective-permute-done.30 = bf16[5,24,768]{2,1,0:T(8,128)(2,1)S(1)} collective-permute-done((bf16[5,24,768]{2,1,0:T(8,128)(2,1)S(1)}, bf16[5,24,768]{2,1,0:T(8,128)(2,1)S(1)}, u32[]{:S(2)}, u32[]{:S(2)}) %collective-permute-start.30) | collective-permute-done | bytes 184352 | tf_op jit(solution)/shard_map/ppermute | solution.py:588
  287.8 6.9 %fusion.1 = f32[4,768,768]{2,1,0:T(8,128)} fusion(bf16[4,2,768,768]{3,2,1,0:T(8,128)(2,1)} %bitcast.37), kind=kLoop, calls=%fused_computation.3 | loop fusion | flops 2359296 | bytes 14155776 | tf_op jit(solution)/shard_map/convert_element_type | solution.py:929
  295.5 2.6 shard_map.224
  298.1 6.9 %fusion = f32[4,768,768]{2,1,0:T(8,128)} fusion(bf16[4,2,768,768]{3,2,1,0:T(8,128)(2,1)} %bitcast.38), kind=kLoop, calls=%fused_computation.1 | loop fusion | flops 2359296 | bytes 14155776 | tf_op jit(solution)/shard_map/convert_element_type | solution.py:935
  (138 shorter events, 47.8 us)
Async XLA Ops:
  7.2 199.5 %reduce-scatter.2.cloned.1.call-start = ((), (), s32[]{:S(2)}) async-start(), calls=%async_computation.1 | async-start | bytes 10616832 | tf_op jit(solution)/shard_map/reduce_scatter | solution.py:795
  8.2 17.8 %collective-permute-start = (bf16[96,768]{1,0:T(8,128)(2,1)S(1)}, bf16[96,768]{1,0:T(8,128)(2,1)S(1)}, u32[]{:S(2)}, u32[]{:S(2)}) collective-permute-start(bf16[96,768]{1,0:T(8,128)(2,1)S(1)} %constant_dynamic-slice_fusion.3), channel_id=1, source_target_pairs={{0,1},{1,0},{2,3},{3,2},{4,5},{5,4},{6,7},{7,6},{8,9},{9,8},{10,11... | collective-permute-start | bytes 442376 | tf_op jit(solution)/shard_map/ppermute | solution.py:588
  11.3 14.8 %collective-permute-start.1 = (bf16[96,768]{1,0:T(8,128)(2,1)S(1)}, bf16[96,768]{1,0:T(8,128)(2,1)S(1)}, u32[]{:S(2)}, u32[]{:S(2)}) collective-permute-start(bf16[96,768]{1,0:T(8,128)(2,1)S(1)} %constant_dynamic-slice_fusion.3), channel_id=1, source_target_pairs={{0,2},{1,3},{2,0},{3,1},{4,6},{5,7},{6,4},{7,5},{8,10},{9,11},{10,... | collective-permute-start | bytes 442376 | tf_op jit(solution)/shard_map/ppermute | solution.py:588
  13.8 12.2 %collective-permute-start.2 = (bf16[96,768]{1,0:T(8,128)(2,1)S(1)}, bf16[96,768]{1,0:T(8,128)(2,1)S(1)}, u32[]{:S(2)}, u32[]{:S(2)}) collective-permute-start(bf16[96,768]{1,0:T(8,128)(2,1)S(1)} %constant_dynamic-slice_fusion.3), channel_id=1, source_target_pairs={{0,3},{1,2},{2,1},{3,0},{4,7},{5,6},{6,5},{7,4},{8,11},{9,10},{10,... | collective-permute-start | bytes 442376 | tf_op jit(solution)/shard_map/ppermute | solution.py:588
  26.1 24.3 %collective-permute-start.3 = (bf16[1024,192]{1,0:T(8,128)(2,1)}, bf16[1024,192]{1,0:T(8,128)(2,1)S(1)}, u32[]{:S(2)}, u32[]{:S(2)}) collective-permute-start(bf16[1024,192]{1,0:T(8,128)(2,1)} %get-tuple-element.88.refs_0_), channel_id=1, source_target_pairs={{0,1},{1,0},{2,3},{3,2},{4,5},{5,4},{6,7},{7,6},{8,9},{9,8},{10,11... | collective-permute-start | bytes 1179656 | tf_op jit(solution)/shard_map/ppermute | solution.py:588
  27.6 25.4 %collective-permute-start.4 = (bf16[1024,192]{1,0:T(8,128)(2,1)}, bf16[1024,192]{1,0:T(8,128)(2,1)S(1)}, u32[]{:S(2)}, u32[]{:S(2)}) collective-permute-start(bf16[1024,192]{1,0:T(8,128)(2,1)} %get-tuple-element.88.refs_0_), channel_id=1, source_target_pairs={{0,2},{1,3},{2,0},{3,1},{4,6},{5,7},{6,4},{7,5},{8,10},{9,11},{10,... | collective-permute-start | bytes 1179656 | tf_op jit(solution)/shard_map/ppermute | solution.py:588
  30.6 24.3 %collective-permute-start.6 = (bf16[3,96,768]{2,1,0:T(8,128)(2,1)S(1)}, bf16[3,96,768]{2,1,0:T(8,128)(2,1)S(1)}, u32[]{:S(2)}, u32[]{:S(2)}) collective-permute-start(bf16[3,96,768]{2,1,0:T(8,128)(2,1)S(1)} %pad_maximum_fusion.2), channel_id=1, source_target_pairs={{0,4},{4,0},{8,12},{12,8},{16,20},{20,16},{24,28},{28,24},{1,5},{5... | collective-permute-start | bytes 1327112 | tf_op jit(solution)/shard_map/ppermute | solution.py:588
  52.9 10.8 %collective-permute-start.5 = (bf16[1024,192]{1,0:T(8,128)(2,1)S(1)}, bf16[1024,192]{1,0:T(8,128)(2,1)S(1)}, u32[]{:S(2)}, u32[]{:S(2)}) collective-permute-start(bf16[1024,192]{1,0:T(8,128)(2,1)S(1)} %collective-permute-done.4.refs_2_), channel_id=1, source_target_pairs={{0,1},{1,0},{2,3},{3,2},{4,5},{5,4},{6,7},{7,6},{8,9},{9,8},{10,11... | collective-permute-start | bytes 1179656 | tf_op jit(solution)/shard_map/ppermute | solution.py:588
  90.2 21.4 %collective-permute-start.7 = (bf16[256,768]{1,0:T(8,128)(2,1)}, bf16[256,768]{1,0:T(8,128)(2,1)S(1)}, u32[]{:S(2)}, u32[]{:S(2)}) collective-permute-start(bf16[256,768]{1,0:T(8,128)(2,1)} %get-tuple-element.93), channel_id=1, source_target_pairs={{0,1},{1,0},{2,3},{3,2},{4,5},{5,4},{6,7},{7,6},{8,9},{9,8},{10,11... | collective-permute-start | bytes 1179656 | tf_op jit(solution)/shard_map/ppermute | solution.py:588
  91.8 19.9 %collective-permute-start.8 = (bf16[256,768]{1,0:T(8,128)(2,1)}, bf16[256,768]{1,0:T(8,128)(2,1)S(1)}, u32[]{:S(2)}, u32[]{:S(2)}) collective-permute-start(bf16[256,768]{1,0:T(8,128)(2,1)} %get-tuple-element.95), channel_id=1, source_target_pairs={{0,1},{1,0},{2,3},{3,2},{4,5},{5,4},{6,7},{7,6},{8,9},{9,8},{10,11... | collective-permute-start | bytes 1179656 | tf_op jit(solution)/shard_map/ppermute | solution.py:588
  111.7 17.9 %collective-permute-start.10 = (bf16[256,768]{1,0:T(8,128)(2,1)}, bf16[256,768]{1,0:T(8,128)(2,1)S(1)}, u32[]{:S(2)}, u32[]{:S(2)}) collective-permute-start(bf16[256,768]{1,0:T(8,128)(2,1)} %get-tuple-element.106), channel_id=1, source_target_pairs={{0,1},{1,0},{2,3},{3,2},{4,5},{5,4},{6,7},{7,6},{8,9},{9,8},{10,11... | collective-permute-start | bytes 1179656 | tf_op jit(solution)/shard_map/ppermute | solution.py:588
  113.2 16.4 %collective-permute-start.9 = (bf16[256,768]{1,0:T(8,128)(2,1)}, bf16[256,768]{1,0:T(8,128)(2,1)S(1)}, u32[]{:S(2)}, u32[]{:S(2)}) collective-permute-start(bf16[256,768]{1,0:T(8,128)(2,1)} %get-tuple-element.102), channel_id=1, source_target_pairs={{0,1},{1,0},{2,3},{3,2},{4,5},{5,4},{6,7},{7,6},{8,9},{9,8},{10,11... | collective-permute-start | bytes 1179656 | tf_op jit(solution)/shard_map/ppermute | solution.py:588
  130.4 157.4 %all-gather.2.cloned.1.call-start = ((), (), s32[]{:S(2)}) async-start(), calls=%async_computation.2 | async-start | bytes 10616832 | tf_op jit(solution)/shard_map/all_gather | solution.py:920
  130.9 16.4 %collective-permute-start.11 = (bf16[256,768]{1,0:T(8,128)(2,1)S(1)}, bf16[256,768]{1,0:T(8,128)(2,1)S(1)}, u32[]{:S(2)}, u32[]{:S(2)}) collective-permute-start(bf16[256,768]{1,0:T(8,128)(2,1)S(1)} %add_convert_fusion.4), channel_id=1, source_target_pairs={{0,2},{1,3},{2,0},{3,1},{4,6},{5,7},{6,4},{7,5},{8,10},{9,11},{10,... | collective-permute-start | bytes 1179656 | tf_op jit(solution)/shard_map/ppermute | solution.py:588
  152.4 7.6 %collective-permute-start.12 = (bf16[256,192]{1,0:T(8,128)(2,1)}, bf16[256,192]{1,0:T(8,128)(2,1)S(1)}, u32[]{:S(2)}, u32[]{:S(2)}) collective-permute-start(bf16[256,192]{1,0:T(8,128)(2,1)} %get-tuple-element.114), channel_id=1, source_target_pairs={{0,1},{1,0},{2,3},{3,2},{4,5},{5,4},{6,7},{7,6},{8,9},{9,8},{10,11... | collective-permute-start | bytes 294920 | tf_op jit(solution)/shard_map/ppermute | solution.py:588
  152.4 12.8 %collective-permute-start.13 = (bf16[256,192]{1,0:T(8,128)(2,1)}, bf16[256,192]{1,0:T(8,128)(2,1)S(1)}, u32[]{:S(2)}, u32[]{:S(2)}) collective-permute-start(bf16[256,192]{1,0:T(8,128)(2,1)} %get-tuple-element.117), channel_id=1, source_target_pairs={{0,2},{1,3},{2,0},{3,1},{4,6},{5,7},{6,4},{7,5},{8,10},{9,11},{10,... | collective-permute-start | bytes 294920 | tf_op jit(solution)/shard_map/ppermute | solution.py:588
  155.1 10.1 %collective-permute-start.14 = (bf16[256,192]{1,0:T(8,128)(2,1)}, bf16[256,192]{1,0:T(8,128)(2,1)S(1)}, u32[]{:S(2)}, u32[]{:S(2)}) collective-permute-start(bf16[256,192]{1,0:T(8,128)(2,1)} %get-tuple-element.118), channel_id=1, source_target_pairs={{0,3},{1,2},{2,1},{3,0},{4,7},{5,6},{6,5},{7,4},{8,11},{9,10},{10,... | collective-permute-start | bytes 294920 | tf_op jit(solution)/shard_map/ppermute | solution.py:588
  165.4 20.0 %collective-permute-start.15 = (bf16[256,768]{1,0:T(8,128)(2,1)S(1)}, bf16[256,768]{1,0:T(8,128)(2,1)S(1)}, u32[]{:S(2)}, u32[]{:S(2)}) collective-permute-start(bf16[256,768]{1,0:T(8,128)(2,1)S(1)} %add_convert_fusion.3), channel_id=1, source_target_pairs={{0,2},{1,3},{2,0},{3,1},{4,6},{5,7},{6,4},{7,5},{8,10},{9,11},{10,... | collective-permute-start | bytes 1179656 | tf_op jit(solution)/shard_map/ppermute | solution.py:588
  185.3 12.3 %collective-permute-start.17 = (bf16[256,768]{1,0:T(8,128)(2,1)}, bf16[256,768]{1,0:T(8,128)(2,1)S(1)}, u32[]{:S(2)}, u32[]{:S(2)}) collective-permute-start(bf16[256,768]{1,0:T(8,128)(2,1)} %get-tuple-element.136), channel_id=1, source_target_pairs={{0,1},{1,0},{2,3},{3,2},{4,5},{5,4},{6,7},{7,6},{8,9},{9,8},{10,11... | collective-permute-start | bytes 1179656 | tf_op jit(solution)/shard_map/ppermute | solution.py:588
  185.4 18.1 %collective-permute-start.16 = (bf16[256,768]{1,0:T(8,128)(2,1)}, bf16[256,768]{1,0:T(8,128)(2,1)}, u32[]{:S(2)}, u32[]{:S(2)}) collective-permute-start(bf16[256,768]{1,0:T(8,128)(2,1)} %get-tuple-element.132), channel_id=1, source_target_pairs={{0,1},{1,0},{2,3},{3,2},{4,5},{5,4},{6,7},{7,6},{8,9},{9,8},{10,11... | collective-permute-start | bytes 1179656 | tf_op jit(solution)/shard_map/ppermute | solution.py:588
  206.9 21.3 %collective-permute-start.18 = (bf16[256,768]{1,0:T(8,128)(2,1)}, bf16[256,768]{1,0:T(8,128)(2,1)}, u32[]{:S(2)}, u32[]{:S(2)}) collective-permute-start(bf16[256,768]{1,0:T(8,128)(2,1)} %add_convert_fusion.2), channel_id=1, source_target_pairs={{0,2},{1,3},{2,0},{3,1},{4,6},{5,7},{6,4},{7,5},{8,10},{9,11},{10,... | collective-permute-start | bytes 1179656 | tf_op jit(solution)/shard_map/ppermute | solution.py:588
  211.8 21.1 %collective-permute-start.20 = (bf16[256,768]{1,0:T(8,128)(2,1)}, bf16[256,768]{1,0:T(8,128)(2,1)S(1)}, u32[]{:S(2)}, u32[]{:S(2)}) collective-permute-start(bf16[256,768]{1,0:T(8,128)(2,1)} %shard_map.219.refs_0_), channel_id=1, source_target_pairs={{0,1},{1,0},{2,3},{3,2},{4,5},{5,4},{6,7},{7,6},{8,9},{9,8},{10,11... | collective-permute-start | bytes 1179656 | tf_op jit(solution)/shard_map/ppermute | solution.py:588
  231.4 22.4 %collective-permute-start.23 = (bf16[8,48,768]{2,1,0:T(8,128)(2,1)S(1)}, bf16[8,48,768]{2,1,0:T(8,128)(2,1)S(1)}, u32[]{:S(2)}, u32[]{:S(2)}) collective-permute-start(bf16[8,48,768]{2,1,0:T(8,128)(2,1)S(1)} %constant_dynamic-slice_fusion.1), channel_id=1, source_target_pairs={{0,8},{4,12},{8,0},{12,4},{16,24},{20,28},{24,16},{28,20},{1,9},{5... | collective-permute-start | bytes 1769480 | tf_op jit(solution)/shard_map/ppermute | solution.py:588
  233.6 20.0 %collective-permute-start.21 = (bf16[256,768]{1,0:T(8,128)(2,1)}, bf16[256,768]{1,0:T(8,128)(2,1)S(1)}, u32[]{:S(2)}, u32[]{:S(2)}) collective-permute-start(bf16[256,768]{1,0:T(8,128)(2,1)} %shard_map.222.refs_0_), channel_id=1, source_target_pairs={{0,2},{1,3},{2,0},{3,1},{4,6},{5,7},{6,4},{7,5},{8,10},{9,11},{10,... | collective-permute-start | bytes 1179656 | tf_op jit(solution)/shard_map/ppermute | solution.py:588
  233.6 20.1 %collective-permute-start.22 = (bf16[256,768]{1,0:T(8,128)(2,1)}, bf16[256,768]{1,0:T(8,128)(2,1)S(1)}, u32[]{:S(2)}, u32[]{:S(2)}) collective-permute-start(bf16[256,768]{1,0:T(8,128)(2,1)} %shard_map.222.refs_0_), channel_id=1, source_target_pairs={{0,1},{1,0},{2,3},{3,2},{4,5},{5,4},{6,7},{7,6},{8,9},{9,8},{10,11... | collective-permute-start | bytes 1179656 | tf_op jit(solution)/shard_map/ppermute | solution.py:588
  253.9 17.5 %collective-permute-start.24 = (bf16[256,768]{1,0:T(8,128)(2,1)S(1)}, bf16[256,768]{1,0:T(8,128)(2,1)}, u32[]{:S(2)}, u32[]{:S(2)}) collective-permute-start(bf16[256,768]{1,0:T(8,128)(2,1)S(1)} %collective-permute-done.21.refs_2_), channel_id=1, source_target_pairs={{0,1},{1,0},{2,3},{3,2},{4,5},{5,4},{6,7},{7,6},{8,9},{9,8},{10,11... | collective-permute-start | bytes 1179656 | tf_op jit(solution)/shard_map/ppermute | solution.py:588
  254.1 15.5 %collective-permute-start.25 = (bf16[8,24,768]{2,1,0:T(8,128)(2,1)S(1)}, bf16[8,24,768]{2,1,0:T(8,128)(2,1)S(1)}, u32[]{:S(2)}, u32[]{:S(2)}) collective-permute-start(bf16[8,24,768]{2,1,0:T(8,128)(2,1)S(1)} %constant_dynamic-slice_fusion), channel_id=1, source_target_pairs={{0,16},{4,20},{8,24},{12,28},{16,0},{20,4},{24,8},{28,12},{1,17},{... | collective-permute-start | bytes 884744 | tf_op jit(solution)/shard_map/ppermute | solution.py:588
  255.4 23.9 %collective-permute-start.29 = (bf16[256,768]{1,0:T(8,128)(2,1)S(1)}, bf16[256,768]{1,0:T(8,128)(2,1)S(1)}, u32[]{:S(2)}, u32[]{:S(2)}) collective-permute-start(bf16[256,768]{1,0:T(8,128)(2,1)S(1)} %copy-done.1), channel_id=1, source_target_pairs={{0,2},{1,3},{2,0},{3,1},{4,6},{5,7},{6,4},{7,5},{8,10},{9,11},{10,... | collective-permute-start | bytes 1179656 | tf_op jit(solution)/shard_map/ppermute | solution.py:588
  271.5 7.7 %collective-permute-start.26 = (bf16[2,24,768]{2,1,0:T(8,128)(2,1)S(1)}, bf16[2,24,768]{2,1,0:T(8,128)(2,1)S(1)}, u32[]{:S(2)}, u32[]{:S(2)}) collective-permute-start(bf16[2,24,768]{2,1,0:T(8,128)(2,1)S(1)} %get-tuple-element.182), channel_id=1, source_target_pairs={{0,1},{1,0},{2,3},{3,2},{4,5},{5,4},{6,7},{7,6},{8,9},{9,8},{10,11... | collective-permute-start | bytes 221192 | tf_op jit(solution)/shard_map/ppermute | solution.py:588
  281.2 13.5 %collective-permute-start.32 = (bf16[256,768]{1,0:T(8,128)(2,1)S(1)}, bf16[256,768]{1,0:T(8,128)(2,1)S(1)}, u32[]{:S(2)}, u32[]{:S(2)}) collective-permute-start(bf16[256,768]{1,0:T(8,128)(2,1)S(1)} %collective-permute-done.29.refs_2_), channel_id=1, source_target_pairs={{0,1},{1,0},{2,3},{3,2},{4,5},{5,4},{6,7},{7,6},{8,9},{9,8},{10,11... | collective-permute-start | bytes 1179656 | tf_op jit(solution)/shard_map/ppermute | solution.py:588
  285.8 8.9 %collective-permute-start.31 = (bf16[5,48,768]{2,1,0:T(8,128)(2,1)S(1)}, bf16[5,48,768]{2,1,0:T(8,128)(2,1)S(1)}, u32[]{:S(2)}, u32[]{:S(2)}) collective-permute-start(bf16[5,48,768]{2,1,0:T(8,128)(2,1)S(1)} %pad_maximum_fusion.3), channel_id=1, source_target_pairs={{0,8},{4,12},{8,0},{12,4},{16,24},{20,28},{24,16},{28,20},{1,9},{5... | collective-permute-start | bytes 1105928 | tf_op jit(solution)/shard_map/ppermute | solution.py:588
  294.9 10.1 %collective-permute-start.33 = (bf16[5,96,768]{2,1,0:T(8,128)(2,1)S(1)}, bf16[5,96,768]{2,1,0:T(8,128)(2,1)S(1)}, u32[]{:S(2)}, u32[]{:S(2)}) collective-permute-start(bf16[5,96,768]{2,1,0:T(8,128)(2,1)S(1)} %pad_maximum_fusion.1), channel_id=1, source_target_pairs={{0,4},{4,0},{8,12},{12,8},{16,20},{20,16},{24,28},{28,24},{1,5},{5... | collective-permute-start | bytes 2211848 | tf_op jit(solution)/shard_map/ppermute | solution.py:588
  (30 other events, 353.0 us)
Sparse Core Ops, SparseCore 0:
  129.8 76.8 reduce-scatter.1
  208.6 65.1 all-gather.1

commit v9 on v8

--- a/solution.py
+++ b/solution.py
@@ -925,21 +925,22 @@
 
     for bit in reversed(bits[3:]):
         late = joined(late, swap(late, "dp", bit), bit)
-    late = joined(late, swap(late, "dp", bits[2]), bits[2])
     grad_w_in = expert_rows.reshape(experts, 2, width, width)[:, 0].astype(F32)
-    got, _, result_three = together(
-        swap(late, "dp", bits[1]), grad_w_in, swap(result_two, "tensor", 1)
-    )
-    late = joined(late, got, bits[1])
+    got = after(swap(late, "dp", bits[2]), grad_w_in)
+    late = joined(late, got, bits[2])
     expert_rows = after(expert_rows, got)
     grad_w_down = expert_rows.reshape(experts, 2, width, width)[:, 1].astype(F32)
+    got, _, result_three = together(
+        swap(late, "dp", bits[1]), grad_w_down, swap(result_two, "tensor", 1)
+    )
+    late = joined(late, got, bits[1])
     result = whole_call(
         functools.partial(place_kernel, PIECES, shares),
         [shaped((rows, width), BF16)],
         [idx, result_share, result_one, result_two, result_three],
         moved=3 * mib,
     )[0]
-    got = after(swap(late, "dp", bits[0]), grad_w_down, result)
+    got = after(swap(late, "dp", bits[0]), result)
     late = joined(late, got, bits[0])
     grad_w_qkv = jnp.swapaxes(late[:3], 1, 2).astype(F32)
     grad_w_out = late[4].astype(F32)

time: 317 us -> 312 us (0.984)
  transfers between devices with their start and end apart: 36 -> 36, of which waited for: 16 -> 17; matrix products, arithmetic and copies ran while one was open for 6% -> 6% of each run, Pallas kernels for 28% -> 28%
where the time goes in v9:
time: 312 us
  Pallas kernels  114 us (37%)
  waiting for transfers between devices  108 us (35%)
  starting transfers between devices  48.9 us (16%)
  other arithmetic  19.8 us (6%)
  between operations  14.4 us (5%)
  local copies, waits for them, and re-layouts  6.63 us (2%)
    ppermute x34, waiting for transfers between devices, swap(): return lax.ppermute(value, axis, [(i, i ^ bit) for i in range(count)])  106 us
    pallas_call x9, Pallas kernels, whole_call(): pl.pallas_call(kernel, out_shape=outs, in_specs=specs, out_specs=[VMEM] *...  52.7 us
    ppermute x34, starting transfers between devices, swap(): return lax.ppermute(value, axis, [(i, i ^ bit) for i in range(count)])  48.8 us
    pallas_call x1, Pallas kernels, body(): pl.pallas_call(functools.partial(moe_fwd_kernel, 0, PIECES, shares, exper...  25.7 us
    pallas_call x1, Pallas kernels, body(): pl.pallas_call(functools.partial(moe_bwd_kernel, 0, shares, experts), gri...  19.3 us
    pallas_call x1, Pallas kernels, body(): pl.pallas_call(functools.partial(moe_weights_kernel, PIECES), grid=(exper...  15.8 us
    convert_element_type x1, other arithmetic, body(): grad_w_in = expert_rows.reshape(experts, 2, width, width)[:, 0].astype(F32)  7.38 us
  transfers between devices with their start and end apart: 36, of which 17 were waited for; matrix products, arithmetic and copies ran while one was open for 6% of the time, Pallas kernels for 28%

profile of v9, /device:TPU:0, one launch (start us, length us, event | category | flops | bytes accessed | tf_op | source)
XLA Modules:
  0.0 311.6 jit_solution(16620584100522277125)
XLA Ops:
  8.2 3.1 collective-permute-start
  11.3 2.6 collective-permute-start.1
  13.9 12.2 %shard_map.213 = (bf16[1024,768]{1,0:T(8,128)(2,1)}, bf16[3,1024,192]{2,1,0:T(8,128)(2,1)}, bf16[1024,192]{1,0:T(8,128)(2,1)}, bf16[1024,192]{1,0:T(8,128)(2,1)}...) custom-call(bf16[1024,768]{1,0:T(8,128)(2,1)} %refs_4_.5, ...), custom_call_target="tpu_custom_call" | custom-call | flops 6000000000 | bytes 8388608 | tf_op jit(solution)/shard_map/pallas_call | solution.py:575
  27.6 3.0 collective-permute-start.4
  30.7 19.8 %collective-permute-done.3.refs_1_ = bf16[1024,192]{1,0:T(8,128)(2,1)S(1)} collective-permute-done((bf16[1024,192]{1,0:T(8,128)(2,1)}, bf16[1024,192]{1,0:T(8,128)(2,1)S(1)}, u32[]{:S(2)}, u32[]{:S(2)}) %collective-permute-start.3) | collective-permute-done | bytes 393248 | tf_op jit(solution)/shard_map/ppermute | solution.py:588
  50.4 2.5 collective-permute-done.4.refs_2_
  55.0 8.8 %collective-permute-done.5.refs_3_ = bf16[1024,192]{1,0:T(8,128)(2,1)S(1)} collective-permute-done((bf16[1024,192]{1,0:T(8,128)(2,1)S(1)}, bf16[1024,192]{1,0:T(8,128)(2,1)S(1)}, u32[]{:S(2)}, u32[]{:S(2)}) %collective-permute-start.5) | collective-permute-done | bytes 393248 | tf_op jit(solution)/shard_map/ppermute | solution.py:588
  64.5 25.7 %shard_map.214 = (bf16[256,768]{1,0:T(8,128)(2,1)}, bf16[256,768]{1,0:T(8,128)(2,1)}, bf16[256,768]{1,0:T(8,128)(2,1)}, bf16[256,768]{1,0:T(8,128)(2,1)}, bf16[4...) custom-call(s32[2]{0:T(128)} %pad_add_fusion.idx, ...), custom_call_target="tpu_custom_call" | custom-call | flops 9663676416 | bytes 33554432 | tf_op jit(solution)/shard_map/pallas_call | solution.py:709
  92.3 19.3 %shard_map.215 = (bf16[256,768]{1,0:T(8,128)(2,1)}, bf16[256,768]{1,0:T(8,128)(2,1)}, bf16[256,768]{1,0:T(8,128)(2,1)}, bf16[256,768]{1,0:T(8,128)(2,1)}, f32[10...) custom-call(s32[2]{0:T(128)} %pad_add_fusion.idx, f32[1024,128]{1,0:T(8,128)} %get-tuple-element.97.refs_0_, ...), custom_call_target="tpu_custom_call" | custom-call | flops 9663676416 | bytes 27262976 | tf_op jit(solution)/shard_map/pallas_call | solution.py:753
  113.8 15.8 %shard_map.216 = (bf16[4,2,768,768]{3,2,1,0:T(8,128)(2,1)}, f32[8,768]{1,0:T(8,128)}) custom-call(bf16[1024,768]{1,0:T(8,128)(2,1)} %refs_5_.5, f32[1024,128]{1,0:T(8,128)} %get-tuple-element.97.refs_0_, f32[1024,128]{1,0:T(8,128)} %get-tuple-element.108.refs_1_, bf16[1024,768]{1,0:T(8,128)(2,1)} %get-tuple-element.109.refs_2_, ...), custom_call_target="tpu_custom_call" | custom-call | flops 9663676416 | bytes 27262976 | tf_op jit(solution)/shard_map/pallas_call | solution.py:778
  132.5 14.8 %collective-permute-done.11.refs_2_ = bf16[256,768]{1,0:T(8,128)(2,1)S(1)} collective-permute-done((bf16[256,768]{1,0:T(8,128)(2,1)S(1)}, bf16[256,768]{1,0:T(8,128)(2,1)S(1)}, u32[]{:S(2)}, u32[]{:S(2)}) %collective-permute-start.11) | collective-permute-done | bytes 393248 | tf_op jit(solution)/shard_map/ppermute | solution.py:588
  148.1 4.3 %shard_map.217 = (bf16[256,192]{1,0:T(8,128)(2,1)}, bf16[256,192]{1,0:T(8,128)(2,1)}, bf16[256,192]{1,0:T(8,128)(2,1)}, bf16[256,192]{1,0:T(8,128)(2,1)}, f32[25...) custom-call(s32[2]{0:T(128)} %pad_add_fusion.idx, bf16[256,768]{1,0:T(8,128)(2,1)} %get-tuple-element.101.refs_0_, ...), custom_call_target="tpu_custom_call" | custom-call | flops 300000000 | bytes 5242880 | tf_op jit(solution)/shard_map/pallas_call | solution.py:575
  152.4 2.7 collective-permute-start.13
  156.8 3.3 %shard_map.218 = bf16[4,192,768]{2,1,0:T(8,128)(2,1)} custom-call(s32[2]{0:T(128)} %pad_add_fusion.idx, bf16[1024,192]{1,0:T(8,128)(2,1)} %get-tuple-element.89.refs_0_, bf16[1024,192]{1,0:T(8,128)(2,1)} %copy-done.3, bf16[1024,192]{1,0:T(8,128)(2,1)} %copy-done.4, bf16[1024,192]{1,0:T(8,128)(2,1)} %copy-done.5, bf16[256,768]{1,0:T(8,128)(2,1)} %get-tuple-element.116.refs_4_), custom_call_target="tpu_custom_call" | custom-call | flops 300000000 | bytes 4194304 | tf_op jit(solution)/shard_map/pallas_call | solution.py:575
  160.1 5.2 %collective-permute-done.13.refs_2_ = bf16[256,192]{1,0:T(8,128)(2,1)S(1)} collective-permute-done((bf16[256,192]{1,0:T(8,128)(2,1)}, bf16[256,192]{1,0:T(8,128)(2,1)S(1)}, u32[]{:S(2)}, u32[]{:S(2)}) %collective-permute-start.13) | collective-permute-done | bytes 98336 | tf_op jit(solution)/shard_map/ppermute | solution.py:588
  165.3 2.5 collective-permute-start.15
  167.9 17.4 %shard_map.220 = (bf16[256,768]{1,0:T(8,128)(2,1)}, bf16[256,768]{1,0:T(8,128)(2,1)}, bf16[256,768]{1,0:T(8,128)(2,1)}, bf16[256,768]{1,0:T(8,128)(2,1)}, bf16[3...) custom-call(s32[2]{0:T(128)} %pad_add_fusion.idx, bf16[256,192]{1,0:T(8,128)(2,1)} %get-tuple-element.121.refs_0_, ...), custom_call_target="tpu_custom_call" | custom-call | flops 14000000000 | bytes 8388608 | tf_op jit(solution)/shard_map/pallas_call | solution.py:575
  187.4 4.1 %shard_map.221 = bf16[3,192,768]{2,1,0:T(8,128)(2,1)} custom-call(bf16[1024,768]{1,0:T(8,128)(2,1)} %get-tuple-element.138.refs_0_, bf16[3,1024,192]{2,1,0:T(8,128)(2,1)} %get-tuple-element.139.refs_1_), custom_call_target="tpu_custom_call" | custom-call | flops 1000000000 | bytes 4194304 | tf_op jit(solution)/shard_map/pallas_call | solution.py:575
  192.9 4.7 %collective-permute-done.17 = bf16[256,768]{1,0:T(8,128)(2,1)S(1)} collective-permute-done((bf16[256,768]{1,0:T(8,128)(2,1)}, bf16[256,768]{1,0:T(8,128)(2,1)S(1)}, u32[]{:S(2)}, u32[]{:S(2)}) %collective-permute-start.17) | collective-permute-done | bytes 393248 | tf_op jit(solution)/shard_map/ppermute | solution.py:588
  197.6 5.9 %collective-permute-done.16.refs_1_ = bf16[256,768]{1,0:T(8,128)(2,1)} collective-permute-done((bf16[256,768]{1,0:T(8,128)(2,1)}, bf16[256,768]{1,0:T(8,128)(2,1)}, u32[]{:S(2)}, u32[]{:S(2)}) %collective-permute-start.16) | collective-permute-done | bytes 393248 | tf_op jit(solution)/shard_map/ppermute | solution.py:588
  204.4 2.4 reduce-scatter.2.cloned.1.call-done
  207.0 2.5 collective-permute-start.18
  214.8 13.4 %collective-permute-done.18.refs_2_ = bf16[256,768]{1,0:T(8,128)(2,1)} collective-permute-done((bf16[256,768]{1,0:T(8,128)(2,1)}, bf16[256,768]{1,0:T(8,128)(2,1)}, u32[]{:S(2)}, u32[]{:S(2)}) %collective-permute-start.18) | collective-permute-done | bytes 393248 | tf_op jit(solution)/shard_map/ppermute | solution.py:588
  228.2 3.2 %shard_map.222.refs_0_ = bf16[256,768]{1,0:T(8,128)(2,1)} custom-call(s32[2]{0:T(128)} %pad_add_fusion.idx, bf16[256,768]{1,0:T(8,128)(2,1)} %get-tuple-element.131.refs_0_, bf16[256,768]{1,0:T(8,128)(2,1)} %collective-permute-done.16.refs_1_, bf16[256,768]{1,0:T(8,128)(2,1)} %collective-permute-done.18.refs_2_, f32[256,768]{1,0:T(8,128)} %get-tuple-element.143.refs_3_, ...), custom_call_target="tpu_custom_call" | custom-call | bytes 5242880 | tf_op jit(solution)/shard_map/pallas_call | solution.py:575
  232.9 3.9 %collective-permute-start.22 = (bf16[256,768]{1,0:T(8,128)(2,1)}, bf16[256,768]{1,0:T(8,128)(2,1)}, u32[]{:S(2)}, u32[]{:S(2)}) collective-permute-start(bf16[256,768]{1,0:T(8,128)(2,1)} %shard_map.222.refs_0_), channel_id=1, source_target_pairs={{0,1},{1,0},{2,3},{3,2},{4,5},{5,4},{6,7},{7,6},{8,9},{9,8},{10,11... | collective-permute-start | bytes 1179656 | tf_op jit(solution)/shard_map/ppermute | solution.py:588
  236.8 16.1 %collective-permute-done.21.refs_2_ = bf16[256,768]{1,0:T(8,128)(2,1)S(1)} collective-permute-done((bf16[256,768]{1,0:T(8,128)(2,1)}, bf16[256,768]{1,0:T(8,128)(2,1)S(1)}, u32[]{:S(2)}, u32[]{:S(2)}) %collective-permute-start.21) | collective-permute-done | bytes 393248 | tf_op jit(solution)/shard_map/ppermute | solution.py:588
  255.4 4.2 %collective-permute-start.29 = (bf16[256,768]{1,0:T(8,128)(2,1)S(1)}, bf16[256,768]{1,0:T(8,128)(2,1)S(1)}, u32[]{:S(2)}, u32[]{:S(2)}) collective-permute-start(bf16[256,768]{1,0:T(8,128)(2,1)S(1)} %copy-done.2), channel_id=1, source_target_pairs={{0,2},{1,3},{2,0},{3,1},{4,6},{5,7},{6,4},{7,5},{8,10},{9,11},{10,... | collective-permute-start | bytes 1179656 | tf_op jit(solution)/shard_map/ppermute | solution.py:588
  259.6 9.7 %collective-permute-done.25 = bf16[8,24,768]{2,1,0:T(8,128)(2,1)S(1)} collective-permute-done((bf16[8,24,768]{2,1,0:T(8,128)(2,1)S(1)}, bf16[8,24,768]{2,1,0:T(8,128)(2,1)S(1)}, u32[]{:S(2)}, u32[]{:S(2)}) %collective-permute-start.25) | collective-permute-done | bytes 294944 | tf_op jit(solution)/shard_map/ppermute | solution.py:588
  275.0 3.2 %shard_map.223 = f32[1024,768]{1,0:T(8,128)} custom-call(s32[2]{0:T(128)} %pad_add_fusion.idx, bf16[256,768]{1,0:T(8,128)(2,1)} %shard_map.222.refs_0_, bf16[256,768]{1,0:T(8,128)(2,1)} %collective-permute-done.22.refs_1_, bf16[256,768]{1,0:T(8,128)(2,1)} %copy-done.7, bf16[256,768]{1,0:T(8,128)(2,1)} %collective-permute-done.24.refs_3_), custom_call_target="tpu_custom_call" | custom-call | bytes 5242880 | tf_op jit(solution)/shard_map/pallas_call | solution.py:575
  282.0 7.4 %fusion.1 = f32[4,768,768]{2,1,0:T(8,128)} fusion(bf16[4,2,768,768]{3,2,1,0:T(8,128)(2,1)} %bitcast.37), kind=kLoop, calls=%fused_computation.3 | loop fusion | flops 2359296 | bytes 14155776 | tf_op jit(solution)/shard_map/convert_element_type | solution.py:928
  291.7 4.6 %fusion = f32[4,768,768]{2,1,0:T(8,128)} fusion(bf16[4,2,768,768]{3,2,1,0:T(8,128)(2,1)S(1)} %bitcast.38), kind=kLoop, calls=%fused_computation.1 | loop fusion | flops 2359296 | bytes 14155776 | tf_op jit(solution)/shard_map/convert_element_type | solution.py:932
  297.8 2.6 shard_map.224
  (136 shorter events, 46.4 us)
Async XLA Ops:
  7.2 199.6 %reduce-scatter.2.cloned.1.call-start = ((), (), s32[]{:S(2)}) async-start(), calls=%async_computation.1 | async-start | bytes 10616832 | tf_op jit(solution)/shard_map/reduce_scatter | solution.py:795
  8.2 17.8 %collective-permute-start = (bf16[96,768]{1,0:T(8,128)(2,1)S(1)}, bf16[96,768]{1,0:T(8,128)(2,1)S(1)}, u32[]{:S(2)}, u32[]{:S(2)}) collective-permute-start(bf16[96,768]{1,0:T(8,128)(2,1)S(1)} %constant_dynamic-slice_fusion.3), channel_id=1, source_target_pairs={{0,1},{1,0},{2,3},{3,2},{4,5},{5,4},{6,7},{7,6},{8,9},{9,8},{10,11... | collective-permute-start | bytes 442376 | tf_op jit(solution)/shard_map/ppermute | solution.py:588
  11.3 14.8 %collective-permute-start.1 = (bf16[96,768]{1,0:T(8,128)(2,1)S(1)}, bf16[96,768]{1,0:T(8,128)(2,1)S(1)}, u32[]{:S(2)}, u32[]{:S(2)}) collective-permute-start(bf16[96,768]{1,0:T(8,128)(2,1)S(1)} %constant_dynamic-slice_fusion.3), channel_id=1, source_target_pairs={{0,2},{1,3},{2,0},{3,1},{4,6},{5,7},{6,4},{7,5},{8,10},{9,11},{10,... | collective-permute-start | bytes 442376 | tf_op jit(solution)/shard_map/ppermute | solution.py:588
  13.8 12.2 %collective-permute-start.2 = (bf16[96,768]{1,0:T(8,128)(2,1)S(1)}, bf16[96,768]{1,0:T(8,128)(2,1)S(1)}, u32[]{:S(2)}, u32[]{:S(2)}) collective-permute-start(bf16[96,768]{1,0:T(8,128)(2,1)S(1)} %constant_dynamic-slice_fusion.3), channel_id=1, source_target_pairs={{0,3},{1,2},{2,1},{3,0},{4,7},{5,6},{6,5},{7,4},{8,11},{9,10},{10,... | collective-permute-start | bytes 442376 | tf_op jit(solution)/shard_map/ppermute | solution.py:588
  26.1 24.3 %collective-permute-start.3 = (bf16[1024,192]{1,0:T(8,128)(2,1)}, bf16[1024,192]{1,0:T(8,128)(2,1)S(1)}, u32[]{:S(2)}, u32[]{:S(2)}) collective-permute-start(bf16[1024,192]{1,0:T(8,128)(2,1)} %get-tuple-element.89.refs_0_), channel_id=1, source_target_pairs={{0,1},{1,0},{2,3},{3,2},{4,5},{5,4},{6,7},{7,6},{8,9},{9,8},{10,11... | collective-permute-start | bytes 1179656 | tf_op jit(solution)/shard_map/ppermute | solution.py:588
  27.6 25.4 %collective-permute-start.4 = (bf16[1024,192]{1,0:T(8,128)(2,1)}, bf16[1024,192]{1,0:T(8,128)(2,1)S(1)}, u32[]{:S(2)}, u32[]{:S(2)}) collective-permute-start(bf16[1024,192]{1,0:T(8,128)(2,1)} %get-tuple-element.89.refs_0_), channel_id=1, source_target_pairs={{0,2},{1,3},{2,0},{3,1},{4,6},{5,7},{6,4},{7,5},{8,10},{9,11},{10,... | collective-permute-start | bytes 1179656 | tf_op jit(solution)/shard_map/ppermute | solution.py:588
  30.6 24.4 %collective-permute-start.6 = (bf16[3,96,768]{2,1,0:T(8,128)(2,1)S(1)}, bf16[3,96,768]{2,1,0:T(8,128)(2,1)S(1)}, u32[]{:S(2)}, u32[]{:S(2)}) collective-permute-start(bf16[3,96,768]{2,1,0:T(8,128)(2,1)S(1)} %pad_maximum_fusion.2), channel_id=1, source_target_pairs={{0,4},{4,0},{8,12},{12,8},{16,20},{20,16},{24,28},{28,24},{1,5},{5... | collective-permute-start | bytes 1327112 | tf_op jit(solution)/shard_map/ppermute | solution.py:588
  53.0 10.8 %collective-permute-start.5 = (bf16[1024,192]{1,0:T(8,128)(2,1)S(1)}, bf16[1024,192]{1,0:T(8,128)(2,1)S(1)}, u32[]{:S(2)}, u32[]{:S(2)}) collective-permute-start(bf16[1024,192]{1,0:T(8,128)(2,1)S(1)} %collective-permute-done.4.refs_2_), channel_id=1, source_target_pairs={{0,1},{1,0},{2,3},{3,2},{4,5},{5,4},{6,7},{7,6},{8,9},{9,8},{10,11... | collective-permute-start | bytes 1179656 | tf_op jit(solution)/shard_map/ppermute | solution.py:588
  90.2 21.4 %collective-permute-start.7 = (bf16[256,768]{1,0:T(8,128)(2,1)}, bf16[256,768]{1,0:T(8,128)(2,1)S(1)}, u32[]{:S(2)}, u32[]{:S(2)}) collective-permute-start(bf16[256,768]{1,0:T(8,128)(2,1)} %get-tuple-element.94), channel_id=1, source_target_pairs={{0,1},{1,0},{2,3},{3,2},{4,5},{5,4},{6,7},{7,6},{8,9},{9,8},{10,11... | collective-permute-start | bytes 1179656 | tf_op jit(solution)/shard_map/ppermute | solution.py:588
  91.8 19.9 %collective-permute-start.8 = (bf16[256,768]{1,0:T(8,128)(2,1)}, bf16[256,768]{1,0:T(8,128)(2,1)S(1)}, u32[]{:S(2)}, u32[]{:S(2)}) collective-permute-start(bf16[256,768]{1,0:T(8,128)(2,1)} %get-tuple-element.96), channel_id=1, source_target_pairs={{0,1},{1,0},{2,3},{3,2},{4,5},{5,4},{6,7},{7,6},{8,9},{9,8},{10,11... | collective-permute-start | bytes 1179656 | tf_op jit(solution)/shard_map/ppermute | solution.py:588
  111.7 17.9 %collective-permute-start.10 = (bf16[256,768]{1,0:T(8,128)(2,1)}, bf16[256,768]{1,0:T(8,128)(2,1)S(1)}, u32[]{:S(2)}, u32[]{:S(2)}) collective-permute-start(bf16[256,768]{1,0:T(8,128)(2,1)} %get-tuple-element.107), channel_id=1, source_target_pairs={{0,1},{1,0},{2,3},{3,2},{4,5},{5,4},{6,7},{7,6},{8,9},{9,8},{10,11... | collective-permute-start | bytes 1179656 | tf_op jit(solution)/shard_map/ppermute | solution.py:588
  113.2 16.4 %collective-permute-start.9 = (bf16[256,768]{1,0:T(8,128)(2,1)}, bf16[256,768]{1,0:T(8,128)(2,1)S(1)}, u32[]{:S(2)}, u32[]{:S(2)}) collective-permute-start(bf16[256,768]{1,0:T(8,128)(2,1)} %get-tuple-element.103), channel_id=1, source_target_pairs={{0,1},{1,0},{2,3},{3,2},{4,5},{5,4},{6,7},{7,6},{8,9},{9,8},{10,11... | collective-permute-start | bytes 1179656 | tf_op jit(solution)/shard_map/ppermute | solution.py:588
  130.4 151.6 %all-gather.2.cloned.1.call-start = ((), (), s32[]{:S(2)}) async-start(), calls=%async_computation.2 | async-start | bytes 10616832 | tf_op jit(solution)/shard_map/all_gather | solution.py:920
  130.9 16.4 %collective-permute-start.11 = (bf16[256,768]{1,0:T(8,128)(2,1)S(1)}, bf16[256,768]{1,0:T(8,128)(2,1)S(1)}, u32[]{:S(2)}, u32[]{:S(2)}) collective-permute-start(bf16[256,768]{1,0:T(8,128)(2,1)S(1)} %add_convert_fusion.4), channel_id=1, source_target_pairs={{0,2},{1,3},{2,0},{3,1},{4,6},{5,7},{6,4},{7,5},{8,10},{9,11},{10,... | collective-permute-start | bytes 1179656 | tf_op jit(solution)/shard_map/ppermute | solution.py:588
  152.4 7.7 %collective-permute-start.12 = (bf16[256,192]{1,0:T(8,128)(2,1)}, bf16[256,192]{1,0:T(8,128)(2,1)S(1)}, u32[]{:S(2)}, u32[]{:S(2)}) collective-permute-start(bf16[256,192]{1,0:T(8,128)(2,1)} %get-tuple-element.115), channel_id=1, source_target_pairs={{0,1},{1,0},{2,3},{3,2},{4,5},{5,4},{6,7},{7,6},{8,9},{9,8},{10,11... | collective-permute-start | bytes 294920 | tf_op jit(solution)/shard_map/ppermute | solution.py:588
  152.4 12.8 %collective-permute-start.13 = (bf16[256,192]{1,0:T(8,128)(2,1)}, bf16[256,192]{1,0:T(8,128)(2,1)S(1)}, u32[]{:S(2)}, u32[]{:S(2)}) collective-permute-start(bf16[256,192]{1,0:T(8,128)(2,1)} %get-tuple-element.118), channel_id=1, source_target_pairs={{0,2},{1,3},{2,0},{3,1},{4,6},{5,7},{6,4},{7,5},{8,10},{9,11},{10,... | collective-permute-start | bytes 294920 | tf_op jit(solution)/shard_map/ppermute | solution.py:588
  155.1 10.1 %collective-permute-start.14 = (bf16[256,192]{1,0:T(8,128)(2,1)}, bf16[256,192]{1,0:T(8,128)(2,1)S(1)}, u32[]{:S(2)}, u32[]{:S(2)}) collective-permute-start(bf16[256,192]{1,0:T(8,128)(2,1)} %get-tuple-element.119), channel_id=1, source_target_pairs={{0,3},{1,2},{2,1},{3,0},{4,7},{5,6},{6,5},{7,4},{8,11},{9,10},{10,... | collective-permute-start | bytes 294920 | tf_op jit(solution)/shard_map/ppermute | solution.py:588
  165.3 20.0 %collective-permute-start.15 = (bf16[256,768]{1,0:T(8,128)(2,1)S(1)}, bf16[256,768]{1,0:T(8,128)(2,1)S(1)}, u32[]{:S(2)}, u32[]{:S(2)}) collective-permute-start(bf16[256,768]{1,0:T(8,128)(2,1)S(1)} %add_convert_fusion.3), channel_id=1, source_target_pairs={{0,2},{1,3},{2,0},{3,1},{4,6},{5,7},{6,4},{7,5},{8,10},{9,11},{10,... | collective-permute-start | bytes 1179656 | tf_op jit(solution)/shard_map/ppermute | solution.py:588
  185.3 12.3 %collective-permute-start.17 = (bf16[256,768]{1,0:T(8,128)(2,1)}, bf16[256,768]{1,0:T(8,128)(2,1)S(1)}, u32[]{:S(2)}, u32[]{:S(2)}) collective-permute-start(bf16[256,768]{1,0:T(8,128)(2,1)} %get-tuple-element.137), channel_id=1, source_target_pairs={{0,1},{1,0},{2,3},{3,2},{4,5},{5,4},{6,7},{7,6},{8,9},{9,8},{10,11... | collective-permute-start | bytes 1179656 | tf_op jit(solution)/shard_map/ppermute | solution.py:588
  185.4 18.1 %collective-permute-start.16 = (bf16[256,768]{1,0:T(8,128)(2,1)}, bf16[256,768]{1,0:T(8,128)(2,1)}, u32[]{:S(2)}, u32[]{:S(2)}) collective-permute-start(bf16[256,768]{1,0:T(8,128)(2,1)} %get-tuple-element.133), channel_id=1, source_target_pairs={{0,1},{1,0},{2,3},{3,2},{4,5},{5,4},{6,7},{7,6},{8,9},{9,8},{10,11... | collective-permute-start | bytes 1179656 | tf_op jit(solution)/shard_map/ppermute | solution.py:588
  207.0 21.3 %collective-permute-start.18 = (bf16[256,768]{1,0:T(8,128)(2,1)}, bf16[256,768]{1,0:T(8,128)(2,1)}, u32[]{:S(2)}, u32[]{:S(2)}) collective-permute-start(bf16[256,768]{1,0:T(8,128)(2,1)} %add_convert_fusion.2), channel_id=1, source_target_pairs={{0,2},{1,3},{2,0},{3,1},{4,6},{5,7},{6,4},{7,5},{8,10},{9,11},{10,... | collective-permute-start | bytes 1179656 | tf_op jit(solution)/shard_map/ppermute | solution.py:588
  211.8 21.1 %collective-permute-start.20 = (bf16[256,768]{1,0:T(8,128)(2,1)}, bf16[256,768]{1,0:T(8,128)(2,1)}, u32[]{:S(2)}, u32[]{:S(2)}) collective-permute-start(bf16[256,768]{1,0:T(8,128)(2,1)} %shard_map.219.refs_0_), channel_id=1, source_target_pairs={{0,1},{1,0},{2,3},{3,2},{4,5},{5,4},{6,7},{7,6},{8,9},{9,8},{10,11... | collective-permute-start | bytes 1179656 | tf_op jit(solution)/shard_map/ppermute | solution.py:588
  231.5 22.5 %collective-permute-start.23 = (bf16[8,48,768]{2,1,0:T(8,128)(2,1)S(1)}, bf16[8,48,768]{2,1,0:T(8,128)(2,1)S(1)}, u32[]{:S(2)}, u32[]{:S(2)}) collective-permute-start(bf16[8,48,768]{2,1,0:T(8,128)(2,1)S(1)} %constant_dynamic-slice_fusion.1), channel_id=1, source_target_pairs={{0,8},{4,12},{8,0},{12,4},{16,24},{20,28},{24,16},{28,20},{1,9},{5... | collective-permute-start | bytes 1769480 | tf_op jit(solution)/shard_map/ppermute | solution.py:588
  232.9 20.0 %collective-permute-start.21 = (bf16[256,768]{1,0:T(8,128)(2,1)}, bf16[256,768]{1,0:T(8,128)(2,1)S(1)}, u32[]{:S(2)}, u32[]{:S(2)}) collective-permute-start(bf16[256,768]{1,0:T(8,128)(2,1)} %shard_map.222.refs_0_), channel_id=1, source_target_pairs={{0,2},{1,3},{2,0},{3,1},{4,6},{5,7},{6,4},{7,5},{8,10},{9,11},{10,... | collective-permute-start | bytes 1179656 | tf_op jit(solution)/shard_map/ppermute | solution.py:588
  232.9 20.2 %collective-permute-start.22 = (bf16[256,768]{1,0:T(8,128)(2,1)}, bf16[256,768]{1,0:T(8,128)(2,1)}, u32[]{:S(2)}, u32[]{:S(2)}) collective-permute-start(bf16[256,768]{1,0:T(8,128)(2,1)} %shard_map.222.refs_0_), channel_id=1, source_target_pairs={{0,1},{1,0},{2,3},{3,2},{4,5},{5,4},{6,7},{7,6},{8,9},{9,8},{10,11... | collective-permute-start | bytes 1179656 | tf_op jit(solution)/shard_map/ppermute | solution.py:588
  253.9 16.5 %collective-permute-start.24 = (bf16[256,768]{1,0:T(8,128)(2,1)S(1)}, bf16[256,768]{1,0:T(8,128)(2,1)}, u32[]{:S(2)}, u32[]{:S(2)}) collective-permute-start(bf16[256,768]{1,0:T(8,128)(2,1)S(1)} %collective-permute-done.21.refs_2_), channel_id=1, source_target_pairs={{0,1},{1,0},{2,3},{3,2},{4,5},{5,4},{6,7},{7,6},{8,9},{9,8},{10,11... | collective-permute-start | bytes 1179656 | tf_op jit(solution)/shard_map/ppermute | solution.py:588
  254.1 15.2 %collective-permute-start.25 = (bf16[8,24,768]{2,1,0:T(8,128)(2,1)S(1)}, bf16[8,24,768]{2,1,0:T(8,128)(2,1)S(1)}, u32[]{:S(2)}, u32[]{:S(2)}) collective-permute-start(bf16[8,24,768]{2,1,0:T(8,128)(2,1)S(1)} %constant_dynamic-slice_fusion), channel_id=1, source_target_pairs={{0,16},{4,20},{8,24},{12,28},{16,0},{20,4},{24,8},{28,12},{1,17},{... | collective-permute-start | bytes 884744 | tf_op jit(solution)/shard_map/ppermute | solution.py:588
  255.4 22.9 %collective-permute-start.29 = (bf16[256,768]{1,0:T(8,128)(2,1)S(1)}, bf16[256,768]{1,0:T(8,128)(2,1)S(1)}, u32[]{:S(2)}, u32[]{:S(2)}) collective-permute-start(bf16[256,768]{1,0:T(8,128)(2,1)S(1)} %copy-done.2), channel_id=1, source_target_pairs={{0,2},{1,3},{2,0},{3,1},{4,6},{5,7},{6,4},{7,5},{8,10},{9,11},{10,... | collective-permute-start | bytes 1179656 | tf_op jit(solution)/shard_map/ppermute | solution.py:588
  270.6 7.7 %collective-permute-start.26 = (bf16[2,24,768]{2,1,0:T(8,128)(2,1)S(1)}, bf16[2,24,768]{2,1,0:T(8,128)(2,1)S(1)}, u32[]{:S(2)}, u32[]{:S(2)}) collective-permute-start(bf16[2,24,768]{2,1,0:T(8,128)(2,1)S(1)} %get-tuple-element.184), channel_id=1, source_target_pairs={{0,1},{1,0},{2,3},{3,2},{4,5},{5,4},{6,7},{7,6},{8,9},{9,8},{10,11... | collective-permute-start | bytes 221192 | tf_op jit(solution)/shard_map/ppermute | solution.py:588
  279.9 9.5 %collective-permute-start.30 = (bf16[5,24,768]{2,1,0:T(8,128)(2,1)S(1)}, bf16[5,24,768]{2,1,0:T(8,128)(2,1)S(1)}, u32[]{:S(2)}, u32[]{:S(2)}) collective-permute-start(bf16[5,24,768]{2,1,0:T(8,128)(2,1)S(1)} %pad_maximum_fusion.5), channel_id=1, source_target_pairs={{0,16},{4,20},{8,24},{12,28},{16,0},{20,4},{24,8},{28,12},{1,17},{... | collective-permute-start | bytes 552968 | tf_op jit(solution)/shard_map/ppermute | solution.py:588
  281.2 15.0 %collective-permute-start.32 = (bf16[256,768]{1,0:T(8,128)(2,1)S(1)}, bf16[256,768]{1,0:T(8,128)(2,1)S(1)}, u32[]{:S(2)}, u32[]{:S(2)}) collective-permute-start(bf16[256,768]{1,0:T(8,128)(2,1)S(1)} %collective-permute-done.29.refs_2_), channel_id=1, source_target_pairs={{0,1},{1,0},{2,3},{3,2},{4,5},{5,4},{6,7},{7,6},{8,9},{9,8},{10,11... | collective-permute-start | bytes 1179656 | tf_op jit(solution)/shard_map/ppermute | solution.py:588
  289.5 8.1 %collective-permute-start.31 = (bf16[5,48,768]{2,1,0:T(8,128)(2,1)S(1)}, bf16[5,48,768]{2,1,0:T(8,128)(2,1)S(1)}, u32[]{:S(2)}, u32[]{:S(2)}) collective-permute-start(bf16[5,48,768]{2,1,0:T(8,128)(2,1)S(1)} %pad_maximum_fusion.3), channel_id=1, source_target_pairs={{0,8},{4,12},{8,0},{12,4},{16,24},{20,28},{24,16},{28,20},{1,9},{5... | collective-permute-start | bytes 1105928 | tf_op jit(solution)/shard_map/ppermute | solution.py:588
  (29 other events, 337.4 us)
Sparse Core Ops, SparseCore 0:
  129.8 76.9 reduce-scatter.1
  208.6 65.1 all-gather.1
